TPU v7x, 32 devices: a whole 2x2x4 slice. The times are simulated.
32 devices in a mesh: dp: 16 (over z, x, core), seq: 2 (over y).
Axes of the slice: x: 2, y: 2, z: 4, core: 2. Of those that a mesh axis runs over, the one named last changes fastest.
Arguments:
- image_tokens: bfloat16 [16, 1024, 384], P('dp', 'seq'), may hold values from -6 to 6
- kept_index: int32 [16, 704], P('dp'), may hold values from 0 to 1023, as said below
- kept_count: int32 [16], P('dp'), may hold values from 616 to 704, as said below
- sample_valid: int32 [16], P('dp'), may hold values 0 or 1
- timestep: int32 [16], P('dp'), may hold values from 0 to 999
- class_label: int32 [16], P('dp'), may hold values from 0 to 999
- class_table: bfloat16 [1000, 384], replicated, may hold values from -6 to 6
- ada_weight: bfloat16 [384, 2304], replicated, may hold values from -0.3125 to 0.3125
- ada_bias: bfloat16 [2304], replicated, may hold values from -3 to 3
- qkv_weight: bfloat16 [384, 1152], replicated, may hold values from -0.3125 to 0.3125
- qv_bias: bfloat16 [2, 384], replicated, may hold values from -3 to 3
- rel_bias: bfloat16 [2, 6, 63], replicated, may hold values from -4 to 4
- out_weight: bfloat16 [384, 384], replicated, may hold values from -0.875 to 0.875
- out_bias: bfloat16 [384], replicated, may hold values from -2 to 2
- fc1_weight: bfloat16 [384, 1536], replicated, may hold values from -0.3125 to 0.3125
- fc1_bias: bfloat16 [1536], replicated, may hold values from -3 to 3
- fc2_weight: bfloat16 [1536, 384], replicated, may hold values from -0.15625 to 0.15625
- fc2_bias: bfloat16 [384], replicated, may hold values from -2 to 2
- grad_full: bfloat16 [16, 1024, 384], P('dp', 'seq'), may hold values from -6 to 6
- grad_masked: bfloat16 [16, 704, 384], P('dp', 'seq'), may hold values from -6 to 6
Outputs:
- out_full: bfloat16 [16, 1024, 384], P('dp', 'seq')
- out_masked: bfloat16 [16, 704, 384], P('dp', 'seq')
- grad_input: float32 [16, 1024, 384], P('dp', 'seq')
- grad_class_table: float32 [1000, 384], replicated
- grad_ada_weight: float32 [384, 2304], replicated
- grad_ada_bias: float32 [2304], replicated
- grad_qkv_weight: float32 [384, 1152], replicated
- grad_qv_bias: float32 [2, 384], replicated
- grad_rel_bias: float32 [2, 6, 63], replicated
- grad_out_weight: float32 [384, 384], replicated
- grad_out_bias: float32 [384], replicated
- grad_fc1_weight: float32 [384, 1536], replicated
- grad_fc1_bias: float32 [1536], replicated
- grad_fc2_weight: float32 [1536, 384], replicated
- grad_fc2_bias: float32 [384], replicated
Inputs may be any that keep to these rules, and one draw needn't show every extreme that they name: `kept_index`: the first kept_count[s] slots of sample s hold distinct positions in rising order; later slots hold 0. `kept_count`: some sample has 704 kept tokens in every draw.
All inputs are finite; a program needn't handle non-finite values. No bound on the sum of `sample_valid` on one device may be relied on, other than what follows from the above.
Results may differ from a plain program's by a relative error of at most 0.015.
The roundings to bfloat16 on the way count: a program that leaves them out, or rounds other values in their place, can miss the bound.
Values may be sent and summed in bfloat16 or wider, within the bound.
No kernel may reach another device: no remote copies, remote signals or barrier semaphores. Data moves between devices by JAX's collectives and lax.ppermute only.
A program may use at most 192 MiB of HBM per device.

v0:
```python
import math

import jax
import jax.numpy as jnp
from jax import lax
from jax.sharding import PartitionSpec as P

D = 384
HEADS = 6
HDIM = 64
GRID = 32


highest = lax.Precision.HIGHEST
big_negative = -1e30


def layer_norm(value):
    average = jnp.mean(value, axis=-1, keepdims=True)
    centred = value - average
    variance = jnp.mean(centred * centred, axis=-1, keepdims=True)
    return centred * lax.rsqrt(variance + 1e-06)


def time_features(moments, width):
    half_width = width // 2
    frequency = jnp.exp(-math.log(10000.0) * jnp.arange(half_width, dtype=jnp.float32) / half_width)
    angles = moments.astype(jnp.float32)[:, None] * frequency[None, :]
    return jnp.concatenate([jnp.cos(angles), jnp.sin(angles)], axis=-1)


def one_hot(values, length):
    return (values[..., None] == jnp.arange(length, dtype=jnp.int32)).astype(jnp.float32)


def offset_table():
    first = jnp.arange(GRID, dtype=jnp.int32)
    offsets = first[None, :] - first[:, None] + GRID - 1
    return one_hot(offsets, 2 * GRID - 1)


def split_heads(value):
    return value.reshape(value.shape[0], value.shape[1], HEADS, HDIM)


def merge_heads(value):
    return value.reshape(value.shape[0], value.shape[1], HEADS * HDIM)


def forward_product(value, weight):
    return lax.dot_general(
        value, weight, (((2,), (0,)), ((), ())), preferred_element_type=jnp.float32
    )


def back_product(grad, weight):
    return lax.dot_general(
        grad, weight, (((2,), (1,)), ((), ())), preferred_element_type=jnp.float32
    )


def contract(left, right):
    return lax.dot_general(
        left, right, (((0, 1), (0, 1)), ((), ())), preferred_element_type=jnp.float32
    )


def position_bias(tables, query_where, key_where):
    tables_low = tables.astype(jnp.bfloat16)
    rows_query = one_hot(query_where // GRID, GRID).astype(jnp.bfloat16)
    rows_key = one_hot(key_where // GRID, GRID).astype(jnp.bfloat16)
    cols_query = one_hot(query_where % GRID, GRID).astype(jnp.bfloat16)
    cols_key = one_hot(key_where % GRID, GRID).astype(jnp.bfloat16)
    row_part = jnp.einsum(
        "sqi,hij->shqj", rows_query, tables_low[0], preferred_element_type=jnp.float32
    ).astype(jnp.bfloat16)
    row_bias = jnp.einsum("shqj,skj->shqk", row_part, rows_key, preferred_element_type=jnp.float32)
    col_part = jnp.einsum(
        "sqi,hij->shqj", cols_query, tables_low[1], preferred_element_type=jnp.float32
    ).astype(jnp.bfloat16)
    col_bias = jnp.einsum("shqj,skj->shqk", col_part, cols_key, preferred_element_type=jnp.float32)
    return row_bias + col_bias


def table_grads(grad_scores, query_where, key_where):
    rows_key = one_hot(key_where // GRID, GRID).astype(jnp.bfloat16)
    cols_key = one_hot(key_where % GRID, GRID).astype(jnp.bfloat16)
    row_part = jnp.einsum(
        "shqk,skj->shqj", grad_scores, rows_key, preferred_element_type=jnp.float32
    )
    row_grad = jnp.einsum(
        "shqj,sqi->hij", row_part, one_hot(query_where // GRID, GRID), precision=highest
    )
    col_part = jnp.einsum(
        "shqk,skj->shqj", grad_scores, cols_key, preferred_element_type=jnp.float32
    )
    col_grad = jnp.einsum(
        "shqj,sqi->hij", col_part, one_hot(query_where % GRID, GRID), precision=highest
    )
    return jnp.stack([row_grad, col_grad])


def attention_scores(query_low, keys_all, bias, key_live):
    raw = jnp.einsum(
        "sqhd,skhd->shqk",
        split_heads(query_low),
        split_heads(keys_all),
        preferred_element_type=jnp.float32,
    )
    scores = raw * (1.0 / math.sqrt(HDIM)) + bias
    return jnp.where(key_live[:, None, None, :], scores, big_negative)


def forward_pass(tokens, query_where, key_where, key_live, modulation, weights):
    (
        qkv_weight,
        qv_bias_f,
        tables,
        out_weight,
        out_bias_f,
        fc1_weight,
        fc1_bias_f,
        fc2_weight,
        fc2_bias_f,
    ) = weights
    shift_one, scale_one, gate_one, shift_two, scale_two, gate_two = [
        modulation[:, number][:, None, :] for number in range(6)
    ]
    normed = layer_norm(tokens)
    lowered = (normed * (1.0 + scale_one) + shift_one).astype(jnp.bfloat16)
    projected = forward_product(lowered, qkv_weight)
    query_low = (projected[..., :D] + qv_bias_f[0]).astype(jnp.bfloat16)
    keys_low = projected[..., D : 2 * D].astype(jnp.bfloat16)
    values_low = (projected[..., 2 * D :] + qv_bias_f[1]).astype(jnp.bfloat16)
    keys_all, values_all = (
        lax.all_gather(keys_low, "seq", axis=1, tiled=True),
        lax.all_gather(values_low, "seq", axis=1, tiled=True),
    )
    bias = position_bias(tables, query_where, key_where)
    scores = attention_scores(query_low, keys_all, bias, key_live)
    maximum = jnp.max(scores, axis=-1, keepdims=True)
    expanded = jnp.exp(scores - maximum)
    total = jnp.sum(expanded, axis=-1, keepdims=True)
    attention = expanded / total
    mixed = jnp.einsum(
        "shqk,skhd->sqhd",
        attention.astype(jnp.bfloat16),
        split_heads(values_all),
        preferred_element_type=jnp.float32,
    )
    merged = merge_heads(mixed).astype(jnp.bfloat16)
    attended = forward_product(merged, out_weight) + out_bias_f
    middle = tokens + gate_one * attended
    second_norm = layer_norm(middle)
    second = (second_norm * (1.0 + scale_two) + shift_two).astype(jnp.bfloat16)
    hidden_pre = forward_product(second, fc1_weight) + fc1_bias_f
    hidden = jax.nn.gelu(hidden_pre).astype(jnp.bfloat16)
    branch = forward_product(hidden, fc2_weight) + fc2_bias_f
    output = middle + gate_two * branch
    saved = {
        "tokens": tokens,
        "normed": normed,
        "lowered": lowered,
        "query_low": query_low,
        "keys_low": keys_low,
        "values_low": values_low,
        "keys_all": keys_all,
        "values_all": values_all,
        "bias": bias,
        "maximum": maximum,
        "total": total,
        "merged": merged,
        "attended": attended,
        "middle": middle,
        "second_norm": second_norm,
        "second": second,
        "hidden_pre": hidden_pre,
        "hidden": hidden,
        "branch": branch,
    }
    return (output, saved)


def backward_pass(saved, cotangent, modulation, weights, query_where, key_where, key_live):
    (
        qkv_weight,
        qv_bias_f,
        tables,
        out_weight,
        out_bias_f,
        fc1_weight,
        fc1_bias_f,
        fc2_weight,
        fc2_bias_f,
    ) = weights
    shift_one, scale_one, gate_one, shift_two, scale_two, gate_two = [
        modulation[:, number][:, None, :] for number in range(6)
    ]
    score_scale = 1.0 / math.sqrt(HDIM)
    grad_branch = (gate_two * cotangent).astype(jnp.bfloat16)
    grad_gate_two = jnp.sum(cotangent * saved["branch"], axis=1)
    grad_fc2 = contract(saved["hidden"], grad_branch)
    grad_fc2_bias = jnp.sum(grad_branch, axis=(0, 1), dtype=jnp.float32)
    grad_hidden = back_product(grad_branch, fc2_weight)
    unused_gelu, gelu_pull = jax.vjp(jax.nn.gelu, saved["hidden_pre"])
    grad_pre = gelu_pull(grad_hidden)[0].astype(jnp.bfloat16)
    grad_fc1 = contract(saved["second"], grad_pre)
    grad_fc1_bias = jnp.sum(grad_pre, axis=(0, 1), dtype=jnp.float32)
    grad_second = back_product(grad_pre, fc1_weight)
    grad_shift_two = jnp.sum(grad_second, axis=1)
    grad_scale_two = jnp.sum(grad_second * saved["second_norm"], axis=1)
    unused_norm, second_pull = jax.vjp(layer_norm, saved["middle"])
    grad_middle = cotangent + second_pull(grad_second * (1.0 + scale_two))[0]
    grad_attended = (gate_one * grad_middle).astype(jnp.bfloat16)
    grad_gate_one = jnp.sum(grad_middle * saved["attended"], axis=1)
    grad_out = contract(saved["merged"], grad_attended)
    grad_out_bias = jnp.sum(grad_attended, axis=(0, 1), dtype=jnp.float32)
    grad_merged = back_product(grad_attended, out_weight).astype(jnp.bfloat16)
    keys_all, values_all = (saved["keys_all"], saved["values_all"])
    query_low = saved["query_low"]
    scores = attention_scores(query_low, keys_all, saved["bias"], key_live)
    attention = jnp.exp(scores - saved["maximum"]) / saved["total"]
    attention_low = attention.astype(jnp.bfloat16)
    grad_weights = jnp.einsum(
        "sqhd,skhd->shqk",
        split_heads(grad_merged),
        split_heads(values_all),
        preferred_element_type=jnp.float32,
    )
    delta = jnp.sum(attention * grad_weights, axis=-1, keepdims=True)
    grad_scores = (attention * (grad_weights - delta)).astype(jnp.bfloat16)
    grad_query = (
        merge_heads(
            jnp.einsum(
                "shqk,skhd->sqhd",
                grad_scores,
                split_heads(keys_all),
                preferred_element_type=jnp.float32,
            )
        )
        * score_scale
    )
    grad_tables = table_grads(grad_scores, query_where, key_where)
    keys_term = (
        merge_heads(
            jnp.einsum(
                "shqk,sqhd->skhd",
                grad_scores,
                split_heads(query_low),
                preferred_element_type=jnp.float32,
            )
        )
        * score_scale
    )
    values_term = merge_heads(
        jnp.einsum(
            "shqk,sqhd->skhd",
            attention_low,
            split_heads(grad_merged),
            preferred_element_type=jnp.float32,
        )
    )
    grad_keys, grad_values = (
        lax.psum_scatter(keys_term, "seq", scatter_dimension=1, tiled=True),
        lax.psum_scatter(values_term, "seq", scatter_dimension=1, tiled=True),
    )
    grad_projected = jnp.concatenate(
        [
            grad_query.astype(jnp.bfloat16),
            grad_keys.astype(jnp.bfloat16),
            grad_values.astype(jnp.bfloat16),
        ],
        axis=-1,
    )
    grad_qkv = contract(saved["lowered"], grad_projected)
    grad_qv = jnp.stack(
        [
            jnp.sum(grad_projected[..., :D], axis=(0, 1), dtype=jnp.float32),
            jnp.sum(grad_projected[..., 2 * D :], axis=(0, 1), dtype=jnp.float32),
        ]
    )
    grad_lowered = back_product(grad_projected, qkv_weight)
    grad_shift_one = jnp.sum(grad_lowered, axis=1)
    grad_scale_one = jnp.sum(grad_lowered * saved["normed"], axis=1)
    unused_first, first_pull = jax.vjp(layer_norm, saved["tokens"])
    grad_tokens = grad_middle + first_pull(grad_lowered * (1.0 + scale_one))[0]
    grad_mods = jnp.stack(
        [
            grad_shift_one,
            grad_scale_one,
            grad_gate_one,
            grad_shift_two,
            grad_scale_two,
            grad_gate_two,
        ],
        axis=1,
    )
    return {
        "tokens": grad_tokens,
        "mods": grad_mods,
        "qkv": grad_qkv,
        "qv": grad_qv,
        "tables": grad_tables,
        "out": grad_out,
        "out_bias": grad_out_bias,
        "fc1": grad_fc1,
        "fc1_bias": grad_fc1_bias,
        "fc2": grad_fc2,
        "fc2_bias": grad_fc2_bias,
    }


def condition_rows(labels, moments, class_table, width):
    label_hot = one_hot(labels, class_table.shape[0])
    class_rows = jnp.dot(
        label_hot.astype(jnp.bfloat16), class_table, preferred_element_type=jnp.float32
    )
    conditioned = class_rows + time_features(moments, width)
    activated = jax.nn.silu(conditioned).astype(jnp.bfloat16)
    return (label_hot, conditioned, activated)


def modulation_grads(grad_mods, label_hot, conditioned, activated, ada_weight):
    grad_ada = jnp.dot(activated.astype(jnp.float32).T, grad_mods, precision=highest)
    grad_ada_bias = jnp.sum(grad_mods, axis=0)
    grad_activated = jnp.dot(grad_mods, ada_weight.astype(jnp.float32).T, precision=highest)
    unused_silu, silu_pull = jax.vjp(jax.nn.silu, conditioned)
    grad_conditioned = silu_pull(grad_activated)[0]
    grad_table = jnp.dot(label_hot.T, grad_conditioned, precision=highest)
    return (grad_table, grad_ada, grad_ada_bias)


def body(
    image_tokens,
    kept_index,
    kept_count,
    sample_valid,
    timestep,
    class_label,
    class_table,
    ada_weight,
    ada_bias,
    qkv_weight,
    qv_bias,
    rel_bias,
    out_weight,
    out_bias,
    fc1_weight,
    fc1_bias,
    fc2_weight,
    fc2_bias,
    grad_full,
    grad_masked,
):
    samples, block_rows, width = image_tokens.shape
    slot_rows = grad_masked.shape[1]
    sequence = block_rows * lax.axis_size("seq")
    seq_place = lax.axis_index("seq")
    label_hot, conditioned, activated = condition_rows(class_label, timestep, class_table, width)
    modulation = (
        jnp.dot(activated, ada_weight, preferred_element_type=jnp.float32)
        + ada_bias.astype(jnp.float32)
    ).reshape(samples, 6, width)
    offsets = offset_table()
    tables = jnp.einsum("cho,ijo->chij", rel_bias.astype(jnp.float32), offsets, precision=highest)
    weights = (
        qkv_weight,
        qv_bias.astype(jnp.float32),
        tables,
        out_weight,
        out_bias.astype(jnp.float32),
        fc1_weight,
        fc1_bias.astype(jnp.float32),
        fc2_weight,
        fc2_bias.astype(jnp.float32),
    )
    valid = sample_valid.astype(jnp.float32)
    own_where = seq_place * block_rows + jnp.arange(block_rows, dtype=jnp.int32)
    full_query_where = jnp.broadcast_to(own_where[None, :], (samples, block_rows))
    full_key_where = jnp.broadcast_to(
        jnp.arange(sequence, dtype=jnp.int32)[None, :], (samples, sequence)
    )
    full_key_live = full_key_where >= 0
    full_output, full_saved = forward_pass(
        image_tokens.astype(jnp.float32),
        full_query_where,
        full_key_where,
        full_key_live,
        modulation,
        weights,
    )
    whole = lax.all_gather(image_tokens, "seq", axis=1, tiled=True)
    slot_start = seq_place * slot_rows
    picked = lax.dynamic_slice_in_dim(kept_index, slot_start, slot_rows, 1)
    slot_numbers = jnp.arange(kept_index.shape[1], dtype=jnp.int32)
    masked_key_live = slot_numbers[None, :] < kept_count[:, None]
    masked_query_live = lax.dynamic_slice_in_dim(masked_key_live, slot_start, slot_rows, 1)
    masked_tokens = jnp.take_along_axis(whole, picked[:, :, None], axis=1).astype(jnp.float32)
    masked_output, masked_saved = forward_pass(
        masked_tokens, picked, kept_index, masked_key_live, modulation, weights
    )
    full_cotangent = grad_full.astype(jnp.float32) * valid[:, None, None]
    masked_weight = valid[:, None] * masked_query_live.astype(jnp.float32)
    masked_cotangent = grad_masked.astype(jnp.float32) * masked_weight[:, :, None]
    full_grads = backward_pass(
        full_saved,
        full_cotangent,
        modulation,
        weights,
        full_query_where,
        full_key_where,
        full_key_live,
    )
    masked_grads = backward_pass(
        masked_saved, masked_cotangent, modulation, weights, picked, kept_index, masked_key_live
    )
    sample_numbers = jnp.arange(samples, dtype=jnp.int32)[:, None]
    spread = (
        jnp.zeros((samples, sequence, width), jnp.float32)
        .at[sample_numbers, picked]
        .add(masked_grads["tokens"])
    )
    slot_share = lax.psum_scatter(
        spread.astype(jnp.bfloat16), "seq", scatter_dimension=1, tiled=True
    ).astype(jnp.float32)
    grad_input = full_grads["tokens"] + slot_share
    grad_mods = (full_grads["mods"] + masked_grads["mods"]).reshape(samples, 6 * width)
    grad_rel = jnp.einsum(
        "chij,ijo->cho", full_grads["tables"] + masked_grads["tables"], offsets, precision=highest
    )
    layer_terms = [
        full_grads["qkv"] + masked_grads["qkv"],
        full_grads["qv"] + masked_grads["qv"],
        grad_rel,
        full_grads["out"] + masked_grads["out"],
        full_grads["out_bias"] + masked_grads["out_bias"],
        full_grads["fc1"] + masked_grads["fc1"],
        full_grads["fc1_bias"] + masked_grads["fc1_bias"],
        full_grads["fc2"] + masked_grads["fc2"],
        full_grads["fc2_bias"] + masked_grads["fc2_bias"],
    ]
    grad_table, grad_ada, grad_ada_bias = modulation_grads(
        grad_mods, label_hot, conditioned, activated, ada_weight
    )
    summed = lax.psum(tuple([grad_table, grad_ada, grad_ada_bias] + layer_terms), ("dp", "seq"))
    summed = tuple(summed)
    out_full = (full_output * valid[:, None, None]).astype(jnp.bfloat16)
    out_masked = (masked_output * masked_weight[:, :, None]).astype(jnp.bfloat16)
    return (out_full, out_masked, grad_input) + summed


def solution(mesh):
    placed = (
        P("dp", "seq", None),
        P("dp", None),
        P("dp"),
        P("dp"),
        P("dp"),
        P("dp"),
        P(),
        P(),
        P(),
        P(),
        P(),
        P(),
        P(),
        P(),
        P(),
        P(),
        P(),
        P(),
        P("dp", "seq", None),
        P("dp", "seq", None),
    )
    return jax.shard_map(
        body,
        mesh=mesh,
        in_specs=placed,
        out_specs=(
            P("dp", "seq", None),
            P("dp", "seq", None),
            P("dp", "seq", None),
            P(),
            P(),
            P(),
            P(),
            P(),
            P(),
            P(),
            P(),
            P(),
            P(),
            P(),
            P(),
        ),
        check_vma=False,
    )
```

profile of v0, /device:TPU:0, one launch (start us, length us, event | category | flops | bytes accessed | tf_op | source)
XLA Modules:
  0.0 1006.8 jit_solution(12695760200433180785)
XLA Ops:
  20.4 12.8 %all_gather.16 = bf16[1,1024,384]{2,1,0:T(8,128)(2,1)} all-gather(bf16[1,512,384]{2,1,0:T(8,128)(2,1)S(1)} %slice.136), channel_id=1, replica_groups=mesh['dp'=16,'seq'=2] {'seq'}, dimensions={1}, use_global_device_ids=true | all-gather | bytes 1179648 | tf_op jit(solution)/shard_map/all_gather | solution.py:136
  34.7 12.9 %all_gather.15 = bf16[1,1024,384]{2,1,0:T(8,128)(2,1)} all-gather(bf16[1,512,384]{2,1,0:T(8,128)(2,1)} %get-tuple-element.137), channel_id=1, replica_groups=mesh['dp'=16,'seq'=2] {'seq'}, dimensions={1}, use_global_device_ids=true | all-gather | bytes 1179648 | tf_op jit(solution)/shard_map/all_gather | solution.py:137
  47.6 2.3 copy.126
  49.9 6.4 fusion.233
  56.3 6.5 fusion.37
  62.7 14.2 %add_add_fusion = f32[6,512,1024]{2,1,0:T(8,128)} fusion(f32[6,512,1024]{2,1,0:T(8,128)} %fusion.37, f32[6,512,1024]{2,1,0:T(8,128)} %fusion.233, bf16[6,32,32]{1,2,0:T(8,128)(2,1)S(1)} %copy.131, s32[1024]{0:T(1024)S(1)} %fusion.180, s32[512]{0:T(512)S(1)} %add_select_fusion.2), kind=kOutput, calls=%fused_computation.7 | convolution fusion | flops 217300992 | bytes 37767168 | tf_op jit(solution)/shard_map/shqj,skj->shqk/dot_general | solution.py:81
  77.0 15.3 %fusion.229 = (f32[6,512]{1,0:T(8,128)S(1)}, f32[6,512,1024]{2,1,0:T(8,128)}) fusion(f32[6,512,1024]{2,1,0:T(8,128)} %add_add_fusion), kind=kOutput, calls=%fused_computation.398 | output fusion | flops 6292479 | bytes 25178112 | tf_op jit(solution)/shard_map/sub | solution.py:142
  92.3 15.2 %fusion.24 = bf16[6,64,512]{2,1,0:T(8,128)(2,1)} fusion(bf16[1024,6,64]{0,2,1:T(8,128)(2,1)S(1)} %bitcast.431, f32[6,512]{1,0:T(8,128)S(1)} %get-tuple-element.149, f32[6,512,1024]{2,1,0:T(8,128)} %add_add_fusion), kind=kOutput, calls=%fused_computation.57 | convolution fusion | flops 412291072 | bytes 13774848 | tf_op jit(solution)/shard_map/shqk,skhd->sqhd/dot_general | solution.py:145
  107.5 2.4 fusion.228
  111.5 4.0 convert_reduce_fusion
  115.5 2.5 fusion.232
  126.3 12.6 %fusion.9 = f32[6,64,1024]{2,1,0:T(8,128)} fusion(bf16[512,6,64]{0,2,1:T(8,128)(2,1)} %bitcast.436, f32[6,512]{1,0:T(8,128)S(1)} %get-tuple-element.149, f32[6,512,1024]{2,1,0:T(8,128)} %add_add_fusion), kind=kOutput, calls=%fused_computation.28 | convolution fusion | flops 412094464 | bytes 14561280 | tf_op jit(solution)/shard_map/shqk,sqhd->skhd/dot_general | solution.py:256
  138.9 10.6 %multiply_reduce_fusion = (f32[6,512]{1,0:T(8,128)S(1)}, f32[6,512,1024]{2,1,0:T(8,128)}) fusion(f32[6,512,1024]{2,1,0:T(8,128)} %get-tuple-element.150, f32[6,512]{1,0:T(8,128)S(1)} %get-tuple-element.149, bf16[512,6,64]{0,2,1:T(8,128)(2,1)} %bitcast.437, bf16[1024,6,64]{0,2,1:T(8,128)(2,1)} %bitcast.430), kind=kOutput, calls=%fused_computation.5 | convolution fusion | flops 412087296 | bytes 26370048 | tf_op jit(solution)/shard_map/sqhd,skhd->shqk/dot_general | solution.py:224
  152.0 6.0 multiply_convert_fusion
  158.0 2.9 convolution_multiply_fusion
  162.0 11.1 %all_gather.17 = bf16[1,1024,384]{2,1,0:T(8,128)(2,1)} all-gather(bf16[1,512,384]{2,1,0:T(8,128)(2,1)} %param.20), channel_id=1, replica_groups=mesh['dp'=16,'seq'=2] {'seq'}, dimensions={1}, use_global_device_ids=true | all-gather | bytes 1179648 | tf_op jit(solution)/shard_map/all_gather | solution.py:392
  174.3 3.3 gather_fusion
  186.4 12.1 %all_gather.19 = bf16[1,704,384]{2,1,0:T(8,128)(2,1)} all-gather(bf16[1,352,384]{2,1,0:T(8,128)(2,1)} %slice.137), channel_id=1, replica_groups=mesh['dp'=16,'seq'=2] {'seq'}, dimensions={1}, use_global_device_ids=true | all-gather | bytes 811008 | tf_op jit(solution)/shard_map/all_gather | solution.py:136
  200.5 8.9 all_gather.18
  211.5 4.9 fusion.234
  216.5 4.7 fusion.40
  221.1 8.7 add_select_fusion
  229.8 9.3 fusion.230
  239.1 9.7 fusion.29
  253.2 2.5 convert_reduce_fusion.1
  263.2 4.4 multiply_reduce_fusion.1
  271.0 2.3 convert_reduce_fusion.8
  273.4 9.8 fusion.20
  283.2 4.7 copy.144
  289.7 3.7 convolution_multiply_fusion.1
  293.4 4.6 copy.142
  299.3 391.1 %all-reduce.10 = (bf16[1,704,384]{2,0,1:T(2,128)(2,1)}, bf16[1,704,384]{2,0,1:T(2,128)(2,1)}) all-reduce(f32[1,704,384]{2,0,1:T(1,128)} %copy.144, f32[1,704,384]{2,0,1:T(1,128)} %copy.142), channel_id=5, replica_groups=mesh['dp'=16,'seq'=2] {'seq'}, use_global_device_ids=true, to_apply=%region_23.24.clone | all-reduce | flops 540672 | bytes 3244032
  697.1 4.9 scatter_custom_fusion
  702.1 2.6 copy.147
  706.4 2.4 fusion.221
  708.8 3.4 fusion.92
  712.3 2.8 convert_reduce_fusion.6
  720.2 2.3 convolution_add_fusion.3
  722.6 2.7 convolution_add_fusion.2
  728.5 3.3 fusion.231
  731.8 2.3 copy.140
  740.4 5.9 convert_reduce_fusion.3
  752.5 3.1 fusion.146
  757.9 5.4 fusion.128
  767.2 42.8 %all-reduce.3 = (f32[2304]{0:T(1024)}, f32[2,384]{1,0:T(2,128)}, f32[2,6,63]{2,1,0:T(8,128)S(1)}, f32[384]{0:T(512)}, f32[1536]{0:T(1024)}, /*index=5*/f32[384]{0:T(512)}) all-reduce(f32[2304]{0:T(1024)S(1)} %add.575, f32[2,384]{1,0:T(2,128)S(1)} %maximum_add_fusion.1, ...), channel_id=1, replica_groups=mesh['dp'=16,'seq'=2] {'dp','seq'}, use_global_device_ids=true, to_apply=%region_42.43 | all-reduce | flops 6132 | bytes 49056 | tf_op jit(solution)/shard_map/psum | solution.py:445
  812.7 174.0 %all-reduce.9.cloned.1.call-done = (f32[1000,384]{1,0:T(8,128)}, f32[384,2304]{1,0:T(8,128)}, f32[384,1152]{1,0:T(8,128)}, f32[384,384]{1,0:T(8,128)}, f32[384,1536]{1,0:T(8,128)}, /*index=5*/f32[1536,384]{1,0:T(8,128)}) async-done(((f32[1000,384]{1,0:T(8,128)}, f32[384,2304]{1,0:T(8,128)}, f32[384,1152]{1,0:T(8,128)}, f32[384,384]{1,0:T(8,128)}, f32[384,1536]{1,0:T(8,128)}, ...) | async-done | bytes 12152848 | tf_op jit(solution)/shard_map/psum | solution.py:445
  986.7 2.6 copy.183
  989.3 4.2 copy.184
  (452 shorter events, 100.8 us)
Async XLA Ops:
  7.2 7.2 copy-start
  7.2 7.5 copy-start.118
  7.2 7.6 copy-start.134
  7.2 8.4 copy-start.25
  7.2 718.1 %reduce-scatter.6.cloned.1.call-start = ((), (), s32[]{:S(2)}) async-start(), calls=%async_computation.4 | async-start | bytes 2359296 | tf_op jit(solution)/shard_map/reduce_scatter | solution.py:265
  7.3 55.4 %copy-start.78 = (s32[512]{0:T(512)}, s32[512]{0:T(512)S(1)}, u32[]{:S(2)}) copy-start(s32[512]{0:T(512)S(1)} %add_select_fusion.2) | copy-start | bytes 6148
  7.3 49.0 %copy-start.76 = (s32[512]{0:T(512)}, s32[512]{0:T(512)S(1)}, u32[]{:S(2)}) copy-start(s32[512]{0:T(512)S(1)} %add_select_fusion.3) | copy-start | bytes 6148
  7.3 48.9 %copy-start.56 = (s32[1024]{0:T(1024)}, s32[1024]{0:T(1024)S(1)}, u32[]{:S(2)}) copy-start(s32[1024]{0:T(1024)S(1)} %add_select_fusion.1) | copy-start | bytes 12292
  7.4 55.4 %copy-start.60 = (s32[1024]{0:T(1024)}, s32[1024]{0:T(1024)S(1)}, u32[]{:S(2)}) copy-start(s32[1024]{0:T(1024)S(1)} %fusion.180) | copy-start | bytes 12292
  7.4 8.7 copy-start.99
  9.5 6.6 copy-start.101
  9.5 6.6 copy-start.103
  10.2 97.2 %copy-start.86 = (f32[384]{0:T(512)}, f32[384]{0:T(512)S(1)}, u32[]{:S(2)}) copy-start(f32[384]{0:T(512)S(1)} %convert_element_type.768) | copy-start | bytes 4612
  10.9 8.4 copy-start.82
  10.9 8.4 copy-start.84
  14.8 96.4 %copy-start.95 = (f32[384]{0:T(512)}, f32[384]{0:T(512)S(1)}, u32[]{:S(2)}) copy-start(f32[384]{0:T(512)S(1)} %get-tuple-element.91) | copy-start | bytes 4612
  15.5 47.2 %copy-start.47 = (bf16[6,32,32]{1,2,0:T(8,128)(2,1)}, bf16[6,32,32]{1,2,0:T(8,128)(2,1)S(1)}, u32[]{:S(2)}) copy-start(bf16[6,32,32]{1,2,0:T(8,128)(2,1)S(1)} %copy.131) | copy-start | bytes 36868
  15.6 40.6 %copy-start.46 = (bf16[6,32,32]{1,2,0:T(8,128)(2,1)}, bf16[6,32,32]{1,2,0:T(8,128)(2,1)S(1)}, u32[]{:S(2)}) copy-start(bf16[6,32,32]{1,2,0:T(8,128)(2,1)S(1)} %copy.130) | copy-start | bytes 36868
  20.4 29.5 %copy-start.11 = (bf16[1,512,384]{1,2,0:T(8,128)(2,1)}, bf16[1,512,384]{1,2,0:T(8,128)(2,1)S(1)}, u32[]{:S(2)}) copy-start(bf16[1,512,384]{1,2,0:T(8,128)(2,1)S(1)} %copy.127) | copy-start | bytes 1179652
  34.7 21.6 %copy-start.6 = (bf16[1,1024,384]{1,2,0:T(8,128)(2,1)}, bf16[1,1024,384]{1,2,0:T(8,128)(2,1)S(1)}, u32[]{:S(2)}) copy-start(bf16[1,1024,384]{1,2,0:T(8,128)(2,1)S(1)} %copy.128) | copy-start | bytes 2359300
  77.0 15.3 %copy-start.44 = (bf16[1,1024,384]{1,2,0:T(8,128)(2,1)S(1)}, bf16[1,1024,384]{1,2,0:T(8,128)(2,1)}, u32[]{:S(2)}) copy-start(bf16[1,1024,384]{1,2,0:T(8,128)(2,1)} %copy.126) | copy-start | bytes 2359300
  92.2 15.2 %copy-start.10 = (bf16[384,384]{1,0:T(8,128)(2,1)S(1)}, bf16[384,384]{1,0:T(8,128)(2,1)}, u32[]{:S(2)}) copy-start(bf16[384,384]{1,0:T(8,128)(2,1)} %param.32) | copy-start | bytes 884740
  123.6 15.2 %copy-start.109 = (f32[512]{0:T(512)}, f32[512]{0:T(512)S(1)}, u32[]{:S(2)}) copy-start(f32[512]{0:T(512)S(1)} %negate_multiply_fusion.3) | copy-start | bytes 6148
  138.9 588.4 %reduce-scatter.4.cloned.1.call-start = ((), (), s32[]{:S(2)}) async-start(), calls=%async_computation.3 | async-start | bytes 2359296 | tf_op jit(solution)/shard_map/reduce_scatter | solution.py:264
  138.9 10.7 %slice-start.4 = ((s8[12582912]{0:T(1024)(128)(4,1)}), s8[4194304]{0:T(1024)(128)(4,1)S(1)}, s32[]{:S(2)}) async-start(s8[12582912]{0:T(1024)(128)(4,1)} %bitcast.407), calls=%async_computation.11 | async-start | bytes 8388608
  138.9 11.9 %slice-start.5 = ((s8[12582912]{0:T(1024)(128)(4,1)}), s8[4194304]{0:T(1024)(128)(4,1)S(1)}, s32[]{:S(2)}) async-start(s8[12582912]{0:T(1024)(128)(4,1)} %bitcast.407), calls=%async_computation.12 | async-start | bytes 8388608
  138.9 13.0 %slice-start.6 = ((s8[12582912]{0:T(1024)(128)(4,1)}), s8[4194304]{0:T(1024)(128)(4,1)S(1)}, s32[]{:S(2)}) async-start(s8[12582912]{0:T(1024)(128)(4,1)} %bitcast.407), calls=%async_computation.13 | async-start | bytes 8388608
  161.1 579.2 %reduce-scatter.8.cloned.1.call-start = ((), (), s32[]{:S(2)}) async-start(), calls=%async_computation.5 | async-start | bytes 1179648 | tf_op jit(solution)/shard_map/reduce_scatter | solution.py:423
  162.0 54.5 %copy-start.58 = (s32[704]{0:T(1024)}, s32[704]{0:T(1024)S(1)}, u32[]{:S(2)}) copy-start(s32[704]{0:T(1024)S(1)} %get-tuple-element.98) | copy-start | bytes 8452
  239.1 9.7 copy-start.69
  250.4 7.1 copy-start.4
  250.7 6.8 copy-start.71
  283.2 6.5 copy-start.16
  289.7 8.3 copy-start.135
  298.0 394.1 %copy-start.117 = (s32[1,352,1]{1,2,0:T(1,128)S(1)}, s32[1,352,1]{1,2,0:T(1,128)}, u32[]{:S(2)}) copy-start(s32[1,352,1]{1,2,0:T(1,128)} %get-tuple-element.147) | copy-start | bytes 4228
  704.6 282.1 %all-reduce.9.cloned.1.call-start = ((), (), s32[]{:S(2)}) async-start(), calls=%async_computation.6 | async-start | bytes 24305664 | tf_op jit(solution)/shard_map/psum | solution.py:445
  712.3 6.2 copy-start.107
  712.3 6.8 copy-start.18
  712.3 6.7 copy-start.30
  712.3 7.9 copy-start.5
  712.3 7.9 copy-start.72
  740.3 7.8 copy-start.92
  740.4 7.8 copy-start.102
  740.4 7.7 copy-start.104
  756.3 7.7 slice-start.2
  757.9 6.0 slice-start.3
  757.9 6.0 copy-start.57
  765.9 45.6 %copy-start.43 = (f32[1,512,384]{1,2,0:T(8,128)S(1)}, f32[1,512,384]{1,2,0:T(8,128)}, u32[]{:S(2)}) copy-start(f32[1,512,384]{1,2,0:T(8,128)} %get-tuple-element.140) | copy-start | bytes 2359300
  (102 other events, 293.3 us)
Sparse Core Ops, SparseCore 0:
  139.0 26.3 reduce-scatter.5
  167.7 29.3 reduce-scatter.3
  704.8 18.3 reduce-scatter.7
  751.8 234.8 all-reduce.8
where the time goes:
time: 1010 us
  blocking collectives  492 us (49%)
  matrix products  187 us (19%)
  waiting for transfers between devices  174 us (17%)
  local copies, waits for them, and re-layouts  70 us (7%)
  other arithmetic  64.5 us (6%)
  between operations  19.2 us (2%)
    unnamed x1, blocking collectives  391 us
    psum x1, waiting for transfers between devices, body(): lax.psum(tuple([grad_table, grad_ada, grad_ada_bias] + layer_terms), ('dp...  174 us
    psum x1, blocking collectives, body(): lax.psum(tuple([grad_table, grad_ada, grad_ada_bias] + layer_terms), ('dp...  42.8 us
    unnamed x307, local copies, waits for them, and re-layouts  32 us
    all_gather x2, blocking collectives, forward_pass(): lax.all_gather(keys_low, 'seq', axis=1, tiled=True)  24.9 us
    dot_general x2, matrix products, forward_pass(): jnp.einsum('shqk,skhd->sqhd', attention.astype(jnp.bfloat16), split_heads...  24.9 us
    sub x2, other arithmetic, forward_pass(): expanded = jnp.exp(scores - maximum)  24.6 us
    dot_general x2, matrix products, position_bias(): jnp.einsum('shqj,skj->shqk', col_part, cols_key, preferred_element_type=j...  22.9 us
  transfers between devices with their start and end apart: 4, of which 1 were waited for; matrix products, arithmetic and copies ran while one was open for 18% of the time, Pallas kernels for 0%

commit v1 on v0

v1 whole, which is shorter than its diff:
```python
import functools
import math

import jax
import jax.numpy as jnp
from jax import lax
from jax.experimental import pallas as pl
from jax.experimental.pallas import tpu as pltpu
from jax.sharding import PartitionSpec as P

D = 384
HEADS = 6
HDIM = 64
GRID = 32
FF = 1536
CHUNK = 512

AXES = ("dp", "seq")
F32 = jnp.float32
BF16 = jnp.bfloat16
MIB = 1024 * 1024
GELU_A = math.sqrt(2.0 / math.pi)
GELU_B = 0.044715

highest = lax.Precision.HIGHEST
big_negative = -1e30
vmem = pl.BlockSpec(memory_space=pltpu.VMEM)
smem = pl.BlockSpec(memory_space=pltpu.SMEM)


def round_up(value, step):
    return -(-value // step) * step


def blocks_of(first, count, most):
    pieces = -(-count // most)
    size = round_up(-(-count // pieces), 16)
    found = []
    at = 0
    while at < count:
        found.append((first + at, min(size, count - at)))
        at += size
    return found


def mm(left, right):
    return lax.dot_general(left, right, (((1,), (0,)), ((), ())), preferred_element_type=F32)


def mm_t(left, right):
    return lax.dot_general(left, right, (((1,), (1,)), ((), ())), preferred_element_type=F32)


def norm_parts(value):
    average = jnp.mean(value, axis=-1, keepdims=True)
    centred = value - average
    variance = jnp.mean(centred * centred, axis=-1, keepdims=True)
    inverse = lax.rsqrt(variance + 1e-06)
    return (centred * inverse, inverse)


def norm_back(normed, inverse, grad):
    first = jnp.mean(grad, axis=-1, keepdims=True)
    second = jnp.mean(grad * normed, axis=-1, keepdims=True)
    return inverse * (grad - first - normed * second)


def place_onehot(position):
    lane = lax.broadcasted_iota(jnp.int32, (position.shape[0], 2 * GRID), 1)
    wanted = jnp.where(lane < GRID, position // GRID, position % GRID + GRID)
    return (lane == wanted).astype(F32).astype(BF16)


def prep_kernel(
    start_ref, tok_ref, kept_ref, picked_ref, where_ref, mod_ref, weight_ref, qv_ref, table_ref,
    qaug_ref, kaug_ref, vaug_ref, a_ref, slot_ref, mask_ref, qs_ref,
):
    total = tok_ref.shape[0]
    own = qaug_ref.shape[1] - picked_ref.shape[0]
    slots = picked_ref.shape[0]
    shift, scale = mod_ref[0:1, :], mod_ref[1:2, :]
    normed, unused = norm_parts(tok_ref[...].astype(F32))
    lowered = (normed * (1.0 + scale) + shift).astype(BF16)
    a_ref[...] = lowered
    query = (mm(lowered, weight_ref[:, :D]) + qv_ref[0:1, :]).astype(BF16)
    scaled = (query.astype(F32) * (1.0 / math.sqrt(HDIM))).astype(BF16)
    qs_ref[...] = scaled
    keys = mm(lowered, weight_ref[:, D : 2 * D]).astype(BF16)
    values = (mm(lowered, weight_ref[:, 2 * D :]) + qv_ref[1:2, :]).astype(BF16)
    key_place = place_onehot(lax.broadcasted_iota(jnp.int32, (total, 1), 0))
    lane = lax.broadcasted_iota(jnp.int32, (total, HDIM), 1)
    ones = (lane == 0).astype(F32).astype(BF16)
    for head in range(HEADS):
        cols = slice(head * HDIM, (head + 1) * HDIM)
        kaug_ref[head] = jnp.concatenate([keys[:, cols], key_place], axis=1)
        vaug_ref[head] = jnp.concatenate([values[:, cols], ones], axis=1)
    chosen = (picked_ref[...] == lax.broadcasted_iota(jnp.int32, (slots, total), 1)).astype(F32)
    chosen = chosen.astype(BF16)
    slot_ref[:, :D] = mm(chosen, tok_ref[...]).astype(BF16)
    slot_ref[:, D:] = mm(chosen, lowered).astype(BF16)
    slot_query = mm(chosen, scaled).astype(BF16)
    own_query = qs_ref[pl.ds(pl.multiple_of(start_ref[0], 16), own), :]
    offsets = mm(place_onehot(where_ref[...]), table_ref[...]).astype(BF16)
    for head in range(HEADS):
        cols = slice(head * HDIM, (head + 1) * HDIM)
        qaug_ref[head, :own] = jnp.concatenate([own_query[:, cols], offsets[:own, cols]], axis=1)
        qaug_ref[head, own:] = jnp.concatenate([slot_query[:, cols], offsets[own:, cols]], axis=1)
    held = kept_ref.shape[0]
    hit = kept_ref[...] == lax.broadcasted_iota(jnp.int32, (held, total), 1)
    count = jnp.sum(hit.astype(F32), axis=0, keepdims=True)
    mask_ref[...] = jnp.broadcast_to(jnp.where(count > 0.0, 0.0, big_negative), mask_ref.shape)


def attend_kernel(own, qaug_ref, kaug_ref, vaug_ref, mask_ref, o_ref, lse_ref):
    rows = qaug_ref.shape[1]
    spans = [(at, size, False) for at, size in blocks_of(0, own, 256)]
    spans += [(at, size, True) for at, size in blocks_of(own, rows - own, 256)]

    def pair(group, carry):
        for at, size, masked in spans:
            outs, logs = [], []
            for side in range(2):
                head = 2 * group + side
                scores = mm_t(qaug_ref[head, at : at + size, :], kaug_ref[head])
                if masked:
                    scores = scores + mask_ref[0:1, :]
                top = jnp.max(scores, axis=-1, keepdims=True)
                spread = jnp.exp(scores - top).astype(BF16)
                mixed = mm(spread, vaug_ref[head])
                total = mixed[:, HDIM : HDIM + 1]
                outs.append(mixed[:, :HDIM] * (1.0 / total))
                logs.append(jnp.broadcast_to(top + jnp.log(total), (size, HDIM)))
            o_ref[group, at : at + size, :] = jnp.concatenate(outs, axis=1)
            lse_ref[group, at : at + size, :] = jnp.concatenate(logs, axis=1)
        return carry

    lax.fori_loop(0, HEADS // 2, pair, 0)


def feed_kernel(
    own, o_ref, tok_ref, slot_ref, cot_full_ref, cot_slot_ref, wgt_ref, mod_ref,
    wout_ref, bout_ref, w1_ref, b1_ref, w2_ref, b2_ref, extra_ref,
    out_full_ref, out_slot_ref, dm_ref, do_ref, small_ref, pay_ref, g1_ref, g2_ref, go_ref, gb1_ref,
):
    rows = o_ref.shape[1]
    slots = rows - own
    g1_ref[...] = jnp.zeros(g1_ref.shape, F32)
    g2_ref[...] = jnp.zeros(g2_ref.shape, F32)
    go_ref[...] = jnp.zeros(go_ref.shape, F32)
    gb1_ref[...] = jnp.zeros(gb1_ref.shape, F32)
    small_ref[...] = jnp.zeros(small_ref.shape, F32)
    gate1, shift2, scale2, gate2 = [mod_ref[n : n + 1, :] for n in range(2, 6)]

    def part(x_ref, cot_ref, out_ref, base, size):
        def step(index, carry):
            at = pl.multiple_of(index * size, 16)
            here = pl.ds(at, size)
            there = pl.ds(pl.multiple_of(base + index * size, 16), size)
            weight = wgt_ref[there, :]
            merged = jnp.concatenate([o_ref[n, there, :] for n in range(HEADS // 2)], axis=1)
            merged = merged.astype(BF16)
            attended = mm(merged, wout_ref[...]) + bout_ref[...]
            middle = x_ref[here, :D].astype(F32) + gate1 * attended
            normed, inverse = norm_parts(middle)
            second = (normed * (1.0 + scale2) + shift2).astype(BF16)
            second_t = second.T
            cot = cot_ref[here, :].astype(F32) * weight
            dz_f = gate2 * cot
            dz = dz_f.astype(BF16)
            branch = jnp.broadcast_to(b2_ref[...], (size, D))
            back = jnp.zeros((size, D), F32)
            for c in range(FF // CHUNK):
                cols = slice(c * CHUNK, (c + 1) * CHUNK)
                u = mm(second, w1_ref[:, cols]) + b1_ref[:, cols]
                square = u * u
                t = jnp.tanh(GELU_A * u * (1.0 + GELU_B * square))
                cdf = 0.5 * (1.0 + t)
                hidden = (u * cdf).astype(BF16)
                slope = cdf + (0.5 * GELU_A) * u * (1.0 - t * t) * (1.0 + (3.0 * GELU_B) * square)
                branch = branch + mm(hidden, w2_ref[cols, :])
                du_f = slope * mm_t(dz, w2_ref[cols, :])
                du = du_f.astype(BF16)
                back = back + mm_t(du, w1_ref[:, cols])
                g2_ref[cols, :] += mm(hidden.T, dz)
                g1_ref[:, cols] += mm(second_t, du)
                gb1_ref[:, cols] += jnp.sum(du.astype(F32), axis=0, keepdims=True)
            out_ref[here, :] = ((middle + gate2 * branch) * weight).astype(BF16)
            dmid = cot + norm_back(normed, inverse, back * (1.0 + scale2))
            dm_ref[there, :] = dmid
            datt = (gate1 * dmid).astype(BF16)
            do_ref[there, :] = mm_t(datt, wout_ref[...]).astype(BF16)
            go_ref[...] += mm(merged.T, datt)
            sums = [
                dmid * attended, back, back * normed, cot * branch,
                dz.astype(F32), datt.astype(F32),
            ]
            for n, value in enumerate(sums):
                small_ref[n : n + 1, :] += jnp.sum(value, axis=0, keepdims=True)
            return carry

        count = x_ref.shape[0] // size
        lax.fori_loop(0, count, step, 0)

    part(tok_ref, cot_full_ref, out_full_ref, 0, blocks_of(0, own, 256)[0][1])
    part(slot_ref, cot_slot_ref, out_slot_ref, own, blocks_of(0, slots, 256)[0][1])
    for n in range(4):
        pay_ref[n * D : (n + 1) * D, :] = g1_ref[:, n * D : (n + 1) * D].astype(BF16)
    pay_ref[FF : 2 * FF, :] = g2_ref[...].astype(BF16)
    pay_ref[2 * FF : 2 * FF + D, :] = go_ref[...].astype(BF16)
    base = 2 * FF + D
    heads = [gb1_ref[:, n * D : (n + 1) * D] for n in range(4)]
    heads += [small_ref[4:5, :], small_ref[5:6, :], jnp.zeros((10, D), F32)]
    pay_ref[base : base + 16, :] = jnp.concatenate(heads, axis=0).astype(BF16)
    pay_ref[base + 16 :, :] = extra_ref[...]


def attend_back_kernel(
    own, qaug_ref, kaug_ref, vaug_ref, mask_ref, o_ref, lse_ref, do_ref, where_ref,
    dq_ref, dk_ref, dv_ref, tab_ref, dkt_ref, dvt_ref,
):
    rows = qaug_ref.shape[1]
    spans = [(at, size, False) for at, size in blocks_of(0, own, 256)]
    spans += [(at, size, True) for at, size in blocks_of(own, rows - own, 256)]

    def pair(group, carry):
        dkt_ref[...] = jnp.zeros(dkt_ref.shape, F32)
        dvt_ref[...] = jnp.zeros(dvt_ref.shape, F32)
        tab_ref[group] = jnp.zeros(tab_ref.shape[1:], F32)
        for at, size, masked in spans:
            place_t = place_onehot(where_ref[at : at + size, :]).T
            dqs, tabs = [], []
            for side in range(2):
                head = 2 * group + side
                lanes = slice(side * HDIM, (side + 1) * HDIM)
                query = qaug_ref[head, at : at + size, :]
                keys = kaug_ref[head]
                scores = mm_t(query, keys)
                if masked:
                    scores = scores + mask_ref[0:1, :]
                weights = jnp.exp(scores - lse_ref[group, at : at + size, side * HDIM : side * HDIM + 1])
                grad_out = do_ref[group, at : at + size, lanes]
                delta = jnp.sum(
                    grad_out.astype(F32) * o_ref[group, at : at + size, lanes], axis=-1, keepdims=True
                )
                dp = mm_t(grad_out, vaug_ref[head, :, :HDIM])
                ds = (weights * (dp - delta)).astype(BF16)
                found = mm(ds, keys)
                dqs.append(found[:, :HDIM] * (1.0 / math.sqrt(HDIM)))
                tabs.append(found[:, HDIM:].astype(BF16))
                dkt_ref[lanes, :] += mm(query[:, :HDIM].T, ds)
                dvt_ref[lanes, :] += mm(grad_out.T, weights.astype(BF16))
            dq_ref[group, at : at + size, :] = jnp.concatenate(dqs, axis=1).astype(BF16)
            tab_ref[group] += mm(place_t, jnp.concatenate(tabs, axis=1))
        dk_ref[group] = dkt_ref[...].astype(BF16).T
        dv_ref[group] = dvt_ref[...].astype(BF16).T
        return carry

    lax.fori_loop(0, HEADS // 2, pair, 0)


def prep_back_kernel(
    own, start_ref, tok_ref, a_ref, slot_ref, picked_ref, mod_ref, weight_ref,
    dq_ref, dk_ref, dv_ref, dm_ref,
    pay_ref, small_ref, dx_ref, dx_own_ref, dxs_ref,
):
    total = tok_ref.shape[0]
    rows = dq_ref.shape[1]
    slots = rows - own
    scale = mod_ref[1:2, :]
    start = pl.multiple_of(start_ref[0], 16)
    here = pl.ds(start, own)

    def joined(ref, span):
        return jnp.concatenate([ref[n, span, :] for n in range(HEADS // 2)], axis=1)

    every = slice(0, total)
    dk, dv = joined(dk_ref, every), joined(dv_ref, every)
    dq_own, dq_slot = joined(dq_ref, slice(0, own)), joined(dq_ref, slice(own, rows))
    lowered_t = a_ref[...].T
    gq = mm(a_ref[here, :].T, dq_own) + mm(slot_ref[:, D:].T, dq_slot)
    pay_ref[0:D, :] = gq.astype(BF16)
    pay_ref[D : 2 * D, :] = mm(lowered_t, dk).astype(BF16)
    pay_ref[2 * D : 3 * D, :] = mm(lowered_t, dv).astype(BF16)
    column = lambda value: jnp.sum(value.astype(F32), axis=0, keepdims=True)
    normed, inverse = norm_parts(tok_ref[...].astype(F32))
    da = mm_t(dk, weight_ref[:, D : 2 * D]) + mm_t(dv, weight_ref[:, 2 * D :])
    shift_sum, scale_sum = column(da), column(da * normed)
    dxs_ref[...] = norm_back(normed, inverse, da * (1.0 + scale))
    own_normed, own_inverse = norm_parts(tok_ref[here, :].astype(F32))
    da = mm_t(dq_own, weight_ref[:, :D])
    shift_sum, scale_sum = shift_sum + column(da), scale_sum + column(da * own_normed)
    dxs_ref[here, :] += dm_ref[:own, :] + norm_back(own_normed, own_inverse, da * (1.0 + scale))
    slot_normed, slot_inverse = norm_parts(slot_ref[:, :D].astype(F32))
    da = mm_t(dq_slot, weight_ref[:, :D])
    shift_sum, scale_sum = shift_sum + column(da), scale_sum + column(da * slot_normed)
    spread = dm_ref[own:, :] + norm_back(slot_normed, slot_inverse, da * (1.0 + scale))
    chosen = (picked_ref[...] == lax.broadcasted_iota(jnp.int32, (slots, total), 1)).astype(F32)
    dxs_ref[...] += mm(chosen.astype(BF16).T, spread.astype(BF16))
    dx_ref[...] = dxs_ref[...].astype(BF16)
    dx_own_ref[...] = dxs_ref[here, :]
    parts = [shift_sum, scale_sum, column(dq_own) + column(dq_slot), column(dv)]
    small_ref[...] = jnp.concatenate(parts + [jnp.zeros((4, D), F32)], axis=0)


def call(kernel, outs, scratch, args, specs=None, flops=0, limit=48):
    return pl.pallas_call(
        kernel,
        out_shape=[jax.ShapeDtypeStruct(shape, dtype) for shape, dtype in outs],
        in_specs=specs if specs is not None else [vmem] * len(args),
        out_specs=[vmem] * len(outs),
        scratch_shapes=[pltpu.VMEM(shape, dtype) for shape, dtype in scratch],
        compiler_params=pltpu.CompilerParams(vmem_limit_bytes=limit * MIB),
        cost_estimate=pl.CostEstimate(flops=flops, bytes_accessed=4 * MIB, transcendentals=0),
    )(*args)


def reduce_all(value, dp, seq):
    rows = value.shape[0]
    place = lax.axis_index("dp")
    side = place % 2
    swap = [(n, n ^ 1) for n in range(dp)]
    groups = [
        [(2 * pair + core) * seq + at for pair in range(dp // 2) for at in range(seq)]
        for core in range(2)
    ]
    peers = dp // 2 * seq
    halves = value.reshape(2, rows // 2, D)
    keep = lax.dynamic_index_in_dim(halves, side, 0, keepdims=False)
    send = lax.dynamic_index_in_dim(halves, 1 - side, 0, keepdims=False)
    got = lax.ppermute(send, "dp", swap)
    mine = (keep.astype(F32) + got.astype(F32)).astype(BF16)
    pieces = lax.all_to_all(
        mine.reshape(peers, rows // 2 // peers, D), AXES, 0, 0, axis_index_groups=groups
    )
    chunk = jnp.sum(pieces.astype(F32), axis=0).astype(BF16)
    wide = jnp.broadcast_to(chunk[None], (peers,) + chunk.shape)
    half = lax.all_to_all(wide, AXES, 0, 0, axis_index_groups=groups).reshape(rows // 2, D)
    other = lax.ppermute(half, "dp", swap)
    first = jnp.where(side == 0, half, other)
    second = jnp.where(side == 0, other, half)
    return jnp.concatenate([first, second], axis=0)


def gather_tokens(tokens, seq):
    rows = tokens.shape[0]
    me = lax.axis_index("seq")
    whole = jnp.zeros((seq, rows, D), tokens.dtype)
    whole = lax.dynamic_update_index_in_dim(whole, tokens, me, 0)
    for step in range(1, seq):
        came = lax.ppermute(tokens, "seq", [(n, (n + step) % seq) for n in range(seq)])
        whole = lax.dynamic_update_index_in_dim(whole, came, (me - step) % seq, 0)
    return whole.reshape(seq * rows, D)


def scatter_rows(partial, own, seq):
    rows = own.shape[0]
    me = lax.axis_index("seq")
    blocks = partial.reshape(seq, rows, D)
    for step in range(1, seq):
        block = lax.dynamic_index_in_dim(blocks, (me + step) % seq, 0, keepdims=False)
        own = own + lax.ppermute(block, "seq", [(n, (n + step) % seq) for n in range(seq)]).astype(F32)
    return own


def time_features(moments):
    half_width = D // 2
    frequency = jnp.exp(-math.log(10000.0) * jnp.arange(half_width, dtype=F32) / half_width)
    angles = moments.astype(F32)[:, None] * frequency[None, :]
    return jnp.concatenate([jnp.cos(angles), jnp.sin(angles)], axis=-1)


def offset_hot():
    first = jnp.arange(GRID, dtype=jnp.int32)
    offsets = first[None, :] - first[:, None] + GRID - 1
    return (offsets[..., None] == jnp.arange(2 * GRID - 1, dtype=jnp.int32)).astype(F32)


def bias_table(rel_bias):
    both = jnp.einsum("cho,ijo->cihj", rel_bias.astype(F32), offset_hot(), precision=highest)
    empty = jnp.zeros_like(both[0])
    top = jnp.concatenate([both[0], empty], axis=-1)
    low = jnp.concatenate([empty, both[1]], axis=-1)
    return jnp.concatenate([top, low], axis=0).reshape(2 * GRID, HEADS * 2 * GRID).astype(BF16)


def body(
    dp, seq, image_tokens, kept_index, kept_count, sample_valid, timestep, class_label, class_table,
    ada_weight, ada_bias, qkv_weight, qv_bias, rel_bias, out_weight, out_bias, fc1_weight,
    fc1_bias, fc2_weight, fc2_bias, grad_full, grad_masked,
):
    samples, own, width = image_tokens.shape
    held = kept_index.shape[1]
    slots = grad_masked.shape[1]
    padded = round_up(slots, 16)
    rows = own + padded
    total = own * seq
    everyone = dp * samples
    classes = class_table.shape[0]
    dp_place, seq_place = lax.axis_index("dp"), lax.axis_index("seq")
    start = (seq_place * own).astype(jnp.int32).reshape(1)

    conditioned = jnp.take(class_table, class_label, axis=0).astype(F32) + time_features(timestep)
    gate = jax.nn.sigmoid(conditioned)
    activated = (conditioned * gate).astype(BF16)
    slope = gate * (1.0 + conditioned * (1.0 - gate))
    modulation = jnp.dot(activated, ada_weight, preferred_element_type=F32) + ada_bias.astype(F32)
    modulation = jnp.pad(modulation.reshape(samples, 6, D), ((0, 0), (0, 2), (0, 0)))
    table = bias_table(rel_bias)
    valid = sample_valid.astype(F32)

    digits = jnp.stack([class_label // GRID, class_label % GRID], axis=1).astype(F32)
    digits = jnp.pad(digits, ((0, 0), (0, D - 2)))
    info = jnp.stack([activated.astype(F32), slope, digits], axis=0)
    info = info * (seq_place == 0).astype(F32)
    extra_rows = round_up(2 * FF + D + 16 + 3 * everyone, dp * seq * 16) - (2 * FF + D + 16)
    spread = (jnp.arange(everyone)[:, None] == dp_place * samples + jnp.arange(samples)[None, :])
    info = jnp.einsum("es,nsd->end", spread.astype(F32), info, precision=highest)
    info = info.transpose(1, 0, 2).reshape(3 * everyone, D).astype(BF16)
    info = jnp.pad(info, ((0, extra_rows - 3 * everyone), (0, 0)))

    slot_numbers = jnp.arange(held, dtype=jnp.int32)
    live_all = slot_numbers[None, :] < kept_count[:, None]
    slot_start = seq_place * slots
    outs = []
    for s in range(samples):
        tokens = image_tokens[s]
        whole = gather_tokens(tokens, seq)
        kept = jnp.where(live_all[s], kept_index[s], -1)[:, None]
        picked = lax.dynamic_slice_in_dim(kept_index[s], slot_start, slots, 0)
        live = lax.dynamic_slice_in_dim(live_all[s], slot_start, slots, 0)
        picked = jnp.pad(picked, (0, padded - slots))[:, None]
        where = jnp.concatenate([start + jnp.arange(own, dtype=jnp.int32), picked[:, 0]])[:, None]
        weight = valid[s] * jnp.concatenate(
            [jnp.ones((own,), F32), jnp.pad(live.astype(F32), (0, padded - slots))]
        )
        cot_slot = jnp.pad(grad_masked[s], ((0, padded - slots), (0, 0)))
        qaug, kaug, vaug, lowered, slot, mask = call(
            prep_kernel,
            [
                ((HEADS, rows, 128), BF16), ((HEADS, total, 128), BF16), ((HEADS, total, 128), BF16),
                ((total, D), BF16), ((padded, 2 * D), BF16), ((8, total), F32),
            ],
            [((total, D), BF16)],
            [start, whole, kept, picked, where, modulation[s], qkv_weight, qv_bias.astype(F32), table],
            specs=[smem] + [vmem] * 8,
        )
        mixed, lse = call(
            functools.partial(attend_kernel, own),
            [((HEADS // 2, rows, 128), F32), ((HEADS // 2, rows, 128), F32)],
            [],
            [qaug, kaug, vaug, mask],
        )
        out_full, out_slot, dmid, dout, small, payload = call(
            functools.partial(feed_kernel, own),
            [
                ((own, D), BF16), ((padded, D), BF16), ((rows, D), F32), ((rows, D), BF16),
                ((8, D), F32), ((2 * FF + D + 16 + extra_rows, D), BF16),
            ],
            [((D, FF), F32), ((FF, D), F32), ((D, D), F32), ((1, FF), F32)],
            [
                mixed, tokens, slot, grad_full[s], cot_slot, weight[:, None], modulation[s],
                out_weight, out_bias.astype(F32)[None], fc1_weight, fc1_bias.astype(F32)[None],
                fc2_weight, fc2_bias.astype(F32)[None], info if s == 0 else jnp.zeros_like(info),
            ],
        )
        dout = dout.reshape(rows, HEADS // 2, 128).transpose(1, 0, 2)
        dq, dk, dv, tab = call(
            functools.partial(attend_back_kernel, own),
            [
                ((HEADS // 2, rows, 128), BF16), ((HEADS // 2, total, 128), BF16),
                ((HEADS // 2, total, 128), BF16), ((HEADS // 2, 2 * GRID, 128), F32),
            ],
            [((128, total), F32), ((128, total), F32)],
            [qaug, kaug, vaug, mask, mixed, lse, dout, where],
        )
        pay_qkv, small_one, dx, dx_own = call(
            functools.partial(prep_back_kernel, own),
            [((3 * D, D), BF16), ((8, D), F32), ((total, D), BF16), ((own, D), F32)],
            [((total, D), F32)],
            [start, whole, lowered, slot, picked, modulation[s], qkv_weight, dq, dk, dv, dmid],
            specs=[smem] + [vmem] * 10,
        )
        grad_input = scatter_rows(dx, dx_own, seq)
        dmod = jnp.concatenate([small_one[0:2], small[0:4]], axis=0)
        outs.append((out_full, out_slot[:slots], grad_input, payload, pay_qkv, small_one[2:4], tab, dmod))

    def sum_of(number):
        if samples == 1:
            return outs[0][number]
        return functools.reduce(jnp.add, [o[number].astype(F32) for o in outs]).astype(outs[0][number].dtype)

    offsets = offset_hot()
    tab = sum_of(6).reshape(HEADS // 2, 2, GRID, 2, 2, GRID)
    tab = jnp.stack([tab[:, 0, :, :, 0, :], tab[:, 1, :, :, 1, :]]).transpose(0, 1, 3, 2, 4)
    tab = tab.reshape(2, HEADS, GRID, GRID)
    grad_rel = jnp.einsum("chij,ijo->cho", tab, offsets, precision=highest)
    grad_rel = jnp.pad(grad_rel, ((0, 0), (0, 0), (0, 1))).reshape(2, D)
    dmods = jnp.stack([o[7] for o in outs], axis=1)
    dmods = jnp.einsum("es,nsd->end", spread.astype(F32), dmods, precision=highest)
    tail = jnp.concatenate([sum_of(5), grad_rel, dmods.reshape(6 * everyone, D)], axis=0)
    tail_rows = round_up(3 * D + tail.shape[0], dp * seq * 8) - 3 * D
    tail = jnp.pad(tail, ((0, tail_rows - tail.shape[0]), (0, 0))).astype(BF16)

    layer = reduce_all(sum_of(3), dp, seq)
    last = reduce_all(jnp.concatenate([sum_of(4), tail], axis=0), dp, seq)

    base = 2 * FF + D
    grad_fc1 = layer[:FF].reshape(4, D, D).transpose(1, 0, 2).reshape(D, FF).astype(F32)
    grad_fc2 = layer[FF : 2 * FF].astype(F32)
    grad_out = layer[2 * FF : base].astype(F32)
    grad_fc1_bias = layer[base : base + 4].reshape(FF).astype(F32)
    grad_fc2_bias = layer[base + 4].astype(F32)
    grad_out_bias = layer[base + 5].astype(F32)
    info = layer[base + 16 : base + 16 + 3 * everyone].reshape(3, everyone, D)
    act_all, slope_all = info[0], info[1].astype(F32)
    label_all = (info[2, :, 0].astype(F32) * GRID + info[2, :, 1].astype(F32)).astype(jnp.int32)

    grad_qkv = last[: 3 * D].reshape(3, D, D).transpose(1, 0, 2).reshape(D, 3 * D).astype(F32)
    grad_qv = last[3 * D : 3 * D + 2].astype(F32)
    grad_rel = last[3 * D + 2 : 3 * D + 4].reshape(2, HEADS, 64)[:, :, :63].astype(F32)
    dmod_all = last[3 * D + 4 : 3 * D + 4 + 6 * everyone].reshape(everyone, 6 * D)
    grad_ada = lax.dot_general(act_all, dmod_all, (((0,), (0,)), ((), ())), preferred_element_type=F32)
    grad_ada_bias = jnp.sum(dmod_all.astype(F32), axis=0)
    grad_act = lax.dot_general(dmod_all, ada_weight, (((1,), (1,)), ((), ())), preferred_element_type=F32)
    grad_cond = slope_all * grad_act
    label_hot = (label_all[:, None] == jnp.arange(classes, dtype=jnp.int32)).astype(F32)
    grad_table = jnp.dot(label_hot.T, grad_cond, precision=highest)

    out_full, out_masked, grad_input = [jnp.stack([o[n] for o in outs]) for n in range(3)]
    return (
        out_full, out_masked, grad_input, grad_table, grad_ada, grad_ada_bias, grad_qkv, grad_qv,
        grad_rel, grad_out, grad_out_bias, grad_fc1, grad_fc1_bias, grad_fc2, grad_fc2_bias,
    )


def solution(mesh):
    split = P("dp", "seq", None)
    placed = (split, P("dp", None)) + (P("dp"),) * 4 + (P(),) * 12 + (split, split)
    return jax.shard_map(
        functools.partial(body, mesh.shape["dp"], mesh.shape["seq"]),
        mesh=mesh,
        in_specs=placed,
        out_specs=(split,) * 3 + (P(),) * 12,
        check_vma=False,
    )
```

time: 1010 us -> 249 us (0.25)
  blocking collectives: 492 us -> 0 us
  matrix products: 187 us -> 8.93 us
  waiting for transfers between devices: 174 us -> 77.2 us
  Pallas kernels: 0 us -> 59.4 us
  other arithmetic: 64.5 us -> 25.7 us
  local copies, waits for them, and re-layouts: 70 us -> 42.1 us
  starting transfers between devices: 0.34 us -> 27 us
  between operations: 19.2 us -> 4.17 us
    unnamed x1 -> x0, blocking collectives: 391 us -> none
    dot_general x53 -> x6, matrix products: 187 us -> 8.93 us  [the longest x1 3.16 us: body(): lax.dot_general(act_all, dmod_all, (((0,), (0,)), ((), ())), preferred_el...]
    psum x1 -> x0, waiting for transfers between devices: 174 us -> none  [body(): lax.psum(tuple([grad_table, grad_ada, grad_ada_bias] + layer_terms), ('dp...]
    pallas_call x0 -> x5, Pallas kernels: none -> 59.4 us  [call(): pl.pallas_call(kernel, out_shape=[jax.ShapeDtypeStruct(shape, dtype) for...]
    all_gather x5 -> x0, blocking collectives: 57.8 us -> none  [the longest x2 24.9 us: forward_pass(): lax.all_gather(keys_low, 'seq', axis=1, tiled=True)]
    all_to_all x0 -> x4, waiting for transfers between devices: none -> 57.4 us  [the longest x2 39.8 us: reduce_all(): lax.all_to_all(mine.reshape(peers, rows // 2 // peers, D), AXES, 0, 0, ax...]
    psum x1 -> x0, blocking collectives: 42.8 us -> none  [body(): lax.psum(tuple([grad_table, grad_ada, grad_ada_bias] + layer_terms), ('dp...]
    sub x3 -> x1, other arithmetic: 24.6 us -> 0.01 us  [offset_hot(): offsets = first[None, :] - first[:, None] + GRID - 1]
  transfers between devices with their start and end apart: 4 -> 10, of which waited for: 1 -> 6; matrix products, arithmetic and copies ran while one was open for 18% -> 13% of each run, Pallas kernels for 0% -> 0%
where the time goes in v1:
time: 249 us; the launch traced here: 244 us
  waiting for transfers between devices  77.2 us (31%)
  Pallas kernels  59.4 us (24%)
  local copies, waits for them, and re-layouts  42.1 us (17%)
  starting transfers between devices  27 us (11%)
  other arithmetic  25.7 us (10%)
  matrix products  8.93 us (4%)
  between operations  4.17 us (2%)
    pallas_call x5, Pallas kernels, call(): pl.pallas_call(kernel, out_shape=[jax.ShapeDtypeStruct(shape, dtype) for...  59.4 us
    all_to_all x2, waiting for transfers between devices, reduce_all(): lax.all_to_all(mine.reshape(peers, rows // 2 // peers, D), AXES, 0, 0, ax...  39.8 us
    ppermute x1, waiting for transfers between devices, scatter_rows(): lax.ppermute(block, 'seq', [(n, (n + step) % seq) for n in range(seq)])  17.7 us
    all_to_all x2, waiting for transfers between devices, reduce_all(): lax.all_to_all(wide, AXES, 0, 0, axis_index_groups=groups)  17.6 us
    unnamed x104, local copies, waits for them, and re-layouts  17.1 us
    all_to_all x2, starting transfers between devices, reduce_all(): lax.all_to_all(wide, AXES, 0, 0, axis_index_groups=groups)  11.9 us
    all_to_all x2, starting transfers between devices, reduce_all(): lax.all_to_all(mine.reshape(peers, rows // 2 // peers, D), AXES, 0, 0, ax...  9.73 us
    convert_element_type x2, other arithmetic, reduce_all(): mine = (keep.astype(F32) + got.astype(F32)).astype(BF16)  5.12 us
  transfers between devices with their start and end apart: 10, of which 6 were waited for; matrix products, arithmetic and copies ran while one was open for 13% of the time, Pallas kernels for 0%

profile of v1, /device:TPU:0, one launch (start us, length us, event | category | flops | bytes accessed | tf_op | source)
XLA Modules:
  0.0 244.5 jit_solution(12146886992584530325)
XLA Ops:
  0.7 3.0 %collective-permute-start = (bf16[512,384]{1,0:T(8,128)(2,1)}, bf16[512,384]{1,0:T(8,128)(2,1)}, u32[]{:S(2)}, u32[]{:S(2)}) collective-permute-start(bf16[512,384]{1,0:T(8,128)(2,1)} %bitcast.109), channel_id=1, source_target_pairs={{0,1},{1,0},{2,3},{3,2},{4,5},{5,4},{6,7},{7,6},{8,9},{9,8},{10,11... | collective-permute-start | bytes 1179656 | tf_op jit(solution)/shard_map/ppermute | solution.py:350
  14.0 0.9 broadcast_in_dim.99.wgt_ref
  16.0 1.1 bitcast_dynamic-update-slice_fusion
  17.1 5.1 %shard_map.307 = (bf16[6,864,128]{2,1,0:T(8,128)(2,1)S(1)}, bf16[6,1024,128]{2,1,0:T(8,128)(2,1)}, bf16[6,1024,128]{2,1,0:T(8,128)(2,1)}, bf16[1024,384]{1,0:T(8...) custom-call(s32[1]{0:T(128)} %bitcast.start_ref, bf16[1024,384]{1,0:T(8,128)(2,1)S(1)} %bitcast.106, ...), custom_call_target="tpu_custom_call" | custom-call | bytes 4194304 | tf_op jit(solution)/shard_map/pallas_call | solution.py:306
  23.1 1.9 copy-done.1
  25.1 12.8 %shard_map.308 = (f32[3,864,128]{2,1,0:T(8,128)S(1)}, f32[3,864,128]{2,1,0:T(8,128)S(1)}) custom-call(bf16[6,864,128]{2,1,0:T(8,128)(2,1)S(1)} %get-tuple-element.37.qaug_ref, bf16[6,1024,128]{2,1,0:T(8,128)(2,1)S(1)} %copy-done.1, bf16[6,1024,128]{2,1,0:T(8,128)(2,1)} %get-tuple-element.39.vaug_ref, f32[8,1024]{1,0:T(8,128)S(1)} %get-tuple-element.40.mask_ref), custom_call_target="tpu_custom_call" | custom-call | bytes 4194304 | tf_op jit(solution)/shard_map/pallas_call | solution.py:306
  37.9 1.1 copy-done.2
  39.0 1.1 copy-done.13
  40.2 18.7 %shard_map.309 = (bf16[512,384]{1,0:T(8,128)(2,1)}, bf16[352,384]{1,0:T(8,128)(2,1)}, f32[864,384]{1,0:T(8,128)}, bf16[864,384]{1,0:T(8,128)(2,1)S(1)}, f32[8,384]{1,0:T(8,128)S(1)}, /*index=5*/bf16[3584,384]{1,0:T(8,128)(2,1)}) custom-call(f32[3,864,128]{2,1,0:T(8,128)} %copy-done.2, bf16[512,384]{1,0:T(8,128)(2,1)S(1)} %bitcast.110, ...), custom_call_target="tpu_custom_call" | custom-call | bytes 4194304 | tf_op jit(solution)/shard_map/pallas_call | solution.py:306
  60.3 2.2 copy.67
  62.5 2.2 copy.68
  64.8 1.3 copy-done.3
  66.1 1.3 copy-done.5
  67.4 1.1 copy-done.7
  69.3 16.3 %shard_map.310 = (bf16[3,864,128]{2,1,0:T(8,128)(2,1)S(1)}, bf16[3,1024,128]{2,1,0:T(8,128)(2,1)S(1)}, bf16[3,1024,128]{2,1,0:T(8,128)(2,1)S(1)}, f32[3,64,128]{2,1,0:T(8,128)S(1)}) custom-call(bf16[6,864,128]{2,1,0:T(8,128)(2,1)S(1)} %copy-done.5, bf16[6,1024,128]{2,1,0:T(8,128)(2,1)} %get-tuple-element.38.kaug_ref, ...), custom_call_target="tpu_custom_call" | custom-call | bytes 4194304 | tf_op jit(solution)/shard_map/pallas_call | solution.py:306
  85.6 6.6 %shard_map.311 = (bf16[1152,384]{1,0:T(8,128)(2,1)}, f32[8,384]{1,0:T(8,128)S(1)}, bf16[1024,384]{1,0:T(8,128)(2,1)S(1)}, f32[512,384]{1,0:T(8,128)S(1)}) custom-call(s32[1]{0:T(128)} %bitcast.start_ref, bf16[1024,384]{1,0:T(8,128)(2,1)S(1)} %bitcast.107, bf16[1024,384]{1,0:T(8,128)(2,1)S(1)} %copy-done.17, bf16[352,768]{1,0:T(8,128)(2,1)S(1)} %get-tuple-element.42.slot_ref, ...), custom_call_target="tpu_custom_call" | custom-call | bytes 4194304 | tf_op jit(solution)/shard_map/pallas_call | solution.py:306
  94.1 1.2 reshape.401
  96.2 2.6 %dynamic-slice_bitcast_fusion = bf16[1792,384]{1,0:T(8,128)(2,1)} fusion(bf16[2,1792,384]{2,1,0:T(8,128)(2,1)} %bitcast.120, s32[]{:T(128)S(6)} %select_n.129), kind=kLoop, calls=%fused_computation.4 | loop fusion | bytes 2752516 | tf_op jit(solution)/shard_map/jit(dynamic_index_in_dim)/squeeze | solution.py:329
  98.8 1.3 pad_maximum_fusion.1
  100.8 2.0 collective-permute-done.4
  102.8 1.9 fusion.4
  104.7 5.9 %all-to-all-start.2 = ((bf16[16,40,384]{2,1,0:T(8,128)(2,1)}), bf16[16,40,384]{2,1,0:T(8,128)(2,1)S(1)}, u32[]{:S(2)}, u32[]{:S(2)}) async-start(bf16[16,40,384]{2,1,0:T(8,128)(2,1)} %bitcast.49), calls=%async_computation.2 | async-start | bytes 983040 | tf_op jit(solution)/shard_map/all_to_all | solution.py:332
  110.6 3.2 %fusion = bf16[1792,384]{1,0:T(8,128)(2,1)} fusion(bf16[1792,384]{1,0:T(8,128)(2,1)} %collective-permute-done.2, bf16[2,1792,384]{2,1,0:T(8,128)(2,1)} %bitcast.121, s32[]{:T(128)S(6)} %select_n.128), kind=kLoop, calls=%fused_computation.1 | loop fusion | flops 2752512 | bytes 4128772 | tf_op jit(solution)/shard_map/convert_element_type | solution.py:331
  113.8 11.6 %all-to-all-done.2 = bf16[16,40,384]{2,1,0:T(8,128)(2,1)S(1)} async-done(((bf16[16,40,384]{2,1,0:T(8,128)(2,1)}), bf16[16,40,384]{2,1,0:T(8,128)(2,1)S(1)}, u32[]{:S(2)}, u32[]{:S(2)}) %all-to-all-start.2) | async-done | bytes 491552 | tf_op jit(solution)/shard_map/all_to_all | solution.py:332
  126.2 3.8 %all-to-all-start = ((bf16[16,112,384]{2,1,0:T(8,128)(2,1)}), bf16[16,112,384]{2,1,0:T(8,128)(2,1)S(1)}, u32[]{:S(2)}, u32[]{:S(2)}) async-start(bf16[16,112,384]{2,1,0:T(8,128)(2,1)} %bitcast.115), calls=%async_computation | async-start | bytes 2752512 | tf_op jit(solution)/shard_map/all_to_all | solution.py:332
  130.0 1.1 reduce_sum.34
  131.1 28.2 %all-to-all-done = bf16[16,112,384]{2,1,0:T(8,128)(2,1)S(1)} async-done(((bf16[16,112,384]{2,1,0:T(8,128)(2,1)}), bf16[16,112,384]{2,1,0:T(8,128)(2,1)S(1)}, u32[]{:S(2)}, u32[]{:S(2)}) %all-to-all-start) | async-done | bytes 1376288 | tf_op jit(solution)/shard_map/all_to_all | solution.py:332
  160.2 7.4 %all-to-all-start.3 = ((bf16[16,40,384]{2,1,0:T(8,128)(2,1)}), bf16[16,40,384]{2,1,0:T(8,128)(2,1)}, u32[]{:S(2)}, u32[]{:S(2)}) async-start(bf16[16,40,384]{2,1,0:T(8,128)(2,1)} %broadcast_in_dim.95), calls=%async_computation.3 | async-start | bytes 983040 | tf_op jit(solution)/shard_map/all_to_all | solution.py:337
  167.8 12.4 %all-to-all-done.3 = bf16[16,40,384]{2,1,0:T(8,128)(2,1)} async-done(((bf16[16,40,384]{2,1,0:T(8,128)(2,1)}), bf16[16,40,384]{2,1,0:T(8,128)(2,1)}, u32[]{:S(2)}, u32[]{:S(2)}) %all-to-all-start.3) | async-done | bytes 491552 | tf_op jit(solution)/shard_map/all_to_all | solution.py:337
  180.1 1.2 broadcast_in_dim.94
  181.3 4.5 %all-to-all-start.1 = ((bf16[16,112,384]{2,1,0:T(8,128)(2,1)}), bf16[16,112,384]{2,1,0:T(8,128)(2,1)}, u32[]{:S(2)}, u32[]{:S(2)}) async-start(bf16[16,112,384]{2,1,0:T(8,128)(2,1)} %broadcast_in_dim.94), calls=%async_computation.1 | async-start | bytes 2752512 | tf_op jit(solution)/shard_map/all_to_all | solution.py:337
  186.7 1.7 collective-permute-start.1
  188.4 17.7 %collective-permute-done.1 = bf16[512,384]{1,0:T(8,128)(2,1)} collective-permute-done((bf16[512,384]{1,0:T(8,128)(2,1)}, bf16[512,384]{1,0:T(8,128)(2,1)}, u32[]{:S(2)}, u32[]{:S(2)}) %collective-permute-start.1) | collective-permute-done | bytes 393248 | tf_op jit(solution)/shard_map/ppermute | solution.py:361
  206.2 1.9 add_bitcast_fusion
  208.1 1.1 broadcast_select_fusion.2
  209.3 5.2 %all-to-all-done.1 = bf16[16,112,384]{2,1,0:T(8,128)(2,1)} async-done(((bf16[16,112,384]{2,1,0:T(8,128)(2,1)}), bf16[16,112,384]{2,1,0:T(8,128)(2,1)}, u32[]{:S(2)}, u32[]{:S(2)}) %all-to-all-start.1) | async-done | bytes 1376288 | tf_op jit(solution)/shard_map/all_to_all | solution.py:337
  216.5 1.3 convert_bitcast_fusion.1
  217.9 2.2 copy.76
  220.1 1.9 copy.78
  222.0 1.5 convert_reduce_fusion
  223.5 1.4 fusion.43
  225.0 3.1 %broadcast_select_fusion = (bf16[1792,384]{1,0:T(8,128)(2,1)S(1)}, bf16[1792,384]{1,0:T(8,128)(2,1)}) fusion(bf16[1792,384]{1,0:T(8,128)(2,1)} %collective-permute-done.3, pred[]{:T(512)S(6)} %eq.77, bf16[16,112,384]{2,1,0:T(8,128)(2,1)} %all-to-all-done.1), kind=kLoop, calls=%fused_computation.5 | loop fusion | flops 1376256 | bytes 5505025 | tf_op jit(solution)/shard_map/jit(_where)/select_n | solution.py:339
  228.1 1.4 fusion.33
  230.9 1.8 slice_convert_fusion
  232.8 3.2 %fusion.25 = f32[384,2304]{1,0:T(8,128)} fusion(bf16[16,2304]{1,0:T(8,128)(2,1)S(1)} %copy-done.37, bf16[1792,384]{1,0:T(8,128)(2,1)} %get-tuple-element.106), kind=kOutput, calls=%fused_computation.58 | convolution fusion | flops 28311552 | bytes 3624960 | tf_op jit(solution)/shard_map/dot_general | solution.py:522
  236.8 2.9 %fusion.1 = (f32[1536,384]{1,0:T(8,128)}, bf16[1536,384]{1,0:T(8,128)(2,1)S(1)}) fusion(bf16[1792,384]{1,0:T(8,128)(2,1)} %get-tuple-element.106, bf16[1792,384]{1,0:T(8,128)(2,1)S(1)} %get-tuple-element.105), kind=kLoop, calls=%fused_computation.8 | loop fusion | flops 2359296 | bytes 7471104 | tf_op jit(solution)/shard_map/convert_element_type | solution.py:509
  239.8 1.7 copy.87
  241.5 2.9 %fusion.21 = f32[1000,384]{1,0:T(8,128)} fusion(s32[16]{0:T(128)S(1)} %convert_bitcast_fusion.2, f32[16,384]{1,0:T(8,128)S(1)} %fusion.43, bf16[1792,384]{1,0:T(8,128)(2,1)} %get-tuple-element.106), kind=kOutput, calls=%fused_computation.53 | convolution fusion | flops 73756288 | bytes 1572928 | tf_op jit(solution)/shard_map/dot_general | solution.py:527
  (167 shorter events, 22.2 us)
Async XLA Ops:
  0.6 7.6 %copy-start = (bf16[384,2304]{1,0:T(8,128)(2,1)S(1)}, bf16[384,2304]{1,0:T(8,128)(2,1)}, u32[]{:S(2)}) copy-start(bf16[384,2304]{1,0:T(8,128)(2,1)} %param.27) | copy-start | bytes 5308420
  0.7 7.9 %copy-start.41 = (bf16[2304]{0:T(1024)(128)(2,1)S(1)}, bf16[2304]{0:T(1024)(128)(2,1)}, u32[]{:S(2)}) copy-start(bf16[2304]{0:T(1024)(128)(2,1)} %param.28) | copy-start | bytes 13828
  0.7 8.0 %copy-start.48 = (bf16[2,6,63]{2,0,1:T(2,128)(2,1)S(1)}, bf16[2,6,63]{2,0,1:T(2,128)(2,1)}, u32[]{:S(2)}) copy-start(bf16[2,6,63]{2,0,1:T(2,128)(2,1)} %param.31) | copy-start | bytes 4540
  0.7 8.9 %copy-start.46 = (bf16[384]{0:T(512)(128)(2,1)S(1)}, bf16[384]{0:T(512)(128)(2,1)}, u32[]{:S(2)}) copy-start(bf16[384]{0:T(512)(128)(2,1)} %param.33) | copy-start | bytes 2308
  0.7 9.5 %copy-start.47 = (bf16[384]{0:T(512)(128)(2,1)S(1)}, bf16[384]{0:T(512)(128)(2,1)}, u32[]{:S(2)}) copy-start(bf16[384]{0:T(512)(128)(2,1)} %param.37) | copy-start | bytes 2308
  0.7 10.0 %copy-start.45 = (bf16[2,384]{1,0:T(2,128)(2,1)S(1)}, bf16[2,384]{1,0:T(2,128)(2,1)}, u32[]{:S(2)}) copy-start(bf16[2,384]{1,0:T(2,128)(2,1)} %param.30) | copy-start | bytes 4612
  0.7 10.0 %copy-start.42 = (bf16[1536]{0:T(1024)(128)(2,1)S(1)}, bf16[1536]{0:T(1024)(128)(2,1)}, u32[]{:S(2)}) copy-start(bf16[1536]{0:T(1024)(128)(2,1)} %param.35) | copy-start | bytes 9220
  0.7 15.3 %collective-permute-start = (bf16[512,384]{1,0:T(8,128)(2,1)}, bf16[512,384]{1,0:T(8,128)(2,1)}, u32[]{:S(2)}, u32[]{:S(2)}) collective-permute-start(bf16[512,384]{1,0:T(8,128)(2,1)} %bitcast.109), channel_id=1, source_target_pairs={{0,1},{1,0},{2,3},{3,2},{4,5},{5,4},{6,7},{7,6},{8,9},{9,8},{10,11... | collective-permute-start | bytes 1179656 | tf_op jit(solution)/shard_map/ppermute | solution.py:350
  4.4 4.2 %copy-start.38 = (s32[32,32]{1,0:T(8,128)}, s32[32,32]{1,0:T(8,128)S(1)}, u32[]{:S(2)}) copy-start(s32[32,32]{1,0:T(8,128)S(1)} %subtract_add_fusion) | copy-start | bytes 12292
  6.4 3.0 %copy-start.43 = (f32[16]{0:T(128)}, f32[16]{0:T(128)S(1)}, u32[]{:S(2)}) copy-start(f32[16]{0:T(128)S(1)} %compare_convert_fusion) | copy-start | bytes 196
  8.2 4.7 %copy-start.40 = (s32[1,704]{1,0:T(1,128)S(1)}, s32[1,704]{1,0:T(1,128)}, u32[]{:S(2)}) copy-start(s32[1,704]{1,0:T(1,128)} %param.21) | copy-start | bytes 8452
  9.2 5.9 %copy-start.11 = (bf16[1,512,384]{2,1,0:T(8,128)(2,1)S(1)}, bf16[1,512,384]{2,1,0:T(8,128)(2,1)}, u32[]{:S(2)}) copy-start(bf16[1,512,384]{2,1,0:T(8,128)(2,1)} %param.20) | copy-start | bytes 1179652
  15.0 2.1 copy-start.6
  15.0 2.1 copy-start.9
  15.0 2.1 copy-start.26
  23.1 14.8 %copy-start.4 = (bf16[6,864,128]{2,1,0:T(8,128)(2,1)}, bf16[6,864,128]{2,1,0:T(8,128)(2,1)S(1)}, u32[]{:S(2)}) copy-start(bf16[6,864,128]{2,1,0:T(8,128)(2,1)S(1)} %get-tuple-element.37.qaug_ref) | copy-start | bytes 3981316
  23.1 14.8 %copy-start.27 = (f32[8,1024]{1,0:T(8,128)}, f32[8,1024]{1,0:T(8,128)S(1)}, u32[]{:S(2)}) copy-start(f32[8,1024]{1,0:T(8,128)S(1)} %get-tuple-element.40.mask_ref) | copy-start | bytes 98308
  23.1 1.9 copy-start.1
  25.0 15.1 %copy-start.8 = (f32[864,1]{1,0:T(8,128)S(1)}, f32[864,1]{1,0:T(8,128)}, u32[]{:S(2)}) copy-start(f32[864,1]{1,0:T(8,128)} %broadcast_in_dim.99.wgt_ref) | copy-start | bytes 10372
  25.0 15.1 %copy-start.12 = (bf16[1,512,384]{2,1,0:T(8,128)(2,1)S(1)}, bf16[1,512,384]{2,1,0:T(8,128)(2,1)}, u32[]{:S(2)}) copy-start(bf16[1,512,384]{2,1,0:T(8,128)(2,1)} %param.20) | copy-start | bytes 1179652
  25.0 15.1 %copy-start.14 = (bf16[384,1536]{1,0:T(8,128)(2,1)S(1)}, bf16[384,1536]{1,0:T(8,128)(2,1)}, u32[]{:S(2)}) copy-start(bf16[384,1536]{1,0:T(8,128)(2,1)} %w1_ref.1) | copy-start | bytes 3538948
  25.0 15.1 %copy-start.15 = (bf16[1536,384]{1,0:T(8,128)(2,1)S(1)}, bf16[1536,384]{1,0:T(8,128)(2,1)}, u32[]{:S(2)}) copy-start(bf16[1536,384]{1,0:T(8,128)(2,1)} %w2_ref.1) | copy-start | bytes 3538948
  25.0 15.1 %copy-start.21 = (bf16[1,512,384]{2,1,0:T(8,128)(2,1)S(1)}, bf16[1,512,384]{2,1,0:T(8,128)(2,1)}, u32[]{:S(2)}) copy-start(bf16[1,512,384]{2,1,0:T(8,128)(2,1)} %param.38) | copy-start | bytes 1179652
  25.0 15.1 %copy-start.22 = (bf16[384,384]{1,0:T(8,128)(2,1)S(1)}, bf16[384,384]{1,0:T(8,128)(2,1)}, u32[]{:S(2)}) copy-start(bf16[384,384]{1,0:T(8,128)(2,1)} %wout_ref.1) | copy-start | bytes 884740
  25.0 15.1 %copy-start.23 = (bf16[1,352,384]{2,1,0:T(8,128)(2,1)S(1)}, bf16[1,352,384]{2,1,0:T(8,128)(2,1)}, u32[]{:S(2)}) copy-start(bf16[1,352,384]{2,1,0:T(8,128)(2,1)} %param.39) | copy-start | bytes 811012
  25.0 15.1 %copy-start.30 = (f32[1,1536]{1,0:T(1,128)S(1)}, f32[1,1536]{1,0:T(1,128)}, u32[]{:S(2)}) copy-start(f32[1,1536]{1,0:T(1,128)} %reshape.431.b1_ref) | copy-start | bytes 18436
  25.1 15.1 %copy-start.31 = (f32[1,384]{1,0:T(1,128)S(1)}, f32[1,384]{1,0:T(1,128)}, u32[]{:S(2)}) copy-start(f32[1,384]{1,0:T(1,128)} %reshape.430.bout_ref) | copy-start | bytes 4612
  25.1 15.1 %copy-start.32 = (f32[1,384]{1,0:T(1,128)S(1)}, f32[1,384]{1,0:T(1,128)}, u32[]{:S(2)}) copy-start(f32[1,384]{1,0:T(1,128)} %reshape.432.b2_ref) | copy-start | bytes 4612
  64.8 1.3 copy-start.3
  66.1 1.3 copy-start.5
  69.3 16.3 %copy-start.10 = (s32[352,1]{1,0:T(8,128)S(1)}, s32[352,1]{1,0:T(8,128)}, u32[]{:S(2)}) copy-start(s32[352,1]{1,0:T(8,128)} %copy.64.picked_ref) | copy-start | bytes 4228
  69.3 16.3 %copy-start.17 = (bf16[1024,384]{1,0:T(8,128)(2,1)S(1)}, bf16[1024,384]{1,0:T(8,128)(2,1)}, u32[]{:S(2)}) copy-start(bf16[1024,384]{1,0:T(8,128)(2,1)} %copy-done.16) | copy-start | bytes 2359300
  85.5 6.6 %copy-start.29 = (f32[3,64,128]{2,1,0:T(8,128)}, f32[3,64,128]{2,1,0:T(8,128)S(1)}, u32[]{:S(2)}) copy-start(f32[3,64,128]{2,1,0:T(8,128)S(1)} %get-tuple-element.57) | copy-start | bytes 294916
  85.5 8.4 %copy-start.34 = (f32[8,384]{1,0:T(8,128)S(1)}, f32[8,384]{1,0:T(8,128)}, u32[]{:S(2)}) copy-start(f32[8,384]{1,0:T(8,128)} %copy-done.33) | copy-start | bytes 36868
  85.6 8.4 %copy-start.44 = (f32[16]{0:T(128)S(1)}, f32[16]{0:T(128)}, u32[]{:S(2)}) copy-start(f32[16]{0:T(128)} %copy-done.43) | copy-start | bytes 196
  93.9 1.7 copy-start.39
  98.8 11.8 %collective-permute-start.2 = (bf16[1792,384]{1,0:T(8,128)(2,1)}, bf16[1792,384]{1,0:T(8,128)(2,1)}, u32[]{:S(2)}, u32[]{:S(2)}) collective-permute-start(bf16[1792,384]{1,0:T(8,128)(2,1)} %dynamic-slice_bitcast_fusion), channel_id=1, source_target_pairs={{0,2},{2,0},{4,6},{6,4},{8,10},{10,8},{12,14},{14,12},{16,18},{18,... | collective-permute-start | bytes 4128776 | tf_op jit(solution)/shard_map/ppermute | solution.py:330
  100.2 2.6 %collective-permute-start.4 = (bf16[640,384]{1,0:T(8,128)(2,1)S(1)}, bf16[640,384]{1,0:T(8,128)(2,1)}, u32[]{:S(2)}, u32[]{:S(2)}) collective-permute-start(bf16[640,384]{1,0:T(8,128)(2,1)S(1)} %dynamic-slice_bitcast_fusion.1), channel_id=1, source_target_pairs={{0,2},{2,0},{4,6},{6,4},{8,10},{10,8},{12,14},{14,12},{16,18},{18,... | collective-permute-start | bytes 1474568 | tf_op jit(solution)/shard_map/ppermute | solution.py:330
  104.7 20.7 %all-to-all-start.2 = ((bf16[16,40,384]{2,1,0:T(8,128)(2,1)}), bf16[16,40,384]{2,1,0:T(8,128)(2,1)S(1)}, u32[]{:S(2)}, u32[]{:S(2)}) async-start(bf16[16,40,384]{2,1,0:T(8,128)(2,1)} %bitcast.49), calls=%async_computation.2 | async-start | bytes 983040 | tf_op jit(solution)/shard_map/all_to_all | solution.py:332
  126.2 33.2 %all-to-all-start = ((bf16[16,112,384]{2,1,0:T(8,128)(2,1)}), bf16[16,112,384]{2,1,0:T(8,128)(2,1)S(1)}, u32[]{:S(2)}, u32[]{:S(2)}) async-start(bf16[16,112,384]{2,1,0:T(8,128)(2,1)} %bitcast.115), calls=%async_computation | async-start | bytes 2752512 | tf_op jit(solution)/shard_map/all_to_all | solution.py:332
  160.2 20.0 %all-to-all-start.3 = ((bf16[16,40,384]{2,1,0:T(8,128)(2,1)}), bf16[16,40,384]{2,1,0:T(8,128)(2,1)}, u32[]{:S(2)}, u32[]{:S(2)}) async-start(bf16[16,40,384]{2,1,0:T(8,128)(2,1)} %broadcast_in_dim.95), calls=%async_computation.3 | async-start | bytes 983040 | tf_op jit(solution)/shard_map/all_to_all | solution.py:337
  181.3 4.6 %copy-start.25 = (bf16[1024,384]{1,0:T(8,128)(2,1)S(1)}, bf16[1024,384]{1,0:T(8,128)(2,1)}, u32[]{:S(2)}) copy-start(bf16[1024,384]{1,0:T(8,128)(2,1)} %copy-done.24) | copy-start | bytes 2359300
  181.3 24.8 %copy-start.19 = (f32[512,384]{1,0:T(8,128)S(1)}, f32[512,384]{1,0:T(8,128)}, u32[]{:S(2)}) copy-start(f32[512,384]{1,0:T(8,128)} %copy-done.18) | copy-start | bytes 2359300
  181.3 33.1 %all-to-all-start.1 = ((bf16[16,112,384]{2,1,0:T(8,128)(2,1)}), bf16[16,112,384]{2,1,0:T(8,128)(2,1)}, u32[]{:S(2)}, u32[]{:S(2)}) async-start(bf16[16,112,384]{2,1,0:T(8,128)(2,1)} %broadcast_in_dim.94), calls=%async_computation.1 | async-start | bytes 2752512 | tf_op jit(solution)/shard_map/all_to_all | solution.py:337
  186.7 19.5 %collective-permute-start.1 = (bf16[512,384]{1,0:T(8,128)(2,1)}, bf16[512,384]{1,0:T(8,128)(2,1)}, u32[]{:S(2)}, u32[]{:S(2)}) collective-permute-start(bf16[512,384]{1,0:T(8,128)(2,1)} %dynamic-slice_bitcast_fusion.2), channel_id=1, source_target_pairs={{0,1},{1,0},{2,3},{3,2},{4,5},{5,4},{6,7},{7,6},{8,9},{9,8},{10,11... | collective-permute-start | bytes 1179656 | tf_op jit(solution)/shard_map/ppermute | solution.py:361
  188.4 19.7 %collective-permute-start.5 = (bf16[640,384]{1,0:T(8,128)(2,1)}, bf16[640,384]{1,0:T(8,128)(2,1)S(1)}, u32[]{:S(2)}, u32[]{:S(2)}) collective-permute-start(bf16[640,384]{1,0:T(8,128)(2,1)} %bitcast.50), channel_id=1, source_target_pairs={{0,2},{2,0},{4,6},{6,4},{8,10},{10,8},{12,14},{14,12},{16,18},{18,... | collective-permute-start | bytes 1474568 | tf_op jit(solution)/shard_map/ppermute | solution.py:338
  214.5 10.5 %collective-permute-start.3 = (bf16[1792,384]{1,0:T(8,128)(2,1)}, bf16[1792,384]{1,0:T(8,128)(2,1)}, u32[]{:S(2)}, u32[]{:S(2)}) collective-permute-start(bf16[1792,384]{1,0:T(8,128)(2,1)} %bitcast.37), channel_id=1, source_target_pairs={{0,2},{2,0},{4,6},{6,4},{8,10},{10,8},{12,14},{14,12},{16,18},{18,... | collective-permute-start | bytes 4128776 | tf_op jit(solution)/shard_map/ppermute | solution.py:338
  224.9 7.8 %copy-start.37 = (bf16[16,2304]{1,0:T(8,128)(2,1)S(1)}, bf16[16,2304]{1,0:T(8,128)(2,1)}, u32[]{:S(2)}) copy-start(bf16[16,2304]{1,0:T(8,128)(2,1)} %reshape.408) | copy-start | bytes 221188
  (11 other events, 9.9 us)

commit v2 on v1

v2 whole, which is shorter than its diff:
```python
import functools
import math

import jax
import jax.numpy as jnp
from jax import lax
from jax.experimental import pallas as pl
from jax.experimental.pallas import tpu as pltpu
from jax.sharding import PartitionSpec as P

D = 384
HEADS = 6
HDIM = 64
GRID = 32
FF = 1536
CHUNK = 512

AXES = ("dp", "seq")
F32 = jnp.float32
BF16 = jnp.bfloat16
MIB = 1024 * 1024
GELU_A = math.sqrt(2.0 / math.pi)
GELU_B = 0.044715

highest = lax.Precision.HIGHEST
big_negative = -1e30
vmem = pl.BlockSpec(memory_space=pltpu.VMEM)
smem = pl.BlockSpec(memory_space=pltpu.SMEM)
hbm = pl.BlockSpec(memory_space=pltpu.HBM)


def round_up(value, step):
    return -(-value // step) * step


def blocks_of(first, count, most):
    pieces = -(-count // most)
    size = round_up(-(-count // pieces), 16)
    found = []
    at = 0
    while at < count:
        found.append((first + at, min(size, count - at)))
        at += size
    return found


def mm(left, right):
    return lax.dot_general(left, right, (((1,), (0,)), ((), ())), preferred_element_type=F32)


def mm_t(left, right):
    return lax.dot_general(left, right, (((1,), (1,)), ((), ())), preferred_element_type=F32)


def norm_parts(value):
    average = jnp.mean(value, axis=-1, keepdims=True)
    centred = value - average
    variance = jnp.mean(centred * centred, axis=-1, keepdims=True)
    inverse = lax.rsqrt(variance + 1e-06)
    return (centred * inverse, inverse)


def norm_back(normed, inverse, grad):
    first = jnp.mean(grad, axis=-1, keepdims=True)
    second = jnp.mean(grad * normed, axis=-1, keepdims=True)
    return inverse * (grad - first - normed * second)


def place_onehot(position, turned=False):
    lane = lax.broadcasted_iota(jnp.int32, (position.shape[0], 2 * GRID), 1)
    if turned:
        lane = jnp.where(lane < GRID, GRID - 1 - lane, 3 * GRID - 1 - lane)
    wanted = jnp.where(lane < GRID, position // GRID, position % GRID + GRID)
    return (lane == wanted).astype(F32).astype(BF16)


class Copies:
    def __init__(self, sems):
        self.sems, self.made = sems, []

    def start(self, source, target):
        copy = pltpu.make_async_copy(source, target, self.sems.at[len(self.made)])
        copy.start()
        self.made.append(copy)

    def wait(self):
        for copy in self.made:
            copy.wait()


def halves_writer(side_ref, keep_ref, send_ref):
    half = keep_ref.shape[0]

    def put(at, value):
        count = value.shape[0]
        for which in range(2):
            first, last = max(at, which * half), min(at + count, (which + 1) * half)
            if first >= last:
                continue
            piece = value[first - at : last - at].astype(BF16)
            span = slice(first - which * half, last - which * half)

            @pl.when(side_ref[0] == which)
            def keep():
                keep_ref[span, :] = piece

            @pl.when(side_ref[0] != which)
            def send():
                send_ref[span, :] = piece

    return put


def prep_kernel(
    own, seq, starts_ref, *refs,
):
    token_refs, refs = refs[:seq], refs[seq:]
    kept_ref, picked_ref, where_ref, mod_ref, weight_ref, qv_ref, table_ref = refs[:7]
    qaug_ref, kaug_ref, vaug_ref, x_ref, mask_ref, a_out, tok_out, slot_out = refs[7:15]
    qs_ref, a_ref, tok_ref, slot_ref, sems = refs[15:]
    copies = Copies(sems)
    total = own * seq
    slots = picked_ref.shape[0]
    for n in range(seq):
        tok_ref[pl.ds(pl.multiple_of(starts_ref[n], 16), own), :] = token_refs[n][...]
    copies.start(tok_ref, tok_out)
    shift, scale = mod_ref[0:1, :], mod_ref[1:2, :]
    normed, unused = norm_parts(tok_ref[...].astype(F32))
    lowered = (normed * (1.0 + scale) + shift).astype(BF16)
    a_ref[...] = lowered
    copies.start(a_ref, a_out)
    query = (mm(lowered, weight_ref[:, :D]) + qv_ref[0:1, :]).astype(BF16)
    scaled = (query.astype(F32) * (1.0 / math.sqrt(HDIM))).astype(BF16)
    qs_ref[...] = scaled
    keys = mm(lowered, weight_ref[:, D : 2 * D]).astype(BF16)
    values = (mm(lowered, weight_ref[:, 2 * D :]) + qv_ref[1:2, :]).astype(BF16)
    key_place = place_onehot(lax.broadcasted_iota(jnp.int32, (total, 1), 0))
    lane = lax.broadcasted_iota(jnp.int32, (total, HDIM), 1)
    ones = (lane == 0).astype(F32).astype(BF16)
    for head in range(HEADS):
        cols = slice(head * HDIM, (head + 1) * HDIM)
        kaug_ref[head] = jnp.concatenate([keys[:, cols], key_place], axis=1)
        vaug_ref[head] = jnp.concatenate([values[:, cols], ones], axis=1)
    chosen = (picked_ref[...] == lax.broadcasted_iota(jnp.int32, (slots, total), 1)).astype(F32)
    chosen = chosen.astype(BF16)
    x_ref[:own, :] = token_refs[0][...]
    x_ref[own:, :] = mm(chosen, tok_ref[...]).astype(BF16)
    slot_ref[...] = mm(chosen, lowered).astype(BF16)
    copies.start(slot_ref, slot_out)
    slot_query = mm(chosen, scaled).astype(BF16)
    own_query = qs_ref[pl.ds(pl.multiple_of(starts_ref[0], 16), own), :]
    offsets = mm(place_onehot(where_ref[...]), table_ref[...]).astype(BF16)
    for head in range(HEADS):
        cols = slice(head * HDIM, (head + 1) * HDIM)
        qaug_ref[head, :own] = jnp.concatenate([own_query[:, cols], offsets[:own, cols]], axis=1)
        qaug_ref[head, own:] = jnp.concatenate([slot_query[:, cols], offsets[own:, cols]], axis=1)
    held = kept_ref.shape[0]
    hit = kept_ref[...] == lax.broadcasted_iota(jnp.int32, (held, total), 1)
    count = jnp.sum(hit.astype(F32), axis=0, keepdims=True)
    mask_ref[...] = jnp.broadcast_to(jnp.where(count > 0.0, 0.0, big_negative), mask_ref.shape)
    copies.wait()


def attend_kernel(
    own, qaug_ref, kaug_ref, vaug_ref, mask_ref, o_ref, lse_ref, qaug_out, kaug_out, vaug_out, sems
):
    rows = qaug_ref.shape[1]
    copies = Copies(sems)
    copies.start(qaug_ref, qaug_out)
    copies.start(kaug_ref, kaug_out)
    copies.start(vaug_ref, vaug_out)
    spans = [(at, size, False) for at, size in blocks_of(0, own, 256)]
    spans += [(at, size, True) for at, size in blocks_of(own, rows - own, 256)]

    def pair(group, carry):
        for at, size, masked in spans:
            outs, logs = [], []
            for side in range(2):
                head = 2 * group + side
                scores = mm_t(qaug_ref[head, at : at + size, :], kaug_ref[head])
                if masked:
                    scores = scores + mask_ref[0:1, :]
                top = jnp.max(scores, axis=-1, keepdims=True)
                spread = jnp.exp(scores - top).astype(BF16)
                mixed = mm(spread, vaug_ref[head])
                total = mixed[:, HDIM : HDIM + 1]
                outs.append(mixed[:, :HDIM] * (1.0 / total))
                logs.append(jnp.broadcast_to(top + jnp.log(total), (size, HDIM)))
            o_ref[group, at : at + size, :] = jnp.concatenate(outs, axis=1)
            lse_ref[group, at : at + size, :] = jnp.concatenate(logs, axis=1)
        return carry

    lax.fori_loop(0, HEADS // 2, pair, 0)
    copies.wait()


def feed_kernel(
    size, own, side_ref, o_ref, lse_ref, x_ref, cot_ref, wgt_ref, mod_ref,
    wout_ref, bout_ref, w1_ref, b1_ref, w2_ref, b2_ref, extra_ref,
    do_ref, small_ref, keep_ref, send_ref, y_full_out, y_slot_out, dm_out, o_out, lse_out, x_out, do_out,
    y_ref, dm_ref, g1_ref, g2_ref, go_ref, gb1_ref, sems,
):
    rows = o_ref.shape[1]
    copies = Copies(sems)
    copies.start(o_ref, o_out)
    copies.start(lse_ref, lse_out)
    copies.start(x_ref, x_out)
    g1_ref[...] = jnp.zeros(g1_ref.shape, F32)
    g2_ref[...] = jnp.zeros(g2_ref.shape, F32)
    go_ref[...] = jnp.zeros(go_ref.shape, F32)
    gb1_ref[...] = jnp.zeros(gb1_ref.shape, F32)
    small_ref[...] = jnp.zeros(small_ref.shape, F32)
    gate1, shift2, scale2, gate2 = [mod_ref[n : n + 1, :] for n in range(2, 6)]

    def step(index, carry):
        here = pl.ds(pl.multiple_of(index * size, 16), size)
        weight = wgt_ref[here, :]
        merged = jnp.concatenate([o_ref[n, here, :] for n in range(HEADS // 2)], axis=1)
        merged = merged.astype(BF16)
        attended = mm(merged, wout_ref[...]) + bout_ref[...]
        middle = x_ref[here, :].astype(F32) + gate1 * attended
        normed, inverse = norm_parts(middle)
        second = (normed * (1.0 + scale2) + shift2).astype(BF16)
        second_t = second.T
        cot = cot_ref[here, :].astype(F32) * weight
        dz = (gate2 * cot).astype(BF16)
        branch = jnp.broadcast_to(b2_ref[...], (size, D))
        back = jnp.zeros((size, D), F32)
        for c in range(FF // CHUNK):
            cols = slice(c * CHUNK, (c + 1) * CHUNK)
            u = mm(second, w1_ref[:, cols]) + b1_ref[:, cols]
            square = u * u
            t = jnp.tanh(GELU_A * u * (1.0 + GELU_B * square))
            cdf = 0.5 * (1.0 + t)
            hidden = (u * cdf).astype(BF16)
            slope = cdf + (0.5 * GELU_A) * u * (1.0 - t * t) * (1.0 + (3.0 * GELU_B) * square)
            branch = branch + mm(hidden, w2_ref[cols, :])
            du = (slope * mm_t(dz, w2_ref[cols, :])).astype(BF16)
            back = back + mm_t(du, w1_ref[:, cols])
            g2_ref[cols, :] += mm(hidden.T, dz)
            g1_ref[:, cols] += mm(second_t, du)
            gb1_ref[:, cols] += jnp.sum(du.astype(F32), axis=0, keepdims=True)
        y_ref[here, :] = ((middle + gate2 * branch) * weight).astype(BF16)
        dmid = cot + norm_back(normed, inverse, back * (1.0 + scale2))
        dm_ref[here, :] = dmid
        datt = (gate1 * dmid).astype(BF16)
        dout = mm_t(datt, wout_ref[...]).astype(BF16)
        for n in range(HEADS // 2):
            do_ref[n, here, :] = dout[:, n * 128 : (n + 1) * 128]
        go_ref[...] += mm(merged.T, datt)
        sums = [
            dmid * attended, back, back * normed, cot * branch, dz.astype(F32), datt.astype(F32),
        ]
        for n, value in enumerate(sums):
            small_ref[n : n + 1, :] += jnp.sum(value, axis=0, keepdims=True)
        return carry

    lax.fori_loop(0, rows // size, step, 0)
    copies.start(dm_ref, dm_out)
    copies.start(do_ref, do_out)
    copies.start(y_ref.at[pl.ds(0, own)], y_full_out)
    copies.start(y_ref.at[pl.ds(own, rows - own)], y_slot_out)
    put = halves_writer(side_ref, keep_ref, send_ref)
    for n in range(4):
        put(n * D, g1_ref[:, n * D : (n + 1) * D])
    put(FF, g2_ref[...])
    put(2 * FF, go_ref[...])
    base = 2 * FF + D
    heads = [gb1_ref[:, n * D : (n + 1) * D] for n in range(4)]
    heads += [small_ref[4:5, :], small_ref[5:6, :], jnp.zeros((10, D), F32)]
    put(base, jnp.concatenate(heads, axis=0))
    put(base + 16, extra_ref[...])
    copies.wait()


def attend_back(own, q_ref, k_ref, v_ref, mask_ref, o_ref, lse_ref, do_ref, where_ref, outs, sums):
    dq_ref, dk_ref, dv_ref, tab_ref = outs
    dkt_ref, dvt_ref = sums
    rows = q_ref.shape[1]
    spans = [(at, size, False) for at, size in blocks_of(0, own, 256)]
    spans += [(at, size, True) for at, size in blocks_of(own, rows - own, 256)]
    dkt_ref[...] = jnp.zeros(dkt_ref.shape, F32)
    dvt_ref[...] = jnp.zeros(dvt_ref.shape, F32)
    tab_ref[...] = jnp.zeros(tab_ref.shape, F32)
    for at, size, masked in spans:
        place_t = place_onehot(where_ref[at : at + size, :], turned=True).T
        dqs, tabs = [], []
        for side in range(2):
            lanes = slice(side * HDIM, (side + 1) * HDIM)
            query = q_ref[side, at : at + size, :]
            keys = k_ref[side]
            scores = mm_t(query, keys)
            if masked:
                scores = scores + mask_ref[0:1, :]
            weights = jnp.exp(scores - lse_ref[at : at + size, side * HDIM : side * HDIM + 1])
            grad_out = do_ref[at : at + size, lanes]
            delta = jnp.sum(grad_out.astype(F32) * o_ref[at : at + size, lanes], axis=-1, keepdims=True)
            dp = mm_t(grad_out, v_ref[side, :, :HDIM])
            ds = (weights * (dp - delta)).astype(BF16)
            found = mm(ds, keys)
            dqs.append(found[:, :HDIM] * (1.0 / math.sqrt(HDIM)))
            tabs.append(found[:, HDIM:].astype(BF16))
            dkt_ref[lanes, :] += mm(query[:, :HDIM].T, ds)
            dvt_ref[lanes, :] += mm(grad_out.T, weights.astype(BF16))
        dq_ref[at : at + size, :] = jnp.concatenate(dqs, axis=1).astype(BF16)
        tab_ref[...] += mm(place_t, jnp.concatenate(tabs, axis=1))
    dk_ref[...] = dkt_ref[...].astype(BF16).T
    dv_ref[...] = dvt_ref[...].astype(BF16).T


def first_back_kernel(
    own, mask_ref, where_ref, *refs,
):
    sources, refs = refs[:6], refs[6:]
    tab_ref, dq_out, dk_out, dv_out, refs = *refs[:4], refs[4:]
    local, refs = refs[:6], refs[6:]
    dq_ref, dk_ref, dv_ref, dkt_ref, dvt_ref, sems = refs
    copies = Copies(sems)
    for source, target in zip(sources, local):
        copies.start(source.at[pl.ds(0, target.shape[0])], target)
    copies.wait()
    q_ref, k_ref, v_ref, o_ref, lse_ref, do_ref = local
    outs = dq_ref.at[0], dk_ref.at[0], dv_ref.at[0], tab_ref.at[0]
    attend_back(
        own, q_ref, k_ref, v_ref, mask_ref, o_ref.at[0], lse_ref.at[0], do_ref.at[0], where_ref, outs,
        (dkt_ref, dvt_ref),
    )
    copies = Copies(sems)
    copies.start(dq_ref, dq_out)
    copies.start(dk_ref, dk_out)
    copies.start(dv_ref, dv_out)
    copies.wait()


def rest_back_kernel(
    own, everyone, scalar_ref, q_ref, k_ref, v_ref, o_ref, lse_ref, do_ref, mask_ref, where_ref, picked_ref, mod_ref,
    prior_ref, tab0_ref, *refs,
):
    sources, refs = refs[:9], refs[9:]
    keep_ref, send_ref, dx_ref, dx_own_ref, refs = *refs[:4], refs[4:]
    local, refs = refs[:9], refs[9:]
    dq_ref, dk_ref, dv_ref, tab_ref, dxs_ref, dkt_ref, dvt_ref, sems = refs
    tok_ref, a_ref, x_ref, slot_ref, weight_ref, dm_ref, dq0_ref, dk0_ref, dv0_ref = local
    step = pl.program_id(0)
    last = pl.num_programs(0) - 1

    def copies():
        return [
            pltpu.make_async_copy(source, target, sems.at[n])
            for n, (source, target) in enumerate(zip(sources, local))
        ]

    @pl.when(step == 0)
    def fetch():
        for copy in copies():
            copy.start()

    @pl.when(step < last)
    def attention():
        outs = dq_ref.at[step], dk_ref.at[step], dv_ref.at[step], tab_ref.at[step]
        attend_back(
            own, q_ref, k_ref, v_ref, mask_ref, o_ref.at[0], lse_ref.at[0], do_ref.at[0], where_ref, outs,
            (dkt_ref, dvt_ref),
        )

    @pl.when(step == last)
    def projections():
        for copy in copies():
            copy.wait()
        groups = dq_ref.shape[0]
        total = tok_ref.shape[0]
        rows = x_ref.shape[0]
        slots = rows - own
        scale = mod_ref[1:2, :]
        here = pl.ds(pl.multiple_of(scalar_ref[1], 16), own)

        def joined(first, rest, span):
            return jnp.concatenate([first[0, span, :]] + [rest[n, span, :] for n in range(groups)], axis=1)

        every = slice(0, total)
        dk, dv = joined(dk0_ref, dk_ref, every), joined(dv0_ref, dv_ref, every)
        dq_own = joined(dq0_ref, dq_ref, slice(0, own))
        dq_slot = joined(dq0_ref, dq_ref, slice(own, rows))
        lowered_t = a_ref[...].T
        put = halves_writer(scalar_ref, keep_ref, send_ref)
        put(0, mm(a_ref[here, :].T, dq_own) + mm(slot_ref[...].T, dq_slot))
        put(D, mm(lowered_t, dk))
        put(2 * D, mm(lowered_t, dv))
        column = lambda value: jnp.sum(value.astype(F32), axis=0, keepdims=True)
        normed, inverse = norm_parts(tok_ref[...].astype(F32))
        da = mm_t(dk, weight_ref[:, D : 2 * D]) + mm_t(dv, weight_ref[:, 2 * D :])
        shift_sum, scale_sum = column(da), column(da * normed)
        dxs_ref[...] = norm_back(normed, inverse, da * (1.0 + scale))
        own_normed, own_inverse = norm_parts(x_ref[:own, :].astype(F32))
        da = mm_t(dq_own, weight_ref[:, :D])
        shift_sum, scale_sum = shift_sum + column(da), scale_sum + column(da * own_normed)
        dxs_ref[here, :] += dm_ref[:own, :] + norm_back(own_normed, own_inverse, da * (1.0 + scale))
        slot_normed, slot_inverse = norm_parts(x_ref[own:, :].astype(F32))
        da = mm_t(dq_slot, weight_ref[:, :D])
        shift_sum, scale_sum = shift_sum + column(da), scale_sum + column(da * slot_normed)
        spread = dm_ref[own:, :] + norm_back(slot_normed, slot_inverse, da * (1.0 + scale))
        chosen = (picked_ref[...] == lax.broadcasted_iota(jnp.int32, (slots, total), 1)).astype(F32)
        dxs_ref[...] += mm(chosen.astype(BF16).T, spread.astype(BF16))
        dx_own_ref[...] = dxs_ref[here, :]
        for n in range(dx_ref.shape[0]):
            dx_ref[n] = dxs_ref[pl.ds(pl.multiple_of(scalar_ref[3 + n], 16), own), :].astype(BF16)
        rel = table_sums([tab0_ref[0]] + [tab_ref[n] for n in range(groups)])
        smalls = jnp.concatenate(
            [
                shift_sum, scale_sum, prior_ref[0:4, :], column(dq_own) + column(dq_slot), column(dv),
                *rel, jnp.zeros((6, D), F32),
            ],
            axis=0,
        ).astype(BF16)
        tail = 2 * keep_ref.shape[0] - 3 * D
        row = lax.broadcasted_iota(jnp.int32, (tail, 16), 0)
        lane = lax.broadcasted_iota(jnp.int32, (tail, 16), 1)
        wanted = jnp.where(row % everyone == scalar_ref[2], row // everyone, -1)
        wanted = jnp.where(row < 6 * everyone, wanted, row - 6 * everyone + 6)
        put(3 * D, mm((lane == wanted).astype(F32).astype(BF16), smalls))


def table_sums(tabs):
    found = ([], [])
    for tab in tabs:
        for side in range(2):
            for part in range(2):
                at = 2 * side * GRID + part * GRID
                square = tab[part * GRID : (part + 1) * GRID, at : at + GRID]
                wide = jnp.concatenate([square, jnp.zeros((GRID, 128 - GRID), F32)], axis=1)
                turned = pltpu.roll(wide, 0, 1, stride=1, stride_axis=0)
                found[part].append(jnp.sum(turned, axis=0, keepdims=True)[:, : 2 * GRID])
    return [jnp.concatenate(parts, axis=1) for parts in found]


def call(kernel, outs, scratch, args, scalars=0, far=0, away=0, copies=0, micros=1, limit=32):
    scratches = [pltpu.VMEM(shape, dtype) for shape, dtype in scratch]
    if copies:
        scratches.append(pltpu.SemaphoreType.DMA((copies,)))
    return pl.pallas_call(
        kernel,
        out_shape=[jax.ShapeDtypeStruct(shape, dtype) for shape, dtype in outs[: len(outs) - away]]
        + [pltpu.HBM(shape, dtype) for shape, dtype in outs[len(outs) - away :]],
        in_specs=[smem] * scalars + [vmem] * (len(args) - scalars - far) + [hbm] * far,
        out_specs=[vmem] * (len(outs) - away) + [hbm] * away,
        scratch_shapes=scratches,
        compiler_params=pltpu.CompilerParams(vmem_limit_bytes=limit * MIB),
        cost_estimate=pl.CostEstimate(flops=micros * 10**9, bytes_accessed=MIB, transcendentals=0),
    )(*args)


def in_hbm(value):
    return pltpu.with_memory_space_constraint(value, pltpu.HBM)


def rest_back_call(own, everyone, arrays, scalars, mod, prior, firsts, tail_half):
    qaug, kaug, vaug, mixed, lse, dout, mask, where, picked, *sources = arrays
    tab0, dq0, dk0, dv0 = firsts
    sources = [*sources, dq0, dk0, dv0]
    rows, total = qaug.shape[1], kaug.shape[1]
    groups = HEADS // 2 - 1
    group = lambda n: jnp.minimum(n, groups - 1) + 1
    heads = lambda count: pl.BlockSpec((2, count, 128), lambda n: (group(n), 0, 0))
    pairs = pl.BlockSpec((1, rows, 128), lambda n: (group(n), 0, 0))
    whole = lambda value: pl.BlockSpec(value.shape, lambda n: (0,) * value.ndim)
    others = total // own - 1
    outs = [((tail_half, D), BF16), ((tail_half, D), BF16), ((others, own, D), BF16), ((own, D), F32)]
    scratch = [(value.shape, value.dtype) for value in sources]
    scratch += [
        ((groups, rows, 128), BF16), ((groups, total, 128), BF16), ((groups, total, 128), BF16),
        ((groups, 2 * GRID, 128), F32), ((total, D), F32), ((128, total), F32), ((128, total), F32),
    ]
    small = [mask, where, picked, mod, prior, tab0]
    return pl.pallas_call(
        functools.partial(rest_back_kernel, own, everyone),
        grid=(groups + 1,),
        out_shape=[jax.ShapeDtypeStruct(shape, dtype) for shape, dtype in outs[:2]]
        + [pltpu.HBM(shape, dtype) for shape, dtype in outs[2:]],
        in_specs=[smem, heads(rows), heads(total), heads(total), pairs, pairs, pairs]
        + [whole(value) for value in small]
        + [hbm] * len(sources),
        out_specs=[pl.BlockSpec(shape, lambda n, r=len(shape): (0,) * r) for shape, unused in outs],
        scratch_shapes=[pltpu.VMEM(shape, dtype) for shape, dtype in scratch]
        + [pltpu.SemaphoreType.DMA((len(sources),))],
        compiler_params=pltpu.CompilerParams(
            vmem_limit_bytes=48 * MIB, dimension_semantics=("arbitrary",)
        ),
        cost_estimate=pl.CostEstimate(flops=18 * 10**9, bytes_accessed=MIB, transcendentals=0),
    )(scalars, *map(in_hbm, (qaug, kaug, vaug, mixed, lse, dout)), *small, *map(in_hbm, sources))


def halves_reader(side_ref, mine_ref, other_ref):
    half = mine_ref.shape[0]

    def get(at, count):
        found = []
        for which in range(2):
            first, last = max(at, which * half), min(at + count, (which + 1) * half)
            if first < last:
                span = slice(first - which * half, last - which * half)
                found.append(jnp.where(side_ref[0] == which, mine_ref[span, :], other_ref[span, :]))
        return found[0] if len(found) == 1 else jnp.concatenate(found, axis=0)

    return get


def layer_kernel(side_ref, mine_ref, other_ref, info_ref, small_ref, g1_out, g2_out, go_out, g1_ref, g2_ref, go_ref, sems):
    get = halves_reader(side_ref, mine_ref, other_ref)
    copies = Copies(sems)
    for n in range(4):
        cols = pl.ds(n * D, D)
        g1_ref[:, cols] = get(n * D, D).astype(F32)
        copies.start(g1_ref.at[:, cols], g1_out.at[:, cols])
        g2_ref[cols, :] = get(FF + n * D, D).astype(F32)
        copies.start(g2_ref.at[cols], g2_out.at[cols])
    go_ref[...] = get(2 * FF, D).astype(F32)
    copies.start(go_ref, go_out)
    base = 2 * FF + D
    small_ref[...] = get(base, 16).astype(F32)[:8]
    info_ref[...] = get(base + 16, info_ref.shape[0])
    copies.wait()


def last_kernel(
    everyone, side_ref, mine_ref, other_ref, info_ref, ada_ref, small_ref, bias_ref,
    gqkv_out, gada_out, table_out, gqkv_ref, gada_ref, table_ref, sems,
):
    get = halves_reader(side_ref, mine_ref, other_ref)
    copies = Copies(sems)
    act_t = info_ref[:everyone, :].T
    back = jnp.zeros((everyone, D), F32)
    for n in range(6):
        cols = pl.ds(n * D, D)
        dmod = get(3 * D + n * everyone, everyone)
        gada_ref[:, cols] = mm(act_t, dmod)
        copies.start(gada_ref.at[:, cols], gada_out.at[:, cols])
        bias_ref[n : n + 1, :] = jnp.sum(dmod.astype(F32), axis=0, keepdims=True)
        back = back + mm_t(dmod, ada_ref[:, cols])
    for n in range(3):
        cols = pl.ds(n * D, D)
        gqkv_ref[:, cols] = get(n * D, D).astype(F32)
        copies.start(gqkv_ref.at[:, cols], gqkv_out.at[:, cols])
    cond = info_ref[everyone : 2 * everyone, :].astype(F32) * back
    high = cond.astype(BF16)
    low = (cond - high.astype(F32)).astype(BF16)
    digits = info_ref[2 * everyone : 3 * everyone, :].astype(F32)
    label = (digits[:, 0:1] * GRID + digits[:, 1:2]).astype(jnp.int32)
    classes = table_ref.shape[0]
    wide = round_up(classes, 128)
    hot = (label == lax.broadcasted_iota(jnp.int32, (everyone, wide), 1)).astype(F32).astype(BF16).T
    table_ref[...] = (mm(hot, high) + mm(hot, low))[:classes]
    copies.start(table_ref, table_out)
    small_ref[...] = get(3 * D + 6 * everyone, 16).astype(F32)[:8]
    copies.wait()


def swap_cores(value, dp):
    return lax.ppermute(value, "dp", [(n, n ^ 1) for n in range(dp)])


def exchange(value, dp, seq):
    groups = [
        [(far * (dp // 2) + 2 * pair + core) * seq + at for pair in range(dp // 4) for at in range(seq)]
        for far in range(2)
        for core in range(2)
    ]
    return lax.all_to_all(value, AXES, 0, 0, axis_index_groups=groups)


def sum_pieces(pieces, dp):
    near = jnp.sum(pieces.astype(F32), axis=0).astype(BF16)
    far = lax.ppermute(near, "dp", [(n, (n + dp // 2) % dp) for n in range(dp)])
    return (near.astype(F32) + far.astype(F32)).astype(BF16)


def spread_out(chunk, dp, seq):
    peers = dp // 4 * seq
    return exchange(jnp.broadcast_to(chunk[None], (peers,) + chunk.shape), dp, seq).reshape(-1, D)


def scatter_rows(partial, seq):
    return [
        lax.ppermute(partial[step - 1], "seq", [(n, (n + step) % seq) for n in range(seq)])
        for step in range(1, seq)
    ]


def time_features(moments):
    half_width = D // 2
    frequency = jnp.exp(-math.log(10000.0) * jnp.arange(half_width, dtype=F32) / half_width)
    angles = moments.astype(F32)[:, None] * frequency[None, :]
    return jnp.concatenate([jnp.cos(angles), jnp.sin(angles)], axis=-1)


def offset_hot():
    first = jnp.arange(GRID, dtype=jnp.int32)
    offsets = first[None, :] - first[:, None] + GRID - 1
    return (offsets[..., None] == jnp.arange(2 * GRID - 1, dtype=jnp.int32)).astype(F32)


def bias_table(rel_bias):
    both = jnp.einsum("cho,ijo->cihj", rel_bias.astype(F32), offset_hot(), precision=highest)
    empty = jnp.zeros_like(both[0])
    top = jnp.concatenate([both[0], empty], axis=-1)
    low = jnp.concatenate([empty, both[1]], axis=-1)
    return jnp.concatenate([top, low], axis=0).reshape(2 * GRID, HEADS * 2 * GRID).astype(BF16)


def body(
    dp, seq, image_tokens, kept_index, kept_count, sample_valid, timestep, class_label, class_table,
    ada_weight, ada_bias, qkv_weight, qv_bias, rel_bias, out_weight, out_bias, fc1_weight,
    fc1_bias, fc2_weight, fc2_bias, grad_full, grad_masked,
):
    samples, own, width = image_tokens.shape
    held = kept_index.shape[1]
    slots = grad_masked.shape[1]
    padded = round_up(slots, 16)
    rows = own + padded
    total = own * seq
    everyone = dp * samples
    classes = class_table.shape[0]
    dp_place, seq_place = lax.axis_index("dp"), lax.axis_index("seq")

    conditioned = jnp.take(class_table, class_label, axis=0).astype(F32) + time_features(timestep)
    gate = jax.nn.sigmoid(conditioned)
    activated = (conditioned * gate).astype(BF16)
    slope = gate * (1.0 + conditioned * (1.0 - gate))
    modulation = jnp.dot(activated, ada_weight, preferred_element_type=F32) + ada_bias.astype(F32)
    modulation = jnp.pad(modulation.reshape(samples, 6, D), ((0, 0), (0, 2), (0, 0)))
    table = bias_table(rel_bias)
    valid = sample_valid.astype(F32)

    digits = jnp.stack([class_label // GRID, class_label % GRID], axis=1).astype(F32)
    digits = jnp.pad(digits, ((0, 0), (0, D - 2)))
    info = jnp.stack([activated.astype(F32), slope, digits], axis=0)
    info = info * (seq_place == 0).astype(F32)
    extra_rows = round_up(2 * FF + D + 16 + 3 * everyone, dp * seq * 8) - (2 * FF + D + 16)
    spread = (jnp.arange(everyone)[:, None] == dp_place * samples + jnp.arange(samples)[None, :])
    info = jnp.einsum("es,nsd->end", spread.astype(F32), info, precision=highest)
    info = info.transpose(1, 0, 2).reshape(3 * everyone, D).astype(BF16)
    info = jnp.pad(info, ((0, extra_rows - 3 * everyone), (0, 0)))

    slot_numbers = jnp.arange(held, dtype=jnp.int32)
    live_all = slot_numbers[None, :] < kept_count[:, None]
    slot_start = seq_place * slots
    peers = dp // 4 * seq
    side = dp_place % 2
    sides = side.astype(jnp.int32).reshape(1)
    half = (2 * FF + D + 16 + extra_rows) // 2
    tail_half = round_up(3 * D + 16 + 6 * everyone, dp * seq * 8) // 2
    starts = ((seq_place - jnp.arange(seq, dtype=jnp.int32)) % seq * own).astype(jnp.int32)
    block = blocks_of(0, rows, 432)[0][1]

    kept_of = []
    for s in range(samples):
        tokens = [image_tokens[s]]
        for step in range(1, seq):
            tokens.append(lax.ppermute(tokens[0], "seq", [(n, (n + step) % seq) for n in range(seq)]))
        kept = jnp.where(live_all[s], kept_index[s], -1)[:, None]
        picked = lax.dynamic_slice_in_dim(kept_index[s], slot_start, slots, 0)
        live = lax.dynamic_slice_in_dim(live_all[s], slot_start, slots, 0)
        picked = jnp.pad(picked, (0, padded - slots))[:, None]
        where = jnp.concatenate([starts[0] + jnp.arange(own, dtype=jnp.int32), picked[:, 0]])[:, None]
        weight = valid[s] * jnp.concatenate(
            [jnp.ones((own,), F32), jnp.pad(live.astype(F32), (0, padded - slots))]
        )
        cot = jnp.concatenate([grad_full[s], jnp.pad(grad_masked[s], ((0, padded - slots), (0, 0)))])
        qaug, kaug, vaug, x, mask, lowered, whole, slot = call(
            functools.partial(prep_kernel, own, seq),
            [
                ((HEADS, rows, 128), BF16), ((HEADS, total, 128), BF16), ((HEADS, total, 128), BF16),
                ((rows, D), BF16), ((8, total), F32),
                ((total, D), BF16), ((total, D), BF16), ((padded, D), BF16),
            ],
            [((total, D), BF16), ((total, D), BF16), ((total, D), BF16), ((padded, D), BF16)],
            [starts, *tokens, kept, picked, where, modulation[s], qkv_weight, qv_bias.astype(F32), table],
            scalars=1, away=3, copies=3, micros=5,
        )
        mixed, lse, qaug_far, kaug_far, vaug_far = call(
            functools.partial(attend_kernel, own),
            [
                ((HEADS // 2, rows, 128), F32), ((HEADS // 2, rows, 128), F32),
                (qaug.shape, BF16), (kaug.shape, BF16), (vaug.shape, BF16),
            ],
            [],
            [qaug, kaug, vaug, mask],
            away=3, copies=3, micros=12,
        )
        dout, small, keep, send, y_full, y_slot, dmid, mixed_far, lse_far, x_far, dout_far = call(
            functools.partial(feed_kernel, block, own),
            [
                ((HEADS // 2, rows, 128), BF16), ((8, D), F32), ((half, D), BF16), ((half, D), BF16),
                ((own, D), BF16), ((padded, D), BF16), ((rows, D), F32), (mixed.shape, F32),
                (lse.shape, F32), (x.shape, BF16), ((HEADS // 2, rows, 128), BF16),
            ],
            [
                ((rows, D), BF16), ((rows, D), F32),
                ((D, FF), F32), ((FF, D), F32), ((D, D), F32), ((1, FF), F32),
            ],
            [
                sides, mixed, lse, x, cot, weight[:, None], modulation[s],
                out_weight, out_bias.astype(F32)[None], fc1_weight, fc1_bias.astype(F32)[None],
                fc2_weight, fc2_bias.astype(F32)[None], info if s == 0 else jnp.zeros_like(info),
            ],
            scalars=1, away=7, copies=7, micros=14,
        )
        kept_of.append(dict(
            mask=mask, where=where,
            far=[
                qaug_far, kaug_far, vaug_far, mixed_far, lse_far, dout_far, mask, where, picked,
                whole, lowered, x_far, slot, qkv_weight, dmid,
            ],
            y_full=y_full, y_slot=y_slot, small=small, keep=keep, send=send,
        ))

    def added(arrays):
        if len(arrays) == 1:
            return arrays[0]
        return functools.reduce(jnp.add, [a.astype(F32) for a in arrays]).astype(arrays[0].dtype)

    keep, send = added([k["keep"] for k in kept_of]), added([k["send"] for k in kept_of])
    got = swap_cores(send, dp)

    firsts = [
        call(
            functools.partial(first_back_kernel, own),
            [
                ((1, 2 * GRID, 128), F32),
                ((1, rows, 128), BF16), ((1, total, 128), BF16), ((1, total, 128), BF16),
            ],
            [
                ((2, rows, 128), BF16), ((2, total, 128), BF16), ((2, total, 128), BF16),
                ((1, rows, 128), F32), ((1, rows, 128), F32), ((1, rows, 128), BF16),
                ((1, rows, 128), BF16), ((1, total, 128), BF16), ((1, total, 128), BF16),
                ((128, total), F32), ((128, total), F32),
            ],
            [k["mask"], k["where"], *map(in_hbm, k["far"][:6])],
            away=3, copies=6, far=6, micros=6,
        )
        for k in kept_of
    ]
    mine = (keep.astype(F32) + got.astype(F32)).astype(BF16)
    mine, firsts = lax.optimization_barrier((mine, firsts))
    pieces = exchange(mine.reshape(peers, half // peers, D), dp, seq)
    tails = []
    for number, (k, first) in enumerate(zip(kept_of, firsts)):
        place = (dp_place * samples + number).astype(jnp.int32)
        others = (seq_place + jnp.arange(1, seq, dtype=jnp.int32)) % seq * own
        scalars = jnp.concatenate([jnp.stack([sides[0], starts[0], place]), others.astype(jnp.int32)])
        tails.append(
            rest_back_call(own, everyone, k["far"], scalars, modulation[number], k["small"], first, tail_half)
        )

    keep, send = added([t[0] for t in tails]), added([t[1] for t in tails])
    got = swap_cores(send, dp)
    mine = (keep.astype(F32) + got.astype(F32)).astype(BF16).reshape(peers, tail_half // peers, D)
    mine, pieces = lax.optimization_barrier((mine, pieces))
    chunk = sum_pieces(pieces, dp)
    last_chunk = sum_pieces(exchange(mine, dp, seq), dp)
    moved = [scatter_rows(t[2], seq) for t in tails]
    layer_half = spread_out(chunk, dp, seq)
    layer_half, last_chunk, moved = lax.optimization_barrier((layer_half, last_chunk, moved))
    last_half = spread_out(last_chunk, dp, seq)
    grad_input = jnp.stack(
        [t[3] + functools.reduce(jnp.add, [m.astype(F32) for m in came]) for t, came in zip(tails, moved)]
    )
    out_full = jnp.stack([k["y_full"] for k in kept_of])
    out_masked = jnp.stack([k["y_slot"][:slots] for k in kept_of])
    info, layer_small, grad_fc1, grad_fc2, grad_out = call(
        layer_kernel,
        [((extra_rows, D), BF16), ((8, D), F32), ((D, FF), F32), ((FF, D), F32), ((D, D), F32)],
        [((D, FF), F32), ((FF, D), F32), ((D, D), F32)],
        [sides, layer_half, swap_cores(layer_half, dp)],
        scalars=1, away=3, copies=9, micros=3,
    )
    last_half, info, layer_small = lax.optimization_barrier((last_half, info, layer_small))
    grad_fc1_bias = layer_small[:4].reshape(FF)
    grad_fc2_bias, grad_out_bias = layer_small[4], layer_small[5]
    last_small, ada_small, grad_qkv, grad_ada, grad_table = call(
        functools.partial(last_kernel, everyone),
        [((8, D), F32), ((8, D), F32), ((D, 3 * D), F32), ((D, 6 * D), F32), ((classes, D), F32)],
        [((D, 3 * D), F32), ((D, 6 * D), F32), ((classes, D), F32)],
        [sides, last_half, swap_cores(last_half, dp), info, ada_weight],
        scalars=1, away=3, copies=10, micros=4,
    )
    grad_qv = last_small[:2]
    grad_rel = last_small[2:4].reshape(2, HEADS, 2 * GRID)[:, :, : 2 * GRID - 1]
    grad_ada_bias = ada_small[:6].reshape(6 * D)
    return (
        out_full, out_masked, grad_input, grad_table, grad_ada, grad_ada_bias, grad_qkv, grad_qv,
        grad_rel, grad_out, grad_out_bias, grad_fc1, grad_fc1_bias, grad_fc2, grad_fc2_bias,
    )


def solution(mesh):
    split = P("dp", "seq", None)
    placed = (split, P("dp", None)) + (P("dp"),) * 4 + (P(),) * 12 + (split, split)
    return jax.shard_map(
        functools.partial(body, mesh.shape["dp"], mesh.shape["seq"]),
        mesh=mesh,
        in_specs=placed,
        out_specs=(split,) * 3 + (P(),) * 12,
        check_vma=False,
    )
```

time: 249 us -> 153 us (0.61); the launches traced: 244 us -> 152 us
  waiting for transfers between devices: 77.2 us -> 38.4 us
  local copies, waits for them, and re-layouts: 42.1 us -> 6.81 us
  other arithmetic: 25.7 us -> 8.79 us
  matrix products: 8.93 us -> 2.38 us
  Pallas kernels: 59.4 us -> 64.6 us
    all_to_all x4, waiting for transfers between devices: 57.4 us -> 8.85 us  [exchange(): return lax.all_to_all(value, AXES, 0, 0, axis_index_groups=groups)]
    pallas_call x0 -> x1, Pallas kernels: none -> 17.9 us  [rest_back_call(): pl.pallas_call(functools.partial(rest_back_kernel, own, everyone), grid=(...]
    unnamed x104 -> x29, local copies, waits for them, and re-layouts: 17.1 us -> 0.68 us
    pallas_call x5 -> x6, Pallas kernels: 59.4 us -> 46.6 us  [call(): pl.pallas_call(kernel, out_shape=[jax.ShapeDtypeStruct(shape, dtype) for...]
    ppermute x6 -> x8, waiting for transfers between devices: 19.8 us -> 29.6 us  [the longest x2 18.7 us: sum_pieces(): far = lax.ppermute(near, 'dp', [(n, (n + dp // 2) % dp) for n in range(dp)])]
    convert_element_type x9 -> x4, other arithmetic: 13.2 us -> 3.74 us  [the longest x1 2.77 us: body(): mine = (keep.astype(F32) + got.astype(F32)).astype(BF16)]
    dot_general x4 -> x0, matrix products: 8.06 us -> none  [the longest x1 3.16 us: body(): lax.dot_general(act_all, dmod_all, (((0,), (0,)), ((), ())), preferred_el...]
    convert_element_type x3 -> x0, local copies, waits for them, and re-layouts: 4.56 us -> none  [the longest x1 2.23 us: body(): last[:3 * D].reshape(3, D, D).transpose(1, 0, 2).reshape(D, 3 * D)]
  transfers between devices with their start and end apart: 10 -> 12, of which waited for: 6 -> 6; matrix products, arithmetic and copies ran while one was open for 13% -> 8% of each run, Pallas kernels for 0% -> 19%
where the time goes in v2:
time: 153 us; the launch traced here: 152 us
  Pallas kernels  64.6 us (42%)
  waiting for transfers between devices  38.4 us (25%)
  starting transfers between devices  27.4 us (18%)
  other arithmetic  8.79 us (6%)
  local copies, waits for them, and re-layouts  6.81 us (4%)
  between operations  3.84 us (3%)
  matrix products  2.38 us (2%)
    pallas_call x6, Pallas kernels, call(): pl.pallas_call(kernel, out_shape=[jax.ShapeDtypeStruct(shape, dtype) for...  46.6 us
    ppermute x2, waiting for transfers between devices, sum_pieces(): far = lax.ppermute(near, 'dp', [(n, (n + dp // 2) % dp) for n in range(dp)])  18.7 us
    all_to_all x4, starting transfers between devices, exchange(): return lax.all_to_all(value, AXES, 0, 0, axis_index_groups=groups)  18.1 us
    pallas_call x1, Pallas kernels, rest_back_call(): pl.pallas_call(functools.partial(rest_back_kernel, own, everyone), grid=(...  17.9 us
    ppermute x1, waiting for transfers between devices, scatter_rows(): lax.ppermute(partial[step - 1], 'seq', [(n, (n + step) % seq) for n in ra...  9.22 us
    all_to_all x4, waiting for transfers between devices, exchange(): return lax.all_to_all(value, AXES, 0, 0, axis_index_groups=groups)  8.85 us
    ppermute x2, starting transfers between devices, sum_pieces(): far = lax.ppermute(near, 'dp', [(n, (n + dp // 2) % dp) for n in range(dp)])  3.91 us
  transfers between devices with their start and end apart: 12, of which 6 were waited for; matrix products, arithmetic and copies ran while one was open for 8% of the time, Pallas kernels for 19%

profile of v2, /device:TPU:0, one launch (start us, length us, event | category | flops | bytes accessed | tf_op | source)
XLA Modules:
  0.0 152.2 jit_solution(16999933592618660789)
XLA Ops:
  0.7 3.0 %collective-permute-start = (bf16[512,384]{1,0:T(8,128)(2,1)}, bf16[512,384]{1,0:T(8,128)(2,1)S(1)}, u32[]{:S(2)}, u32[]{:S(2)}) collective-permute-start(bf16[512,384]{1,0:T(8,128)(2,1)} %bitcast.63), channel_id=1, source_target_pairs={{0,1},{1,0},{2,3},{3,2},{4,5},{5,4},{6,7},{7,6},{8,9},{9,8},{10,11... | collective-permute-start | bytes 1179656 | tf_op jit(solution)/shard_map/ppermute | solution.py:658
  6.5 0.8 dynamic-slice_reduce_fusion
  7.3 0.8 convert_convert_fusion
  8.1 0.1 fusion.11
  8.2 1.9 %convolution_reduce_fusion = f32[2304]{0:T(1024)S(1)} fusion(bf16[384,1]{0,1:T(2,128)(2,1)S(1)} %reshape.351, bf16[384,2304]{1,0:T(8,128)(2,1)} %ada_ref.1), kind=kOutput, calls=%fused_computation.3 | convolution fusion | flops 1769472 | bytes 1779456 | tf_op jit(solution)/shard_map/dot_general | solution.py:628
  10.2 0.5 fusion
  10.7 0.1 add_convert_fusion.4
  10.9 0.1 fusion.7
  11.1 0.1 convert_element_type.159.refs_8_
  11.3 0.1 copy.41.refs_3_.picked_ref
  11.4 0.2 copy.38
  11.6 0.2 broadcast_in_dim.84.refs_4_.where_ref
  11.8 0.2 broadcast_in_dim.83.wgt_ref
  12.0 1.3 pad_maximum_fusion.cot_ref
  13.4 5.6 %shard_map.307 = (bf16[6,864,128]{2,1,0:T(8,128)(2,1)S(1)}, bf16[6,1024,128]{2,1,0:T(8,128)(2,1)S(1)}, bf16[6,1024,128]{2,1,0:T(8,128)(2,1)S(1)}, bf16[864,384]{...) custom-call(s32[2]{0:T(128)S(1)} %fusion.15.starts_ref, ...), custom_call_target="tpu_custom_call" | custom-call | flops 5000000000 | bytes 1048576 | tf_op jit(solution)/shard_map/pallas_call | solution.py:440
  19.0 11.5 %shard_map.308 = (f32[3,864,128]{2,1,0:T(8,128)S(1)}, f32[3,864,128]{2,1,0:T(8,128)S(1)}, bf16[6,864,128]{2,1,0:T(8,128)(2,1)}, bf16[6,1024,128]{2,1,0:T(8,128)(2,1)}, bf16[6,1024,128]{2,1,0:T(8,128)(2,1)}) custom-call(bf16[6,864,128]{2,1,0:T(8,128)(2,1)S(1)} %get-tuple-element.69.qaug_ref, bf16[6,1024,128]{2,1,0:T(8,128)(2,1)S(1)} %get-tuple-element.70.kaug_ref, ...), custom_call_target="tpu_custom_call" | custom-call | flops 12000000000 | bytes 1048576 | tf_op jit(solution)/shard_map/pallas_call | solution.py:440
  30.6 15.3 %shard_map.309 = (bf16[3,864,128]{2,1,0:T(8,128)(2,1)}, f32[8,384]{1,0:T(8,128)S(1)}, bf16[1792,384]{1,0:T(8,128)(2,1)S(1)}, bf16[1792,384]{1,0:T(8,128)(2,1)}, ...) custom-call(s32[1]{0:T(128)} %bitcast.side_ref, ...), custom_call_target="tpu_custom_call" | custom-call | flops 14000000000 | bytes 1048576 | tf_op jit(solution)/shard_map/pallas_call | solution.py:440
  45.9 0.1 pad_add_fusion.1.scalar_ref
  46.0 7.1 %shard_map.310 = (f32[1,64,128]{2,1,0:T(8,128)S(1)}, bf16[1,864,128]{2,1,0:T(8,128)(2,1)}, bf16[1,1024,128]{2,1,0:T(8,128)(2,1)}, bf16[1,1024,128]{2,1,0:T(8,128)(2,1)}) custom-call(f32[8,1024]{1,0:T(8,128)S(1)} %get-tuple-element.72.mask_ref, s32[864,1]{1,0:T(8,128)S(1)} %broadcast_in_dim.84.refs_4_.where_ref, ...), custom_call_target="tpu_custom_call" | custom-call | flops 6000000000 | bytes 1048576 | tf_op jit(solution)/shard_map/pallas_call | solution.py:440
  53.1 2.8 %add_convert_fusion = bf16[1792,384]{1,0:T(8,128)(2,1)} fusion(bf16[1792,384]{1,0:T(8,128)(2,1)} %collective-permute-done.1, bf16[1792,384]{1,0:T(8,128)(2,1)S(1)} %get-tuple-element.85), kind=kLoop, calls=%fused_computation | loop fusion | flops 2752512 | bytes 4128768 | tf_op jit(solution)/shard_map/convert_element_type | solution.py:742
  55.9 4.6 %all-to-all-start = ((bf16[8,224,384]{2,1,0:T(8,128)(2,1)}), bf16[8,224,384]{2,1,0:T(8,128)(2,1)S(1)}, u32[]{:S(2)}, u32[]{:S(2)}) async-start(bf16[8,224,384]{2,1,0:T(8,128)(2,1)} %bitcast.65), calls=%async_computation | async-start | bytes 2752512 | tf_op jit(solution)/shard_map/all_to_all | solution.py:567
  60.5 17.9 %shard_map.311 = (bf16[640,384]{1,0:T(8,128)(2,1)S(1)}, bf16[640,384]{1,0:T(8,128)(2,1)S(1)}, bf16[1,512,384]{2,1,0:T(8,128)(2,1)}, f32[512,384]{1,0:T(8,128)}) custom-call(s32[4]{0:T(128)S(1)} %pad_add_fusion.1.scalar_ref, bf16[6,864,128]{2,1,0:T(8,128)(2,1)} %get-tuple-element.78.refs_0_.q_ref, bf16[6,1024,128]{2,1,0:T(8,128)(2,1)} %get-tuple-element.79.refs_1_.k_ref, ...), custom_call_target="tpu_custom_call" | custom-call | flops 17999998976 | bytes 1048576 | tf_op jit(solution)/shard_map/pallas_call | solution.py:474
  78.4 0.3 collective-permute-start.2
  78.7 1.6 %collective-permute-done.2 = bf16[640,384]{1,0:T(8,128)(2,1)S(1)} collective-permute-done((bf16[640,384]{1,0:T(8,128)(2,1)S(1)}, bf16[640,384]{1,0:T(8,128)(2,1)S(1)}, u32[]{:S(2)}, u32[]{:S(2)}) %collective-permute-start.2) | collective-permute-done | bytes 491552 | tf_op jit(solution)/shard_map/ppermute | solution.py:558
  80.4 0.9 add_convert_fusion.1
  81.3 5.1 %all-to-all-start.2 = ((bf16[8,80,384]{2,1,0:T(8,128)(2,1)}), bf16[8,80,384]{2,1,0:T(8,128)(2,1)S(1)}, u32[]{:S(2)}, u32[]{:S(2)}) async-start(bf16[8,80,384]{2,1,0:T(8,128)(2,1)} %bitcast.29), calls=%async_computation.2 | async-start | bytes 983040 | tf_op jit(solution)/shard_map/all_to_all | solution.py:567
  86.4 0.2 reduce_sum.24
  86.6 2.7 %collective-permute-start.3 = (bf16[224,384]{1,0:T(8,128)(2,1)S(1)}, bf16[224,384]{1,0:T(8,128)(2,1)S(1)}, u32[]{:S(2)}, u32[]{:S(2)}) collective-permute-start(bf16[224,384]{1,0:T(8,128)(2,1)S(1)} %reduce_sum.24), channel_id=1, source_target_pairs={{0,16},{2,18},{4,20},{6,22},{8,24},{10,26},{12,28},{14,30},{16,0},... | collective-permute-start | bytes 516104 | tf_op jit(solution)/shard_map/ppermute | solution.py:572
  89.2 6.6 %collective-permute-done.3 = bf16[224,384]{1,0:T(8,128)(2,1)S(1)} collective-permute-done((bf16[224,384]{1,0:T(8,128)(2,1)S(1)}, bf16[224,384]{1,0:T(8,128)(2,1)S(1)}, u32[]{:S(2)}, u32[]{:S(2)}) %collective-permute-start.3) | collective-permute-done | bytes 172064 | tf_op jit(solution)/shard_map/ppermute | solution.py:572
  95.9 3.2 %all-to-all-done.2 = bf16[8,80,384]{2,1,0:T(8,128)(2,1)S(1)} async-done(((bf16[8,80,384]{2,1,0:T(8,128)(2,1)}), bf16[8,80,384]{2,1,0:T(8,128)(2,1)S(1)}, u32[]{:S(2)}, u32[]{:S(2)}) %all-to-all-start.2) | async-done | bytes 491552 | tf_op jit(solution)/shard_map/all_to_all | solution.py:567
  99.1 1.2 broadcast_in_dim.78
  100.3 4.7 %all-to-all-start.1 = ((bf16[8,224,384]{2,1,0:T(8,128)(2,1)}), bf16[8,224,384]{2,1,0:T(8,128)(2,1)S(1)}, u32[]{:S(2)}, u32[]{:S(2)}) async-start(bf16[8,224,384]{2,1,0:T(8,128)(2,1)} %broadcast_in_dim.78), calls=%async_computation.1 | async-start | bytes 2752512 | tf_op jit(solution)/shard_map/all_to_all | solution.py:567
  105.1 2.0 %collective-permute-start.5 = (bf16[512,384]{1,0:T(8,128)(2,1)S(1)}, bf16[512,384]{1,0:T(8,128)(2,1)S(1)}, u32[]{:S(2)}, u32[]{:S(2)}) collective-permute-start(bf16[512,384]{1,0:T(8,128)(2,1)S(1)} %bitcast.73), channel_id=1, source_target_pairs={{0,1},{1,0},{2,3},{3,2},{4,5},{5,4},{6,7},{7,6},{8,9},{9,8},{10,11... | collective-permute-start | bytes 1179656 | tf_op jit(solution)/shard_map/ppermute | solution.py:583
  107.1 1.2 collective-permute-start.4
  108.4 12.1 %collective-permute-done.4 = bf16[80,384]{1,0:T(8,128)(2,1)S(1)} collective-permute-done((bf16[80,384]{1,0:T(8,128)(2,1)S(1)}, bf16[80,384]{1,0:T(8,128)(2,1)S(1)}, u32[]{:S(2)}, u32[]{:S(2)}) %collective-permute-start.4) | collective-permute-done | bytes 61472 | tf_op jit(solution)/shard_map/ppermute | solution.py:572
  120.5 9.2 %collective-permute-done.5 = bf16[512,384]{1,0:T(8,128)(2,1)S(1)} collective-permute-done((bf16[512,384]{1,0:T(8,128)(2,1)S(1)}, bf16[512,384]{1,0:T(8,128)(2,1)S(1)}, u32[]{:S(2)}, u32[]{:S(2)}) %collective-permute-start.5) | collective-permute-done | bytes 393248 | tf_op jit(solution)/shard_map/ppermute | solution.py:583
  129.7 0.8 broadcast_in_dim.79
  130.5 3.6 %all-to-all-start.3 = ((bf16[8,80,384]{2,1,0:T(8,128)(2,1)}), bf16[8,80,384]{2,1,0:T(8,128)(2,1)S(1)}, u32[]{:S(2)}, u32[]{:S(2)}) async-start(bf16[8,80,384]{2,1,0:T(8,128)(2,1)} %broadcast_in_dim.79), calls=%async_computation.3 | async-start | bytes 983040 | tf_op jit(solution)/shard_map/all_to_all | solution.py:567
  134.2 3.8 %shard_map.312 = (bf16[112,384]{1,0:T(8,128)(2,1)S(1)}, f32[8,384]{1,0:T(8,128)S(1)}, f32[384,1536]{1,0:T(8,128)}, f32[1536,384]{1,0:T(8,128)}, f32[384,384]{1,0:T(8,128)}) custom-call(s32[1]{0:T(128)} %bitcast.side_ref, bf16[1792,384]{1,0:T(8,128)(2,1)S(1)} %bitcast.57, bf16[1792,384]{1,0:T(8,128)(2,1)} %collective-permute-done.6.other_ref), custom_call_target="tpu_custom_call" | custom-call | flops 3000000000 | bytes 1048576 | tf_op jit(solution)/shard_map/pallas_call | solution.py:440
  138.0 5.6 %all-to-all-done.3 = bf16[8,80,384]{2,1,0:T(8,128)(2,1)S(1)} async-done(((bf16[8,80,384]{2,1,0:T(8,128)(2,1)}), bf16[8,80,384]{2,1,0:T(8,128)(2,1)S(1)}, u32[]{:S(2)}, u32[]{:S(2)}) %all-to-all-start.3) | async-done | bytes 491552 | tf_op jit(solution)/shard_map/all_to_all | solution.py:567
  143.7 2.1 %add_bitcast_fusion = f32[1,512,384]{2,1,0:T(8,128)} fusion(f32[512,384]{1,0:T(8,128)} %get-tuple-element.100, bf16[512,384]{1,0:T(8,128)(2,1)S(1)} %collective-permute-done.5), kind=kLoop, calls=%fused_computation.5 | loop fusion | flops 393216 | bytes 1966080 | tf_op jit(solution)/shard_map/stack | solution.py:764
  145.7 0.6 reshape.320
  146.3 0.6 slice_reduce_fusion
  147.0 3.4 %shard_map.313 = (f32[8,384]{1,0:T(8,128)S(1)}, f32[8,384]{1,0:T(8,128)S(1)}, f32[384,1152]{1,0:T(8,128)}, f32[384,2304]{1,0:T(8,128)}, f32[1000,384]{1,0:T(8,128)}) custom-call(s32[1]{0:T(128)} %bitcast.side_ref, bf16[640,384]{1,0:T(8,128)(2,1)S(1)} %bitcast.59, bf16[640,384]{1,0:T(8,128)(2,1)S(1)} %collective-permute-done.7.other_ref, ...), custom_call_target="tpu_custom_call" | custom-call | flops 4000000000 | bytes 1048576 | tf_op jit(solution)/shard_map/pallas_call | solution.py:440
  150.3 0.6 fusion.18
  150.9 0.1 reshape.319
  151.0 0.6 copy.47
  151.6 0.6 reshape.318
  (63 shorter events, 0.7 us)
Async XLA Ops:
  0.6 9.5 %copy-start.7 = (bf16[2304]{0:T(1024)(128)(2,1)S(1)}, bf16[2304]{0:T(1024)(128)(2,1)}, u32[]{:S(2)}) copy-start(bf16[2304]{0:T(1024)(128)(2,1)} %param.28) | copy-start | bytes 13828
  0.7 9.5 %copy-start.13 = (bf16[2,6,63]{2,0,1:T(2,128)(2,1)S(1)}, bf16[2,6,63]{2,0,1:T(2,128)(2,1)}, u32[]{:S(2)}) copy-start(bf16[2,6,63]{2,0,1:T(2,128)(2,1)} %param.31) | copy-start | bytes 4540
  0.7 12.7 %collective-permute-start = (bf16[512,384]{1,0:T(8,128)(2,1)}, bf16[512,384]{1,0:T(8,128)(2,1)S(1)}, u32[]{:S(2)}, u32[]{:S(2)}) collective-permute-start(bf16[512,384]{1,0:T(8,128)(2,1)} %bitcast.63), channel_id=1, source_target_pairs={{0,1},{1,0},{2,3},{3,2},{4,5},{5,4},{6,7},{7,6},{8,9},{9,8},{10,11... | collective-permute-start | bytes 1179656 | tf_op jit(solution)/shard_map/ppermute | solution.py:658
  8.2 2.9 %copy-start.10 = (bf16[384]{0:T(512)(128)(2,1)S(1)}, bf16[384]{0:T(512)(128)(2,1)}, u32[]{:S(2)}) copy-start(bf16[384]{0:T(512)(128)(2,1)} %param.33) | copy-start | bytes 2308
  8.2 2.9 %copy-start.11 = (bf16[384]{0:T(512)(128)(2,1)S(1)}, bf16[384]{0:T(512)(128)(2,1)}, u32[]{:S(2)}) copy-start(bf16[384]{0:T(512)(128)(2,1)} %param.37) | copy-start | bytes 2308
  8.2 2.9 %copy-start.9 = (bf16[2,384]{1,0:T(2,128)(2,1)S(1)}, bf16[2,384]{1,0:T(2,128)(2,1)}, u32[]{:S(2)}) copy-start(bf16[2,384]{1,0:T(2,128)(2,1)} %param.30) | copy-start | bytes 4612
  8.2 2.9 %copy-start.8 = (bf16[1536]{0:T(1024)(128)(2,1)S(1)}, bf16[1536]{0:T(1024)(128)(2,1)}, u32[]{:S(2)}) copy-start(bf16[1536]{0:T(1024)(128)(2,1)} %param.35) | copy-start | bytes 9220
  8.2 3.2 %copy-start.6 = (s32[1,704]{1,0:T(1,128)S(1)}, s32[1,704]{1,0:T(1,128)}, u32[]{:S(2)}) copy-start(s32[1,704]{1,0:T(1,128)} %param.21) | copy-start | bytes 8452
  11.8 1.5 %copy-start.3 = (bf16[384,1152]{1,0:T(8,128)(2,1)S(1)}, bf16[384,1152]{1,0:T(8,128)(2,1)}, u32[]{:S(2)}) copy-start(bf16[384,1152]{1,0:T(8,128)(2,1)} %refs_4_.1) | copy-start | bytes 2654212
  11.8 1.5 %copy-start.4 = (bf16[1,512,384]{2,1,0:T(8,128)(2,1)S(1)}, bf16[1,512,384]{2,1,0:T(8,128)(2,1)}, u32[]{:S(2)}) copy-start(bf16[1,512,384]{2,1,0:T(8,128)(2,1)} %param.20) | copy-start | bytes 1179652
  19.0 11.6 %copy-start.1 = (bf16[384,1536]{1,0:T(8,128)(2,1)S(1)}, bf16[384,1536]{1,0:T(8,128)(2,1)}, u32[]{:S(2)}) copy-start(bf16[384,1536]{1,0:T(8,128)(2,1)} %w1_ref.1) | copy-start | bytes 3538948
  19.0 11.6 %copy-start.2 = (bf16[1536,384]{1,0:T(8,128)(2,1)S(1)}, bf16[1536,384]{1,0:T(8,128)(2,1)}, u32[]{:S(2)}) copy-start(bf16[1536,384]{1,0:T(8,128)(2,1)} %w2_ref.1) | copy-start | bytes 3538948
  19.0 11.6 %copy-start.5 = (bf16[384,384]{1,0:T(8,128)(2,1)S(1)}, bf16[384,384]{1,0:T(8,128)(2,1)}, u32[]{:S(2)}) copy-start(bf16[384,384]{1,0:T(8,128)(2,1)} %wout_ref.1) | copy-start | bytes 884740
  45.8 7.3 %collective-permute-start.1 = (bf16[1792,384]{1,0:T(8,128)(2,1)}, bf16[1792,384]{1,0:T(8,128)(2,1)}, u32[]{:S(2)}, u32[]{:S(2)}) collective-permute-start(bf16[1792,384]{1,0:T(8,128)(2,1)} %get-tuple-element.86), channel_id=1, source_target_pairs={{0,2},{2,0},{4,6},{6,4},{8,10},{10,8},{12,14},{14,12},{16,18},{18,... | collective-permute-start | bytes 4128776 | tf_op jit(solution)/shard_map/ppermute | solution.py:558
  55.9 25.4 %all-to-all-start = ((bf16[8,224,384]{2,1,0:T(8,128)(2,1)}), bf16[8,224,384]{2,1,0:T(8,128)(2,1)S(1)}, u32[]{:S(2)}, u32[]{:S(2)}) async-start(bf16[8,224,384]{2,1,0:T(8,128)(2,1)} %bitcast.65), calls=%async_computation | async-start | bytes 2752512 | tf_op jit(solution)/shard_map/all_to_all | solution.py:567
  78.4 1.9 %collective-permute-start.2 = (bf16[640,384]{1,0:T(8,128)(2,1)S(1)}, bf16[640,384]{1,0:T(8,128)(2,1)S(1)}, u32[]{:S(2)}, u32[]{:S(2)}) collective-permute-start(bf16[640,384]{1,0:T(8,128)(2,1)S(1)} %get-tuple-element.102), channel_id=1, source_target_pairs={{0,2},{2,0},{4,6},{6,4},{8,10},{10,8},{12,14},{14,12},{16,18},{18,... | collective-permute-start | bytes 1474568 | tf_op jit(solution)/shard_map/ppermute | solution.py:558
  81.3 17.8 %all-to-all-start.2 = ((bf16[8,80,384]{2,1,0:T(8,128)(2,1)}), bf16[8,80,384]{2,1,0:T(8,128)(2,1)S(1)}, u32[]{:S(2)}, u32[]{:S(2)}) async-start(bf16[8,80,384]{2,1,0:T(8,128)(2,1)} %bitcast.29), calls=%async_computation.2 | async-start | bytes 983040 | tf_op jit(solution)/shard_map/all_to_all | solution.py:567
  86.6 9.3 %collective-permute-start.3 = (bf16[224,384]{1,0:T(8,128)(2,1)S(1)}, bf16[224,384]{1,0:T(8,128)(2,1)S(1)}, u32[]{:S(2)}, u32[]{:S(2)}) collective-permute-start(bf16[224,384]{1,0:T(8,128)(2,1)S(1)} %reduce_sum.24), channel_id=1, source_target_pairs={{0,16},{2,18},{4,20},{6,22},{8,24},{10,26},{12,28},{14,30},{16,0},... | collective-permute-start | bytes 516104 | tf_op jit(solution)/shard_map/ppermute | solution.py:572
  100.3 4.7 %copy-start.12 = (bf16[1,512,384]{2,1,0:T(8,128)(2,1)S(1)}, bf16[1,512,384]{2,1,0:T(8,128)(2,1)}, u32[]{:S(2)}) copy-start(bf16[1,512,384]{2,1,0:T(8,128)(2,1)} %get-tuple-element.106) | copy-start | bytes 1179652
  100.3 29.4 %all-to-all-start.1 = ((bf16[8,224,384]{2,1,0:T(8,128)(2,1)}), bf16[8,224,384]{2,1,0:T(8,128)(2,1)S(1)}, u32[]{:S(2)}, u32[]{:S(2)}) async-start(bf16[8,224,384]{2,1,0:T(8,128)(2,1)} %broadcast_in_dim.78), calls=%async_computation.1 | async-start | bytes 2752512 | tf_op jit(solution)/shard_map/all_to_all | solution.py:567
  105.1 24.7 %collective-permute-start.5 = (bf16[512,384]{1,0:T(8,128)(2,1)S(1)}, bf16[512,384]{1,0:T(8,128)(2,1)S(1)}, u32[]{:S(2)}, u32[]{:S(2)}) collective-permute-start(bf16[512,384]{1,0:T(8,128)(2,1)S(1)} %bitcast.73), channel_id=1, source_target_pairs={{0,1},{1,0},{2,3},{3,2},{4,5},{5,4},{6,7},{7,6},{8,9},{9,8},{10,11... | collective-permute-start | bytes 1179656 | tf_op jit(solution)/shard_map/ppermute | solution.py:583
  107.1 13.3 %collective-permute-start.4 = (bf16[80,384]{1,0:T(8,128)(2,1)S(1)}, bf16[80,384]{1,0:T(8,128)(2,1)S(1)}, u32[]{:S(2)}, u32[]{:S(2)}) collective-permute-start(bf16[80,384]{1,0:T(8,128)(2,1)S(1)} %reduce_sum.25), channel_id=1, source_target_pairs={{0,16},{2,18},{4,20},{6,22},{8,24},{10,26},{12,28},{14,30},{16,0},... | collective-permute-start | bytes 184328 | tf_op jit(solution)/shard_map/ppermute | solution.py:572
  129.7 4.5 %collective-permute-start.6 = (bf16[1792,384]{1,0:T(8,128)(2,1)S(1)}, bf16[1792,384]{1,0:T(8,128)(2,1)}, u32[]{:S(2)}, u32[]{:S(2)}) collective-permute-start(bf16[1792,384]{1,0:T(8,128)(2,1)S(1)} %bitcast.56), channel_id=1, source_target_pairs={{0,2},{2,0},{4,6},{6,4},{8,10},{10,8},{12,14},{14,12},{16,18},{18,... | collective-permute-start | bytes 4128776 | tf_op jit(solution)/shard_map/ppermute | solution.py:558
  130.5 13.1 %all-to-all-start.3 = ((bf16[8,80,384]{2,1,0:T(8,128)(2,1)}), bf16[8,80,384]{2,1,0:T(8,128)(2,1)S(1)}, u32[]{:S(2)}, u32[]{:S(2)}) async-start(bf16[8,80,384]{2,1,0:T(8,128)(2,1)} %broadcast_in_dim.79), calls=%async_computation.3 | async-start | bytes 983040 | tf_op jit(solution)/shard_map/all_to_all | solution.py:567
  138.0 8.9 %copy-start = (bf16[384,2304]{1,0:T(8,128)(2,1)S(1)}, bf16[384,2304]{1,0:T(8,128)(2,1)}, u32[]{:S(2)}) copy-start(bf16[384,2304]{1,0:T(8,128)(2,1)} %ada_ref.1) | copy-start | bytes 5308420
  143.7 3.3 %collective-permute-start.7 = (bf16[640,384]{1,0:T(8,128)(2,1)S(1)}, bf16[640,384]{1,0:T(8,128)(2,1)S(1)}, u32[]{:S(2)}, u32[]{:S(2)}) collective-permute-start(bf16[640,384]{1,0:T(8,128)(2,1)S(1)} %bitcast.58), channel_id=1, source_target_pairs={{0,2},{2,0},{4,6},{6,4},{8,10},{10,8},{12,14},{14,12},{16,18},{18,... | collective-permute-start | bytes 1474568 | tf_op jit(solution)/shard_map/ppermute | solution.py:558

commit v3 on v2

v3 whole, which is shorter than its diff:
```python
import functools
import math

import jax
import jax.numpy as jnp
from jax import lax
from jax.experimental import pallas as pl
from jax.experimental.pallas import tpu as pltpu
from jax.sharding import PartitionSpec as P

D = 384
HEADS = 6
HDIM = 64
GRID = 32
FF = 1536
CHUNK = 256

AXES = ("dp", "seq")
F32 = jnp.float32
BF16 = jnp.bfloat16
MIB = 1024 * 1024
GELU_A = math.sqrt(2.0 / math.pi)
GELU_B = 0.044715

highest = lax.Precision.HIGHEST
big_negative = -1e30
vmem = pl.BlockSpec(memory_space=pltpu.VMEM)
smem = pl.BlockSpec(memory_space=pltpu.SMEM)
hbm = pl.BlockSpec(memory_space=pltpu.HBM)


def round_up(value, step):
    return -(-value // step) * step


def blocks_of(first, count, most):
    pieces = -(-count // most)
    size = round_up(-(-count // pieces), 16)
    found = []
    at = 0
    while at < count:
        found.append((first + at, min(size, count - at)))
        at += size
    return found


def mm(left, right):
    return lax.dot_general(left, right, (((1,), (0,)), ((), ())), preferred_element_type=F32)


def mm_t(left, right):
    return lax.dot_general(left, right, (((1,), (1,)), ((), ())), preferred_element_type=F32)


def norm_parts(value):
    average = jnp.mean(value, axis=-1, keepdims=True)
    centred = value - average
    variance = jnp.mean(centred * centred, axis=-1, keepdims=True)
    inverse = lax.rsqrt(variance + 1e-06)
    return (centred * inverse, inverse)


def norm_back(normed, inverse, grad):
    first = jnp.mean(grad, axis=-1, keepdims=True)
    second = jnp.mean(grad * normed, axis=-1, keepdims=True)
    return inverse * (grad - first - normed * second)


def place_onehot(position, turned=False):
    lane = lax.broadcasted_iota(jnp.int32, (position.shape[0], 2 * GRID), 1)
    if turned:
        lane = jnp.where(lane < GRID, GRID - 1 - lane, 3 * GRID - 1 - lane)
    wanted = jnp.where(lane < GRID, position // GRID, position % GRID + GRID)
    return (lane == wanted).astype(F32).astype(BF16)


class Copies:
    def __init__(self, sems):
        self.sems, self.made = sems, []

    def start(self, source, target):
        copy = pltpu.make_async_copy(source, target, self.sems.at[len(self.made)])
        copy.start()
        self.made.append(copy)

    def wait(self):
        for copy in self.made:
            copy.wait()


def split_halves(copies, side, payload_ref, keep_ref, send_ref):
    half = keep_ref.shape[0]
    for which, target in ((side, keep_ref), (1 - side, send_ref)):
        copies.start(payload_ref.at[pl.ds(pl.multiple_of(which * half, 16), half)], target)


def prep_kernel(
    own, seq, starts_ref, *refs,
):
    token_refs, refs = refs[:seq], refs[seq:]
    kept_ref, picked_ref, where_ref, mod_ref, weight_ref, qv_ref, table_ref = refs[:7]
    qaug_ref, kaug_ref, vaug_ref, x_ref, mask_ref, a_out, tok_out, slot_out = refs[7:15]
    qs_ref, a_ref, tok_ref, slot_ref, sems = refs[15:]
    copies = Copies(sems)
    total = own * seq
    slots = picked_ref.shape[0]
    for n in range(seq):
        tok_ref[pl.ds(pl.multiple_of(starts_ref[n], 16), own), :] = token_refs[n][...]
    copies.start(tok_ref, tok_out)
    shift, scale = mod_ref[0:1, :], mod_ref[1:2, :]
    normed, unused = norm_parts(tok_ref[...].astype(F32))
    lowered = (normed * (1.0 + scale) + shift).astype(BF16)
    a_ref[...] = lowered
    copies.start(a_ref, a_out)
    query = (mm(lowered, weight_ref[:, :D]) + qv_ref[0:1, :]).astype(BF16)
    scaled = (query.astype(F32) * (1.0 / math.sqrt(HDIM))).astype(BF16)
    qs_ref[...] = scaled
    keys = mm(lowered, weight_ref[:, D : 2 * D]).astype(BF16)
    values = (mm(lowered, weight_ref[:, 2 * D :]) + qv_ref[1:2, :]).astype(BF16)
    key_place = place_onehot(lax.broadcasted_iota(jnp.int32, (total, 1), 0))
    lane = lax.broadcasted_iota(jnp.int32, (total, HDIM), 1)
    ones = (lane < 2).astype(F32).astype(BF16)
    for head in range(HEADS):
        cols = slice(head * HDIM, (head + 1) * HDIM)
        kaug_ref[head] = jnp.concatenate([keys[:, cols], key_place], axis=1)
        vaug_ref[head] = jnp.concatenate([values[:, cols], ones], axis=1)
    chosen = (picked_ref[...] == lax.broadcasted_iota(jnp.int32, (slots, total), 1)).astype(F32)
    chosen = chosen.astype(BF16)
    x_ref[:own, :] = token_refs[0][...]
    x_ref[own:, :] = mm(chosen, tok_ref[...]).astype(BF16)
    slot_ref[...] = mm(chosen, lowered).astype(BF16)
    copies.start(slot_ref, slot_out)
    slot_query = mm(chosen, scaled).astype(BF16)
    own_query = qs_ref[pl.ds(pl.multiple_of(starts_ref[0], 16), own), :]
    offsets = mm(place_onehot(where_ref[...]), table_ref[...]).astype(BF16)
    for head in range(HEADS):
        cols = slice(head * HDIM, (head + 1) * HDIM)
        qaug_ref[head, :own] = jnp.concatenate([own_query[:, cols], offsets[:own, cols]], axis=1)
        qaug_ref[head, own:] = jnp.concatenate([slot_query[:, cols], offsets[own:, cols]], axis=1)
    held = kept_ref.shape[0]
    hit = kept_ref[...] == lax.broadcasted_iota(jnp.int32, (held, total), 1)
    count = jnp.sum(hit.astype(F32), axis=0, keepdims=True)
    mask_ref[...] = jnp.broadcast_to(jnp.where(count > 0.0, 0.0, big_negative), mask_ref.shape)
    copies.wait()


def attend_kernel(
    own, qaug_ref, kaug_ref, vaug_ref, mask_ref, o_ref, inverse_ref, e_out, qaug_out, kaug_out, vaug_out, e_ref, sems
):
    rows = qaug_ref.shape[1]
    copies = Copies(sems)
    copies.start(qaug_ref, qaug_out)
    copies.start(kaug_ref, kaug_out)
    copies.start(vaug_ref, vaug_out)
    spans = [(at, size, False) for at, size in blocks_of(0, own, 256)]
    spans += [(at, size, True) for at, size in blocks_of(own, rows - own, 256)]

    def pair(group, carry):
        items = [(side, *span) for side in range(2) for span in spans]
        scores, spread = {}, {}
        for n in range(len(items) + 2):
            if n < len(items):
                side, at, size, masked = items[n]
                head = 2 * group + side
                scores[n] = mm_t(qaug_ref[head, at : at + size, :], kaug_ref[head])
                if masked:
                    scores[n] = scores[n] + mask_ref[0:1, :]
            if 0 <= n - 1 < len(items):
                side, at, size, masked = items[n - 1]
                found = scores.pop(n - 1)
                spread[n - 1] = jnp.exp(found - jnp.max(found, axis=-1, keepdims=True)).astype(BF16)
                e_ref[2 * group + side, at : at + size, :] = spread[n - 1]
            if 0 <= n - 2:
                side, at, size, masked = items[n - 2]
                mixed = mm(spread.pop(n - 2), vaug_ref[2 * group + side])
                inverse = 1.0 / mixed[:, HDIM : HDIM + 1]
                lanes = slice(side * HDIM, (side + 1) * HDIM)
                o_ref[group, at : at + size, lanes] = mixed[:, :HDIM] * inverse
                inverse_ref[group, at : at + size, lanes] = jnp.broadcast_to(inverse, (size, HDIM))
        pltpu.make_async_copy(e_ref.at[pl.ds(2 * group, 2)], e_out.at[pl.ds(2 * group, 2)], sems.at[3 + group]).start()
        return carry

    lax.fori_loop(0, HEADS // 2, pair, 0)
    for group in range(HEADS // 2):
        heads = pl.ds(2 * group, 2)
        pltpu.make_async_copy(e_ref.at[heads], e_out.at[heads], sems.at[3 + group]).wait()
    copies.wait()


def feed_kernel(
    side_ref, o_ref, x_ref, cot_ref, wgt_ref, mod_ref, wout_ref, bout_ref, w1_ref, b1_ref, w2_ref, extra_ref,
    att_ref, hidden_ref, du_ref, keep_ref, send_ref, pay_ref, sems,
):
    rows = x_ref.shape[0]
    gate1, shift2, scale2, gate2 = [mod_ref[n : n + 1, :] for n in range(2, 6)]
    merged = jnp.concatenate([o_ref[n] for n in range(HEADS // 2)], axis=1).astype(BF16)
    attended = mm(merged, wout_ref[...]) + bout_ref[...]
    att_ref[...] = attended
    normed, unused = norm_parts(x_ref[...].astype(F32) + gate1 * attended)
    second = (normed * (1.0 + scale2) + shift2).astype(BF16)
    dz = (gate2 * (cot_ref[...].astype(F32) * wgt_ref[...])).astype(BF16)

    def products(c):
        cols = slice(c * CHUNK, (c + 1) * CHUNK)
        return mm(second, w1_ref[:, cols]) + b1_ref[:, cols], mm_t(dz, w2_ref[cols, :])

    chunks = FF // CHUNK
    ready = products(0)
    for c in range(chunks):
        u, back_u = ready
        if c + 1 < chunks:
            ready = products(c + 1)
        cols = slice(c * CHUNK, (c + 1) * CHUNK)
        square = u * u
        t = jnp.tanh(u * (square * (GELU_A * GELU_B) + GELU_A))
        cdf = t * 0.5 + 0.5
        hidden_ref[:, cols] = (u * cdf).astype(BF16)
        slope = cdf * ((1.0 - t) * (u * (square * (3.0 * GELU_A * GELU_B) + GELU_A)) + 1.0)
        du_ref[:, cols] = (slope * back_u).astype(BF16)
    ones = jnp.ones((16, rows), BF16)
    grad = mm(jnp.concatenate([second.T, ones], axis=0), du_ref[...])
    heads = []
    for n in range(4):
        cols = slice(n * D, (n + 1) * D)
        pay_ref[cols, :] = grad[:D, cols].astype(BF16)
        heads.append(grad[D : D + 1, cols])
    pay_ref[FF : 2 * FF, :] = mm(hidden_ref[...].T, dz).astype(BF16)
    heads += [jnp.sum(dz.astype(F32), axis=0, keepdims=True), jnp.zeros((11, D), F32)]
    pay_ref[2 * FF : 2 * FF + 16, :] = jnp.concatenate(heads, axis=0).astype(BF16)
    pay_ref[2 * FF + 16 :, :] = extra_ref[...]
    copies = Copies(sems)
    split_halves(copies, side_ref[0], pay_ref, keep_ref, send_ref)
    copies.wait()


def feed_rest_kernel(
    own, o_ref, inverse_ref, x_ref, cot_ref, wgt_ref, mod_ref, wout_ref, w1_ref, w2_ref, b2_ref,
    att_ref, hidden_ref, du_ref,
    small_ref, y_full_out, y_slot_out, dm_out, x_out, do_out, go_out, y_ref, dm_ref, do_ref, go_ref, sems,
):
    rows = x_ref.shape[0]
    copies = Copies(sems)
    copies.start(x_ref, x_out)
    gate1, shift2, scale2, gate2 = [mod_ref[n : n + 1, :] for n in range(2, 6)]
    weight = wgt_ref[...]
    back = mm_t(du_ref[...], w1_ref[...])
    branch = mm(hidden_ref[...], w2_ref[...]) + b2_ref[...]
    attended = att_ref[...]
    middle = x_ref[...].astype(F32) + gate1 * attended
    normed, inverse = norm_parts(middle)
    cot = cot_ref[...].astype(F32) * weight
    y_ref[...] = ((middle + gate2 * branch) * weight).astype(BF16)
    copies.start(y_ref.at[pl.ds(0, own)], y_full_out)
    copies.start(y_ref.at[pl.ds(own, rows - own)], y_slot_out)
    dmid = cot + norm_back(normed, inverse, back * (1.0 + scale2))
    dm_ref[...] = dmid
    copies.start(dm_ref, dm_out)
    datt = (gate1 * dmid).astype(BF16)
    merged_f = jnp.concatenate([o_ref[n] for n in range(HEADS // 2)], axis=1)
    dout = mm_t(datt, wout_ref[...]) * jnp.concatenate([inverse_ref[n] for n in range(HEADS // 2)], axis=1)
    dout = dout.astype(BF16).astype(F32)
    product = dout * merged_f
    high = product.astype(BF16)
    low = (product - high.astype(F32)).astype(BF16)
    row = lax.broadcasted_iota(jnp.int32, (D, 128), 0)
    lane = lax.broadcasted_iota(jnp.int32, (D, 128), 1)
    heads = jnp.where(row // HDIM == lane // 2, -1.0, 0.0).astype(BF16)
    less = mm(high, heads) + mm(low, heads)
    lane = lax.broadcasted_iota(jnp.int32, (rows, 128), 1)
    kept = less.astype(BF16).astype(F32)
    pair = jnp.where(lane % 2 == 0, kept, less - kept)
    for head in range(HEADS):
        tile = dout[:, head // 2 * 128 : (head // 2 + 1) * 128]
        if head % 2:
            tile = pltpu.roll(tile, HDIM, 1)
        more = pltpu.roll(pair, HDIM - 2 * head, 1)
        more = jnp.where(lane < HDIM + 2, more, 0.0)
        do_ref[head] = jnp.where(lane < HDIM, tile, more).astype(BF16)
    copies.start(do_ref, do_out)
    go_ref[...] = mm(merged_f.astype(BF16).T, datt).astype(BF16)
    copies.start(go_ref, go_out)
    column = lambda value: jnp.sum(value.astype(F32), axis=0, keepdims=True)
    sums = [dmid * attended, back, back * normed, cot * branch, datt]
    small_ref[...] = jnp.concatenate([column(value) for value in sums] + [jnp.zeros((3, D), F32)], axis=0)
    copies.wait()


def attend_back(own, e_ref, q_ref, k_ref, v_ref, do_ref, place_ref, outs, sums):
    dq_ref, dk_ref, dv_ref, tab_ref = outs
    dkt_ref, dvt_ref, part_ref = sums
    rows = q_ref.shape[1]
    spans = blocks_of(0, own, 256) + blocks_of(own, rows - own, 256)
    items = [(side, *span) for side in range(2) for span in spans]
    grads, found = {}, {}
    for n in range(len(items) + 2):
        if n < len(items):
            side, at, size = items[n]
            grads[n] = mm_t(do_ref[side, at : at + size, :], v_ref[side])
        if 0 <= n - 1 < len(items):
            side, at, size = items[n - 1]
            found[n - 1] = (e_ref[side, at : at + size, :].astype(F32) * grads.pop(n - 1)).astype(BF16)
        if 0 <= n - 2:
            side, at, size = items[n - 2]
            lanes = slice(side * HDIM, (side + 1) * HDIM)
            ds = found.pop(n - 2)
            dq = mm(ds, k_ref[side])
            dq_ref[at : at + size, lanes] = (dq[:, :HDIM] * (1.0 / math.sqrt(HDIM))).astype(BF16)
            part_ref[at : at + size, lanes] = dq[:, HDIM:].astype(BF16)
            dkt = mm(q_ref[side, at : at + size, :HDIM].T, ds)
            dvt = mm(do_ref[side, at : at + size, :HDIM].T, e_ref[side, at : at + size, :])
            if at == 0:
                dkt_ref[lanes, :] = dkt
                dvt_ref[lanes, :] = dvt
            else:
                dkt_ref[lanes, :] += dkt
                dvt_ref[lanes, :] += dvt
    tab_ref[...] = mm(place_ref[...], part_ref[...])
    dk_ref[...] = dkt_ref[...].astype(BF16).T
    dv_ref[...] = dvt_ref[...].astype(BF16).T


def back_kernel(own, everyone, scalar_ref, where_ref, picked_ref, mod_ref, prior_ref, *refs):
    group_sources, refs = refs[:5], refs[5:]
    sources, refs = refs[:7], refs[7:]
    keep_ref, send_ref, dx_ref, dx_own_ref, refs = *refs[:4], refs[4:]
    group_local, refs = refs[:5], refs[5:]
    local, refs = refs[:7], refs[7:]
    dq_ref, dk_ref, dv_ref, tab_ref, normed_ref, inverse_ref, dxs_ref, dkt_ref, dvt_ref, pay_ref = refs[:10]
    place_ref, part_ref, group_sems, sems, pay_sems = refs[10:]
    tok_ref, a_ref, x_ref, slot_ref, weight_ref, dm_ref, go_ref = local
    step = pl.program_id(0)
    last = pl.num_programs(0) - 1
    slot = step % 2

    def fetches(group, place):
        return [
            pltpu.make_async_copy(source.at[pl.ds(2 * group, 2)], target.at[place], group_sems.at[place, n])
            for n, (source, target) in enumerate(zip(group_sources, group_local))
        ]

    def copies():
        return [
            pltpu.make_async_copy(source, target, sems.at[n])
            for n, (source, target) in enumerate(zip(sources, local))
        ]

    @pl.when(step == 0)
    def first():
        whole = copies()
        whole[0].start()
        for copy in fetches(0, 0):
            copy.start()
        for copy in whole[1:]:
            copy.start()
        for copy in fetches(1, 1):
            copy.start()
        place_ref[...] = place_onehot(where_ref[...], turned=True).T
        whole[0].wait()
        normed, inverse = norm_parts(tok_ref[...].astype(F32))
        normed_ref[...] = normed
        inverse_ref[...] = jnp.broadcast_to(inverse, inverse_ref.shape)

    @pl.when((step > 0) & (step + 1 < last))
    def following():
        for copy in fetches(step + 1, 1 - slot):
            copy.start()

    @pl.when(step < last)
    def attention():
        for copy in fetches(step, slot):
            copy.wait()
        outs = dq_ref.at[step], dk_ref.at[step], dv_ref.at[step], tab_ref.at[step]
        attend_back(own, *[ref.at[slot] for ref in group_local], place_ref, outs, (dkt_ref, dvt_ref, part_ref))

    @pl.when(step == last)
    def projections():
        for copy in copies()[1:]:
            copy.wait()
        groups = dq_ref.shape[0]
        total = tok_ref.shape[0]
        rows = x_ref.shape[0]
        slots = rows - own
        scale = mod_ref[1:2, :]
        here = pl.ds(pl.multiple_of(scalar_ref[1], 16), own)

        def joined(ref, span):
            return jnp.concatenate([ref[n, span, :] for n in range(groups)], axis=1)

        every = slice(0, total)
        dk, dv = joined(dk_ref, every), joined(dv_ref, every)
        dq_own, dq_slot = joined(dq_ref, slice(0, own)), joined(dq_ref, slice(own, rows))
        column = lambda value: jnp.sum(value.astype(F32), axis=0, keepdims=True)
        lowered_t = a_ref[...].T
        pay_ref[0:D, :] = (mm(a_ref[here, :].T, dq_own) + mm(slot_ref[...].T, dq_slot)).astype(BF16)
        pay_ref[D : 2 * D, :] = mm(lowered_t, dk).astype(BF16)
        pay_ref[2 * D : 3 * D, :] = mm(lowered_t, dv).astype(BF16)
        pay_ref[3 * D : 4 * D, :] = go_ref[...]
        slot_normed, slot_inverse = norm_parts(x_ref[own:, :].astype(F32))
        da = mm_t(dq_slot, weight_ref[:, :D])
        shift_sum, scale_sum = column(da), column(da * slot_normed)
        spread = dm_ref[own:, :] + norm_back(slot_normed, slot_inverse, da * (1.0 + scale))
        chosen = (picked_ref[...] == lax.broadcasted_iota(jnp.int32, (slots, total), 1)).astype(F32)
        moved = mm(chosen.astype(BF16).T, spread.astype(BF16))
        dxs_ref[...] = mm_t(dk, weight_ref[:, D : 2 * D]) + mm_t(dv, weight_ref[:, 2 * D :])
        dxs_ref[here, :] += mm_t(dq_own, weight_ref[:, :D])
        da = dxs_ref[...]
        normed = normed_ref[...]
        shift_sum, scale_sum = shift_sum + column(da), scale_sum + column(da * normed)
        inverse = jnp.concatenate([inverse_ref[...]] * (D // 128), axis=1)
        dxs_ref[...] = moved + norm_back(normed, inverse, da * (1.0 + scale))
        dx_own_ref[...] = dxs_ref[here, :] + dm_ref[:own, :]
        for n in range(dx_ref.shape[0]):
            dx_ref[n] = dxs_ref[pl.ds(pl.multiple_of(scalar_ref[3 + n], 16), own), :].astype(BF16)
        rel = table_sums([tab_ref[n] for n in range(groups)])
        smalls = jnp.concatenate(
            [
                shift_sum, scale_sum, prior_ref[0:4, :], column(dq_own) + column(dq_slot), column(dv),
                *rel, prior_ref[4:5, :], jnp.zeros((5, D), F32),
            ],
            axis=0,
        ).astype(BF16)
        tail = pay_ref.shape[0] - 4 * D
        row = lax.broadcasted_iota(jnp.int32, (tail, 16), 0)
        lane = lax.broadcasted_iota(jnp.int32, (tail, 16), 1)
        wanted = jnp.where(row % everyone == scalar_ref[2], row // everyone, -1)
        wanted = jnp.where(row < 6 * everyone, wanted, row - 6 * everyone + 6)
        pay_ref[4 * D :, :] = mm((lane == wanted).astype(F32).astype(BF16), smalls).astype(BF16)
        halves = Copies(pay_sems)
        split_halves(halves, scalar_ref[0], pay_ref, keep_ref, send_ref)
        halves.wait()


def table_sums(tabs):
    found = ([], [])
    for tab in tabs:
        for side in range(2):
            for part in range(2):
                at = 2 * side * GRID + part * GRID
                square = tab[part * GRID : (part + 1) * GRID, at : at + GRID]
                wide = jnp.concatenate([square, jnp.zeros((GRID, 128 - GRID), F32)], axis=1)
                turned = pltpu.roll(wide, 0, 1, stride=1, stride_axis=0)
                found[part].append(jnp.sum(turned, axis=0, keepdims=True)[:, : 2 * GRID])
    return [jnp.concatenate(parts, axis=1) for parts in found]


def call(kernel, outs, scratch, args, scalars=0, far=0, away=0, copies=0, micros=1, limit=32):
    scratches = [pltpu.VMEM(shape, dtype) for shape, dtype in scratch]
    if copies:
        scratches.append(pltpu.SemaphoreType.DMA((copies,)))
    return pl.pallas_call(
        kernel,
        out_shape=[jax.ShapeDtypeStruct(shape, dtype) for shape, dtype in outs[: len(outs) - away]]
        + [pltpu.HBM(shape, dtype) for shape, dtype in outs[len(outs) - away :]],
        in_specs=[smem] * scalars + [vmem] * (len(args) - scalars - far) + [hbm] * far,
        out_specs=[vmem] * (len(outs) - away) + [hbm] * away,
        scratch_shapes=scratches,
        compiler_params=pltpu.CompilerParams(vmem_limit_bytes=limit * MIB),
        cost_estimate=pl.CostEstimate(flops=micros * 10**9, bytes_accessed=MIB, transcendentals=0),
    )(*args)


def in_hbm(value):
    return pltpu.with_memory_space_constraint(value, pltpu.HBM)


def add_kernel(left_ref, right_ref, sum_ref):
    sum_ref[...] = (left_ref[...].astype(F32) + right_ref[...].astype(F32)).astype(BF16)


def add_call(left, right, micros):
    return call(add_kernel, [(left.shape, BF16)], [], [left, right], micros=micros)[0]


def back_call(own, everyone, groups_of, sources, scalars, where, picked, mod, prior, tail_half):
    rows, total = groups_of[1].shape[1], groups_of[2].shape[1]
    groups = HEADS // 2
    others = total // own - 1
    whole = lambda shape: pl.BlockSpec(shape, lambda n: (0,) * len(shape))
    outs = [((tail_half, D), BF16), ((tail_half, D), BF16), ((others, own, D), BF16), ((own, D), F32)]
    scratch = [((2, 2) + value.shape[1:], value.dtype) for value in groups_of]
    scratch += [(value.shape, value.dtype) for value in sources]
    scratch += [
        ((groups, rows, 128), BF16), ((groups, total, 128), BF16), ((groups, total, 128), BF16),
        ((groups, 2 * GRID, 128), F32), ((total, D), F32), ((total, 128), F32), ((total, D), F32),
        ((128, total), F32), ((128, total), F32), ((2 * tail_half, D), BF16),
        ((2 * GRID, rows), BF16), ((rows, 128), BF16),
    ]
    small = [where, picked, mod, prior]
    return pl.pallas_call(
        functools.partial(back_kernel, own, everyone),
        grid=(groups + 1,),
        out_shape=[jax.ShapeDtypeStruct(shape, dtype) for shape, dtype in outs[:2]]
        + [pltpu.HBM(shape, dtype) for shape, dtype in outs[2:]],
        in_specs=[smem] + [whole(value.shape) for value in small] + [hbm] * (len(groups_of) + len(sources)),
        out_specs=[vmem, vmem] + [whole(shape) for shape, unused in outs[2:]],
        scratch_shapes=[pltpu.VMEM(shape, dtype) for shape, dtype in scratch]
        + [pltpu.SemaphoreType.DMA((2, 5)), pltpu.SemaphoreType.DMA((7,)), pltpu.SemaphoreType.DMA((2,))],
        compiler_params=pltpu.CompilerParams(
            vmem_limit_bytes=48 * MIB, dimension_semantics=("arbitrary",)
        ),
        cost_estimate=pl.CostEstimate(flops=18 * 10**9, bytes_accessed=MIB, transcendentals=0),
    )(scalars, *small, *map(in_hbm, groups_of), *map(in_hbm, sources))


def halves_reader(side_ref, mine_ref, other_ref):
    half = mine_ref.shape[0]

    def get(at, count):
        found = []
        for which in range(2):
            first, last = max(at, which * half), min(at + count, (which + 1) * half)
            if first < last:
                span = slice(first - which * half, last - which * half)
                found.append(jnp.where(side_ref[0] == which, mine_ref[span, :], other_ref[span, :]))
        return found[0] if len(found) == 1 else jnp.concatenate(found, axis=0)

    return get


def layer_kernel(side_ref, mine_ref, other_ref, info_ref, small_ref, g1_out, g2_out, g1_ref, g2_ref, sems):
    get = halves_reader(side_ref, mine_ref, other_ref)
    copies = Copies(sems)
    for n in range(4):
        cols = pl.ds(n * D, D)
        g1_ref[:, cols] = get(n * D, D).astype(F32)
        copies.start(g1_ref.at[:, cols], g1_out.at[:, cols])
        g2_ref[cols, :] = get(FF + n * D, D).astype(F32)
        copies.start(g2_ref.at[cols], g2_out.at[cols])
    small_ref[...] = get(2 * FF, 16).astype(F32)[:8]
    info_ref[...] = get(2 * FF + 16, info_ref.shape[0])
    copies.wait()


def last_kernel(
    everyone, side_ref, mine_ref, other_ref, info_ref, ada_ref, qv_ref, rel_ref, out_bias_ref, ada_bias_ref,
    gqkv_out, gada_out, table_out, go_out, gqkv_ref, gada_ref, table_ref, go_ref, sems,
):
    get = halves_reader(side_ref, mine_ref, other_ref)
    copies = Copies(sems)
    act_t = info_ref[:everyone, :].T
    back = jnp.zeros((everyone, D), F32)
    for n in range(6):
        cols = pl.ds(n * D, D)
        dmod = get(4 * D + n * everyone, everyone)
        gada_ref[:, cols] = mm(act_t, dmod)
        copies.start(gada_ref.at[:, cols], gada_out.at[:, cols])
        ada_bias_ref[cols] = jnp.sum(dmod.astype(F32), axis=0)
        back = back + mm_t(dmod, ada_ref[:, cols])
    for n in range(3):
        cols = pl.ds(n * D, D)
        gqkv_ref[:, cols] = get(n * D, D).astype(F32)
        copies.start(gqkv_ref.at[:, cols], gqkv_out.at[:, cols])
    go_ref[...] = get(3 * D, D).astype(F32)
    copies.start(go_ref, go_out)
    cond = info_ref[everyone : 2 * everyone, :].astype(F32) * back
    high = cond.astype(BF16)
    low = (cond - high.astype(F32)).astype(BF16)
    digits = info_ref[2 * everyone : 3 * everyone, :].astype(F32)
    label = (digits[:, 0:1] * GRID + digits[:, 1:2]).astype(jnp.int32)
    classes = table_ref.shape[0]
    wide = round_up(classes, 128)
    hot = (label == lax.broadcasted_iota(jnp.int32, (everyone, wide), 1)).astype(F32).astype(BF16).T
    table_ref[...] = (mm(hot, high) + mm(hot, low))[:classes]
    copies.start(table_ref, table_out)
    small = get(4 * D + 6 * everyone, 16).astype(F32)
    qv_ref[...] = small[:2]
    for part in range(2):
        for head in range(HEADS):
            at = 2 * GRID * head
            rel_ref[part, head : head + 1, :] = small[2 + part : 3 + part, at : at + 2 * GRID - 1]
    out_bias_ref[...] = small[4]
    copies.wait()


def swap_cores(value, dp):
    return lax.ppermute(value, "dp", [(n, n ^ 1) for n in range(dp)])


def exchange(value, dp, seq):
    groups = [
        [(far * (dp // 2) + 2 * pair + core) * seq + at for pair in range(dp // 4) for at in range(seq)]
        for far in range(2)
        for core in range(2)
    ]
    return lax.all_to_all(value, AXES, 0, 0, axis_index_groups=groups)


def sum_pieces(pieces, dp):
    near = jnp.sum(pieces.astype(F32), axis=0).astype(BF16)
    far = lax.ppermute(near, "dp", [(n, (n + dp // 2) % dp) for n in range(dp)])
    return (near.astype(F32) + far.astype(F32)).astype(BF16)


def spread_out(chunk, dp, seq):
    peers = dp // 4 * seq
    return exchange(jnp.broadcast_to(chunk[None], (peers,) + chunk.shape), dp, seq).reshape(-1, D)


def scatter_rows(partial, seq):
    return [
        lax.ppermute(partial[step - 1], "seq", [(n, (n + step) % seq) for n in range(seq)])
        for step in range(1, seq)
    ]


def time_features(moments):
    half_width = D // 2
    frequency = jnp.exp(-math.log(10000.0) * jnp.arange(half_width, dtype=F32) / half_width)
    angles = moments.astype(F32)[:, None] * frequency[None, :]
    return jnp.concatenate([jnp.cos(angles), jnp.sin(angles)], axis=-1)


def offset_hot():
    first = jnp.arange(GRID, dtype=jnp.int32)
    offsets = first[None, :] - first[:, None] + GRID - 1
    return (offsets[..., None] == jnp.arange(2 * GRID - 1, dtype=jnp.int32)).astype(F32)


def bias_table(rel_bias):
    both = jnp.einsum("cho,ijo->cihj", rel_bias.astype(F32), offset_hot(), precision=highest)
    empty = jnp.zeros_like(both[0])
    top = jnp.concatenate([both[0], empty], axis=-1)
    low = jnp.concatenate([empty, both[1]], axis=-1)
    return jnp.concatenate([top, low], axis=0).reshape(2 * GRID, HEADS * 2 * GRID).astype(BF16)


def body(
    dp, seq, image_tokens, kept_index, kept_count, sample_valid, timestep, class_label, class_table,
    ada_weight, ada_bias, qkv_weight, qv_bias, rel_bias, out_weight, out_bias, fc1_weight,
    fc1_bias, fc2_weight, fc2_bias, grad_full, grad_masked,
):
    samples, own, width = image_tokens.shape
    held = kept_index.shape[1]
    slots = grad_masked.shape[1]
    padded = round_up(slots, 16)
    rows = own + padded
    total = own * seq
    everyone = dp * samples
    classes = class_table.shape[0]
    dp_place, seq_place = lax.axis_index("dp"), lax.axis_index("seq")

    conditioned = jnp.take(class_table, class_label, axis=0).astype(F32) + time_features(timestep)
    gate = jax.nn.sigmoid(conditioned)
    activated = (conditioned * gate).astype(BF16)
    slope = gate * (1.0 + conditioned * (1.0 - gate))
    modulation = jnp.dot(activated, ada_weight, preferred_element_type=F32) + ada_bias.astype(F32)
    modulation = jnp.pad(modulation.reshape(samples, 6, D), ((0, 0), (0, 2), (0, 0)))
    table = bias_table(rel_bias)
    valid = sample_valid.astype(F32)

    digits = jnp.stack([class_label // GRID, class_label % GRID], axis=1).astype(F32)
    digits = jnp.pad(digits, ((0, 0), (0, D - 2)))
    info = jnp.stack([activated.astype(F32), slope, digits], axis=0)
    info = info * (seq_place == 0).astype(F32)
    extra_rows = round_up(2 * FF + 16 + 3 * everyone, dp * seq * 4) - (2 * FF + 16)
    spread = (jnp.arange(everyone)[:, None] == dp_place * samples + jnp.arange(samples)[None, :])
    info = jnp.einsum("es,nsd->end", spread.astype(F32), info, precision=highest)
    info = info.transpose(1, 0, 2).reshape(3 * everyone, D).astype(BF16)
    info = jnp.pad(info, ((0, extra_rows - 3 * everyone), (0, 0)))

    slot_numbers = jnp.arange(held, dtype=jnp.int32)
    live_all = slot_numbers[None, :] < kept_count[:, None]
    slot_start = seq_place * slots
    peers = dp // 4 * seq
    side = dp_place % 2
    sides = side.astype(jnp.int32).reshape(1)
    half = (2 * FF + 16 + extra_rows) // 2
    tail_half = round_up(4 * D + 16 + 6 * everyone, dp * seq * 4) // 2
    starts = ((seq_place - jnp.arange(seq, dtype=jnp.int32)) % seq * own).astype(jnp.int32)

    kept_of = []
    for s in range(samples):
        tokens = [image_tokens[s]]
        for step in range(1, seq):
            tokens.append(lax.ppermute(tokens[0], "seq", [(n, (n + step) % seq) for n in range(seq)]))
        kept = jnp.where(live_all[s], kept_index[s], -1)[:, None]
        picked = lax.dynamic_slice_in_dim(kept_index[s], slot_start, slots, 0)
        live = lax.dynamic_slice_in_dim(live_all[s], slot_start, slots, 0)
        picked = jnp.pad(picked, (0, padded - slots))[:, None]
        where = jnp.concatenate([starts[0] + jnp.arange(own, dtype=jnp.int32), picked[:, 0]])[:, None]
        weight = valid[s] * jnp.concatenate(
            [jnp.ones((own,), F32), jnp.pad(live.astype(F32), (0, padded - slots))]
        )
        cot = jnp.concatenate([grad_full[s], jnp.pad(grad_masked[s], ((0, padded - slots), (0, 0)))])
        qaug, kaug, vaug, x, mask, lowered, whole, slot = call(
            functools.partial(prep_kernel, own, seq),
            [
                ((HEADS, rows, 128), BF16), ((HEADS, total, 128), BF16), ((HEADS, total, 128), BF16),
                ((rows, D), BF16), ((8, total), F32),
                ((total, D), BF16), ((total, D), BF16), ((padded, D), BF16),
            ],
            [((total, D), BF16), ((total, D), BF16), ((total, D), BF16), ((padded, D), BF16)],
            [starts, *tokens, kept, picked, where, modulation[s], qkv_weight, qv_bias.astype(F32), table],
            scalars=1, away=3, copies=3, micros=5,
        )
        mixed, inverse, spread_far, qaug_far, kaug_far, vaug_far = call(
            functools.partial(attend_kernel, own),
            [
                ((HEADS // 2, rows, 128), F32), ((HEADS // 2, rows, 128), F32),
                ((HEADS, rows, total), BF16), (qaug.shape, BF16), (kaug.shape, BF16), (vaug.shape, BF16),
            ],
            [((HEADS, rows, total), BF16)],
            [qaug, kaug, vaug, mask],
            away=4, copies=3 + HEADS, micros=10, limit=40,
        )
        attended, hidden, du, keep, send = call(
            feed_kernel,
            [((rows, D), F32), ((rows, FF), BF16), ((rows, FF), BF16), ((half, D), BF16), ((half, D), BF16)],
            [((2 * half, D), BF16)],
            [
                sides, mixed, x, cot, weight[:, None], modulation[s], out_weight, out_bias.astype(F32)[None],
                fc1_weight, fc1_bias.astype(F32)[None], fc2_weight, info if s == 0 else jnp.zeros_like(info),
            ],
            scalars=1, copies=2, micros=10, limit=32,
        )
        kept_of.append(dict(
            rest=[
                mixed, inverse, x, cot, weight[:, None], modulation[s], out_weight, fc1_weight, fc2_weight,
                fc2_bias.astype(F32)[None], attended, hidden, du,
            ],
            groups=[spread_far, qaug_far, kaug_far, vaug_far], sources=[whole, lowered, slot, qkv_weight],
            where=where, picked=picked, keep=keep, send=send,
        ))

    def added(arrays):
        if len(arrays) == 1:
            return arrays[0]
        return functools.reduce(jnp.add, [a.astype(F32) for a in arrays]).astype(arrays[0].dtype)

    keep, send = added([k["keep"] for k in kept_of]), added([k["send"] for k in kept_of])
    got = swap_cores(send, dp)

    rests = [
        call(
            functools.partial(feed_rest_kernel, own),
            [
                ((8, D), F32), ((own, D), BF16), ((padded, D), BF16), ((rows, D), F32), ((rows, D), BF16),
                ((HEADS, rows, 128), BF16), ((D, D), BF16),
            ],
            [((rows, D), BF16), ((rows, D), F32), ((HEADS, rows, 128), BF16), ((D, D), BF16)],
            k["rest"],
            away=6, copies=6, micros=6, limit=32,
        )
        for k in kept_of
    ]
    mine = (keep.astype(F32) + got.astype(F32)).astype(BF16)
    mine, rests = lax.optimization_barrier((mine, rests))
    pieces = exchange(mine.reshape(peers, half // peers, D), dp, seq)
    tails = []
    for number, (k, rest) in enumerate(zip(kept_of, rests)):
        small, unused_full, unused_slot, dmid, x_far, dout_far, grad_out = rest
        place = (dp_place * samples + number).astype(jnp.int32)
        others = (seq_place + jnp.arange(1, seq, dtype=jnp.int32)) % seq * own
        scalars = jnp.concatenate([jnp.stack([sides[0], starts[0], place]), others.astype(jnp.int32)])
        whole, lowered, slot, weights = k["sources"]
        tails.append(
            back_call(
                own, everyone, [*k["groups"], dout_far], [whole, lowered, x_far, slot, weights, dmid, grad_out],
                scalars, k["where"], k["picked"], modulation[number], small, tail_half,
            )
        )

    keep, send = added([t[0] for t in tails]), added([t[1] for t in tails])
    keep, send, pieces = lax.optimization_barrier((keep, send, pieces))
    got = swap_cores(send, dp)
    mine = add_call(keep, got, 30).reshape(peers, tail_half // peers, D)
    chunk = sum_pieces(pieces, dp)
    last_chunk = sum_pieces(exchange(mine, dp, seq), dp)
    moved = [scatter_rows(t[2], seq) for t in tails]
    chunk, moved = lax.optimization_barrier((chunk, moved))
    layer_half = spread_out(chunk, dp, seq)
    layer_half, last_chunk = lax.optimization_barrier((layer_half, last_chunk))
    last_half = spread_out(last_chunk, dp, seq)
    grad_input = jnp.stack(
        [t[3] + functools.reduce(jnp.add, [m.astype(F32) for m in came]) for t, came in zip(tails, moved)]
    )
    out_full = jnp.stack([rest[1] for rest in rests])
    out_masked = jnp.stack([rest[2][:slots] for rest in rests])
    info, layer_small, grad_fc1, grad_fc2 = call(
        layer_kernel,
        [((extra_rows, D), BF16), ((8, D), F32), ((D, FF), F32), ((FF, D), F32)],
        [((D, FF), F32), ((FF, D), F32)],
        [sides, layer_half, swap_cores(layer_half, dp)],
        scalars=1, away=2, copies=8, micros=3,
    )
    grad_fc1_bias = layer_small[:4].reshape(FF)
    grad_fc2_bias = layer_small[4]
    last_half, info, grad_fc1_bias, grad_fc2_bias, grad_input = lax.optimization_barrier(
        (last_half, info, grad_fc1_bias, grad_fc2_bias, grad_input)
    )
    grad_qv, grad_rel, grad_out_bias, grad_ada_bias, grad_qkv, grad_ada, grad_table, grad_out = call(
        functools.partial(last_kernel, everyone),
        [
            ((2, D), F32), ((2, HEADS, 2 * GRID - 1), F32), ((D,), F32), ((6 * D,), F32),
            ((D, 3 * D), F32), ((D, 6 * D), F32), ((classes, D), F32), ((D, D), F32),
        ],
        [((D, 3 * D), F32), ((D, 6 * D), F32), ((classes, D), F32), ((D, D), F32)],
        [sides, last_half, swap_cores(last_half, dp), info, ada_weight],
        scalars=1, away=4, copies=11, micros=4, limit=16,
    )
    return (
        out_full, out_masked, grad_input, grad_table, grad_ada, grad_ada_bias, grad_qkv, grad_qv,
        grad_rel, grad_out, grad_out_bias, grad_fc1, grad_fc1_bias, grad_fc2, grad_fc2_bias,
    )


def solution(mesh):
    split = P("dp", "seq", None)
    placed = (split, P("dp", None)) + (P("dp"),) * 4 + (P(),) * 12 + (split, split)
    return jax.shard_map(
        functools.partial(body, mesh.shape["dp"], mesh.shape["seq"]),
        mesh=mesh,
        in_specs=placed,
        out_specs=(split,) * 3 + (P(),) * 12,
        check_vma=False,
    )
```

time: 153 us -> 144 us (0.941)
  Pallas kernels: 64.6 us -> 59.4 us
  starting transfers between devices: 27.4 us -> 30.2 us
  waiting for transfers between devices: 38.4 us -> 36.1 us
  other arithmetic: 8.79 us -> 6.57 us
  local copies, waits for them, and re-layouts: 6.81 us -> 4.88 us
    pallas_call x6 -> x7, Pallas kernels: 46.6 us -> 40.1 us  [call(): pl.pallas_call(kernel, out_shape=[jax.ShapeDtypeStruct(shape, dtype) for...]
    ppermute x4, waiting for transfers between devices: 1.66 us -> 4.17 us  [swap_cores(): return lax.ppermute(value, 'dp', [(n, n ^ 1) for n in range(dp)])]
    ppermute x1, waiting for transfers between devices: 9.22 us -> 7.24 us  [scatter_rows(): lax.ppermute(partial[step - 1], 'seq', [(n, (n + step) % seq) for n in ra...]
    all_to_all x4, waiting for transfers between devices: 8.85 us -> 7 us  [exchange(): return lax.all_to_all(value, AXES, 0, 0, axis_index_groups=groups)]
  transfers between devices with their start and end apart: 12 -> 12, of which waited for: 6 -> 8; matrix products, arithmetic and copies ran while one was open for 8% -> 7% of each run, Pallas kernels for 19% -> 20%
where the time goes in v3:
time: 144 us; the launch traced here: 143 us
  Pallas kernels  59.4 us (41%)
  waiting for transfers between devices  36.1 us (25%)
  starting transfers between devices  30.2 us (21%)
  other arithmetic  6.57 us (5%)
  local copies, waits for them, and re-layouts  4.88 us (3%)
  between operations  3.84 us (3%)
  matrix products  2.36 us (2%)
    pallas_call x7, Pallas kernels, call(): pl.pallas_call(kernel, out_shape=[jax.ShapeDtypeStruct(shape, dtype) for...  40.1 us
    all_to_all x4, starting transfers between devices, exchange(): return lax.all_to_all(value, AXES, 0, 0, axis_index_groups=groups)  19.5 us
    pallas_call x1, Pallas kernels, back_call(): pl.pallas_call(functools.partial(back_kernel, own, everyone), grid=(group...  19.3 us
    ppermute x2, waiting for transfers between devices, sum_pieces(): far = lax.ppermute(near, 'dp', [(n, (n + dp // 2) % dp) for n in range(dp)])  17.1 us
    ppermute x1, waiting for transfers between devices, scatter_rows(): lax.ppermute(partial[step - 1], 'seq', [(n, (n + step) % seq) for n in ra...  7.24 us
    all_to_all x4, waiting for transfers between devices, exchange(): return lax.all_to_all(value, AXES, 0, 0, axis_index_groups=groups)  7 us
    ppermute x2, starting transfers between devices, sum_pieces(): far = lax.ppermute(near, 'dp', [(n, (n + dp // 2) % dp) for n in range(dp)])  5.28 us
    ppermute x4, waiting for transfers between devices, swap_cores(): return lax.ppermute(value, 'dp', [(n, n ^ 1) for n in range(dp)])  4.17 us
  transfers between devices with their start and end apart: 12, of which 8 were waited for; matrix products, arithmetic and copies ran while one was open for 7% of the time, Pallas kernels for 20%

profile of v3, /device:TPU:0, one launch (start us, length us, event | category | flops | bytes accessed | tf_op | source)
XLA Modules:
  0.0 143.3 jit_solution(6887706812685303305)
XLA Ops:
  0.7 3.0 %collective-permute-start = (bf16[512,384]{1,0:T(8,128)(2,1)}, bf16[512,384]{1,0:T(8,128)(2,1)S(1)}, u32[]{:S(2)}, u32[]{:S(2)}) collective-permute-start(bf16[512,384]{1,0:T(8,128)(2,1)} %bitcast.58), channel_id=1, source_target_pairs={{0,1},{1,0},{2,3},{3,2},{4,5},{5,4},{6,7},{7,6},{8,9},{9,8},{10,11... | collective-permute-start | bytes 1179656 | tf_op jit(solution)/shard_map/ppermute | solution.py:675
  5.8 0.8 convert_convert_fusion
  6.6 0.1 fusion.11
  6.7 1.8 %convolution_reduce_fusion = f32[2304]{0:T(1024)S(1)} fusion(bf16[384,1]{0,1:T(2,128)(2,1)S(1)} %reshape.343, bf16[384,2304]{1,0:T(8,128)(2,1)} %ada_ref.1), kind=kOutput, calls=%fused_computation.3 | convolution fusion | flops 1769472 | bytes 1779456 | tf_op jit(solution)/shard_map/dot_general | solution.py:646
  8.7 0.5 fusion
  9.2 0.1 dynamic-slice_reduce_fusion
  10.0 0.1 fusion.7
  10.3 0.1 multiply_convert_fusion
  10.4 0.2 copy.38
  10.5 0.1 copy.41.refs_3_.picked_ref
  10.7 0.2 broadcast_in_dim.84.refs_4_.where_ref
  10.9 0.1 convert_element_type.150.refs_8_
  11.1 0.2 broadcast_in_dim.85.wgt_ref
  11.3 1.2 pad_maximum_fusion.cot_ref
  12.5 0.5 collective-permute-done.refs_1_
  13.0 5.6 %shard_map.307 = (bf16[6,864,128]{2,1,0:T(8,128)(2,1)S(1)}, bf16[6,1024,128]{2,1,0:T(8,128)(2,1)S(1)}, bf16[6,1024,128]{2,1,0:T(8,128)(2,1)S(1)}, bf16[864,384]{...) custom-call(s32[2]{0:T(128)S(1)} %fusion.15.starts_ref, ...), custom_call_target="tpu_custom_call" | custom-call | flops 5000000000 | bytes 1048576 | tf_op jit(solution)/shard_map/pallas_call | solution.py:450
  18.7 10.2 %shard_map.308 = (f32[3,864,128]{2,1,0:T(8,128)S(1)}, f32[3,864,128]{2,1,0:T(8,128)S(1)}, bf16[6,864,1024]{2,1,0:T(8,128)(2,1)}, bf16[6,864,128]{2,1,0:T(8,128)(...) custom-call(bf16[6,864,128]{2,1,0:T(8,128)(2,1)S(1)} %get-tuple-element.77.qaug_ref, ...), custom_call_target="tpu_custom_call" | custom-call | flops 10000000000 | bytes 1048576 | tf_op jit(solution)/shard_map/pallas_call | solution.py:450
  28.9 8.5 %shard_map.309 = (f32[864,384]{1,0:T(8,128)S(1)}, bf16[864,1536]{1,0:T(8,128)(2,1)S(1)}, bf16[864,1536]{1,0:T(8,128)(2,1)S(1)}, bf16[1600,384]{1,0:T(8,128)(2,1)S(1)}, bf16[1600,384]{1,0:T(8,128)(2,1)S(1)}) custom-call(s32[1]{0:T(128)} %bitcast.side_ref, f32[3,864,128]{2,1,0:T(8,128)S(1)} %get-tuple-element.81.o_ref, ...), custom_call_target="tpu_custom_call" | custom-call | flops 10000000000 | bytes 1048576 | tf_op jit(solution)/shard_map/pallas_call | solution.py:450
  37.5 5.9 %shard_map.310 = (f32[8,384]{1,0:T(8,128)S(1)}, bf16[512,384]{1,0:T(8,128)(2,1)}, bf16[352,384]{1,0:T(8,128)(2,1)}, f32[864,384]{1,0:T(8,128)}, bf16[864,384]{1,...) custom-call(f32[3,864,128]{2,1,0:T(8,128)S(1)} %get-tuple-element.81.o_ref, ...), custom_call_target="tpu_custom_call" | custom-call | flops 6000000000 | bytes 1048576 | tf_op jit(solution)/shard_map/pallas_call | solution.py:450
  43.4 1.4 add_convert_fusion
  44.8 5.0 %all-to-all-start = ((bf16[8,200,384]{2,1,0:T(8,128)(2,1)}), bf16[8,200,384]{2,1,0:T(8,128)(2,1)}, u32[]{:S(2)}, u32[]{:S(2)}) async-start(bf16[8,200,384]{2,1,0:T(8,128)(2,1)} %bitcast.29), calls=%async_computation | async-start | bytes 2457600 | tf_op jit(solution)/shard_map/all_to_all | solution.py:585
  49.8 0.1 pad_add_fusion.1.scalar_ref
  49.9 19.3 %shard_map.311 = (bf16[832,384]{1,0:T(8,128)(2,1)S(1)}, bf16[832,384]{1,0:T(8,128)(2,1)S(1)}, bf16[1,512,384]{2,1,0:T(8,128)(2,1)}, f32[512,384]{1,0:T(8,128)}) custom-call(s32[4]{0:T(128)S(1)} %pad_add_fusion.1.scalar_ref, s32[864,1]{1,0:T(8,128)S(1)} %broadcast_in_dim.84.refs_4_.where_ref, s32[352,1]{1,0:T(8,128)S(1)} %copy.41.refs_3_.picked_ref, ...), custom_call_target="tpu_custom_call" | custom-call | flops 17999998976 | bytes 1048576 | tf_op jit(solution)/shard_map/pallas_call | solution.py:489
  69.2 0.3 collective-permute-start.4
  69.5 1.9 %collective-permute-done.4.right_ref = bf16[832,384]{1,0:T(8,128)(2,1)S(1)} collective-permute-done((bf16[832,384]{1,0:T(8,128)(2,1)S(1)}, bf16[832,384]{1,0:T(8,128)(2,1)S(1)}, u32[]{:S(2)}, u32[]{:S(2)}) %collective-permute-start.4) | collective-permute-done | bytes 639008 | tf_op jit(solution)/shard_map/ppermute | solution.py:576
  71.4 1.0 shard_map.312
  72.4 5.1 %all-to-all-start.2 = ((bf16[8,104,384]{2,1,0:T(8,128)(2,1)}), bf16[8,104,384]{2,1,0:T(8,128)(2,1)S(1)}, u32[]{:S(2)}, u32[]{:S(2)}) async-start(bf16[8,104,384]{2,1,0:T(8,128)(2,1)} %bitcast.32), calls=%async_computation.2 | async-start | bytes 1277952 | tf_op jit(solution)/shard_map/all_to_all | solution.py:585
  77.5 2.0 %collective-permute-start.3 = (bf16[512,384]{1,0:T(8,128)(2,1)S(1)}, bf16[512,384]{1,0:T(8,128)(2,1)S(1)}, u32[]{:S(2)}, u32[]{:S(2)}) collective-permute-start(bf16[512,384]{1,0:T(8,128)(2,1)S(1)} %bitcast.66), channel_id=1, source_target_pairs={{0,1},{1,0},{2,3},{3,2},{4,5},{5,4},{6,7},{7,6},{8,9},{9,8},{10,11... | collective-permute-start | bytes 1179656 | tf_op jit(solution)/shard_map/ppermute | solution.py:601
  79.5 1.5 %reduce_sum.24 = bf16[200,384]{1,0:T(8,128)(2,1)S(1)} reduce(bf16[8,200,384]{2,1,0:T(8,128)(2,1)} %all-to-all-done, bf16[]{:T(256)} %constant.121.clone.1), dimensions={0}, to_apply=%region_0.1 | reduce | flops 537600 | bytes 1382402 | tf_op jit(solution)/shard_map/reduce_sum | solution.py:589
  81.0 2.6 %collective-permute-start.2 = (bf16[200,384]{1,0:T(8,128)(2,1)S(1)}, bf16[200,384]{1,0:T(8,128)(2,1)S(1)}, u32[]{:S(2)}, u32[]{:S(2)}) collective-permute-start(bf16[200,384]{1,0:T(8,128)(2,1)S(1)} %reduce_sum.24), channel_id=1, source_target_pairs={{0,16},{2,18},{4,20},{6,22},{8,24},{10,26},{12,28},{14,30},{16,0},... | collective-permute-start | bytes 460808 | tf_op jit(solution)/shard_map/ppermute | solution.py:590
  83.6 4.5 %collective-permute-done.2 = bf16[200,384]{1,0:T(8,128)(2,1)S(1)} collective-permute-done((bf16[200,384]{1,0:T(8,128)(2,1)S(1)}, bf16[200,384]{1,0:T(8,128)(2,1)S(1)}, u32[]{:S(2)}, u32[]{:S(2)}) %collective-permute-start.2) | collective-permute-done | bytes 153632 | tf_op jit(solution)/shard_map/ppermute | solution.py:590
  88.2 7.2 %collective-permute-done.3 = bf16[512,384]{1,0:T(8,128)(2,1)S(1)} collective-permute-done((bf16[512,384]{1,0:T(8,128)(2,1)S(1)}, bf16[512,384]{1,0:T(8,128)(2,1)S(1)}, u32[]{:S(2)}, u32[]{:S(2)}) %collective-permute-start.3) | collective-permute-done | bytes 393248 | tf_op jit(solution)/shard_map/ppermute | solution.py:601
  95.4 1.1 broadcast_in_dim.79
  96.5 3.6 %all-to-all-start.1 = ((bf16[8,200,384]{2,1,0:T(8,128)(2,1)}), bf16[8,200,384]{2,1,0:T(8,128)(2,1)S(1)}, u32[]{:S(2)}, u32[]{:S(2)}) async-start(bf16[8,200,384]{2,1,0:T(8,128)(2,1)} %broadcast_in_dim.79), calls=%async_computation.1 | async-start | bytes 2457600 | tf_op jit(solution)/shard_map/all_to_all | solution.py:585
  100.2 0.1 reduce_sum.25
  100.3 2.6 %collective-permute-start.5 = (bf16[104,384]{1,0:T(8,128)(2,1)S(1)}, bf16[104,384]{1,0:T(8,128)(2,1)S(1)}, u32[]{:S(2)}, u32[]{:S(2)}) collective-permute-start(bf16[104,384]{1,0:T(8,128)(2,1)S(1)} %reduce_sum.25), channel_id=1, source_target_pairs={{0,16},{2,18},{4,20},{6,22},{8,24},{10,26},{12,28},{14,30},{16,0},... | collective-permute-start | bytes 239624 | tf_op jit(solution)/shard_map/ppermute | solution.py:590
  102.9 12.6 %collective-permute-done.5 = bf16[104,384]{1,0:T(8,128)(2,1)S(1)} collective-permute-done((bf16[104,384]{1,0:T(8,128)(2,1)S(1)}, bf16[104,384]{1,0:T(8,128)(2,1)S(1)}, u32[]{:S(2)}, u32[]{:S(2)}) %collective-permute-start.5) | collective-permute-done | bytes 79904 | tf_op jit(solution)/shard_map/ppermute | solution.py:590
  115.6 2.0 %all-to-all-done.1 = bf16[8,200,384]{2,1,0:T(8,128)(2,1)S(1)} async-done(((bf16[8,200,384]{2,1,0:T(8,128)(2,1)}), bf16[8,200,384]{2,1,0:T(8,128)(2,1)S(1)}, u32[]{:S(2)}, u32[]{:S(2)}) %all-to-all-start.1) | async-done | bytes 1228832 | tf_op jit(solution)/shard_map/all_to_all | solution.py:585
  117.6 0.9 broadcast_in_dim.80
  118.5 5.8 %all-to-all-start.3 = ((bf16[8,104,384]{2,1,0:T(8,128)(2,1)}), bf16[8,104,384]{2,1,0:T(8,128)(2,1)}, u32[]{:S(2)}, u32[]{:S(2)}) async-start(bf16[8,104,384]{2,1,0:T(8,128)(2,1)} %broadcast_in_dim.80), calls=%async_computation.3 | async-start | bytes 1277952 | tf_op jit(solution)/shard_map/all_to_all | solution.py:585
  124.3 0.9 add_bitcast_fusion
  125.2 3.7 %shard_map.313 = (bf16[112,384]{1,0:T(8,128)(2,1)S(1)}, f32[8,384]{1,0:T(8,128)S(1)}, f32[384,1536]{1,0:T(8,128)}, f32[1536,384]{1,0:T(8,128)}) custom-call(s32[1]{0:T(128)} %bitcast.side_ref, bf16[1600,384]{1,0:T(8,128)(2,1)S(1)} %bitcast.55, bf16[1600,384]{1,0:T(8,128)(2,1)} %collective-permute-done.6.other_ref), custom_call_target="tpu_custom_call" | custom-call | flops 3000000000 | bytes 1048576 | tf_op jit(solution)/shard_map/pallas_call | solution.py:450
  129.0 0.6 reshape.312
  129.6 0.6 slice_reduce_fusion
  130.2 5.0 %all-to-all-done.3 = bf16[8,104,384]{2,1,0:T(8,128)(2,1)} async-done(((bf16[8,104,384]{2,1,0:T(8,128)(2,1)}), bf16[8,104,384]{2,1,0:T(8,128)(2,1)}, u32[]{:S(2)}, u32[]{:S(2)}) %all-to-all-start.3) | async-done | bytes 639008 | tf_op jit(solution)/shard_map/all_to_all | solution.py:585
  135.2 2.3 %collective-permute-done.7.other_ref = bf16[832,384]{1,0:T(8,128)(2,1)S(1)} collective-permute-done((bf16[832,384]{1,0:T(8,128)(2,1)}, bf16[832,384]{1,0:T(8,128)(2,1)S(1)}, u32[]{:S(2)}, u32[]{:S(2)}) %collective-permute-start.7) | collective-permute-done | bytes 639008 | tf_op jit(solution)/shard_map/ppermute | solution.py:576
  137.4 5.2 %shard_map.314 = (f32[2,384]{1,0:T(2,128)}, f32[2,6,63]{2,1,0:T(8,128)S(1)}, f32[384]{0:T(512)}, f32[2304]{0:T(1024)}, f32[384,1152]{1,0:T(8,128)}, /*index=5*/f...) custom-call(s32[1]{0:T(128)} %bitcast.side_ref, bf16[832,384]{1,0:T(8,128)(2,1)} %bitcast.33.mine_ref, ...), custom_call_target="tpu_custom_call" | custom-call | flops 4000000000 | bytes 1048576 | tf_op jit(solution)/shard_map/pallas_call | solution.py:450
  142.7 0.6 copy.47
  (64 shorter events, 0.6 us)
Async XLA Ops:
  0.6 7.9 %copy-start.9 = (bf16[2304]{0:T(1024)(128)(2,1)S(1)}, bf16[2304]{0:T(1024)(128)(2,1)}, u32[]{:S(2)}) copy-start(bf16[2304]{0:T(1024)(128)(2,1)} %param.28) | copy-start | bytes 13828
  0.7 8.0 %copy-start.15 = (bf16[2,6,63]{2,0,1:T(2,128)(2,1)S(1)}, bf16[2,6,63]{2,0,1:T(2,128)(2,1)}, u32[]{:S(2)}) copy-start(bf16[2,6,63]{2,0,1:T(2,128)(2,1)} %param.31) | copy-start | bytes 4540
  0.7 8.5 %copy-start.8 = (s32[1,704]{1,0:T(1,128)S(1)}, s32[1,704]{1,0:T(1,128)}, u32[]{:S(2)}) copy-start(s32[1,704]{1,0:T(1,128)} %param.21) | copy-start | bytes 8452
  0.7 12.4 %collective-permute-start = (bf16[512,384]{1,0:T(8,128)(2,1)}, bf16[512,384]{1,0:T(8,128)(2,1)S(1)}, u32[]{:S(2)}, u32[]{:S(2)}) collective-permute-start(bf16[512,384]{1,0:T(8,128)(2,1)} %bitcast.58), channel_id=1, source_target_pairs={{0,1},{1,0},{2,3},{3,2},{4,5},{5,4},{6,7},{7,6},{8,9},{9,8},{10,11... | collective-permute-start | bytes 1179656 | tf_op jit(solution)/shard_map/ppermute | solution.py:675
  8.6 2.3 %copy-start.11 = (bf16[2,384]{1,0:T(2,128)(2,1)S(1)}, bf16[2,384]{1,0:T(2,128)(2,1)}, u32[]{:S(2)}) copy-start(bf16[2,384]{1,0:T(2,128)(2,1)} %param.30) | copy-start | bytes 4612
  8.6 2.7 %copy-start.12 = (bf16[384]{0:T(512)(128)(2,1)S(1)}, bf16[384]{0:T(512)(128)(2,1)}, u32[]{:S(2)}) copy-start(bf16[384]{0:T(512)(128)(2,1)} %param.33) | copy-start | bytes 2308
  8.6 2.7 %copy-start.10 = (bf16[1536]{0:T(1024)(128)(2,1)S(1)}, bf16[1536]{0:T(1024)(128)(2,1)}, u32[]{:S(2)}) copy-start(bf16[1536]{0:T(1024)(128)(2,1)} %param.35) | copy-start | bytes 9220
  8.6 2.7 %copy-start.7 = (bf16[1,352,384]{2,1,0:T(8,128)(2,1)S(1)}, bf16[1,352,384]{2,1,0:T(8,128)(2,1)}, u32[]{:S(2)}) copy-start(bf16[1,352,384]{2,1,0:T(8,128)(2,1)} %param.39) | copy-start | bytes 811012
  11.0 2.0 %copy-start.3 = (bf16[384,1152]{1,0:T(8,128)(2,1)S(1)}, bf16[384,1152]{1,0:T(8,128)(2,1)}, u32[]{:S(2)}) copy-start(bf16[384,1152]{1,0:T(8,128)(2,1)} %refs_9_.1) | copy-start | bytes 2654212
  11.0 2.0 %copy-start.4 = (bf16[1,512,384]{2,1,0:T(8,128)(2,1)S(1)}, bf16[1,512,384]{2,1,0:T(8,128)(2,1)}, u32[]{:S(2)}) copy-start(bf16[1,512,384]{2,1,0:T(8,128)(2,1)} %param.20) | copy-start | bytes 1179652
  18.7 10.2 %copy-start.1 = (bf16[384,1536]{1,0:T(8,128)(2,1)S(1)}, bf16[384,1536]{1,0:T(8,128)(2,1)}, u32[]{:S(2)}) copy-start(bf16[384,1536]{1,0:T(8,128)(2,1)} %w1_ref.3) | copy-start | bytes 3538948
  18.7 10.2 %copy-start.2 = (bf16[1536,384]{1,0:T(8,128)(2,1)S(1)}, bf16[1536,384]{1,0:T(8,128)(2,1)}, u32[]{:S(2)}) copy-start(bf16[1536,384]{1,0:T(8,128)(2,1)} %w2_ref.3) | copy-start | bytes 3538948
  18.7 10.2 %copy-start.5 = (bf16[384,384]{1,0:T(8,128)(2,1)S(1)}, bf16[384,384]{1,0:T(8,128)(2,1)}, u32[]{:S(2)}) copy-start(bf16[384,384]{1,0:T(8,128)(2,1)} %wout_ref.3) | copy-start | bytes 884740
  28.9 8.6 %copy-start.13 = (bf16[384]{0:T(512)(128)(2,1)S(1)}, bf16[384]{0:T(512)(128)(2,1)}, u32[]{:S(2)}) copy-start(bf16[384]{0:T(512)(128)(2,1)} %param.37) | copy-start | bytes 2308
  37.4 6.1 %collective-permute-start.1 = (bf16[1600,384]{1,0:T(8,128)(2,1)S(1)}, bf16[1600,384]{1,0:T(8,128)(2,1)S(1)}, u32[]{:S(2)}, u32[]{:S(2)}) collective-permute-start(bf16[1600,384]{1,0:T(8,128)(2,1)S(1)} %get-tuple-element.84), channel_id=1, source_target_pairs={{0,2},{2,0},{4,6},{6,4},{8,10},{10,8},{12,14},{14,12},{16,18},{18,... | collective-permute-start | bytes 3686408 | tf_op jit(solution)/shard_map/ppermute | solution.py:576
  44.8 24.4 %all-to-all-start = ((bf16[8,200,384]{2,1,0:T(8,128)(2,1)}), bf16[8,200,384]{2,1,0:T(8,128)(2,1)}, u32[]{:S(2)}, u32[]{:S(2)}) async-start(bf16[8,200,384]{2,1,0:T(8,128)(2,1)} %bitcast.29), calls=%async_computation | async-start | bytes 2457600 | tf_op jit(solution)/shard_map/all_to_all | solution.py:585
  69.2 8.2 %copy-start.14 = (bf16[1,512,384]{2,1,0:T(8,128)(2,1)S(1)}, bf16[1,512,384]{2,1,0:T(8,128)(2,1)}, u32[]{:S(2)}) copy-start(bf16[1,512,384]{2,1,0:T(8,128)(2,1)} %get-tuple-element.114) | copy-start | bytes 1179652
  69.2 2.1 %collective-permute-start.4 = (bf16[832,384]{1,0:T(8,128)(2,1)S(1)}, bf16[832,384]{1,0:T(8,128)(2,1)S(1)}, u32[]{:S(2)}, u32[]{:S(2)}) collective-permute-start(bf16[832,384]{1,0:T(8,128)(2,1)S(1)} %get-tuple-element.117), channel_id=1, source_target_pairs={{0,2},{2,0},{4,6},{6,4},{8,10},{10,8},{12,14},{14,12},{16,18},{18,... | collective-permute-start | bytes 1916936 | tf_op jit(solution)/shard_map/ppermute | solution.py:576
  72.4 23.0 %all-to-all-start.2 = ((bf16[8,104,384]{2,1,0:T(8,128)(2,1)}), bf16[8,104,384]{2,1,0:T(8,128)(2,1)S(1)}, u32[]{:S(2)}, u32[]{:S(2)}) async-start(bf16[8,104,384]{2,1,0:T(8,128)(2,1)} %bitcast.32), calls=%async_computation.2 | async-start | bytes 1277952 | tf_op jit(solution)/shard_map/all_to_all | solution.py:585
  77.5 17.9 %collective-permute-start.3 = (bf16[512,384]{1,0:T(8,128)(2,1)S(1)}, bf16[512,384]{1,0:T(8,128)(2,1)S(1)}, u32[]{:S(2)}, u32[]{:S(2)}) collective-permute-start(bf16[512,384]{1,0:T(8,128)(2,1)S(1)} %bitcast.66), channel_id=1, source_target_pairs={{0,1},{1,0},{2,3},{3,2},{4,5},{5,4},{6,7},{7,6},{8,9},{9,8},{10,11... | collective-permute-start | bytes 1179656 | tf_op jit(solution)/shard_map/ppermute | solution.py:601
  81.0 7.1 %collective-permute-start.2 = (bf16[200,384]{1,0:T(8,128)(2,1)S(1)}, bf16[200,384]{1,0:T(8,128)(2,1)S(1)}, u32[]{:S(2)}, u32[]{:S(2)}) collective-permute-start(bf16[200,384]{1,0:T(8,128)(2,1)S(1)} %reduce_sum.24), channel_id=1, source_target_pairs={{0,16},{2,18},{4,20},{6,22},{8,24},{10,26},{12,28},{14,30},{16,0},... | collective-permute-start | bytes 460808 | tf_op jit(solution)/shard_map/ppermute | solution.py:590
  96.5 21.1 %all-to-all-start.1 = ((bf16[8,200,384]{2,1,0:T(8,128)(2,1)}), bf16[8,200,384]{2,1,0:T(8,128)(2,1)S(1)}, u32[]{:S(2)}, u32[]{:S(2)}) async-start(bf16[8,200,384]{2,1,0:T(8,128)(2,1)} %broadcast_in_dim.79), calls=%async_computation.1 | async-start | bytes 2457600 | tf_op jit(solution)/shard_map/all_to_all | solution.py:585
  100.2 24.1 %copy-start.6 = (f32[512,384]{1,0:T(8,128)S(1)}, f32[512,384]{1,0:T(8,128)}, u32[]{:S(2)}) copy-start(f32[512,384]{1,0:T(8,128)} %get-tuple-element.122) | copy-start | bytes 2359300
  100.3 15.3 %collective-permute-start.5 = (bf16[104,384]{1,0:T(8,128)(2,1)S(1)}, bf16[104,384]{1,0:T(8,128)(2,1)S(1)}, u32[]{:S(2)}, u32[]{:S(2)}) collective-permute-start(bf16[104,384]{1,0:T(8,128)(2,1)S(1)} %reduce_sum.25), channel_id=1, source_target_pairs={{0,16},{2,18},{4,20},{6,22},{8,24},{10,26},{12,28},{14,30},{16,0},... | collective-permute-start | bytes 239624 | tf_op jit(solution)/shard_map/ppermute | solution.py:590
  117.6 7.6 %collective-permute-start.6 = (bf16[1600,384]{1,0:T(8,128)(2,1)S(1)}, bf16[1600,384]{1,0:T(8,128)(2,1)}, u32[]{:S(2)}, u32[]{:S(2)}) collective-permute-start(bf16[1600,384]{1,0:T(8,128)(2,1)S(1)} %bitcast.54), channel_id=1, source_target_pairs={{0,2},{2,0},{4,6},{6,4},{8,10},{10,8},{12,14},{14,12},{16,18},{18,... | collective-permute-start | bytes 3686408 | tf_op jit(solution)/shard_map/ppermute | solution.py:576
  118.5 16.7 %all-to-all-start.3 = ((bf16[8,104,384]{2,1,0:T(8,128)(2,1)}), bf16[8,104,384]{2,1,0:T(8,128)(2,1)}, u32[]{:S(2)}, u32[]{:S(2)}) async-start(bf16[8,104,384]{2,1,0:T(8,128)(2,1)} %broadcast_in_dim.80), calls=%async_computation.3 | async-start | bytes 1277952 | tf_op jit(solution)/shard_map/all_to_all | solution.py:585
  125.2 12.2 %copy-start = (bf16[384,2304]{1,0:T(8,128)(2,1)S(1)}, bf16[384,2304]{1,0:T(8,128)(2,1)}, u32[]{:S(2)}) copy-start(bf16[384,2304]{1,0:T(8,128)(2,1)} %ada_ref.1) | copy-start | bytes 5308420
  135.1 2.3 %collective-permute-start.7 = (bf16[832,384]{1,0:T(8,128)(2,1)}, bf16[832,384]{1,0:T(8,128)(2,1)S(1)}, u32[]{:S(2)}, u32[]{:S(2)}) collective-permute-start(bf16[832,384]{1,0:T(8,128)(2,1)} %bitcast.33.mine_ref), channel_id=1, source_target_pairs={{0,2},{2,0},{4,6},{6,4},{8,10},{10,8},{12,14},{14,12},{16,18},{18,... | collective-permute-start | bytes 1916936 | tf_op jit(solution)/shard_map/ppermute | solution.py:576

commit v4 on v3

--- a/solution.py
+++ b/solution.py
@@ -76,12 +76,13 @@
 
 class Copies:
     def __init__(self, sems):
-        self.sems, self.made = sems, []
+        self.sems, self.made, self.count = sems, [], 0
 
     def start(self, source, target):
-        copy = pltpu.make_async_copy(source, target, self.sems.at[len(self.made)])
+        copy = pltpu.make_async_copy(source, target, self.sems.at[self.count])
         copy.start()
         self.made.append(copy)
+        self.count += 1
 
     def wait(self):
         for copy in self.made:
@@ -94,53 +95,187 @@
         copies.start(payload_ref.at[pl.ds(pl.multiple_of(which * half, 16), half)], target)
 
 
-def prep_kernel(
-    own, seq, starts_ref, *refs,
+SIDE, PLACE, SLOT_START, COUNT, VALID, LABEL, SEQ_PLACE, STARTS = range(8)
+
+
+def row_span(scalar_ref, number, count):
+    return pl.ds(pl.multiple_of(scalar_ref[number], 16), count)
+
+
+def slot_places(scalar_ref, kept_ref, slots):
+    return kept_ref[pl.ds(pl.multiple_of(scalar_ref[SLOT_START], 8), slots), :]
+
+
+def row_places(scalar_ref, kept_ref, own, slots):
+    mine = lax.broadcasted_iota(jnp.int32, (own, 1), 0) + scalar_ref[STARTS]
+    return jnp.concatenate([mine, slot_places(scalar_ref, kept_ref, slots)], axis=0)
+
+
+def row_weights(scalar_ref, own, slots, rows):
+    row = lax.broadcasted_iota(jnp.int32, (rows, 1), 0)
+    kept = (row < own + slots) & (row - own + scalar_ref[SLOT_START] < scalar_ref[COUNT])
+    return jnp.where((row < own) | kept, scalar_ref[VALID], 0).astype(F32)
+
+
+def project(tokens, mod_ref, weight_ref, line_ref):
+    normed, unused = norm_parts(tokens.astype(F32))
+    lowered = (normed * (1.0 + mod_ref[1:2, :]) + mod_ref[0:1, :]).astype(BF16)
+    query = (mm(lowered, weight_ref[:, :D]) + line_ref[QV_LINE : QV_LINE + 1, :]).astype(BF16)
+    scaled = (query.astype(F32) * (1.0 / math.sqrt(HDIM))).astype(BF16)
+    keys = mm(lowered, weight_ref[:, D : 2 * D]).astype(BF16)
+    values = (mm(lowered, weight_ref[:, 2 * D :]) + line_ref[QV_LINE + 1 : QV_LINE + 2, :]).astype(BF16)
+    return lowered, scaled, keys, values
+
+
+def head_cols(head):
+    return slice(head * HDIM, (head + 1) * HDIM)
+
+
+def ones_lanes(count):
+    return (lax.broadcasted_iota(jnp.int32, (count, HDIM), 1) < 2).astype(F32).astype(BF16)
+
+
+def bias_table(rel_ref):
+    lane = lax.broadcasted_iota(jnp.int32, (GRID, 128), 1)
+    parts = []
+    for part in range(2):
+        tiles = []
+        for group in range(HEADS // 2):
+            tile = jnp.zeros((GRID, 128), F32)
+            for side in range(2):
+                head = 2 * group + side
+                line = rel_ref[head, part : part + 1, :].astype(F32)
+                line = jnp.concatenate([line, jnp.zeros((1, 128 - line.shape[1]), F32)], axis=1)
+                first = side * HDIM + part * GRID
+                turned = pltpu.roll(
+                    jnp.broadcast_to(line, (GRID, 128)), (first + 128 - (GRID - 1)) % 128, 1,
+                    stride=1, stride_axis=0,
+                )
+                tile = jnp.where((lane >= first) & (lane < first + GRID), turned, tile)
+            tiles.append(tile)
+        parts.append(jnp.concatenate(tiles, axis=1))
+    return jnp.concatenate(parts, axis=0).astype(BF16)
+
+
+QV_LINE, OUT_LINE, FC1_LINE, FC2_LINE = 6, 8, 9, 13
+
+
+def time_features(moment):
+    half = D // 2
+    lane = lax.broadcasted_iota(jnp.int32, (1, D), 1)
+    number = jnp.where(lane < half, lane, lane - half).astype(F32)
+    angle = moment.astype(F32) * jnp.exp(-math.log(10000.0) * number / half)
+    return jnp.where(lane < half, jnp.cos(angle), jnp.sin(angle))
+
+
+def own_kernel(
+    start_ref, count_ref, valid_ref, moment_ref, label_ref,
+    *refs,
 ):
+    sources, outs, local, sems = refs[:11], refs[11:23], refs[23:34], refs[34]
+    scalar_ref, kept_ref, fact_ref, line_ref, mod_ref, a_ref, qs_ref, qaug_ref, kaug_ref, vaug_ref = outs[:10]
+    offset_ref, mask_ref = outs[10:]
+    kept_in, rel_ref, ada_bias_ref, qv_bias_ref, out_bias_ref, fc1_bias_ref, fc2_bias_ref = local[:7]
+    table_ref, ada_ref, tok_ref, weight_ref = local[7:]
+    fetched = [pltpu.make_async_copy(*pair, sems.at[n]) for n, pair in enumerate(zip(sources, local))]
+    for copy in fetched:
+        copy.start()
+    for copy in fetched[:7]:
+        copy.wait()
+    own = tok_ref.shape[0]
+    slots = offset_ref.shape[0]
+    total = mask_ref.shape[1]
+    held = kept_ref.shape[0]
+    label = label_ref[0]
+    for n in range(scalar_ref.shape[0]):
+        scalar_ref[n] = start_ref[n]
+    scalar_ref[COUNT] = count_ref[0]
+    scalar_ref[VALID] = valid_ref[0]
+    scalar_ref[LABEL] = label
+    width = round_up(held, 128)
+    kept = jnp.concatenate([kept_in[...], jnp.zeros((1, width - kept_in.shape[1]), jnp.int32)], axis=1)
+    kept_ref[...] = jnp.broadcast_to(kept, (8, width)).T[:held, :1]
+    place = place_onehot(row_places(start_ref, kept_ref, own, slots))
+    offsets = mm(place, bias_table(rel_ref)).astype(BF16)
+    offset_ref[...] = offsets[own:]
+    number = lax.broadcasted_iota(jnp.int32, (held, 1), 0)
+    live = jnp.where(number < count_ref[0], kept_ref[...], -1)
+    hit = live == lax.broadcasted_iota(jnp.int32, (held, total), 1)
+    count = jnp.sum(hit.astype(F32), axis=0, keepdims=True)
+    mask_ref[...] = jnp.broadcast_to(jnp.where(count > 0.0, 0.0, big_negative), mask_ref.shape)
+    for n in range(6):
+        line_ref[n : n + 1, :] = ada_bias_ref[pl.ds(n * D, D)].astype(F32).reshape(1, D)
+    line_ref[QV_LINE : QV_LINE + 2, :] = qv_bias_ref[...].astype(F32)
+    line_ref[OUT_LINE : OUT_LINE + 1, :] = out_bias_ref[...].astype(F32).reshape(1, D)
+    for n in range(4):
+        line_ref[FC1_LINE + n : FC1_LINE + n + 1, :] = fc1_bias_ref[pl.ds(n * D, D)].astype(F32).reshape(1, D)
+    line_ref[FC2_LINE : FC2_LINE + 1, :] = fc2_bias_ref[...].astype(F32).reshape(1, D)
+    line_ref[FC2_LINE + 1 :, :] = jnp.zeros((2, D), F32)
+    for copy in fetched[7:]:
+        copy.wait()
+    hot = lax.broadcasted_iota(jnp.int32, (16, table_ref.shape[0]), 1) == label
+    conditioned = mm(hot.astype(F32).astype(BF16), table_ref[...]) + time_features(moment_ref[0])
+    gate = 1.0 / (1.0 + jnp.exp(-conditioned))
+    activated = (conditioned * gate).astype(BF16)
+    line = lax.broadcasted_iota(jnp.int32, (16, D), 0)
+    slope = gate * (1.0 + conditioned * (1.0 - gate))
+    fact_ref[...] = jnp.where(line == 0, activated.astype(F32), jnp.where(line == 1, slope, 0.0)).astype(BF16)
+    for n in range(6):
+        mod_ref[n : n + 1, :] = mm(activated, ada_ref[:, n * D : (n + 1) * D])[:1] + line_ref[n : n + 1, :]
+    mod_ref[6:8, :] = jnp.zeros((2, D), F32)
+    lowered, scaled, keys, values = project(tok_ref[...], mod_ref, weight_ref, line_ref)
+    a_ref[...] = lowered
+    qs_ref[...] = scaled
+    for head in range(HEADS):
+        cols = head_cols(head)
+        qaug_ref[head] = jnp.concatenate([scaled[:, cols], offsets[:own, cols]], axis=1)
+        kaug_ref[head] = jnp.concatenate([keys[:, cols], place[:own]], axis=1)
+        vaug_ref[head] = jnp.concatenate([values[:, cols], ones_lanes(own)], axis=1)
+
+
+def prep_kernel(seq, scalar_ref, *refs):
     token_refs, refs = refs[:seq], refs[seq:]
-    kept_ref, picked_ref, where_ref, mod_ref, weight_ref, qv_ref, table_ref = refs[:7]
-    qaug_ref, kaug_ref, vaug_ref, x_ref, mask_ref, a_out, tok_out, slot_out = refs[7:15]
-    qs_ref, a_ref, tok_ref, slot_ref, sems = refs[15:]
+    own_a_ref, own_qs_ref, own_qaug_ref, own_kaug_ref, own_vaug_ref, offset_ref = refs[:6]
+    kept_ref, mod_ref, weight_ref, line_ref = refs[6:10]
+    qaug_ref, kaug_ref, vaug_ref, x_ref, a_out, tok_out, slot_out = refs[10:17]
+    qs_ref, a_ref, tok_ref, slot_ref, sems = refs[17:]
     copies = Copies(sems)
-    total = own * seq
-    slots = picked_ref.shape[0]
+    own = token_refs[0].shape[0]
+    slots, total = offset_ref.shape[0], tok_ref.shape[0]
     for n in range(seq):
-        tok_ref[pl.ds(pl.multiple_of(starts_ref[n], 16), own), :] = token_refs[n][...]
+        tok_ref[row_span(scalar_ref, STARTS + n, own), :] = token_refs[n][...]
     copies.start(tok_ref, tok_out)
-    shift, scale = mod_ref[0:1, :], mod_ref[1:2, :]
-    normed, unused = norm_parts(tok_ref[...].astype(F32))
-    lowered = (normed * (1.0 + scale) + shift).astype(BF16)
-    a_ref[...] = lowered
+    others = [token_refs[n][...] for n in range(1, seq)]
+    others = others[0] if seq == 2 else jnp.concatenate(others, axis=0)
+    lowered, scaled, keys, values = project(others, mod_ref, weight_ref, line_ref)
+    here = row_span(scalar_ref, STARTS, own)
+    a_ref[here, :] = own_a_ref[...]
+    qs_ref[here, :] = own_qs_ref[...]
+    for head in range(HEADS):
+        kaug_ref[head, here, :] = own_kaug_ref[head]
+        vaug_ref[head, here, :] = own_vaug_ref[head]
+        qaug_ref[head, :own, :] = own_qaug_ref[head]
+    for n in range(1, seq):
+        there = row_span(scalar_ref, STARTS + n, own)
+        span = slice((n - 1) * own, n * own)
+        a_ref[there, :] = lowered[span]
+        qs_ref[there, :] = scaled[span]
+        place = place_onehot(lax.broadcasted_iota(jnp.int32, (own, 1), 0) + scalar_ref[STARTS + n])
+        for head in range(HEADS):
+            cols = head_cols(head)
+            kaug_ref[head, there, :] = jnp.concatenate([keys[span, cols], place], axis=1)
+            vaug_ref[head, there, :] = jnp.concatenate([values[span, cols], ones_lanes(own)], axis=1)
     copies.start(a_ref, a_out)
-    query = (mm(lowered, weight_ref[:, :D]) + qv_ref[0:1, :]).astype(BF16)
-    scaled = (query.astype(F32) * (1.0 / math.sqrt(HDIM))).astype(BF16)
-    qs_ref[...] = scaled
-    keys = mm(lowered, weight_ref[:, D : 2 * D]).astype(BF16)
-    values = (mm(lowered, weight_ref[:, 2 * D :]) + qv_ref[1:2, :]).astype(BF16)
-    key_place = place_onehot(lax.broadcasted_iota(jnp.int32, (total, 1), 0))
-    lane = lax.broadcasted_iota(jnp.int32, (total, HDIM), 1)
-    ones = (lane < 2).astype(F32).astype(BF16)
-    for head in range(HEADS):
-        cols = slice(head * HDIM, (head + 1) * HDIM)
-        kaug_ref[head] = jnp.concatenate([keys[:, cols], key_place], axis=1)
-        vaug_ref[head] = jnp.concatenate([values[:, cols], ones], axis=1)
-    chosen = (picked_ref[...] == lax.broadcasted_iota(jnp.int32, (slots, total), 1)).astype(F32)
-    chosen = chosen.astype(BF16)
+    chosen = slot_places(scalar_ref, kept_ref, slots) == lax.broadcasted_iota(jnp.int32, (slots, total), 1)
+    chosen = chosen.astype(F32).astype(BF16)
     x_ref[:own, :] = token_refs[0][...]
     x_ref[own:, :] = mm(chosen, tok_ref[...]).astype(BF16)
-    slot_ref[...] = mm(chosen, lowered).astype(BF16)
+    slot_ref[...] = mm(chosen, a_ref[...]).astype(BF16)
     copies.start(slot_ref, slot_out)
-    slot_query = mm(chosen, scaled).astype(BF16)
-    own_query = qs_ref[pl.ds(pl.multiple_of(starts_ref[0], 16), own), :]
-    offsets = mm(place_onehot(where_ref[...]), table_ref[...]).astype(BF16)
+    query = mm(chosen, qs_ref[...]).astype(BF16)
     for head in range(HEADS):
-        cols = slice(head * HDIM, (head + 1) * HDIM)
-        qaug_ref[head, :own] = jnp.concatenate([own_query[:, cols], offsets[:own, cols]], axis=1)
-        qaug_ref[head, own:] = jnp.concatenate([slot_query[:, cols], offsets[own:, cols]], axis=1)
-    held = kept_ref.shape[0]
-    hit = kept_ref[...] == lax.broadcasted_iota(jnp.int32, (held, total), 1)
-    count = jnp.sum(hit.astype(F32), axis=0, keepdims=True)
-    mask_ref[...] = jnp.broadcast_to(jnp.where(count > 0.0, 0.0, big_negative), mask_ref.shape)
+        cols = head_cols(head)
+        qaug_ref[head, own:, :] = jnp.concatenate([query[:, cols], offset_ref[:, cols]], axis=1)
     copies.wait()
 
 
@@ -187,22 +322,32 @@
     copies.wait()
 
 
+def cotangents(scalar_ref, slots, full_ref, slot_ref):
+    own = full_ref.shape[0]
+    weight = row_weights(scalar_ref, own, slots, own + slot_ref.shape[0])
+    return weight, jnp.concatenate([full_ref[...], slot_ref[...]], axis=0).astype(F32) * weight
+
+
 def feed_kernel(
-    side_ref, o_ref, x_ref, cot_ref, wgt_ref, mod_ref, wout_ref, bout_ref, w1_ref, b1_ref, w2_ref, extra_ref,
+    slots, everyone, scalar_ref, o_ref, x_ref, cot_full_ref, cot_slot_ref, mod_ref, wout_ref, w1_ref,
+    w2_ref, line_ref, fact_ref,
     att_ref, hidden_ref, du_ref, keep_ref, send_ref, pay_ref, sems,
 ):
     rows = x_ref.shape[0]
     gate1, shift2, scale2, gate2 = [mod_ref[n : n + 1, :] for n in range(2, 6)]
     merged = jnp.concatenate([o_ref[n] for n in range(HEADS // 2)], axis=1).astype(BF16)
-    attended = mm(merged, wout_ref[...]) + bout_ref[...]
+    attended = mm(merged, wout_ref[...]) + line_ref[OUT_LINE : OUT_LINE + 1, :]
     att_ref[...] = attended
     normed, unused = norm_parts(x_ref[...].astype(F32) + gate1 * attended)
     second = (normed * (1.0 + scale2) + shift2).astype(BF16)
-    dz = (gate2 * (cot_ref[...].astype(F32) * wgt_ref[...])).astype(BF16)
+    unused, cot = cotangents(scalar_ref, slots, cot_full_ref, cot_slot_ref)
+    dz = (gate2 * cot).astype(BF16)
+
+    bias = jnp.concatenate([line_ref[FC1_LINE + n : FC1_LINE + n + 1, :] for n in range(4)], axis=1)
 
     def products(c):
         cols = slice(c * CHUNK, (c + 1) * CHUNK)
-        return mm(second, w1_ref[:, cols]) + b1_ref[:, cols], mm_t(dz, w2_ref[cols, :])
+        return mm(second, w1_ref[:, cols]) + bias[:, cols], mm_t(dz, w2_ref[cols, :])
 
     chunks = FF // CHUNK
     ready = products(0)
@@ -227,28 +372,37 @@
     pay_ref[FF : 2 * FF, :] = mm(hidden_ref[...].T, dz).astype(BF16)
     heads += [jnp.sum(dz.astype(F32), axis=0, keepdims=True), jnp.zeros((11, D), F32)]
     pay_ref[2 * FF : 2 * FF + 16, :] = jnp.concatenate(heads, axis=0).astype(BF16)
-    pay_ref[2 * FF + 16 :, :] = extra_ref[...]
+    lane = lax.broadcasted_iota(jnp.int32, (16, D), 1)
+    line = lax.broadcasted_iota(jnp.int32, (16, D), 0)
+    label = scalar_ref[LABEL]
+    digits = jnp.where(lane == 0, label // GRID, jnp.where(lane == 1, label % GRID, 0)).astype(F32)
+    facts = jnp.where(line == 2, digits, fact_ref[...].astype(F32)).astype(BF16)
+    extra = pay_ref.shape[0] - 2 * FF - 16
+    row = lax.broadcasted_iota(jnp.int32, (extra, 16), 0)
+    mine = (row % everyone == scalar_ref[PLACE]) & (row < 3 * everyone) & (scalar_ref[SEQ_PLACE] == 0)
+    hot = lax.broadcasted_iota(jnp.int32, (extra, 16), 1) == jnp.where(mine, row // everyone, -1)
+    pay_ref[2 * FF + 16 :, :] = mm(hot.astype(F32).astype(BF16), facts).astype(BF16)
     copies = Copies(sems)
-    split_halves(copies, side_ref[0], pay_ref, keep_ref, send_ref)
+    split_halves(copies, scalar_ref[SIDE], pay_ref, keep_ref, send_ref)
     copies.wait()
 
 
 def feed_rest_kernel(
-    own, o_ref, inverse_ref, x_ref, cot_ref, wgt_ref, mod_ref, wout_ref, w1_ref, w2_ref, b2_ref,
+    slots, scalar_ref, o_ref, inverse_ref, x_ref, cot_full_ref, cot_slot_ref, mod_ref, wout_ref, w1_ref,
+    w2_ref, line_ref,
     att_ref, hidden_ref, du_ref,
     small_ref, y_full_out, y_slot_out, dm_out, x_out, do_out, go_out, y_ref, dm_ref, do_ref, go_ref, sems,
 ):
-    rows = x_ref.shape[0]
+    rows, own = x_ref.shape[0], cot_full_ref.shape[0]
     copies = Copies(sems)
     copies.start(x_ref, x_out)
     gate1, shift2, scale2, gate2 = [mod_ref[n : n + 1, :] for n in range(2, 6)]
-    weight = wgt_ref[...]
+    weight, cot = cotangents(scalar_ref, slots, cot_full_ref, cot_slot_ref)
     back = mm_t(du_ref[...], w1_ref[...])
-    branch = mm(hidden_ref[...], w2_ref[...]) + b2_ref[...]
+    branch = mm(hidden_ref[...], w2_ref[...]) + line_ref[FC2_LINE : FC2_LINE + 1, :]
     attended = att_ref[...]
     middle = x_ref[...].astype(F32) + gate1 * attended
     normed, inverse = norm_parts(middle)
-    cot = cot_ref[...].astype(F32) * weight
     y_ref[...] = ((middle + gate2 * branch) * weight).astype(BF16)
     copies.start(y_ref.at[pl.ds(0, own)], y_full_out)
     copies.start(y_ref.at[pl.ds(own, rows - own)], y_slot_out)
@@ -319,7 +473,7 @@
     dv_ref[...] = dvt_ref[...].astype(BF16).T
 
 
-def back_kernel(own, everyone, scalar_ref, where_ref, picked_ref, mod_ref, prior_ref, *refs):
+def back_kernel(own, everyone, scalar_ref, kept_ref, mod_ref, prior_ref, *refs):
     group_sources, refs = refs[:5], refs[5:]
     sources, refs = refs[:7], refs[7:]
     keep_ref, send_ref, dx_ref, dx_own_ref, refs = *refs[:4], refs[4:]
@@ -354,7 +508,8 @@
             copy.start()
         for copy in fetches(1, 1):
             copy.start()
-        place_ref[...] = place_onehot(where_ref[...], turned=True).T
+        slots = x_ref.shape[0] - own
+        place_ref[...] = place_onehot(row_places(scalar_ref, kept_ref, own, slots), turned=True).T
         whole[0].wait()
         normed, inverse = norm_parts(tok_ref[...].astype(F32))
         normed_ref[...] = normed
@@ -381,7 +536,7 @@
         rows = x_ref.shape[0]
         slots = rows - own
         scale = mod_ref[1:2, :]
-        here = pl.ds(pl.multiple_of(scalar_ref[1], 16), own)
+        here = row_span(scalar_ref, STARTS, own)
 
         def joined(ref, span):
             return jnp.concatenate([ref[n, span, :] for n in range(groups)], axis=1)
@@ -399,7 +554,8 @@
         da = mm_t(dq_slot, weight_ref[:, :D])
         shift_sum, scale_sum = column(da), column(da * slot_normed)
         spread = dm_ref[own:, :] + norm_back(slot_normed, slot_inverse, da * (1.0 + scale))
-        chosen = (picked_ref[...] == lax.broadcasted_iota(jnp.int32, (slots, total), 1)).astype(F32)
+        chosen = slot_places(scalar_ref, kept_ref, slots) == lax.broadcasted_iota(jnp.int32, (slots, total), 1)
+        chosen = chosen.astype(F32)
         moved = mm(chosen.astype(BF16).T, spread.astype(BF16))
         dxs_ref[...] = mm_t(dk, weight_ref[:, D : 2 * D]) + mm_t(dv, weight_ref[:, 2 * D :])
         dxs_ref[here, :] += mm_t(dq_own, weight_ref[:, :D])
@@ -409,8 +565,9 @@
         inverse = jnp.concatenate([inverse_ref[...]] * (D // 128), axis=1)
         dxs_ref[...] = moved + norm_back(normed, inverse, da * (1.0 + scale))
         dx_own_ref[...] = dxs_ref[here, :] + dm_ref[:own, :]
-        for n in range(dx_ref.shape[0]):
-            dx_ref[n] = dxs_ref[pl.ds(pl.multiple_of(scalar_ref[3 + n], 16), own), :].astype(BF16)
+        others = dx_ref.shape[0]
+        for n in range(others):
+            dx_ref[n] = dxs_ref[row_span(scalar_ref, STARTS + 1 + others + n, own), :].astype(BF16)
         rel = table_sums([tab_ref[n] for n in range(groups)])
         smalls = jnp.concatenate(
             [
@@ -422,11 +579,11 @@
         tail = pay_ref.shape[0] - 4 * D
         row = lax.broadcasted_iota(jnp.int32, (tail, 16), 0)
         lane = lax.broadcasted_iota(jnp.int32, (tail, 16), 1)
-        wanted = jnp.where(row % everyone == scalar_ref[2], row // everyone, -1)
+        wanted = jnp.where(row % everyone == scalar_ref[PLACE], row // everyone, -1)
         wanted = jnp.where(row < 6 * everyone, wanted, row - 6 * everyone + 6)
         pay_ref[4 * D :, :] = mm((lane == wanted).astype(F32).astype(BF16), smalls).astype(BF16)
         halves = Copies(pay_sems)
-        split_halves(halves, scalar_ref[0], pay_ref, keep_ref, send_ref)
+        split_halves(halves, scalar_ref[SIDE], pay_ref, keep_ref, send_ref)
         halves.wait()
 
 
@@ -459,6 +616,19 @@
     )(*args)
 
 
+def own_call(outs, scalars, sources):
+    return pl.pallas_call(
+        own_kernel,
+        out_shape=[jax.ShapeDtypeStruct(shape, dtype) for shape, dtype in outs],
+        in_specs=[smem] * len(scalars) + [hbm] * len(sources),
+        out_specs=[smem] + [vmem] * (len(outs) - 1),
+        scratch_shapes=[pltpu.VMEM(value.shape, value.dtype) for value in sources]
+        + [pltpu.SemaphoreType.DMA((len(sources),))],
+        compiler_params=pltpu.CompilerParams(vmem_limit_bytes=16 * MIB),
+        cost_estimate=pl.CostEstimate(flops=3 * 10**9, bytes_accessed=MIB, transcendentals=0),
+    )(*scalars, *map(in_hbm, sources))
+
+
 def in_hbm(value):
     return pltpu.with_memory_space_constraint(value, pltpu.HBM)
 
@@ -471,7 +641,7 @@
     return call(add_kernel, [(left.shape, BF16)], [], [left, right], micros=micros)[0]
 
 
-def back_call(own, everyone, groups_of, sources, scalars, where, picked, mod, prior, tail_half):
+def back_call(own, everyone, groups_of, sources, scalars, kept, mod, prior, tail_half):
     rows, total = groups_of[1].shape[1], groups_of[2].shape[1]
     groups = HEADS // 2
     others = total // own - 1
@@ -485,7 +655,7 @@
         ((128, total), F32), ((128, total), F32), ((2 * tail_half, D), BF16),
         ((2 * GRID, rows), BF16), ((rows, 128), BF16),
     ]
-    small = [where, picked, mod, prior]
+    small = [kept, mod, prior]
     return pl.pallas_call(
         functools.partial(back_kernel, own, everyone),
         grid=(groups + 1,),
@@ -532,26 +702,29 @@
 
 
 def last_kernel(
-    everyone, side_ref, mine_ref, other_ref, info_ref, ada_ref, qv_ref, rel_ref, out_bias_ref, ada_bias_ref,
-    gqkv_out, gada_out, table_out, go_out, gqkv_ref, gada_ref, table_ref, go_ref, sems,
+    everyone, side_ref, mine_ref, other_ref, info_ref, ada_in, qv_ref, rel_ref, out_bias_ref, ada_bias_ref,
+    gqkv_out, gada_out, table_out, go_out, gqkv_ref, gada_ref, table_ref, go_ref, ada_ref, sems,
 ):
     get = halves_reader(side_ref, mine_ref, other_ref)
     copies = Copies(sems)
-    act_t = info_ref[:everyone, :].T
-    back = jnp.zeros((everyone, D), F32)
-    for n in range(6):
-        cols = pl.ds(n * D, D)
-        dmod = get(4 * D + n * everyone, everyone)
-        gada_ref[:, cols] = mm(act_t, dmod)
-        copies.start(gada_ref.at[:, cols], gada_out.at[:, cols])
-        ada_bias_ref[cols] = jnp.sum(dmod.astype(F32), axis=0)
-        back = back + mm_t(dmod, ada_ref[:, cols])
+    copies.start(ada_in, ada_ref)
     for n in range(3):
         cols = pl.ds(n * D, D)
         gqkv_ref[:, cols] = get(n * D, D).astype(F32)
         copies.start(gqkv_ref.at[:, cols], gqkv_out.at[:, cols])
     go_ref[...] = get(3 * D, D).astype(F32)
     copies.start(go_ref, go_out)
+    act_t = info_ref[:everyone, :].T
+    dmods = [get(4 * D + n * everyone, everyone) for n in range(6)]
+    for n in range(6):
+        cols = pl.ds(n * D, D)
+        gada_ref[:, cols] = mm(act_t, dmods[n])
+        copies.start(gada_ref.at[:, cols], gada_out.at[:, cols])
+        ada_bias_ref[cols] = jnp.sum(dmods[n].astype(F32), axis=0)
+    copies.made.pop(0).wait()
+    back = jnp.zeros((everyone, D), F32)
+    for n in range(6):
+        back = back + mm_t(dmods[n], ada_ref[:, n * D : (n + 1) * D])
     cond = info_ref[everyone : 2 * everyone, :].astype(F32) * back
     high = cond.astype(BF16)
     low = (cond - high.astype(F32)).astype(BF16)
@@ -567,7 +740,7 @@
     for part in range(2):
         for head in range(HEADS):
             at = 2 * GRID * head
-            rel_ref[part, head : head + 1, :] = small[2 + part : 3 + part, at : at + 2 * GRID - 1]
+            rel_ref[head, part : part + 1, :] = small[2 + part : 3 + part, at : at + 2 * GRID - 1]
     out_bias_ref[...] = small[4]
     copies.wait()
 
@@ -601,27 +774,6 @@
         lax.ppermute(partial[step - 1], "seq", [(n, (n + step) % seq) for n in range(seq)])
         for step in range(1, seq)
     ]
-
-
-def time_features(moments):
-    half_width = D // 2
-    frequency = jnp.exp(-math.log(10000.0) * jnp.arange(half_width, dtype=F32) / half_width)
-    angles = moments.astype(F32)[:, None] * frequency[None, :]
-    return jnp.concatenate([jnp.cos(angles), jnp.sin(angles)], axis=-1)
-
-
-def offset_hot():
-    first = jnp.arange(GRID, dtype=jnp.int32)
-    offsets = first[None, :] - first[:, None] + GRID - 1
-    return (offsets[..., None] == jnp.arange(2 * GRID - 1, dtype=jnp.int32)).astype(F32)
-
-
-def bias_table(rel_bias):
-    both = jnp.einsum("cho,ijo->cihj", rel_bias.astype(F32), offset_hot(), precision=highest)
-    empty = jnp.zeros_like(both[0])
-    top = jnp.concatenate([both[0], empty], axis=-1)
-    low = jnp.concatenate([empty, both[1]], axis=-1)
-    return jnp.concatenate([top, low], axis=0).reshape(2 * GRID, HEADS * 2 * GRID).astype(BF16)
 
 
 def body(
@@ -639,59 +791,50 @@
     classes = class_table.shape[0]
     dp_place, seq_place = lax.axis_index("dp"), lax.axis_index("seq")
 
-    conditioned = jnp.take(class_table, class_label, axis=0).astype(F32) + time_features(timestep)
-    gate = jax.nn.sigmoid(conditioned)
-    activated = (conditioned * gate).astype(BF16)
-    slope = gate * (1.0 + conditioned * (1.0 - gate))
-    modulation = jnp.dot(activated, ada_weight, preferred_element_type=F32) + ada_bias.astype(F32)
-    modulation = jnp.pad(modulation.reshape(samples, 6, D), ((0, 0), (0, 2), (0, 0)))
-    table = bias_table(rel_bias)
-    valid = sample_valid.astype(F32)
-
-    digits = jnp.stack([class_label // GRID, class_label % GRID], axis=1).astype(F32)
-    digits = jnp.pad(digits, ((0, 0), (0, D - 2)))
-    info = jnp.stack([activated.astype(F32), slope, digits], axis=0)
-    info = info * (seq_place == 0).astype(F32)
     extra_rows = round_up(2 * FF + 16 + 3 * everyone, dp * seq * 4) - (2 * FF + 16)
-    spread = (jnp.arange(everyone)[:, None] == dp_place * samples + jnp.arange(samples)[None, :])
-    info = jnp.einsum("es,nsd->end", spread.astype(F32), info, precision=highest)
-    info = info.transpose(1, 0, 2).reshape(3 * everyone, D).astype(BF16)
-    info = jnp.pad(info, ((0, extra_rows - 3 * everyone), (0, 0)))
-
-    slot_numbers = jnp.arange(held, dtype=jnp.int32)
-    live_all = slot_numbers[None, :] < kept_count[:, None]
-    slot_start = seq_place * slots
     peers = dp // 4 * seq
     side = dp_place % 2
     sides = side.astype(jnp.int32).reshape(1)
     half = (2 * FF + 16 + extra_rows) // 2
     tail_half = round_up(4 * D + 16 + 6 * everyone, dp * seq * 4) // 2
-    starts = ((seq_place - jnp.arange(seq, dtype=jnp.int32)) % seq * own).astype(jnp.int32)
-
     kept_of = []
     for s in range(samples):
         tokens = [image_tokens[s]]
         for step in range(1, seq):
             tokens.append(lax.ppermute(tokens[0], "seq", [(n, (n + step) % seq) for n in range(seq)]))
-        kept = jnp.where(live_all[s], kept_index[s], -1)[:, None]
-        picked = lax.dynamic_slice_in_dim(kept_index[s], slot_start, slots, 0)
-        live = lax.dynamic_slice_in_dim(live_all[s], slot_start, slots, 0)
-        picked = jnp.pad(picked, (0, padded - slots))[:, None]
-        where = jnp.concatenate([starts[0] + jnp.arange(own, dtype=jnp.int32), picked[:, 0]])[:, None]
-        weight = valid[s] * jnp.concatenate(
-            [jnp.ones((own,), F32), jnp.pad(live.astype(F32), (0, padded - slots))]
+        number = jnp.arange(STARTS + 2 * seq - 1, dtype=jnp.int32)
+        block = number - STARTS
+        scalars = jnp.where(block < seq, seq_place - block, seq_place + block - seq + 1) % seq * own
+        entries = {
+            SIDE: side, PLACE: dp_place * samples + s, SLOT_START: seq_place * slots, SEQ_PLACE: seq_place,
+        }
+        for at, entry in entries.items():
+            scalars = jnp.where(number == at, entry, scalars)
+        places = scalars.astype(jnp.int32)
+        held_rows = held + padded - slots
+        cot_slot = jnp.pad(grad_masked[s], ((0, padded - slots), (0, 0)))
+        one = slice(s, s + 1)
+        scalars, kept, facts, lines, mod, *owned, mask = own_call(
+            [
+                (places.shape, jnp.int32), ((held_rows, 1), jnp.int32), ((16, D), BF16), ((16, D), F32),
+                ((8, D), F32), ((own, D), BF16), ((own, D), BF16), ((HEADS, own, 128), BF16),
+                ((HEADS, own, 128), BF16), ((HEADS, own, 128), BF16), ((padded, D), BF16), ((8, total), F32),
+            ],
+            [places, kept_count[one], sample_valid[one], timestep[one], class_label[one]],
+            [
+                kept_index[one], rel_bias.transpose(1, 0, 2), ada_bias, qv_bias, out_bias, fc1_bias, fc2_bias,
+                class_table, ada_weight, tokens[0], qkv_weight,
+            ],
         )
-        cot = jnp.concatenate([grad_full[s], jnp.pad(grad_masked[s], ((0, padded - slots), (0, 0)))])
-        qaug, kaug, vaug, x, mask, lowered, whole, slot = call(
-            functools.partial(prep_kernel, own, seq),
+        qaug, kaug, vaug, x, lowered, whole, slot = call(
+            functools.partial(prep_kernel, seq),
             [
                 ((HEADS, rows, 128), BF16), ((HEADS, total, 128), BF16), ((HEADS, total, 128), BF16),
-                ((rows, D), BF16), ((8, total), F32),
-                ((total, D), BF16), ((total, D), BF16), ((padded, D), BF16),
+                ((rows, D), BF16), ((total, D), BF16), ((total, D), BF16), ((padded, D), BF16),
             ],
             [((total, D), BF16), ((total, D), BF16), ((total, D), BF16), ((padded, D), BF16)],
-            [starts, *tokens, kept, picked, where, modulation[s], qkv_weight, qv_bias.astype(F32), table],
-            scalars=1, away=3, copies=3, micros=5,
+            [scalars, *tokens, *owned, kept, mod, qkv_weight, lines],
+            scalars=1, away=3, copies=3, micros=3, limit=16,
         )
         mixed, inverse, spread_far, qaug_far, kaug_far, vaug_far = call(
             functools.partial(attend_kernel, own),
@@ -701,25 +844,25 @@
             ],
             [((HEADS, rows, total), BF16)],
             [qaug, kaug, vaug, mask],
-            away=4, copies=3 + HEADS, micros=10, limit=40,
+            away=4, copies=3 + HEADS, micros=10, limit=32,
         )
         attended, hidden, du, keep, send = call(
-            feed_kernel,
+            functools.partial(feed_kernel, slots, everyone),
             [((rows, D), F32), ((rows, FF), BF16), ((rows, FF), BF16), ((half, D), BF16), ((half, D), BF16)],
             [((2 * half, D), BF16)],
             [
-                sides, mixed, x, cot, weight[:, None], modulation[s], out_weight, out_bias.astype(F32)[None],
-                fc1_weight, fc1_bias.astype(F32)[None], fc2_weight, info if s == 0 else jnp.zeros_like(info),
+                scalars, mixed, x, grad_full[s], cot_slot, mod, out_weight, fc1_weight, fc2_weight, lines,
+                facts,
             ],
-            scalars=1, copies=2, micros=10, limit=32,
+            scalars=1, copies=2, micros=10, limit=24,
         )
         kept_of.append(dict(
             rest=[
-                mixed, inverse, x, cot, weight[:, None], modulation[s], out_weight, fc1_weight, fc2_weight,
-                fc2_bias.astype(F32)[None], attended, hidden, du,
+                scalars, mixed, inverse, x, grad_full[s], cot_slot, mod, out_weight, fc1_weight, fc2_weight,
+                lines, attended, hidden, du,
             ],
             groups=[spread_far, qaug_far, kaug_far, vaug_far], sources=[whole, lowered, slot, qkv_weight],
-            where=where, picked=picked, keep=keep, send=send,
+            small=[scalars, kept, mod], keep=keep, send=send,
         ))
 
     def added(arrays):
@@ -732,14 +875,14 @@
 
     rests = [
         call(
-            functools.partial(feed_rest_kernel, own),
+            functools.partial(feed_rest_kernel, slots),
             [
                 ((8, D), F32), ((own, D), BF16), ((padded, D), BF16), ((rows, D), F32), ((rows, D), BF16),
                 ((HEADS, rows, 128), BF16), ((D, D), BF16),
             ],
             [((rows, D), BF16), ((rows, D), F32), ((HEADS, rows, 128), BF16), ((D, D), BF16)],
             k["rest"],
-            away=6, copies=6, micros=6, limit=32,
+            scalars=1, away=6, copies=6, micros=6, limit=24,
         )
         for k in kept_of
     ]
@@ -747,16 +890,13 @@
     mine, rests = lax.optimization_barrier((mine, rests))
     pieces = exchange(mine.reshape(peers, half // peers, D), dp, seq)
     tails = []
-    for number, (k, rest) in enumerate(zip(kept_of, rests)):
+    for k, rest in zip(kept_of, rests):
         small, unused_full, unused_slot, dmid, x_far, dout_far, grad_out = rest
-        place = (dp_place * samples + number).astype(jnp.int32)
-        others = (seq_place + jnp.arange(1, seq, dtype=jnp.int32)) % seq * own
-        scalars = jnp.concatenate([jnp.stack([sides[0], starts[0], place]), others.astype(jnp.int32)])
         whole, lowered, slot, weights = k["sources"]
         tails.append(
             back_call(
                 own, everyone, [*k["groups"], dout_far], [whole, lowered, x_far, slot, weights, dmid, grad_out],
-                scalars, k["where"], k["picked"], modulation[number], small, tail_half,
+                *k["small"], small, tail_half,
             )
         )
 
@@ -766,14 +906,12 @@
     mine = add_call(keep, got, 30).reshape(peers, tail_half // peers, D)
     chunk = sum_pieces(pieces, dp)
     last_chunk = sum_pieces(exchange(mine, dp, seq), dp)
-    moved = [scatter_rows(t[2], seq) for t in tails]
-    chunk, moved = lax.optimization_barrier((chunk, moved))
+    first_moved = [scatter_rows(t[2][:, : own // 2], seq) for t in tails]
+    chunk, first_moved = lax.optimization_barrier((chunk, first_moved))
+    last_moved = [scatter_rows(t[2][:, own // 2 :], seq) for t in tails]
     layer_half = spread_out(chunk, dp, seq)
     layer_half, last_chunk = lax.optimization_barrier((layer_half, last_chunk))
     last_half = spread_out(last_chunk, dp, seq)
-    grad_input = jnp.stack(
-        [t[3] + functools.reduce(jnp.add, [m.astype(F32) for m in came]) for t, came in zip(tails, moved)]
-    )
     out_full = jnp.stack([rest[1] for rest in rests])
     out_masked = jnp.stack([rest[2][:slots] for rest in rests])
     info, layer_small, grad_fc1, grad_fc2 = call(
@@ -785,19 +923,26 @@
     )
     grad_fc1_bias = layer_small[:4].reshape(FF)
     grad_fc2_bias = layer_small[4]
-    last_half, info, grad_fc1_bias, grad_fc2_bias, grad_input = lax.optimization_barrier(
-        (last_half, info, grad_fc1_bias, grad_fc2_bias, grad_input)
+    last_half, info, grad_fc1_bias, grad_fc2_bias = lax.optimization_barrier(
+        (last_half, info, grad_fc1_bias, grad_fc2_bias)
     )
     grad_qv, grad_rel, grad_out_bias, grad_ada_bias, grad_qkv, grad_ada, grad_table, grad_out = call(
         functools.partial(last_kernel, everyone),
         [
-            ((2, D), F32), ((2, HEADS, 2 * GRID - 1), F32), ((D,), F32), ((6 * D,), F32),
+            ((2, D), F32), ((HEADS, 2, 2 * GRID - 1), F32), ((D,), F32), ((6 * D,), F32),
             ((D, 3 * D), F32), ((D, 6 * D), F32), ((classes, D), F32), ((D, D), F32),
         ],
-        [((D, 3 * D), F32), ((D, 6 * D), F32), ((classes, D), F32), ((D, D), F32)],
-        [sides, last_half, swap_cores(last_half, dp), info, ada_weight],
-        scalars=1, away=4, copies=11, micros=4, limit=16,
+        [((D, 3 * D), F32), ((D, 6 * D), F32), ((classes, D), F32), ((D, D), F32), (ada_weight.shape, BF16)],
+        [sides, last_half, swap_cores(last_half, dp), info, in_hbm(ada_weight)],
+        scalars=1, far=1, away=4, copies=12, micros=4, limit=16,
     )
+    grad_rel = grad_rel.transpose(1, 0, 2)
+    grad_qkv, last_moved = lax.optimization_barrier((grad_qkv, last_moved))
+    grad_input = []
+    for tail, *moved in zip(tails, first_moved, last_moved):
+        came = [jnp.concatenate(both).astype(F32) for both in zip(*moved)]
+        grad_input.append(functools.reduce(jnp.add, came, tail[3]))
+    grad_input = jnp.stack(grad_input)
     return (
         out_full, out_masked, grad_input, grad_table, grad_ada, grad_ada_bias, grad_qkv, grad_qv,
         grad_rel, grad_out, grad_out_bias, grad_fc1, grad_fc1_bias, grad_fc2, grad_fc2_bias,

time: 144 us -> 139 us (0.965)
  other arithmetic: 6.57 us -> 2.67 us
  Pallas kernels: 59.4 us -> 62.4 us
  matrix products: 2.36 us -> 0 us
    pallas_call x0 -> x1, Pallas kernels: none -> 4.89 us  [own_call(): pl.pallas_call(own_kernel, out_shape=[jax.ShapeDtypeStruct(shape, dtype)...]
    ppermute x1 -> x2, waiting for transfers between devices: 7.24 us -> 2.86 us  [scatter_rows(): lax.ppermute(partial[step - 1], 'seq', [(n, (n + step) % seq) for n in ra...]
    all_to_all x4, waiting for transfers between devices: 7 us -> 9.7 us  [exchange(): return lax.all_to_all(value, AXES, 0, 0, axis_index_groups=groups)]
    dot_general x2 -> x0, matrix products: 2.36 us -> none  [the longest x1 1.84 us: body(): jnp.dot(activated, ada_weight, preferred_element_type=F32)]
    pallas_call x7, Pallas kernels: 40.1 us -> 37.9 us  [call(): pl.pallas_call(kernel, out_shape=[jax.ShapeDtypeStruct(shape, dtype) for...]
  transfers between devices with their start and end apart: 12 -> 13, of which waited for: 8 -> 9; matrix products, arithmetic and copies ran while one was open for 7% -> 2% of each run, Pallas kernels for 20% -> 28%
where the time goes in v4:
time: 139 us
  Pallas kernels  62.4 us (45%)
  waiting for transfers between devices  35.3 us (25%)
  starting transfers between devices  30.8 us (22%)
  local copies, waits for them, and re-layouts  4.01 us (3%)
  between operations  3.48 us (3%)
  other arithmetic  2.67 us (2%)
    pallas_call x7, Pallas kernels, call(): pl.pallas_call(kernel, out_shape=[jax.ShapeDtypeStruct(shape, dtype) for...  37.9 us
    all_to_all x4, starting transfers between devices, exchange(): return lax.all_to_all(value, AXES, 0, 0, axis_index_groups=groups)  20.5 us
    pallas_call x1, Pallas kernels, back_call(): pl.pallas_call(functools.partial(back_kernel, own, everyone), grid=(group...  19.7 us
    ppermute x2, waiting for transfers between devices, sum_pieces(): far = lax.ppermute(near, 'dp', [(n, (n + dp // 2) % dp) for n in range(dp)])  17.7 us
    all_to_all x4, waiting for transfers between devices, exchange(): return lax.all_to_all(value, AXES, 0, 0, axis_index_groups=groups)  9.7 us
    pallas_call x1, Pallas kernels, own_call(): pl.pallas_call(own_kernel, out_shape=[jax.ShapeDtypeStruct(shape, dtype)...  4.89 us
    ppermute x2, starting transfers between devices, sum_pieces(): far = lax.ppermute(near, 'dp', [(n, (n + dp // 2) % dp) for n in range(dp)])  4.14 us
    ppermute x4, waiting for transfers between devices, swap_cores(): return lax.ppermute(value, 'dp', [(n, n ^ 1) for n in range(dp)])  3.2 us
  transfers between devices with their start and end apart: 13, of which 9 were waited for; matrix products, arithmetic and copies ran while one was open for 2% of the time, Pallas kernels for 28%

profile of v4, /device:TPU:0, one launch (start us, length us, event | category | flops | bytes accessed | tf_op | source)
XLA Modules:
  0.0 138.7 jit_solution(1873126164834144512)
XLA Ops:
  0.6 3.0 %collective-permute-start = (bf16[512,384]{1,0:T(8,128)(2,1)}, bf16[512,384]{1,0:T(8,128)(2,1)S(1)}, u32[]{:S(2)}, u32[]{:S(2)}) collective-permute-start(bf16[512,384]{1,0:T(8,128)(2,1)} %bitcast.22), channel_id=1, source_target_pairs={{0,1},{1,0},{2,3},{3,2},{4,5},{5,4},{6,7},{7,6},{8,9},{9,8},{10,11... | collective-permute-start | bytes 1179656 | tf_op jit(solution)/shard_map/ppermute | solution.py:804
  6.3 0.0 copy-start.2
  6.3 0.0 copy-start.3
  6.3 4.9 %shard_map.307 = (s32[10]{0:T(128)S(1)}, s32[704,1]{1,0:T(8,128)S(1)}, bf16[16,384]{1,0:T(8,128)(2,1)S(1)}, f32[16,384]{1,0:T(8,128)S(1)}, f32[8,384]{1,0:T(8,12...) custom-call(s32[10]{0:T(128)S(1)} %compare_select_fusion.6.start_ref, ...), custom_call_target="tpu_custom_call" | custom-call | flops 3000000000 | bytes 1048576 | tf_op jit(solution)/shard_map/pallas_call | solution.py:620
  11.2 1.8 %collective-permute-done.refs_1_ = bf16[512,384]{1,0:T(8,128)(2,1)S(1)} collective-permute-done((bf16[512,384]{1,0:T(8,128)(2,1)}, bf16[512,384]{1,0:T(8,128)(2,1)S(1)}, u32[]{:S(2)}, u32[]{:S(2)}) %collective-permute-start) | collective-permute-done | bytes 393248 | tf_op jit(solution)/shard_map/ppermute | solution.py:804
  13.0 3.6 %shard_map.308 = (bf16[6,864,128]{2,1,0:T(8,128)(2,1)S(1)}, bf16[6,1024,128]{2,1,0:T(8,128)(2,1)S(1)}, bf16[6,1024,128]{2,1,0:T(8,128)(2,1)S(1)}, bf16[864,384]{...) custom-call(s32[10]{0:T(128)S(1)} %get-tuple-element.89.scalar_ref, ...), custom_call_target="tpu_custom_call" | custom-call | flops 3000000000 | bytes 1048576 | tf_op jit(solution)/shard_map/pallas_call | solution.py:607
  16.7 0.0 copy-start
  16.7 0.0 copy-start.1
  16.7 0.0 copy-start.4
  16.7 0.0 copy-start.5
  16.7 0.0 copy-start.6
  16.7 10.2 %shard_map.309 = (f32[3,864,128]{2,1,0:T(8,128)S(1)}, f32[3,864,128]{2,1,0:T(8,128)S(1)}, bf16[6,864,1024]{2,1,0:T(8,128)(2,1)}, bf16[6,864,128]{2,1,0:T(8,128)(...) custom-call(bf16[6,864,128]{2,1,0:T(8,128)(2,1)S(1)} %get-tuple-element.99.qaug_ref, ...), custom_call_target="tpu_custom_call" | custom-call | flops 10000000000 | bytes 1048576 | tf_op jit(solution)/shard_map/pallas_call | solution.py:607
  26.9 9.1 %shard_map.310 = (f32[864,384]{1,0:T(8,128)S(1)}, bf16[864,1536]{1,0:T(8,128)(2,1)S(1)}, bf16[864,1536]{1,0:T(8,128)(2,1)S(1)}, bf16[1600,384]{1,0:T(8,128)(2,1)S(1)}, bf16[1600,384]{1,0:T(8,128)(2,1)S(1)}) custom-call(s32[10]{0:T(128)S(1)} %get-tuple-element.89.scalar_ref, f32[3,864,128]{2,1,0:T(8,128)S(1)} %get-tuple-element.103.o_ref, ...), custom_call_target="tpu_custom_call" | custom-call | flops 10000000000 | bytes 1048576 | tf_op jit(solution)/shard_map/pallas_call | solution.py:607
  36.0 0.1 collective-permute-start.1
  36.1 6.5 %shard_map.311 = (f32[8,384]{1,0:T(8,128)S(1)}, bf16[512,384]{1,0:T(8,128)(2,1)}, bf16[352,384]{1,0:T(8,128)(2,1)}, f32[864,384]{1,0:T(8,128)}, bf16[864,384]{1,...) custom-call(s32[10]{0:T(128)S(1)} %get-tuple-element.89.scalar_ref, ...), custom_call_target="tpu_custom_call" | custom-call | flops 6000000000 | bytes 1048576 | tf_op jit(solution)/shard_map/pallas_call | solution.py:607
  42.6 1.4 add_convert_fusion
  44.0 5.0 %all-to-all-start = ((bf16[8,200,384]{2,1,0:T(8,128)(2,1)}), bf16[8,200,384]{2,1,0:T(8,128)(2,1)S(1)}, u32[]{:S(2)}, u32[]{:S(2)}) async-start(bf16[8,200,384]{2,1,0:T(8,128)(2,1)} %bitcast.6), calls=%async_computation | async-start | bytes 2457600 | tf_op jit(solution)/shard_map/all_to_all | solution.py:758
  48.9 19.7 %shard_map.312 = (bf16[832,384]{1,0:T(8,128)(2,1)S(1)}, bf16[832,384]{1,0:T(8,128)(2,1)S(1)}, bf16[1,512,384]{2,1,0:T(8,128)(2,1)}, f32[512,384]{1,0:T(8,128)}) custom-call(s32[10]{0:T(128)S(1)} %get-tuple-element.89.scalar_ref, s32[704,1]{1,0:T(8,128)S(1)} %get-tuple-element.96.refs_8_.kept_ref, f32[8,384]{1,0:T(8,128)S(1)} %get-tuple-element.97.refs_9_.mod_ref, ...), custom_call_target="tpu_custom_call" | custom-call | flops 17999998976 | bytes 1048576 | tf_op jit(solution)/shard_map/pallas_call | solution.py:659
  68.6 0.3 collective-permute-start.4
  68.9 1.9 %collective-permute-done.4.right_ref = bf16[832,384]{1,0:T(8,128)(2,1)S(1)} collective-permute-done((bf16[832,384]{1,0:T(8,128)(2,1)S(1)}, bf16[832,384]{1,0:T(8,128)(2,1)S(1)}, u32[]{:S(2)}, u32[]{:S(2)}) %collective-permute-start.4) | collective-permute-done | bytes 639008 | tf_op jit(solution)/shard_map/ppermute | solution.py:749
  70.8 1.0 shard_map.313
  71.8 5.2 %all-to-all-start.2 = ((bf16[8,104,384]{2,1,0:T(8,128)(2,1)}), bf16[8,104,384]{2,1,0:T(8,128)(2,1)S(1)}, u32[]{:S(2)}, u32[]{:S(2)}) async-start(bf16[8,104,384]{2,1,0:T(8,128)(2,1)} %bitcast.10), calls=%async_computation.2 | async-start | bytes 1277952 | tf_op jit(solution)/shard_map/all_to_all | solution.py:758
  77.0 0.2 reduce_sum.24
  77.2 2.7 %collective-permute-start.2 = (bf16[200,384]{1,0:T(8,128)(2,1)S(1)}, bf16[200,384]{1,0:T(8,128)(2,1)S(1)}, u32[]{:S(2)}, u32[]{:S(2)}) collective-permute-start(bf16[200,384]{1,0:T(8,128)(2,1)S(1)} %reduce_sum.24), channel_id=1, source_target_pairs={{0,16},{2,18},{4,20},{6,22},{8,24},{10,26},{12,28},{14,30},{16,0},... | collective-permute-start | bytes 460808 | tf_op jit(solution)/shard_map/ppermute | solution.py:763
  79.8 0.7 slice_bitcast_fusion
  80.6 2.0 %collective-permute-start.3 = (bf16[256,384]{1,0:T(8,128)(2,1)S(1)}, bf16[256,384]{1,0:T(8,128)(2,1)S(1)}, u32[]{:S(2)}, u32[]{:S(2)}) collective-permute-start(bf16[256,384]{1,0:T(8,128)(2,1)S(1)} %get-tuple-element.164), channel_id=1, source_target_pairs={{0,1},{1,0},{2,3},{3,2},{4,5},{5,4},{6,7},{7,6},{8,9},{9,8},{10,11... | collective-permute-start | bytes 589832 | tf_op jit(solution)/shard_map/ppermute | solution.py:774
  82.6 5.1 %collective-permute-done.2 = bf16[200,384]{1,0:T(8,128)(2,1)S(1)} collective-permute-done((bf16[200,384]{1,0:T(8,128)(2,1)S(1)}, bf16[200,384]{1,0:T(8,128)(2,1)S(1)}, u32[]{:S(2)}, u32[]{:S(2)}) %collective-permute-start.2) | collective-permute-done | bytes 153632 | tf_op jit(solution)/shard_map/ppermute | solution.py:763
  87.7 2.8 %collective-permute-done.3 = bf16[256,384]{1,0:T(8,128)(2,1)S(1)} collective-permute-done((bf16[256,384]{1,0:T(8,128)(2,1)S(1)}, bf16[256,384]{1,0:T(8,128)(2,1)S(1)}, u32[]{:S(2)}, u32[]{:S(2)}) %collective-permute-start.3) | collective-permute-done | bytes 196640 | tf_op jit(solution)/shard_map/ppermute | solution.py:774
  90.5 0.3 all-to-all-done.2
  90.8 1.1 broadcast_in_dim.29
  91.9 4.8 %all-to-all-start.1 = ((bf16[8,200,384]{2,1,0:T(8,128)(2,1)}), bf16[8,200,384]{2,1,0:T(8,128)(2,1)S(1)}, u32[]{:S(2)}, u32[]{:S(2)}) async-start(bf16[8,200,384]{2,1,0:T(8,128)(2,1)} %broadcast_in_dim.29), calls=%async_computation.1 | async-start | bytes 2457600 | tf_op jit(solution)/shard_map/all_to_all | solution.py:758
  96.7 0.1 reduce_sum.25
  96.8 1.5 %collective-permute-start.5 = (bf16[104,384]{1,0:T(8,128)(2,1)S(1)}, bf16[104,384]{1,0:T(8,128)(2,1)S(1)}, u32[]{:S(2)}, u32[]{:S(2)}) collective-permute-start(bf16[104,384]{1,0:T(8,128)(2,1)S(1)} %reduce_sum.25), channel_id=1, source_target_pairs={{0,16},{2,18},{4,20},{6,22},{8,24},{10,26},{12,28},{14,30},{16,0},... | collective-permute-start | bytes 239624 | tf_op jit(solution)/shard_map/ppermute | solution.py:763
  98.2 12.7 %collective-permute-done.5 = bf16[104,384]{1,0:T(8,128)(2,1)S(1)} collective-permute-done((bf16[104,384]{1,0:T(8,128)(2,1)S(1)}, bf16[104,384]{1,0:T(8,128)(2,1)S(1)}, u32[]{:S(2)}, u32[]{:S(2)}) %collective-permute-start.5) | collective-permute-done | bytes 79904 | tf_op jit(solution)/shard_map/ppermute | solution.py:763
  110.9 2.2 %all-to-all-done.1 = bf16[8,200,384]{2,1,0:T(8,128)(2,1)S(1)} async-done(((bf16[8,200,384]{2,1,0:T(8,128)(2,1)}), bf16[8,200,384]{2,1,0:T(8,128)(2,1)S(1)}, u32[]{:S(2)}, u32[]{:S(2)}) %all-to-all-start.1) | async-done | bytes 1228832 | tf_op jit(solution)/shard_map/all_to_all | solution.py:758
  113.1 0.9 broadcast_in_dim.30
  114.0 5.6 %all-to-all-start.3 = ((bf16[8,104,384]{2,1,0:T(8,128)(2,1)}), bf16[8,104,384]{2,1,0:T(8,128)(2,1)S(1)}, u32[]{:S(2)}, u32[]{:S(2)}) async-start(bf16[8,104,384]{2,1,0:T(8,128)(2,1)} %broadcast_in_dim.30), calls=%async_computation.3 | async-start | bytes 1277952 | tf_op jit(solution)/shard_map/all_to_all | solution.py:758
  119.6 0.0 collective-permute-done.6.other_ref
  119.6 0.0 copy-start.9
  119.6 2.3 %shard_map.314 = (bf16[112,384]{1,0:T(8,128)(2,1)S(1)}, f32[8,384]{1,0:T(8,128)S(1)}, f32[384,1536]{1,0:T(8,128)}, f32[1536,384]{1,0:T(8,128)}) custom-call(s32[1]{0:T(128)} %bitcast.8.side_ref, bf16[1600,384]{1,0:T(8,128)(2,1)S(1)} %bitcast.19, bf16[1600,384]{1,0:T(8,128)(2,1)S(1)} %collective-permute-done.6.other_ref), custom_call_target="tpu_custom_call" | custom-call | flops 3000000000 | bytes 1048576 | tf_op jit(solution)/shard_map/pallas_call | solution.py:607
  122.0 0.6 reshape.55
  122.6 0.6 slice_reduce_fusion
  123.2 7.2 %all-to-all-done.3 = bf16[8,104,384]{2,1,0:T(8,128)(2,1)S(1)} async-done(((bf16[8,104,384]{2,1,0:T(8,128)(2,1)}), bf16[8,104,384]{2,1,0:T(8,128)(2,1)S(1)}, u32[]{:S(2)}, u32[]{:S(2)}) %all-to-all-start.3) | async-done | bytes 639008 | tf_op jit(solution)/shard_map/all_to_all | solution.py:758
  130.4 0.7 collective-permute-start.8
  131.1 1.3 collective-permute-done.7.other_ref
  132.5 5.2 %shard_map.315 = (f32[2,384]{1,0:T(2,128)}, f32[6,2,63]{2,1,0:T(2,128)}, f32[384]{0:T(512)}, f32[2304]{0:T(1024)}, f32[384,1152]{1,0:T(8,128)}, /*index=5*/f32[3...) custom-call(s32[1]{0:T(128)} %bitcast.8.side_ref, bf16[832,384]{1,0:T(8,128)(2,1)S(1)} %bitcast.21, ...), custom_call_target="tpu_custom_call" | custom-call | flops 4000000000 | bytes 1048576 | tf_op jit(solution)/shard_map/pallas_call | solution.py:607
  137.7 0.0 collective-permute-done.8
  137.7 0.9 add_bitcast_fusion
  (24 shorter events, 0.1 us)
Async XLA Ops:
  0.6 12.4 %collective-permute-start = (bf16[512,384]{1,0:T(8,128)(2,1)}, bf16[512,384]{1,0:T(8,128)(2,1)S(1)}, u32[]{:S(2)}, u32[]{:S(2)}) collective-permute-start(bf16[512,384]{1,0:T(8,128)(2,1)} %bitcast.22), channel_id=1, source_target_pairs={{0,1},{1,0},{2,3},{3,2},{4,5},{5,4},{6,7},{7,6},{8,9},{9,8},{10,11... | collective-permute-start | bytes 1179656 | tf_op jit(solution)/shard_map/ppermute | solution.py:804
  6.3 6.7 %copy-start.2 = (bf16[384,1152]{1,0:T(8,128)(2,1)S(1)}, bf16[384,1152]{1,0:T(8,128)(2,1)}, u32[]{:S(2)}) copy-start(bf16[384,1152]{1,0:T(8,128)(2,1)} %refs_9_.1) | copy-start | bytes 2654212
  6.3 6.7 %copy-start.3 = (bf16[1,512,384]{2,1,0:T(8,128)(2,1)S(1)}, bf16[1,512,384]{2,1,0:T(8,128)(2,1)}, u32[]{:S(2)}) copy-start(bf16[1,512,384]{2,1,0:T(8,128)(2,1)} %param.20) | copy-start | bytes 1179652
  16.7 10.2 %copy-start = (bf16[384,1536]{1,0:T(8,128)(2,1)S(1)}, bf16[384,1536]{1,0:T(8,128)(2,1)}, u32[]{:S(2)}) copy-start(bf16[384,1536]{1,0:T(8,128)(2,1)} %w1_ref.3) | copy-start | bytes 3538948
  16.7 10.2 %copy-start.1 = (bf16[1536,384]{1,0:T(8,128)(2,1)S(1)}, bf16[1536,384]{1,0:T(8,128)(2,1)}, u32[]{:S(2)}) copy-start(bf16[1536,384]{1,0:T(8,128)(2,1)} %w2_ref.3) | copy-start | bytes 3538948
  16.7 10.2 %copy-start.4 = (bf16[1,512,384]{2,1,0:T(8,128)(2,1)S(1)}, bf16[1,512,384]{2,1,0:T(8,128)(2,1)}, u32[]{:S(2)}) copy-start(bf16[1,512,384]{2,1,0:T(8,128)(2,1)} %param.38) | copy-start | bytes 1179652
  16.7 10.2 %copy-start.5 = (bf16[384,384]{1,0:T(8,128)(2,1)S(1)}, bf16[384,384]{1,0:T(8,128)(2,1)}, u32[]{:S(2)}) copy-start(bf16[384,384]{1,0:T(8,128)(2,1)} %wout_ref.3) | copy-start | bytes 884740
  16.7 10.2 %copy-start.6 = (bf16[1,352,384]{2,1,0:T(8,128)(2,1)S(1)}, bf16[1,352,384]{2,1,0:T(8,128)(2,1)}, u32[]{:S(2)}) copy-start(bf16[1,352,384]{2,1,0:T(8,128)(2,1)} %param.39) | copy-start | bytes 811012
  36.0 6.5 %collective-permute-start.1 = (bf16[1600,384]{1,0:T(8,128)(2,1)S(1)}, bf16[1600,384]{1,0:T(8,128)(2,1)S(1)}, u32[]{:S(2)}, u32[]{:S(2)}) collective-permute-start(bf16[1600,384]{1,0:T(8,128)(2,1)S(1)} %get-tuple-element.107), channel_id=1, source_target_pairs={{0,2},{2,0},{4,6},{6,4},{8,10},{10,8},{12,14},{14,12},{16,18},{18,... | collective-permute-start | bytes 3686408 | tf_op jit(solution)/shard_map/ppermute | solution.py:749
  44.0 24.7 %all-to-all-start = ((bf16[8,200,384]{2,1,0:T(8,128)(2,1)}), bf16[8,200,384]{2,1,0:T(8,128)(2,1)S(1)}, u32[]{:S(2)}, u32[]{:S(2)}) async-start(bf16[8,200,384]{2,1,0:T(8,128)(2,1)} %bitcast.6), calls=%async_computation | async-start | bytes 2457600 | tf_op jit(solution)/shard_map/all_to_all | solution.py:758
  68.6 2.1 %collective-permute-start.4 = (bf16[832,384]{1,0:T(8,128)(2,1)S(1)}, bf16[832,384]{1,0:T(8,128)(2,1)S(1)}, u32[]{:S(2)}, u32[]{:S(2)}) collective-permute-start(bf16[832,384]{1,0:T(8,128)(2,1)S(1)} %get-tuple-element.142), channel_id=1, source_target_pairs={{0,2},{2,0},{4,6},{6,4},{8,10},{10,8},{12,14},{14,12},{16,18},{18,... | collective-permute-start | bytes 1916936 | tf_op jit(solution)/shard_map/ppermute | solution.py:749
  71.8 8.1 %copy-start.8 = (bf16[1,512,384]{2,1,0:T(8,128)(2,1)S(1)}, bf16[1,512,384]{2,1,0:T(8,128)(2,1)}, u32[]{:S(2)}) copy-start(bf16[1,512,384]{2,1,0:T(8,128)(2,1)} %get-tuple-element.138) | copy-start | bytes 1179652
  71.8 19.0 %all-to-all-start.2 = ((bf16[8,104,384]{2,1,0:T(8,128)(2,1)}), bf16[8,104,384]{2,1,0:T(8,128)(2,1)S(1)}, u32[]{:S(2)}, u32[]{:S(2)}) async-start(bf16[8,104,384]{2,1,0:T(8,128)(2,1)} %bitcast.10), calls=%async_computation.2 | async-start | bytes 1277952 | tf_op jit(solution)/shard_map/all_to_all | solution.py:758
  77.2 10.5 %collective-permute-start.2 = (bf16[200,384]{1,0:T(8,128)(2,1)S(1)}, bf16[200,384]{1,0:T(8,128)(2,1)S(1)}, u32[]{:S(2)}, u32[]{:S(2)}) collective-permute-start(bf16[200,384]{1,0:T(8,128)(2,1)S(1)} %reduce_sum.24), channel_id=1, source_target_pairs={{0,16},{2,18},{4,20},{6,22},{8,24},{10,26},{12,28},{14,30},{16,0},... | collective-permute-start | bytes 460808 | tf_op jit(solution)/shard_map/ppermute | solution.py:763
  80.6 9.9 %collective-permute-start.3 = (bf16[256,384]{1,0:T(8,128)(2,1)S(1)}, bf16[256,384]{1,0:T(8,128)(2,1)S(1)}, u32[]{:S(2)}, u32[]{:S(2)}) collective-permute-start(bf16[256,384]{1,0:T(8,128)(2,1)S(1)} %get-tuple-element.164), channel_id=1, source_target_pairs={{0,1},{1,0},{2,3},{3,2},{4,5},{5,4},{6,7},{7,6},{8,9},{9,8},{10,11... | collective-permute-start | bytes 589832 | tf_op jit(solution)/shard_map/ppermute | solution.py:774
  90.5 1.4 %copy-start.10 = (bf16[256,384]{1,0:T(8,128)(2,1)}, bf16[256,384]{1,0:T(8,128)(2,1)S(1)}, u32[]{:S(2)}) copy-start(bf16[256,384]{1,0:T(8,128)(2,1)S(1)} %collective-permute-done.3) | copy-start | bytes 589828
  91.9 21.2 %all-to-all-start.1 = ((bf16[8,200,384]{2,1,0:T(8,128)(2,1)}), bf16[8,200,384]{2,1,0:T(8,128)(2,1)S(1)}, u32[]{:S(2)}, u32[]{:S(2)}) async-start(bf16[8,200,384]{2,1,0:T(8,128)(2,1)} %broadcast_in_dim.29), calls=%async_computation.1 | async-start | bytes 2457600 | tf_op jit(solution)/shard_map/all_to_all | solution.py:758
  96.8 14.1 %collective-permute-start.5 = (bf16[104,384]{1,0:T(8,128)(2,1)S(1)}, bf16[104,384]{1,0:T(8,128)(2,1)S(1)}, u32[]{:S(2)}, u32[]{:S(2)}) collective-permute-start(bf16[104,384]{1,0:T(8,128)(2,1)S(1)} %reduce_sum.25), channel_id=1, source_target_pairs={{0,16},{2,18},{4,20},{6,22},{8,24},{10,26},{12,28},{14,30},{16,0},... | collective-permute-start | bytes 239624 | tf_op jit(solution)/shard_map/ppermute | solution.py:763
  113.1 6.5 %collective-permute-start.6 = (bf16[1600,384]{1,0:T(8,128)(2,1)S(1)}, bf16[1600,384]{1,0:T(8,128)(2,1)S(1)}, u32[]{:S(2)}, u32[]{:S(2)}) collective-permute-start(bf16[1600,384]{1,0:T(8,128)(2,1)S(1)} %bitcast.18), channel_id=1, source_target_pairs={{0,2},{2,0},{4,6},{6,4},{8,10},{10,8},{12,14},{14,12},{16,18},{18,... | collective-permute-start | bytes 3686408 | tf_op jit(solution)/shard_map/ppermute | solution.py:749
  114.0 16.3 %all-to-all-start.3 = ((bf16[8,104,384]{2,1,0:T(8,128)(2,1)}), bf16[8,104,384]{2,1,0:T(8,128)(2,1)S(1)}, u32[]{:S(2)}, u32[]{:S(2)}) async-start(bf16[8,104,384]{2,1,0:T(8,128)(2,1)} %broadcast_in_dim.30), calls=%async_computation.3 | async-start | bytes 1277952 | tf_op jit(solution)/shard_map/all_to_all | solution.py:758
  119.6 10.8 %copy-start.9 = (bf16[256,384]{1,0:T(8,128)(2,1)S(1)}, bf16[256,384]{1,0:T(8,128)(2,1)}, u32[]{:S(2)}) copy-start(bf16[256,384]{1,0:T(8,128)(2,1)} %get-tuple-element.163) | copy-start | bytes 589828
  130.4 2.1 %collective-permute-start.7 = (bf16[832,384]{1,0:T(8,128)(2,1)S(1)}, bf16[832,384]{1,0:T(8,128)(2,1)S(1)}, u32[]{:S(2)}, u32[]{:S(2)}) collective-permute-start(bf16[832,384]{1,0:T(8,128)(2,1)S(1)} %bitcast.20), channel_id=1, source_target_pairs={{0,2},{2,0},{4,6},{6,4},{8,10},{10,8},{12,14},{14,12},{16,18},{18,... | collective-permute-start | bytes 1916936 | tf_op jit(solution)/shard_map/ppermute | solution.py:749
  130.4 7.3 %copy-start.7 = (f32[512,384]{1,0:T(8,128)S(1)}, f32[512,384]{1,0:T(8,128)}, u32[]{:S(2)}) copy-start(f32[512,384]{1,0:T(8,128)} %get-tuple-element.133) | copy-start | bytes 2359300
  130.4 7.3 %copy-start.11 = (bf16[256,384]{1,0:T(8,128)(2,1)S(1)}, bf16[256,384]{1,0:T(8,128)(2,1)}, u32[]{:S(2)}) copy-start(bf16[256,384]{1,0:T(8,128)(2,1)} %copy-done.10) | copy-start | bytes 589828
  130.4 7.3 %collective-permute-start.8 = (bf16[256,384]{1,0:T(8,128)(2,1)S(1)}, bf16[256,384]{1,0:T(8,128)(2,1)S(1)}, u32[]{:S(2)}, u32[]{:S(2)}) collective-permute-start(bf16[256,384]{1,0:T(8,128)(2,1)S(1)} %copy-done.9), channel_id=1, source_target_pairs={{0,1},{1,0},{2,3},{3,2},{4,5},{5,4},{6,7},{7,6},{8,9},{9,8},{10,11... | collective-permute-start | bytes 589832 | tf_op jit(solution)/shard_map/ppermute | solution.py:774

commit v5 on v4

--- a/solution.py
+++ b/solution.py
@@ -87,6 +87,14 @@
     def wait(self):
         for copy in self.made:
             copy.wait()
+
+
+def half_copies(side, payload_ref, keep_ref, send_ref, sems, which):
+    for target, chosen in ((keep_ref, side == which), (send_ref, side != which)):
+
+        @pl.when(chosen)
+        def start():
+            pltpu.make_async_copy(payload_ref.at[which], target, sems.at[which]).start()
 
 
 def split_halves(copies, side, payload_ref, keep_ref, send_ref):
@@ -158,6 +166,7 @@
 
 
 QV_LINE, OUT_LINE, FC1_LINE, FC2_LINE = 6, 8, 9, 13
+COND_LINE = 6
 
 
 def time_features(moment):
@@ -172,9 +181,9 @@
     start_ref, count_ref, valid_ref, moment_ref, label_ref,
     *refs,
 ):
-    sources, outs, local, sems = refs[:11], refs[11:23], refs[23:34], refs[34]
-    scalar_ref, kept_ref, fact_ref, line_ref, mod_ref, a_ref, qs_ref, qaug_ref, kaug_ref, vaug_ref = outs[:10]
-    offset_ref, mask_ref = outs[10:]
+    sources, outs, local, sems = refs[:11], refs[11:22], refs[22:33], refs[33]
+    scalar_ref, kept_ref, line_ref, mod_ref, a_ref, qs_ref, qaug_ref, kaug_ref, vaug_ref = outs[:9]
+    offset_ref, mask_ref = outs[9:]
     kept_in, rel_ref, ada_bias_ref, qv_bias_ref, out_bias_ref, fc1_bias_ref, fc2_bias_ref = local[:7]
     table_ref, ada_ref, tok_ref, weight_ref = local[7:]
     fetched = [pltpu.make_async_copy(*pair, sems.at[n]) for n, pair in enumerate(zip(sources, local))]
@@ -217,12 +226,10 @@
     conditioned = mm(hot.astype(F32).astype(BF16), table_ref[...]) + time_features(moment_ref[0])
     gate = 1.0 / (1.0 + jnp.exp(-conditioned))
     activated = (conditioned * gate).astype(BF16)
-    line = lax.broadcasted_iota(jnp.int32, (16, D), 0)
-    slope = gate * (1.0 + conditioned * (1.0 - gate))
-    fact_ref[...] = jnp.where(line == 0, activated.astype(F32), jnp.where(line == 1, slope, 0.0)).astype(BF16)
     for n in range(6):
         mod_ref[n : n + 1, :] = mm(activated, ada_ref[:, n * D : (n + 1) * D])[:1] + line_ref[n : n + 1, :]
-    mod_ref[6:8, :] = jnp.zeros((2, D), F32)
+    mod_ref[COND_LINE : COND_LINE + 1, :] = conditioned[:1]
+    mod_ref[COND_LINE + 1 :, :] = jnp.zeros((1, D), F32)
     lowered, scaled, keys, values = project(tok_ref[...], mod_ref, weight_ref, line_ref)
     a_ref[...] = lowered
     qs_ref[...] = scaled
@@ -289,9 +296,16 @@
     copies.start(vaug_ref, vaug_out)
     spans = [(at, size, False) for at, size in blocks_of(0, own, 256)]
     spans += [(at, size, True) for at, size in blocks_of(own, rows - own, 256)]
+    items = [(side, *span) for side in range(2) for span in spans]
+
+    def e_copy(head, n):
+        side, at, size, masked = items[n]
+        span = pl.ds(at, size)
+        return pltpu.make_async_copy(
+            e_ref.at[head, span], e_out.at[head, span], sems.at[3 + len(spans) * head + n % len(spans)]
+        )
 
     def pair(group, carry):
-        items = [(side, *span) for side in range(2) for span in spans]
         scores, spread = {}, {}
         for n in range(len(items) + 2):
             if n < len(items):
@@ -305,6 +319,7 @@
                 found = scores.pop(n - 1)
                 spread[n - 1] = jnp.exp(found - jnp.max(found, axis=-1, keepdims=True)).astype(BF16)
                 e_ref[2 * group + side, at : at + size, :] = spread[n - 1]
+                e_copy(2 * group + side, n - 1).start()
             if 0 <= n - 2:
                 side, at, size, masked = items[n - 2]
                 mixed = mm(spread.pop(n - 2), vaug_ref[2 * group + side])
@@ -312,13 +327,12 @@
                 lanes = slice(side * HDIM, (side + 1) * HDIM)
                 o_ref[group, at : at + size, lanes] = mixed[:, :HDIM] * inverse
                 inverse_ref[group, at : at + size, lanes] = jnp.broadcast_to(inverse, (size, HDIM))
-        pltpu.make_async_copy(e_ref.at[pl.ds(2 * group, 2)], e_out.at[pl.ds(2 * group, 2)], sems.at[3 + group]).start()
         return carry
 
     lax.fori_loop(0, HEADS // 2, pair, 0)
-    for group in range(HEADS // 2):
-        heads = pl.ds(2 * group, 2)
-        pltpu.make_async_copy(e_ref.at[heads], e_out.at[heads], sems.at[3 + group]).wait()
+    for head in range(HEADS):
+        for n in range(len(spans)):
+            e_copy(head, head % 2 * len(spans) + n).wait()
     copies.wait()
 
 
@@ -329,8 +343,8 @@
 
 
 def feed_kernel(
-    slots, everyone, scalar_ref, o_ref, x_ref, cot_full_ref, cot_slot_ref, mod_ref, wout_ref, w1_ref,
-    w2_ref, line_ref, fact_ref,
+    slots, scalar_ref, o_ref, x_ref, cot_full_ref, cot_slot_ref, mod_ref, wout_ref, w1_ref,
+    w2_ref, line_ref,
     att_ref, hidden_ref, du_ref, keep_ref, send_ref, pay_ref, sems,
 ):
     rows = x_ref.shape[0]
@@ -362,29 +376,23 @@
         hidden_ref[:, cols] = (u * cdf).astype(BF16)
         slope = cdf * ((1.0 - t) * (u * (square * (3.0 * GELU_A * GELU_B) + GELU_A)) + 1.0)
         du_ref[:, cols] = (slope * back_u).astype(BF16)
+    spare = pay_ref.shape[1] - FF
+    pay_ref[0, FF:, :] = jnp.zeros((spare, D), BF16)
+    pay_ref[1, FF:, :] = jnp.zeros((spare, D), BF16)
     ones = jnp.ones((16, rows), BF16)
     grad = mm(jnp.concatenate([second.T, ones], axis=0), du_ref[...])
     heads = []
     for n in range(4):
         cols = slice(n * D, (n + 1) * D)
-        pay_ref[cols, :] = grad[:D, cols].astype(BF16)
+        pay_ref[0, cols, :] = grad[:D, cols].astype(BF16)
         heads.append(grad[D : D + 1, cols])
-    pay_ref[FF : 2 * FF, :] = mm(hidden_ref[...].T, dz).astype(BF16)
     heads += [jnp.sum(dz.astype(F32), axis=0, keepdims=True), jnp.zeros((11, D), F32)]
-    pay_ref[2 * FF : 2 * FF + 16, :] = jnp.concatenate(heads, axis=0).astype(BF16)
-    lane = lax.broadcasted_iota(jnp.int32, (16, D), 1)
-    line = lax.broadcasted_iota(jnp.int32, (16, D), 0)
-    label = scalar_ref[LABEL]
-    digits = jnp.where(lane == 0, label // GRID, jnp.where(lane == 1, label % GRID, 0)).astype(F32)
-    facts = jnp.where(line == 2, digits, fact_ref[...].astype(F32)).astype(BF16)
-    extra = pay_ref.shape[0] - 2 * FF - 16
-    row = lax.broadcasted_iota(jnp.int32, (extra, 16), 0)
-    mine = (row % everyone == scalar_ref[PLACE]) & (row < 3 * everyone) & (scalar_ref[SEQ_PLACE] == 0)
-    hot = lax.broadcasted_iota(jnp.int32, (extra, 16), 1) == jnp.where(mine, row // everyone, -1)
-    pay_ref[2 * FF + 16 :, :] = mm(hot.astype(F32).astype(BF16), facts).astype(BF16)
-    copies = Copies(sems)
-    split_halves(copies, scalar_ref[SIDE], pay_ref, keep_ref, send_ref)
-    copies.wait()
+    pay_ref[0, FF : FF + 16, :] = jnp.concatenate(heads, axis=0).astype(BF16)
+    pay_ref[1, :FF, :] = mm(hidden_ref[...].T, dz).astype(BF16)
+    for which in range(2):
+        half_copies(scalar_ref[SIDE], pay_ref, keep_ref, send_ref, sems, which)
+    for which in range(2):
+        pltpu.make_async_copy(pay_ref.at[which], keep_ref, sems.at[which]).wait()
 
 
 def feed_rest_kernel(
@@ -569,18 +577,25 @@
         for n in range(others):
             dx_ref[n] = dxs_ref[row_span(scalar_ref, STARTS + 1 + others + n, own), :].astype(BF16)
         rel = table_sums([tab_ref[n] for n in range(groups)])
+        first = jnp.where(scalar_ref[SEQ_PLACE] == 0, 1, 0)
+        label = scalar_ref[LABEL]
+        number = lax.broadcasted_iota(jnp.int32, (1, D), 1)
+        digits = jnp.where(number == scalar_ref[PLACE], label // GRID * first, 0)
+        digits = jnp.where(number == 128 + scalar_ref[PLACE], label % GRID * first, digits).astype(F32)
         smalls = jnp.concatenate(
             [
                 shift_sum, scale_sum, prior_ref[0:4, :], column(dq_own) + column(dq_slot), column(dv),
-                *rel, prior_ref[4:5, :], jnp.zeros((5, D), F32),
+                *rel, prior_ref[4:5, :], digits, mod_ref[COND_LINE : COND_LINE + 1, :], jnp.zeros((3, D), F32),
             ],
             axis=0,
         ).astype(BF16)
         tail = pay_ref.shape[0] - 4 * D
         row = lax.broadcasted_iota(jnp.int32, (tail, 16), 0)
         lane = lax.broadcasted_iota(jnp.int32, (tail, 16), 1)
-        wanted = jnp.where(row % everyone == scalar_ref[PLACE], row // everyone, -1)
-        wanted = jnp.where(row < 6 * everyone, wanted, row - 6 * everyone + 6)
+        kind = jnp.where(row < 6 * everyone, row // everyone, jnp.where(scalar_ref[SEQ_PLACE] == 0, 12, -1))
+        wanted = jnp.where(row % everyone == scalar_ref[PLACE], kind, -1)
+        after = row - 7 * everyone
+        wanted = jnp.where(after < 0, wanted, jnp.where(after < 6, after + 6, -1))
         pay_ref[4 * D :, :] = mm((lane == wanted).astype(F32).astype(BF16), smalls).astype(BF16)
         halves = Copies(pay_sems)
         split_halves(halves, scalar_ref[SIDE], pay_ref, keep_ref, send_ref)
@@ -633,12 +648,38 @@
     return pltpu.with_memory_space_constraint(value, pltpu.HBM)
 
 
-def add_kernel(left_ref, right_ref, sum_ref):
-    sum_ref[...] = (left_ref[...].astype(F32) + right_ref[...].astype(F32)).astype(BF16)
+def add_kernel(pieces, left_ref, right_ref, sum_out, sum_ref, sems):
+    copies = Copies(sems)
+    rows = sum_ref.shape[0] // pieces
+    for n in range(pieces):
+        span = pl.ds(n * rows, rows)
+        sum_ref[span, :] = (left_ref[span, :].astype(F32) + right_ref[span, :].astype(F32)).astype(BF16)
+        copies.start(sum_ref.at[span], sum_out.at[span])
+    copies.wait()
 
 
 def add_call(left, right, micros):
-    return call(add_kernel, [(left.shape, BF16)], [], [left, right], micros=micros)[0]
+    pieces = 4 if left.shape[0] % 64 == 0 else 1
+    out = (left.shape, BF16)
+    return call(
+        functools.partial(add_kernel, pieces), [out], [out], [left, right], away=1, copies=pieces, micros=micros,
+        limit=8,
+    )[0]
+
+
+def spread_kernel(near_ref, far_ref, wide_out, sum_ref, sems):
+    sum_ref[...] = (near_ref[...].astype(F32) + far_ref[...].astype(F32)).astype(BF16)
+    copies = Copies(sems)
+    for n in range(wide_out.shape[0]):
+        copies.start(sum_ref, wide_out.at[n])
+    copies.wait()
+
+
+def spread_call(near, far, peers):
+    return call(
+        spread_kernel, [((peers,) + near.shape, BF16)], [(near.shape, BF16)], [near, far], away=1, copies=peers,
+        limit=8,
+    )[0]
 
 
 def back_call(own, everyone, groups_of, sources, scalars, kept, mod, prior, tail_half):
@@ -687,22 +728,25 @@
     return get
 
 
-def layer_kernel(side_ref, mine_ref, other_ref, info_ref, small_ref, g1_out, g2_out, g1_ref, g2_ref, sems):
+def layer_kernel(side_ref, mine_ref, other_ref, bias1_ref, bias2_ref, g1_out, g2_out, g1_ref, g2_ref, sems):
     get = halves_reader(side_ref, mine_ref, other_ref)
     copies = Copies(sems)
+    half = mine_ref.shape[0]
     for n in range(4):
         cols = pl.ds(n * D, D)
         g1_ref[:, cols] = get(n * D, D).astype(F32)
         copies.start(g1_ref.at[:, cols], g1_out.at[:, cols])
-        g2_ref[cols, :] = get(FF + n * D, D).astype(F32)
+        g2_ref[cols, :] = get(half + n * D, D).astype(F32)
         copies.start(g2_ref.at[cols], g2_out.at[cols])
-    small_ref[...] = get(2 * FF, 16).astype(F32)[:8]
-    info_ref[...] = get(2 * FF + 16, info_ref.shape[0])
+    small = get(FF, 16).astype(F32)
+    for n in range(4):
+        bias1_ref[pl.ds(n * D, D)] = small[n]
+    bias2_ref[...] = small[4]
     copies.wait()
 
 
 def last_kernel(
-    everyone, side_ref, mine_ref, other_ref, info_ref, ada_in, qv_ref, rel_ref, out_bias_ref, ada_bias_ref,
+    everyone, side_ref, mine_ref, other_ref, ada_in, qv_ref, rel_ref, out_bias_ref, ada_bias_ref,
     gqkv_out, gada_out, table_out, go_out, gqkv_ref, gada_ref, table_ref, go_ref, ada_ref, sems,
 ):
     get = halves_reader(side_ref, mine_ref, other_ref)
@@ -714,7 +758,9 @@
         copies.start(gqkv_ref.at[:, cols], gqkv_out.at[:, cols])
     go_ref[...] = get(3 * D, D).astype(F32)
     copies.start(go_ref, go_out)
-    act_t = info_ref[:everyone, :].T
+    cond = get(4 * D + 6 * everyone, everyone).astype(F32)
+    gate = 1.0 / (1.0 + jnp.exp(-cond))
+    act_t = (cond * gate).astype(BF16).T
     dmods = [get(4 * D + n * everyone, everyone) for n in range(6)]
     for n in range(6):
         cols = pl.ds(n * D, D)
@@ -725,17 +771,16 @@
     back = jnp.zeros((everyone, D), F32)
     for n in range(6):
         back = back + mm_t(dmods[n], ada_ref[:, n * D : (n + 1) * D])
-    cond = info_ref[everyone : 2 * everyone, :].astype(F32) * back
-    high = cond.astype(BF16)
-    low = (cond - high.astype(F32)).astype(BF16)
-    digits = info_ref[2 * everyone : 3 * everyone, :].astype(F32)
-    label = (digits[:, 0:1] * GRID + digits[:, 1:2]).astype(jnp.int32)
+    back = gate * (1.0 + cond * (1.0 - gate)) * back
+    high = back.astype(BF16)
+    low = (back - high.astype(F32)).astype(BF16)
+    small = get(4 * D + 7 * everyone, 16).astype(F32)
+    label = (small[5:6, :everyone] * GRID + small[5:6, 128 : 128 + everyone]).astype(jnp.int32)
     classes = table_ref.shape[0]
     wide = round_up(classes, 128)
-    hot = (label == lax.broadcasted_iota(jnp.int32, (everyone, wide), 1)).astype(F32).astype(BF16).T
+    hot = (label == lax.broadcasted_iota(jnp.int32, (wide, everyone), 0)).astype(F32).astype(BF16)
     table_ref[...] = (mm(hot, high) + mm(hot, low))[:classes]
     copies.start(table_ref, table_out)
-    small = get(4 * D + 6 * everyone, 16).astype(F32)
     qv_ref[...] = small[:2]
     for part in range(2):
         for head in range(HEADS):
@@ -758,15 +803,62 @@
     return lax.all_to_all(value, AXES, 0, 0, axis_index_groups=groups)
 
 
-def sum_pieces(pieces, dp):
-    near = jnp.sum(pieces.astype(F32), axis=0).astype(BF16)
-    far = lax.ppermute(near, "dp", [(n, (n + dp // 2) % dp) for n in range(dp)])
-    return (near.astype(F32) + far.astype(F32)).astype(BF16)
-
-
-def spread_out(chunk, dp, seq):
-    peers = dp // 4 * seq
-    return exchange(jnp.broadcast_to(chunk[None], (peers,) + chunk.shape), dp, seq).reshape(-1, D)
+def near_sum(pieces):
+    return jnp.sum(pieces.astype(F32), axis=0).astype(BF16)
+
+
+def far_half(near, dp):
+    return lax.ppermute(near, "dp", [(n, (n + dp // 2) % dp) for n in range(dp)])
+
+
+def assemble_kernel(cut, place_ref, pair_ref, a1_ref, b1_ref, a2_ref, b2_ref, half_ref):
+    rows = pair_ref.shape[1]
+    for near in range(2):
+        for x in range(2):
+            for y in range(2):
+                at = (place_ref[0] ^ (4 * near + 2 * x + y)) * rows
+                if x:
+                    half_ref[pl.ds(pl.multiple_of(at, 16), cut), :] = a2_ref[y, near]
+                elif y:
+                    half_ref[pl.ds(pl.multiple_of(at, 16), cut), :] = a1_ref[near]
+                else:
+                    half_ref[pl.ds(pl.multiple_of(at, 16), cut), :] = pair_ref[near, :cut, :]
+                rest = pl.ds(pl.multiple_of(at + cut, 16), rows - cut)
+                if y:
+                    half_ref[rest, :] = b2_ref[x, near]
+                elif x:
+                    half_ref[rest, :] = b1_ref[near]
+                else:
+                    half_ref[rest, :] = pair_ref[near, cut:, :]
+
+
+def after(value, *others):
+    return lax.optimization_barrier((value, *others))[0]
+
+
+def gather_chunks(chunk, last_near, before, finish, dp, seq):
+    rows = chunk.shape[0]
+    cut = round_up(rows // 2, 16)
+    place = lax.axis_index("dp") % (dp // 2) // 2 * seq + lax.axis_index("seq")
+    along_x = lambda value: lax.ppermute(value, "dp", [(n, n ^ 2) for n in range(dp)])
+    along_y = lambda value: lax.ppermute(value, "seq", [(n, n ^ 1) for n in range(seq)])
+    chunk = after(chunk, last_near, before)
+    last_wide = finish(last_near)
+    pair = jnp.stack([chunk, lax.ppermute(chunk, "dp", [(n, n ^ 4) for n in range(dp)])])
+    a, b = pair[:, :cut], pair[:, cut:]
+    a1, b1 = along_y(a), along_x(b)
+    a, b = jnp.stack([a, a1]), jnp.stack([b, b1])
+    a, b, last_wide = lax.optimization_barrier((a, b, last_wide))
+    a2, b2 = along_x(a), along_y(b)
+    held = (a2, b2)
+
+    def assemble(a2, b2):
+        return call(
+            functools.partial(assemble_kernel, cut), [((8 * rows, D), BF16)], [],
+            [place.astype(jnp.int32).reshape(1), pair, a1, b1, a2, b2], scalars=1, limit=8,
+        )[0]
+
+    return (a2, b2), assemble, last_wide, held
 
 
 def scatter_rows(partial, seq):
@@ -791,12 +883,11 @@
     classes = class_table.shape[0]
     dp_place, seq_place = lax.axis_index("dp"), lax.axis_index("seq")
 
-    extra_rows = round_up(2 * FF + 16 + 3 * everyone, dp * seq * 4) - (2 * FF + 16)
+    half = round_up(FF + 16, dp * seq * 4)
     peers = dp // 4 * seq
     side = dp_place % 2
     sides = side.astype(jnp.int32).reshape(1)
-    half = (2 * FF + 16 + extra_rows) // 2
-    tail_half = round_up(4 * D + 16 + 6 * everyone, dp * seq * 4) // 2
+    tail_half = round_up(4 * D + 16 + 7 * everyone, dp * seq * 4) // 2
     kept_of = []
     for s in range(samples):
         tokens = [image_tokens[s]]
@@ -814,9 +905,9 @@
         held_rows = held + padded - slots
         cot_slot = jnp.pad(grad_masked[s], ((0, padded - slots), (0, 0)))
         one = slice(s, s + 1)
-        scalars, kept, facts, lines, mod, *owned, mask = own_call(
+        scalars, kept, lines, mod, *owned, mask = own_call(
             [
-                (places.shape, jnp.int32), ((held_rows, 1), jnp.int32), ((16, D), BF16), ((16, D), F32),
+                (places.shape, jnp.int32), ((held_rows, 1), jnp.int32), ((16, D), F32),
                 ((8, D), F32), ((own, D), BF16), ((own, D), BF16), ((HEADS, own, 128), BF16),
                 ((HEADS, own, 128), BF16), ((HEADS, own, 128), BF16), ((padded, D), BF16), ((8, total), F32),
             ],
@@ -844,15 +935,14 @@
             ],
             [((HEADS, rows, total), BF16)],
             [qaug, kaug, vaug, mask],
-            away=4, copies=3 + HEADS, micros=10, limit=32,
+            away=4, copies=3 + 8 * HEADS, micros=10, limit=32,
         )
         attended, hidden, du, keep, send = call(
-            functools.partial(feed_kernel, slots, everyone),
+            functools.partial(feed_kernel, slots),
             [((rows, D), F32), ((rows, FF), BF16), ((rows, FF), BF16), ((half, D), BF16), ((half, D), BF16)],
-            [((2 * half, D), BF16)],
+            [((2, half, D), BF16)],
             [
                 scalars, mixed, x, grad_full[s], cot_slot, mod, out_weight, fc1_weight, fc2_weight, lines,
-                facts,
             ],
             scalars=1, copies=2, micros=10, limit=24,
         )
@@ -886,7 +976,7 @@
         )
         for k in kept_of
     ]
-    mine = (keep.astype(F32) + got.astype(F32)).astype(BF16)
+    mine = add_call(keep, got, 1)
     mine, rests = lax.optimization_barrier((mine, rests))
     pieces = exchange(mine.reshape(peers, half // peers, D), dp, seq)
     tails = []
@@ -903,28 +993,38 @@
     keep, send = added([t[0] for t in tails]), added([t[1] for t in tails])
     keep, send, pieces = lax.optimization_barrier((keep, send, pieces))
     got = swap_cores(send, dp)
-    mine = add_call(keep, got, 30).reshape(peers, tail_half // peers, D)
-    chunk = sum_pieces(pieces, dp)
-    last_chunk = sum_pieces(exchange(mine, dp, seq), dp)
+    mine = add_call(keep, got, 1).reshape(peers, tail_half // peers, D)
+    pieces, mine = lax.optimization_barrier((pieces, mine))
+    near = near_sum(pieces)
+    far = far_half(near, dp)
     first_moved = [scatter_rows(t[2][:, : own // 2], seq) for t in tails]
-    chunk, first_moved = lax.optimization_barrier((chunk, first_moved))
     last_moved = [scatter_rows(t[2][:, own // 2 :], seq) for t in tails]
-    layer_half = spread_out(chunk, dp, seq)
-    layer_half, last_chunk = lax.optimization_barrier((layer_half, last_chunk))
-    last_half = spread_out(last_chunk, dp, seq)
+    last_near = near_sum(exchange(mine, dp, seq))
+
+    def finish(last_near):
+        wide = spread_call(last_near, far_half(last_near, dp), peers)
+        return wide
+
+    if dp == 16 and seq == 2:
+        chunk = (near.astype(F32) + far.astype(F32)).astype(BF16)
+        parts, assemble, last_wide, held = gather_chunks(chunk, last_near, first_moved, finish, dp, seq)
+    else:
+        parts = exchange(spread_call(near, far, peers), dp, seq).reshape(half, D)
+        assemble = lambda whole: whole
+        parts = (parts,)
+        held = parts
+        last_wide = finish(last_near)
+    last_half = exchange(last_wide, dp, seq).reshape(tail_half, D)
     out_full = jnp.stack([rest[1] for rest in rests])
     out_masked = jnp.stack([rest[2][:slots] for rest in rests])
-    info, layer_small, grad_fc1, grad_fc2 = call(
+    layer_half = assemble(*parts)
+    last_half = after(last_half, layer_half)
+    grad_fc1_bias, grad_fc2_bias, grad_fc1, grad_fc2 = call(
         layer_kernel,
-        [((extra_rows, D), BF16), ((8, D), F32), ((D, FF), F32), ((FF, D), F32)],
+        [((FF,), F32), ((D,), F32), ((D, FF), F32), ((FF, D), F32)],
         [((D, FF), F32), ((FF, D), F32)],
         [sides, layer_half, swap_cores(layer_half, dp)],
         scalars=1, away=2, copies=8, micros=3,
-    )
-    grad_fc1_bias = layer_small[:4].reshape(FF)
-    grad_fc2_bias = layer_small[4]
-    last_half, info, grad_fc1_bias, grad_fc2_bias = lax.optimization_barrier(
-        (last_half, info, grad_fc1_bias, grad_fc2_bias)
     )
     grad_qv, grad_rel, grad_out_bias, grad_ada_bias, grad_qkv, grad_ada, grad_table, grad_out = call(
         functools.partial(last_kernel, everyone),
@@ -933,7 +1033,7 @@
             ((D, 3 * D), F32), ((D, 6 * D), F32), ((classes, D), F32), ((D, D), F32),
         ],
         [((D, 3 * D), F32), ((D, 6 * D), F32), ((classes, D), F32), ((D, D), F32), (ada_weight.shape, BF16)],
-        [sides, last_half, swap_cores(last_half, dp), info, in_hbm(ada_weight)],
+        [sides, last_half, swap_cores(last_half, dp), in_hbm(ada_weight)],
         scalars=1, far=1, away=4, copies=12, micros=4, limit=16,
     )
     grad_rel = grad_rel.transpose(1, 0, 2)

time: 139 us -> 130 us (0.935)
  waiting for transfers between devices: 35.3 us -> 29.4 us
  local copies, waits for them, and re-layouts: 4.01 us -> 0.1 us
  Pallas kernels: 62.4 us -> 64.6 us
    ppermute x2 -> x7, starting transfers between devices: 4.14 us -> 10.9 us  [the longest x1 3.31 us: gather_chunks(): lax.ppermute(chunk, 'dp', [(n, n ^ 4) for n in range(dp)])]
    all_to_all x4 -> x3, starting transfers between devices: 20.5 us -> 14 us  [exchange(): return lax.all_to_all(value, AXES, 0, 0, axis_index_groups=groups)]
    ppermute x2 -> x7, waiting for transfers between devices: 17.7 us -> 13.9 us  [the longest x2 7.12 us: gather_chunks(): lax.ppermute(value, 'seq', [(n, n ^ 1) for n in range(seq)])]
    ppermute x2, waiting for transfers between devices: 2.86 us -> 0.01 us  [scatter_rows(): lax.ppermute(partial[step - 1], 'seq', [(n, (n + step) % seq) for n in ra...]
    pallas_call x7 -> x10, Pallas kernels: 37.9 us -> 40 us  [call(): pl.pallas_call(kernel, out_shape=[jax.ShapeDtypeStruct(shape, dtype) for...]
    broadcast_in_dim x2 -> x0, local copies, waits for them, and re-layouts: 2.02 us -> none  [spread_out(): jnp.broadcast_to(chunk[None], (peers,) + chunk.shape)]
    all_to_all x4 -> x3, waiting for transfers between devices: 9.7 us -> 11.5 us  [exchange(): return lax.all_to_all(value, AXES, 0, 0, axis_index_groups=groups)]
    convert_element_type x3 -> x1, other arithmetic: 1.44 us -> 0.05 us  [body(): chunk = (near.astype(F32) + far.astype(F32)).astype(BF16)]
  transfers between devices with their start and end apart: 13 -> 17, of which waited for: 9 -> 11; matrix products, arithmetic and copies ran while one was open for 2% -> 0% of each run, Pallas kernels for 28% -> 31%
where the time goes in v5:
time: 130 us
  Pallas kernels  64.6 us (50%)
  starting transfers between devices  30.4 us (23%)
  waiting for transfers between devices  29.4 us (23%)
  between operations  3.62 us (3%)
  other arithmetic  1.49 us (1%)
    pallas_call x10, Pallas kernels, call(): pl.pallas_call(kernel, out_shape=[jax.ShapeDtypeStruct(shape, dtype) for...  40 us
    pallas_call x1, Pallas kernels, back_call(): pl.pallas_call(functools.partial(back_kernel, own, everyone), grid=(group...  19.7 us
    all_to_all x3, starting transfers between devices, exchange(): return lax.all_to_all(value, AXES, 0, 0, axis_index_groups=groups)  14 us
    all_to_all x3, waiting for transfers between devices, exchange(): return lax.all_to_all(value, AXES, 0, 0, axis_index_groups=groups)  11.5 us
    ppermute x2, waiting for transfers between devices, gather_chunks(): lax.ppermute(value, 'seq', [(n, n ^ 1) for n in range(seq)])  7.12 us
    pallas_call x1, Pallas kernels, own_call(): pl.pallas_call(own_kernel, out_shape=[jax.ShapeDtypeStruct(shape, dtype)...  4.89 us
    ppermute x2, waiting for transfers between devices, gather_chunks(): lax.ppermute(value, 'dp', [(n, n ^ 2) for n in range(dp)])  3.79 us
    ppermute x1, starting transfers between devices, gather_chunks(): lax.ppermute(chunk, 'dp', [(n, n ^ 4) for n in range(dp)])  3.31 us
  transfers between devices with their start and end apart: 17, of which 11 were waited for; matrix products, arithmetic and copies ran while one was open for 0% of the time, Pallas kernels for 31%

profile of v5, /device:TPU:0, one launch (start us, length us, event | category | flops | bytes accessed | tf_op | source)
XLA Modules:
  0.0 129.6 jit_solution(620927681745662513)
XLA Ops:
  0.6 3.0 %collective-permute-start = (bf16[512,384]{1,0:T(8,128)(2,1)}, bf16[512,384]{1,0:T(8,128)(2,1)S(1)}, u32[]{:S(2)}, u32[]{:S(2)}) collective-permute-start(bf16[512,384]{1,0:T(8,128)(2,1)} %bitcast.30), channel_id=1, source_target_pairs={{0,1},{1,0},{2,3},{3,2},{4,5},{5,4},{6,7},{7,6},{8,9},{9,8},{10,11... | collective-permute-start | bytes 1179656 | tf_op jit(solution)/shard_map/ppermute | solution.py:895
  6.3 0.0 copy-start.2
  6.3 0.0 copy-start.3
  6.3 4.9 %shard_map.307 = (s32[10]{0:T(128)S(1)}, s32[704,1]{1,0:T(8,128)S(1)}, f32[16,384]{1,0:T(8,128)S(1)}, f32[8,384]{1,0:T(8,128)S(1)}, bf16[512,384]{1,0:T(8,128)(2...) custom-call(s32[10]{0:T(128)S(1)} %compare_select_fusion.6.start_ref, ...), custom_call_target="tpu_custom_call" | custom-call | flops 3000000000 | bytes 1048576 | tf_op jit(solution)/shard_map/pallas_call | solution.py:635
  11.2 1.8 %collective-permute-done.refs_1_ = bf16[512,384]{1,0:T(8,128)(2,1)S(1)} collective-permute-done((bf16[512,384]{1,0:T(8,128)(2,1)}, bf16[512,384]{1,0:T(8,128)(2,1)S(1)}, u32[]{:S(2)}, u32[]{:S(2)}) %collective-permute-start) | collective-permute-done | bytes 393248 | tf_op jit(solution)/shard_map/ppermute | solution.py:895
  13.0 3.6 %shard_map.308 = (bf16[6,864,128]{2,1,0:T(8,128)(2,1)S(1)}, bf16[6,1024,128]{2,1,0:T(8,128)(2,1)S(1)}, bf16[6,1024,128]{2,1,0:T(8,128)(2,1)S(1)}, bf16[864,384]{...) custom-call(s32[10]{0:T(128)S(1)} %get-tuple-element.87.scalar_ref, ...), custom_call_target="tpu_custom_call" | custom-call | flops 3000000000 | bytes 1048576 | tf_op jit(solution)/shard_map/pallas_call | solution.py:622
  16.7 0.0 copy-start
  16.7 0.0 copy-start.1
  16.7 0.0 copy-start.4
  16.7 0.0 copy-start.5
  16.7 9.6 %shard_map.309 = (f32[3,864,128]{2,1,0:T(8,128)S(1)}, f32[3,864,128]{2,1,0:T(8,128)S(1)}, bf16[6,864,1024]{2,1,0:T(8,128)(2,1)}, bf16[6,864,128]{2,1,0:T(8,128)(...) custom-call(bf16[6,864,128]{2,1,0:T(8,128)(2,1)S(1)} %get-tuple-element.97.qaug_ref, ...), custom_call_target="tpu_custom_call" | custom-call | flops 10000000000 | bytes 1048576 | tf_op jit(solution)/shard_map/pallas_call | solution.py:622
  26.4 9.1 %shard_map.310 = (f32[864,384]{1,0:T(8,128)S(1)}, bf16[864,1536]{1,0:T(8,128)(2,1)S(1)}, bf16[864,1536]{1,0:T(8,128)(2,1)S(1)}, bf16[1664,384]{1,0:T(8,128)(2,1)S(1)}, bf16[1664,384]{1,0:T(8,128)(2,1)S(1)}) custom-call(s32[10]{0:T(128)S(1)} %get-tuple-element.87.scalar_ref, f32[3,864,128]{2,1,0:T(8,128)S(1)} %get-tuple-element.101.o_ref, ...), custom_call_target="tpu_custom_call" | custom-call | flops 10000000000 | bytes 1048576 | tf_op jit(solution)/shard_map/pallas_call | solution.py:622
  35.5 0.1 collective-permute-start.1
  35.5 6.2 %shard_map.312 = (f32[8,384]{1,0:T(8,128)S(1)}, bf16[512,384]{1,0:T(8,128)(2,1)}, bf16[352,384]{1,0:T(8,128)(2,1)}, f32[864,384]{1,0:T(8,128)}, bf16[864,384]{1,...) custom-call(s32[10]{0:T(128)S(1)} %get-tuple-element.87.scalar_ref, ...), custom_call_target="tpu_custom_call" | custom-call | flops 6000000000 | bytes 1048576 | tf_op jit(solution)/shard_map/pallas_call | solution.py:622
  41.8 1.2 shard_map.311
  43.0 5.0 %all-to-all-start = ((bf16[8,208,384]{2,1,0:T(8,128)(2,1)}), bf16[8,208,384]{2,1,0:T(8,128)(2,1)S(1)}, u32[]{:S(2)}, u32[]{:S(2)}) async-start(bf16[8,208,384]{2,1,0:T(8,128)(2,1)} %bitcast.42), calls=%async_computation | async-start | bytes 2555904 | tf_op jit(solution)/shard_map/all_to_all | solution.py:803
  47.9 19.7 %shard_map.313 = (bf16[832,384]{1,0:T(8,128)(2,1)S(1)}, bf16[832,384]{1,0:T(8,128)(2,1)S(1)}, bf16[1,512,384]{2,1,0:T(8,128)(2,1)}, f32[512,384]{1,0:T(8,128)}) custom-call(s32[10]{0:T(128)S(1)} %get-tuple-element.87.scalar_ref, s32[704,1]{1,0:T(8,128)S(1)} %get-tuple-element.94.refs_8_.kept_ref, f32[8,384]{1,0:T(8,128)S(1)} %get-tuple-element.95.refs_9_.mod_ref, ...), custom_call_target="tpu_custom_call" | custom-call | flops 17999998976 | bytes 1048576 | tf_op jit(solution)/shard_map/pallas_call | solution.py:700
  67.7 0.3 collective-permute-start.3
  67.9 1.9 %collective-permute-done.3.right_ref = bf16[832,384]{1,0:T(8,128)(2,1)S(1)} collective-permute-done((bf16[832,384]{1,0:T(8,128)(2,1)S(1)}, bf16[832,384]{1,0:T(8,128)(2,1)S(1)}, u32[]{:S(2)}, u32[]{:S(2)}) %collective-permute-start.3) | collective-permute-done | bytes 639008 | tf_op jit(solution)/shard_map/ppermute | solution.py:794
  69.8 0.9 shard_map.314
  70.7 0.0 copy-start.8
  70.7 5.2 %all-to-all-start.1 = ((bf16[8,104,384]{2,1,0:T(8,128)(2,1)}), bf16[8,104,384]{2,1,0:T(8,128)(2,1)S(1)}, u32[]{:S(2)}, u32[]{:S(2)}) async-start(bf16[8,104,384]{2,1,0:T(8,128)(2,1)} %bitcast.48), calls=%async_computation.1 | async-start | bytes 1277952 | tf_op jit(solution)/shard_map/all_to_all | solution.py:803
  75.9 0.2 reduce_sum.24
  76.1 2.7 %collective-permute-start.4 = (bf16[208,384]{1,0:T(8,128)(2,1)S(1)}, bf16[208,384]{1,0:T(8,128)(2,1)S(1)}, u32[]{:S(2)}, u32[]{:S(2)}) collective-permute-start(bf16[208,384]{1,0:T(8,128)(2,1)S(1)} %reduce_sum.24), channel_id=1, source_target_pairs={{0,16},{2,18},{4,20},{6,22},{8,24},{10,26},{12,28},{14,30},{16,0},... | collective-permute-start | bytes 479240 | tf_op jit(solution)/shard_map/ppermute | solution.py:811
  78.8 2.1 %collective-permute-start.2 = (bf16[256,384]{1,0:T(8,128)(2,1)S(1)}, bf16[256,384]{1,0:T(8,128)(2,1)S(1)}, u32[]{:S(2)}, u32[]{:S(2)}) collective-permute-start(bf16[256,384]{1,0:T(8,128)(2,1)S(1)} %get-tuple-element.160), channel_id=1, source_target_pairs={{0,1},{1,0},{2,3},{3,2},{4,5},{5,4},{6,7},{7,6},{8,9},{9,8},{10,11... | collective-permute-start | bytes 589832 | tf_op jit(solution)/shard_map/ppermute | solution.py:866
  80.9 8.9 %all-to-all-done.1 = bf16[8,104,384]{2,1,0:T(8,128)(2,1)S(1)} async-done(((bf16[8,104,384]{2,1,0:T(8,128)(2,1)}), bf16[8,104,384]{2,1,0:T(8,128)(2,1)S(1)}, u32[]{:S(2)}, u32[]{:S(2)}) %all-to-all-start.1) | async-done | bytes 639008 | tf_op jit(solution)/shard_map/all_to_all | solution.py:803
  89.8 0.1 reduce_sum.25.near_ref
  89.9 0.1 collective-permute-start.8
  90.1 3.3 %collective-permute-start.5 = (bf16[208,384]{1,0:T(8,128)(2,1)S(1)}, bf16[208,384]{1,0:T(8,128)(2,1)S(1)}, u32[]{:S(2)}, u32[]{:S(2)}) collective-permute-start(bf16[208,384]{1,0:T(8,128)(2,1)S(1)} %add_convert_fusion), channel_id=1, source_target_pairs={{0,8},{2,10},{4,12},{6,14},{8,0},{10,2},{12,4},{14,6},{16,24},{18,... | collective-permute-start | bytes 479240 | tf_op jit(solution)/shard_map/ppermute | solution.py:847
  93.4 2.7 %collective-permute-done.8.far_ref = bf16[104,384]{1,0:T(8,128)(2,1)S(1)} collective-permute-done((bf16[104,384]{1,0:T(8,128)(2,1)S(1)}, bf16[104,384]{1,0:T(8,128)(2,1)S(1)}, u32[]{:S(2)}, u32[]{:S(2)}) %collective-permute-start.8) | collective-permute-done | bytes 79904 | tf_op jit(solution)/shard_map/ppermute | solution.py:811
  96.1 0.9 shard_map.315
  97.0 0.2 collective-permute-done.5
  97.3 1.3 %collective-permute-start.7 = (bf16[2,96,384]{2,1,0:T(8,128)(2,1)S(1)}, bf16[2,96,384]{2,1,0:T(8,128)(2,1)S(1)}, u32[]{:S(2)}, u32[]{:S(2)}) collective-permute-start(bf16[2,96,384]{2,1,0:T(8,128)(2,1)S(1)} %fusion.1), channel_id=1, source_target_pairs={{0,4},{2,6},{4,0},{6,2},{8,12},{10,14},{12,8},{14,10},{16,20},{18,... | collective-permute-start | bytes 442376 | tf_op jit(solution)/shard_map/ppermute | solution.py:843
  98.6 1.5 %collective-permute-start.6 = (bf16[2,112,384]{2,1,0:T(8,128)(2,1)S(1)}, bf16[2,112,384]{2,1,0:T(8,128)(2,1)S(1)}, u32[]{:S(2)}, u32[]{:S(2)}) collective-permute-start(bf16[2,112,384]{2,1,0:T(8,128)(2,1)S(1)} %fusion), channel_id=1, source_target_pairs={{0,1},{1,0},{2,3},{3,2},{4,5},{5,4},{6,7},{7,6},{8,9},{9,8},{10,11... | collective-permute-start | bytes 516104 | tf_op jit(solution)/shard_map/ppermute | solution.py:844
  100.1 2.4 %collective-permute-done.7.b1_ref = bf16[2,96,384]{2,1,0:T(8,128)(2,1)S(1)} collective-permute-done((bf16[2,96,384]{2,1,0:T(8,128)(2,1)S(1)}, bf16[2,96,384]{2,1,0:T(8,128)(2,1)S(1)}, u32[]{:S(2)}, u32[]{:S(2)}) %collective-permute-start.7) | collective-permute-done | bytes 147488 | tf_op jit(solution)/shard_map/ppermute | solution.py:843
  102.5 1.6 %collective-permute-done.6.a1_ref = bf16[2,112,384]{2,1,0:T(8,128)(2,1)S(1)} collective-permute-done((bf16[2,112,384]{2,1,0:T(8,128)(2,1)S(1)}, bf16[2,112,384]{2,1,0:T(8,128)(2,1)S(1)}, u32[]{:S(2)}, u32[]{:S(2)}) %collective-permute-start.6) | collective-permute-done | bytes 172064 | tf_op jit(solution)/shard_map/ppermute | solution.py:844
  104.1 0.8 collective-permute-start.9
  105.0 1.2 collective-permute-start.10
  106.2 3.8 %all-to-all-start.2 = ((bf16[8,104,384]{2,1,0:T(8,128)(2,1)}), bf16[8,104,384]{2,1,0:T(8,128)(2,1)S(1)}, u32[]{:S(2)}, u32[]{:S(2)}) async-start(bf16[8,104,384]{2,1,0:T(8,128)(2,1)} %shard_map.315), calls=%async_computation.2 | async-start | bytes 1277952 | tf_op jit(solution)/shard_map/all_to_all | solution.py:803
  110.0 5.6 %collective-permute-done.10.b2_ref = bf16[2,2,96,384]{3,2,1,0:T(8,128)(2,1)S(1)} collective-permute-done((bf16[2,2,96,384]{3,2,1,0:T(8,128)(2,1)S(1)}, bf16[2,2,96,384]{3,2,1,0:T(8,128)(2,1)S(1)}, u32[]{:S(2)}, u32[]{:S(2)}) %collective-permute-start.10) | collective-permute-done | bytes 294944 | tf_op jit(solution)/shard_map/ppermute | solution.py:844
  115.6 1.4 %collective-permute-done.9.a2_ref = bf16[2,2,112,384]{3,2,1,0:T(8,128)(2,1)S(1)} collective-permute-done((bf16[2,2,112,384]{3,2,1,0:T(8,128)(2,1)S(1)}, bf16[2,2,112,384]{3,2,1,0:T(8,128)(2,1)S(1)}, u32[]{:S(2)}, u32[]{:S(2)}) %collective-permute-start.9) | collective-permute-done | bytes 344096 | tf_op jit(solution)/shard_map/ppermute | solution.py:843
  117.0 0.1 shard_map.316.mine_ref
  117.1 0.1 collective-permute-start.13
  117.2 2.6 %all-to-all-done.2 = bf16[8,104,384]{2,1,0:T(8,128)(2,1)S(1)} async-done(((bf16[8,104,384]{2,1,0:T(8,128)(2,1)}), bf16[8,104,384]{2,1,0:T(8,128)(2,1)S(1)}, u32[]{:S(2)}, u32[]{:S(2)}) %all-to-all-start.2) | async-done | bytes 639008 | tf_op jit(solution)/shard_map/all_to_all | solution.py:803
  119.8 0.4 collective-permute-done.13.other_ref
  120.2 2.9 %shard_map.318 = (f32[1536]{0:T(1024)}, f32[384]{0:T(512)}, f32[384,1536]{1,0:T(8,128)}, f32[1536,384]{1,0:T(8,128)}) custom-call(s32[1]{0:T(128)} %bitcast.7.side_ref, bf16[1664,384]{1,0:T(8,128)(2,1)S(1)} %shard_map.316.mine_ref, bf16[1664,384]{1,0:T(8,128)(2,1)S(1)} %collective-permute-done.13.other_ref), custom_call_target="tpu_custom_call" | custom-call | flops 3000000000 | bytes 1048576 | tf_op jit(solution)/shard_map/pallas_call | solution.py:622
  123.1 5.5 %shard_map.317 = (f32[2,384]{1,0:T(2,128)}, f32[6,2,63]{2,1,0:T(2,128)}, f32[384]{0:T(512)}, f32[2304]{0:T(1024)}, f32[384,1152]{1,0:T(8,128)}, /*index=5*/f32[3...) custom-call(s32[1]{0:T(128)} %bitcast.7.side_ref, bf16[832,384]{1,0:T(8,128)(2,1)S(1)} %bitcast.27, ...), custom_call_target="tpu_custom_call" | custom-call | flops 4000000000 | bytes 1048576 | tf_op jit(solution)/shard_map/pallas_call | solution.py:622
  128.6 1.0 add_bitcast_fusion
  (33 shorter events, 0.4 us)
Async XLA Ops:
  0.6 12.4 %collective-permute-start = (bf16[512,384]{1,0:T(8,128)(2,1)}, bf16[512,384]{1,0:T(8,128)(2,1)S(1)}, u32[]{:S(2)}, u32[]{:S(2)}) collective-permute-start(bf16[512,384]{1,0:T(8,128)(2,1)} %bitcast.30), channel_id=1, source_target_pairs={{0,1},{1,0},{2,3},{3,2},{4,5},{5,4},{6,7},{7,6},{8,9},{9,8},{10,11... | collective-permute-start | bytes 1179656 | tf_op jit(solution)/shard_map/ppermute | solution.py:895
  6.3 6.7 %copy-start.2 = (bf16[384,1152]{1,0:T(8,128)(2,1)S(1)}, bf16[384,1152]{1,0:T(8,128)(2,1)}, u32[]{:S(2)}) copy-start(bf16[384,1152]{1,0:T(8,128)(2,1)} %refs_9_.1) | copy-start | bytes 2654212
  6.3 6.7 %copy-start.3 = (bf16[1,512,384]{2,1,0:T(8,128)(2,1)S(1)}, bf16[1,512,384]{2,1,0:T(8,128)(2,1)}, u32[]{:S(2)}) copy-start(bf16[1,512,384]{2,1,0:T(8,128)(2,1)} %param.20) | copy-start | bytes 1179652
  16.7 9.7 %copy-start = (bf16[384,1536]{1,0:T(8,128)(2,1)S(1)}, bf16[384,1536]{1,0:T(8,128)(2,1)}, u32[]{:S(2)}) copy-start(bf16[384,1536]{1,0:T(8,128)(2,1)} %w1_ref.3) | copy-start | bytes 3538948
  16.7 9.7 %copy-start.1 = (bf16[1536,384]{1,0:T(8,128)(2,1)S(1)}, bf16[1536,384]{1,0:T(8,128)(2,1)}, u32[]{:S(2)}) copy-start(bf16[1536,384]{1,0:T(8,128)(2,1)} %w2_ref.3) | copy-start | bytes 3538948
  16.7 9.7 %copy-start.4 = (bf16[1,512,384]{2,1,0:T(8,128)(2,1)S(1)}, bf16[1,512,384]{2,1,0:T(8,128)(2,1)}, u32[]{:S(2)}) copy-start(bf16[1,512,384]{2,1,0:T(8,128)(2,1)} %param.38) | copy-start | bytes 1179652
  16.7 9.7 %copy-start.5 = (bf16[384,384]{1,0:T(8,128)(2,1)S(1)}, bf16[384,384]{1,0:T(8,128)(2,1)}, u32[]{:S(2)}) copy-start(bf16[384,384]{1,0:T(8,128)(2,1)} %wout_ref.3) | copy-start | bytes 884740
  16.7 9.7 %copy-start.6 = (bf16[1,352,384]{2,1,0:T(8,128)(2,1)S(1)}, bf16[1,352,384]{2,1,0:T(8,128)(2,1)}, u32[]{:S(2)}) copy-start(bf16[1,352,384]{2,1,0:T(8,128)(2,1)} %param.39) | copy-start | bytes 811012
  35.5 6.3 %collective-permute-start.1 = (bf16[1664,384]{1,0:T(8,128)(2,1)S(1)}, bf16[1664,384]{1,0:T(8,128)(2,1)S(1)}, u32[]{:S(2)}, u32[]{:S(2)}) collective-permute-start(bf16[1664,384]{1,0:T(8,128)(2,1)S(1)} %get-tuple-element.104), channel_id=1, source_target_pairs={{0,2},{2,0},{4,6},{6,4},{8,10},{10,8},{12,14},{14,12},{16,18},{18,... | collective-permute-start | bytes 3833864 | tf_op jit(solution)/shard_map/ppermute | solution.py:794
  43.0 24.7 %all-to-all-start = ((bf16[8,208,384]{2,1,0:T(8,128)(2,1)}), bf16[8,208,384]{2,1,0:T(8,128)(2,1)S(1)}, u32[]{:S(2)}, u32[]{:S(2)}) async-start(bf16[8,208,384]{2,1,0:T(8,128)(2,1)} %bitcast.42), calls=%async_computation | async-start | bytes 2555904 | tf_op jit(solution)/shard_map/all_to_all | solution.py:803
  67.7 2.1 %collective-permute-start.3 = (bf16[832,384]{1,0:T(8,128)(2,1)S(1)}, bf16[832,384]{1,0:T(8,128)(2,1)S(1)}, u32[]{:S(2)}, u32[]{:S(2)}) collective-permute-start(bf16[832,384]{1,0:T(8,128)(2,1)S(1)} %get-tuple-element.137), channel_id=1, source_target_pairs={{0,2},{2,0},{4,6},{6,4},{8,10},{10,8},{12,14},{14,12},{16,18},{18,... | collective-permute-start | bytes 1916936 | tf_op jit(solution)/shard_map/ppermute | solution.py:794
  70.7 8.1 %copy-start.8 = (bf16[1,512,384]{2,1,0:T(8,128)(2,1)S(1)}, bf16[1,512,384]{2,1,0:T(8,128)(2,1)}, u32[]{:S(2)}) copy-start(bf16[1,512,384]{2,1,0:T(8,128)(2,1)} %get-tuple-element.131) | copy-start | bytes 1179652
  70.7 19.1 %all-to-all-start.1 = ((bf16[8,104,384]{2,1,0:T(8,128)(2,1)}), bf16[8,104,384]{2,1,0:T(8,128)(2,1)S(1)}, u32[]{:S(2)}, u32[]{:S(2)}) async-start(bf16[8,104,384]{2,1,0:T(8,128)(2,1)} %bitcast.48), calls=%async_computation.1 | async-start | bytes 1277952 | tf_op jit(solution)/shard_map/all_to_all | solution.py:803
  76.1 13.9 %collective-permute-start.4 = (bf16[208,384]{1,0:T(8,128)(2,1)S(1)}, bf16[208,384]{1,0:T(8,128)(2,1)S(1)}, u32[]{:S(2)}, u32[]{:S(2)}) collective-permute-start(bf16[208,384]{1,0:T(8,128)(2,1)S(1)} %reduce_sum.24), channel_id=1, source_target_pairs={{0,16},{2,18},{4,20},{6,22},{8,24},{10,26},{12,28},{14,30},{16,0},... | collective-permute-start | bytes 479240 | tf_op jit(solution)/shard_map/ppermute | solution.py:811
  78.8 11.2 %collective-permute-start.2 = (bf16[256,384]{1,0:T(8,128)(2,1)S(1)}, bf16[256,384]{1,0:T(8,128)(2,1)S(1)}, u32[]{:S(2)}, u32[]{:S(2)}) collective-permute-start(bf16[256,384]{1,0:T(8,128)(2,1)S(1)} %get-tuple-element.160), channel_id=1, source_target_pairs={{0,1},{1,0},{2,3},{3,2},{4,5},{5,4},{6,7},{7,6},{8,9},{9,8},{10,11... | collective-permute-start | bytes 589832 | tf_op jit(solution)/shard_map/ppermute | solution.py:866
  89.9 6.2 %collective-permute-start.8 = (bf16[104,384]{1,0:T(8,128)(2,1)S(1)}, bf16[104,384]{1,0:T(8,128)(2,1)S(1)}, u32[]{:S(2)}, u32[]{:S(2)}) collective-permute-start(bf16[104,384]{1,0:T(8,128)(2,1)S(1)} %reduce_sum.25.near_ref), channel_id=1, source_target_pairs={{0,16},{2,18},{4,20},{6,22},{8,24},{10,26},{12,28},{14,30},{16,0},... | collective-permute-start | bytes 239624 | tf_op jit(solution)/shard_map/ppermute | solution.py:811
  90.0 7.0 %copy-start.9 = (bf16[256,384]{1,0:T(8,128)(2,1)}, bf16[256,384]{1,0:T(8,128)(2,1)S(1)}, u32[]{:S(2)}) copy-start(bf16[256,384]{1,0:T(8,128)(2,1)S(1)} %collective-permute-done.2) | copy-start | bytes 589828
  90.1 7.2 %collective-permute-start.5 = (bf16[208,384]{1,0:T(8,128)(2,1)S(1)}, bf16[208,384]{1,0:T(8,128)(2,1)S(1)}, u32[]{:S(2)}, u32[]{:S(2)}) collective-permute-start(bf16[208,384]{1,0:T(8,128)(2,1)S(1)} %add_convert_fusion), channel_id=1, source_target_pairs={{0,8},{2,10},{4,12},{6,14},{8,0},{10,2},{12,4},{14,6},{16,24},{18,... | collective-permute-start | bytes 479240 | tf_op jit(solution)/shard_map/ppermute | solution.py:847
  97.3 5.2 %collective-permute-start.7 = (bf16[2,96,384]{2,1,0:T(8,128)(2,1)S(1)}, bf16[2,96,384]{2,1,0:T(8,128)(2,1)S(1)}, u32[]{:S(2)}, u32[]{:S(2)}) collective-permute-start(bf16[2,96,384]{2,1,0:T(8,128)(2,1)S(1)} %fusion.1), channel_id=1, source_target_pairs={{0,4},{2,6},{4,0},{6,2},{8,12},{10,14},{12,8},{14,10},{16,20},{18,... | collective-permute-start | bytes 442376 | tf_op jit(solution)/shard_map/ppermute | solution.py:843
  98.6 5.5 %collective-permute-start.6 = (bf16[2,112,384]{2,1,0:T(8,128)(2,1)S(1)}, bf16[2,112,384]{2,1,0:T(8,128)(2,1)S(1)}, u32[]{:S(2)}, u32[]{:S(2)}) collective-permute-start(bf16[2,112,384]{2,1,0:T(8,128)(2,1)S(1)} %fusion), channel_id=1, source_target_pairs={{0,1},{1,0},{2,3},{3,2},{4,5},{5,4},{6,7},{7,6},{8,9},{9,8},{10,11... | collective-permute-start | bytes 516104 | tf_op jit(solution)/shard_map/ppermute | solution.py:844
  104.1 12.9 %collective-permute-start.9 = (bf16[2,2,112,384]{3,2,1,0:T(8,128)(2,1)S(1)}, bf16[2,2,112,384]{3,2,1,0:T(8,128)(2,1)S(1)}, u32[]{:S(2)}, u32[]{:S(2)}) collective-permute-start(bf16[2,2,112,384]{3,2,1,0:T(8,128)(2,1)S(1)} %pad_maximum_fusion.1), channel_id=1, source_target_pairs={{0,4},{2,6},{4,0},{6,2},{8,12},{10,14},{12,8},{14,10},{16,20},{18,... | collective-permute-start | bytes 1032200 | tf_op jit(solution)/shard_map/ppermute | solution.py:843
  105.0 10.6 %collective-permute-start.10 = (bf16[2,2,96,384]{3,2,1,0:T(8,128)(2,1)S(1)}, bf16[2,2,96,384]{3,2,1,0:T(8,128)(2,1)S(1)}, u32[]{:S(2)}, u32[]{:S(2)}) collective-permute-start(bf16[2,2,96,384]{3,2,1,0:T(8,128)(2,1)S(1)} %pad_maximum_fusion.2), channel_id=1, source_target_pairs={{0,1},{1,0},{2,3},{3,2},{4,5},{5,4},{6,7},{7,6},{8,9},{9,8},{10,11... | collective-permute-start | bytes 884744 | tf_op jit(solution)/shard_map/ppermute | solution.py:844
  106.2 13.6 %all-to-all-start.2 = ((bf16[8,104,384]{2,1,0:T(8,128)(2,1)}), bf16[8,104,384]{2,1,0:T(8,128)(2,1)S(1)}, u32[]{:S(2)}, u32[]{:S(2)}) async-start(bf16[8,104,384]{2,1,0:T(8,128)(2,1)} %shard_map.315), calls=%async_computation.2 | async-start | bytes 1277952 | tf_op jit(solution)/shard_map/all_to_all | solution.py:803
  117.1 3.1 %collective-permute-start.13 = (bf16[1664,384]{1,0:T(8,128)(2,1)S(1)}, bf16[1664,384]{1,0:T(8,128)(2,1)S(1)}, u32[]{:S(2)}, u32[]{:S(2)}) collective-permute-start(bf16[1664,384]{1,0:T(8,128)(2,1)S(1)} %shard_map.316.mine_ref), channel_id=1, source_target_pairs={{0,2},{2,0},{4,6},{6,4},{8,10},{10,8},{12,14},{14,12},{16,18},{18,... | collective-permute-start | bytes 3833864 | tf_op jit(solution)/shard_map/ppermute | solution.py:794
  119.8 3.3 %collective-permute-start.11 = (bf16[832,384]{1,0:T(8,128)(2,1)S(1)}, bf16[832,384]{1,0:T(8,128)(2,1)S(1)}, u32[]{:S(2)}, u32[]{:S(2)}) collective-permute-start(bf16[832,384]{1,0:T(8,128)(2,1)S(1)} %bitcast.26), channel_id=1, source_target_pairs={{0,2},{2,0},{4,6},{6,4},{8,10},{10,8},{12,14},{14,12},{16,18},{18,... | collective-permute-start | bytes 1916936 | tf_op jit(solution)/shard_map/ppermute | solution.py:794
  119.8 8.8 %collective-permute-start.12 = (bf16[256,384]{1,0:T(8,128)(2,1)S(1)}, bf16[256,384]{1,0:T(8,128)(2,1)S(1)}, u32[]{:S(2)}, u32[]{:S(2)}) collective-permute-start(bf16[256,384]{1,0:T(8,128)(2,1)S(1)} %get-tuple-element.159), channel_id=1, source_target_pairs={{0,1},{1,0},{2,3},{3,2},{4,5},{5,4},{6,7},{7,6},{8,9},{9,8},{10,11... | collective-permute-start | bytes 589832 | tf_op jit(solution)/shard_map/ppermute | solution.py:866
  123.1 5.5 %copy-start.7 = (f32[512,384]{1,0:T(8,128)S(1)}, f32[512,384]{1,0:T(8,128)}, u32[]{:S(2)}) copy-start(f32[512,384]{1,0:T(8,128)} %get-tuple-element.130) | copy-start | bytes 2359300
  123.1 5.5 %copy-start.10 = (bf16[256,384]{1,0:T(8,128)(2,1)S(1)}, bf16[256,384]{1,0:T(8,128)(2,1)}, u32[]{:S(2)}) copy-start(bf16[256,384]{1,0:T(8,128)(2,1)} %copy-done.9) | copy-start | bytes 589828

commit v6 on v5

--- a/solution.py
+++ b/solution.py
@@ -345,7 +345,7 @@
 def feed_kernel(
     slots, scalar_ref, o_ref, x_ref, cot_full_ref, cot_slot_ref, mod_ref, wout_ref, w1_ref,
     w2_ref, line_ref,
-    att_ref, hidden_ref, du_ref, keep_ref, send_ref, pay_ref, sems,
+    att_ref, hidden_ref, du_ref, bias_ref, keep_ref, send_ref, pay_ref, sems,
 ):
     rows = x_ref.shape[0]
     gate1, shift2, scale2, gate2 = [mod_ref[n : n + 1, :] for n in range(2, 6)]
@@ -376,9 +376,6 @@
         hidden_ref[:, cols] = (u * cdf).astype(BF16)
         slope = cdf * ((1.0 - t) * (u * (square * (3.0 * GELU_A * GELU_B) + GELU_A)) + 1.0)
         du_ref[:, cols] = (slope * back_u).astype(BF16)
-    spare = pay_ref.shape[1] - FF
-    pay_ref[0, FF:, :] = jnp.zeros((spare, D), BF16)
-    pay_ref[1, FF:, :] = jnp.zeros((spare, D), BF16)
     ones = jnp.ones((16, rows), BF16)
     grad = mm(jnp.concatenate([second.T, ones], axis=0), du_ref[...])
     heads = []
@@ -386,9 +383,11 @@
         cols = slice(n * D, (n + 1) * D)
         pay_ref[0, cols, :] = grad[:D, cols].astype(BF16)
         heads.append(grad[D : D + 1, cols])
-    heads += [jnp.sum(dz.astype(F32), axis=0, keepdims=True), jnp.zeros((11, D), F32)]
-    pay_ref[0, FF : FF + 16, :] = jnp.concatenate(heads, axis=0).astype(BF16)
+    heads += [jnp.sum(dz.astype(F32), axis=0, keepdims=True), jnp.zeros((3, D), F32)]
+    bias_ref[...] = jnp.concatenate(heads, axis=0)
     pay_ref[1, :FF, :] = mm(hidden_ref[...].T, dz).astype(BF16)
+    if pay_ref.shape[1] > FF:
+        pay_ref[:, FF:, :] = jnp.zeros((2, pay_ref.shape[1] - FF, D), BF16)
     for which in range(2):
         half_copies(scalar_ref[SIDE], pay_ref, keep_ref, send_ref, sems, which)
     for which in range(2):
@@ -398,7 +397,7 @@
 def feed_rest_kernel(
     slots, scalar_ref, o_ref, inverse_ref, x_ref, cot_full_ref, cot_slot_ref, mod_ref, wout_ref, w1_ref,
     w2_ref, line_ref,
-    att_ref, hidden_ref, du_ref,
+    att_ref, hidden_ref, du_ref, bias_ref,
     small_ref, y_full_out, y_slot_out, dm_out, x_out, do_out, go_out, y_ref, dm_ref, do_ref, go_ref, sems,
 ):
     rows, own = x_ref.shape[0], cot_full_ref.shape[0]
@@ -443,7 +442,8 @@
     copies.start(go_ref, go_out)
     column = lambda value: jnp.sum(value.astype(F32), axis=0, keepdims=True)
     sums = [dmid * attended, back, back * normed, cot * branch, datt]
-    small_ref[...] = jnp.concatenate([column(value) for value in sums] + [jnp.zeros((3, D), F32)], axis=0)
+    sums = [column(value) for value in sums] + [bias_ref[:5, :], jnp.zeros((6, D), F32)]
+    small_ref[...] = jnp.concatenate(sums, axis=0)
     copies.wait()
 
 
@@ -585,17 +585,18 @@
         smalls = jnp.concatenate(
             [
                 shift_sum, scale_sum, prior_ref[0:4, :], column(dq_own) + column(dq_slot), column(dv),
-                *rel, prior_ref[4:5, :], digits, mod_ref[COND_LINE : COND_LINE + 1, :], jnp.zeros((3, D), F32),
+                *rel, prior_ref[4:5, :], digits, prior_ref[5:10, :], mod_ref[COND_LINE : COND_LINE + 1, :],
+                jnp.zeros((14, D), F32),
             ],
             axis=0,
         ).astype(BF16)
         tail = pay_ref.shape[0] - 4 * D
-        row = lax.broadcasted_iota(jnp.int32, (tail, 16), 0)
-        lane = lax.broadcasted_iota(jnp.int32, (tail, 16), 1)
-        kind = jnp.where(row < 6 * everyone, row // everyone, jnp.where(scalar_ref[SEQ_PLACE] == 0, 12, -1))
+        row = lax.broadcasted_iota(jnp.int32, (tail, 32), 0)
+        lane = lax.broadcasted_iota(jnp.int32, (tail, 32), 1)
+        kind = jnp.where(row < 6 * everyone, row // everyone, jnp.where(scalar_ref[SEQ_PLACE] == 0, 17, -1))
         wanted = jnp.where(row % everyone == scalar_ref[PLACE], kind, -1)
         after = row - 7 * everyone
-        wanted = jnp.where(after < 0, wanted, jnp.where(after < 6, after + 6, -1))
+        wanted = jnp.where(after < 0, wanted, jnp.where(after < 11, after + 6, -1))
         pay_ref[4 * D :, :] = mm((lane == wanted).astype(F32).astype(BF16), smalls).astype(BF16)
         halves = Copies(pay_sems)
         split_halves(halves, scalar_ref[SIDE], pay_ref, keep_ref, send_ref)
@@ -728,26 +729,55 @@
     return get
 
 
-def layer_kernel(side_ref, mine_ref, other_ref, bias1_ref, bias2_ref, g1_out, g2_out, g1_ref, g2_ref, sems):
-    get = halves_reader(side_ref, mine_ref, other_ref)
-    copies = Copies(sems)
-    half = mine_ref.shape[0]
-    for n in range(4):
-        cols = pl.ds(n * D, D)
-        g1_ref[:, cols] = get(n * D, D).astype(F32)
-        copies.start(g1_ref.at[:, cols], g1_out.at[:, cols])
-        g2_ref[cols, :] = get(half + n * D, D).astype(F32)
-        copies.start(g2_ref.at[cols], g2_out.at[cols])
-    small = get(FF, 16).astype(F32)
-    for n in range(4):
-        bias1_ref[pl.ds(n * D, D)] = small[n]
-    bias2_ref[...] = small[4]
-    copies.wait()
+def widen_half(core, half_ref, g1_out, g2_out, wide_ref, sems):
+    for which in range(2):
+
+        @pl.when(core == which)
+        def widen():
+            copies = Copies(sems)
+            for n in range(4):
+                rows = pl.ds(n * D, D)
+                wide_ref[rows, :] = half_ref[rows, :].astype(F32)
+                copies.start(wide_ref.at[rows], g2_out.at[rows] if which else g1_out.at[:, rows])
+            copies.wait()
+
+
+def near_half_kernel(side_ref, half_ref, g1_out, g2_out, wide_ref, sems):
+    widen_half(side_ref[0], half_ref, g1_out, g2_out, wide_ref, sems)
+
+
+def far_half_kernel(side_ref, half_ref, g1_in, g2_in, g1_out, g2_out, wide_ref, sems):
+    widen_half(1 - side_ref[0], half_ref, g1_out, g2_out, wide_ref, sems)
+
+
+def widen_near(sides, layer_half):
+    return pl.pallas_call(
+        near_half_kernel,
+        out_shape=[pltpu.HBM((D, FF), F32), pltpu.HBM((FF, D), F32)],
+        in_specs=[smem, vmem],
+        out_specs=[hbm, hbm],
+        scratch_shapes=[pltpu.VMEM((FF, D), F32), pltpu.SemaphoreType.DMA((4,))],
+        compiler_params=pltpu.CompilerParams(vmem_limit_bytes=8 * MIB),
+        cost_estimate=pl.CostEstimate(flops=10**9, bytes_accessed=MIB, transcendentals=0),
+    )(sides, layer_half)
+
+
+def widen_far(sides, other, first):
+    return pl.pallas_call(
+        far_half_kernel,
+        out_shape=[pltpu.HBM((D, FF), F32), pltpu.HBM((FF, D), F32)],
+        in_specs=[smem, vmem, hbm, hbm],
+        out_specs=[hbm, hbm],
+        input_output_aliases={2: 0, 3: 1},
+        scratch_shapes=[pltpu.VMEM((FF, D), F32), pltpu.SemaphoreType.DMA((4,))],
+        compiler_params=pltpu.CompilerParams(vmem_limit_bytes=8 * MIB),
+        cost_estimate=pl.CostEstimate(flops=10**9, bytes_accessed=MIB, transcendentals=0),
+    )(sides, other, *map(in_hbm, first))
 
 
 def last_kernel(
-    everyone, side_ref, mine_ref, other_ref, ada_in, qv_ref, rel_ref, out_bias_ref, ada_bias_ref,
-    gqkv_out, gada_out, table_out, go_out, gqkv_ref, gada_ref, table_ref, go_ref, ada_ref, sems,
+    everyone, side_ref, mine_ref, other_ref, ada_in, qv_ref, rel_ref, out_bias_ref, ada_bias_ref, bias1_ref,
+    bias2_ref, gqkv_out, gada_out, table_out, go_out, gqkv_ref, gada_ref, table_ref, go_ref, ada_ref, sems,
 ):
     get = halves_reader(side_ref, mine_ref, other_ref)
     copies = Copies(sems)
@@ -762,31 +792,41 @@
     gate = 1.0 / (1.0 + jnp.exp(-cond))
     act_t = (cond * gate).astype(BF16).T
     dmods = [get(4 * D + n * everyone, everyone) for n in range(6)]
-    for n in range(6):
-        cols = pl.ds(n * D, D)
-        gada_ref[:, cols] = mm(act_t, dmods[n])
-        copies.start(gada_ref.at[:, cols], gada_out.at[:, cols])
-        ada_bias_ref[cols] = jnp.sum(dmods[n].astype(F32), axis=0)
-    copies.made.pop(0).wait()
-    back = jnp.zeros((everyone, D), F32)
-    for n in range(6):
-        back = back + mm_t(dmods[n], ada_ref[:, n * D : (n + 1) * D])
-    back = gate * (1.0 + cond * (1.0 - gate)) * back
-    high = back.astype(BF16)
-    low = (back - high.astype(F32)).astype(BF16)
     small = get(4 * D + 7 * everyone, 16).astype(F32)
-    label = (small[5:6, :everyone] * GRID + small[5:6, 128 : 128 + everyone]).astype(jnp.int32)
-    classes = table_ref.shape[0]
-    wide = round_up(classes, 128)
-    hot = (label == lax.broadcasted_iota(jnp.int32, (wide, everyone), 0)).astype(F32).astype(BF16)
-    table_ref[...] = (mm(hot, high) + mm(hot, low))[:classes]
-    copies.start(table_ref, table_out)
+
+    def ada():
+        for n in range(6):
+            cols = pl.ds(n * D, D)
+            gada_ref[:, cols] = mm(act_t, dmods[n])
+            copies.start(gada_ref.at[:, cols], gada_out.at[:, cols])
+            ada_bias_ref[cols] = jnp.sum(dmods[n].astype(F32), axis=0)
+
+    def table():
+        copies.made.pop(0).wait()
+        back = jnp.zeros((everyone, D), F32)
+        for n in range(6):
+            back = back + mm_t(dmods[n], ada_ref[:, n * D : (n + 1) * D])
+        back = gate * (1.0 + cond * (1.0 - gate)) * back
+        high = back.astype(BF16)
+        low = (back - high.astype(F32)).astype(BF16)
+        label = (small[5:6, :everyone] * GRID + small[5:6, 128 : 128 + everyone]).astype(jnp.int32)
+        classes = table_ref.shape[0]
+        wide = round_up(classes, 128)
+        hot = (label == lax.broadcasted_iota(jnp.int32, (wide, everyone), 0)).astype(F32).astype(BF16)
+        table_ref[...] = (mm(hot, high) + mm(hot, low))[:classes]
+        copies.start(table_ref, table_out)
+
+    ada()
+    table()
     qv_ref[...] = small[:2]
     for part in range(2):
         for head in range(HEADS):
             at = 2 * GRID * head
             rel_ref[head, part : part + 1, :] = small[2 + part : 3 + part, at : at + 2 * GRID - 1]
     out_bias_ref[...] = small[4]
+    for n in range(4):
+        bias1_ref[pl.ds(n * D, D)] = small[6 + n]
+    bias2_ref[...] = small[10]
     copies.wait()
 
 
@@ -848,7 +888,7 @@
     a, b = pair[:, :cut], pair[:, cut:]
     a1, b1 = along_y(a), along_x(b)
     a, b = jnp.stack([a, a1]), jnp.stack([b, b1])
-    a, b, last_wide = lax.optimization_barrier((a, b, last_wide))
+    a, b = after((a, b), last_wide)
     a2, b2 = along_x(a), along_y(b)
     held = (a2, b2)
 
@@ -883,7 +923,7 @@
     classes = class_table.shape[0]
     dp_place, seq_place = lax.axis_index("dp"), lax.axis_index("seq")
 
-    half = round_up(FF + 16, dp * seq * 4)
+    half = round_up(FF, dp * seq * 4)
     peers = dp // 4 * seq
     side = dp_place % 2
     sides = side.astype(jnp.int32).reshape(1)
@@ -937,9 +977,12 @@
             [qaug, kaug, vaug, mask],
             away=4, copies=3 + 8 * HEADS, micros=10, limit=32,
         )
-        attended, hidden, du, keep, send = call(
+        attended, hidden, du, biases, keep, send = call(
             functools.partial(feed_kernel, slots),
-            [((rows, D), F32), ((rows, FF), BF16), ((rows, FF), BF16), ((half, D), BF16), ((half, D), BF16)],
+            [
+                ((rows, D), F32), ((rows, FF), BF16), ((rows, FF), BF16), ((8, D), F32), ((half, D), BF16),
+                ((half, D), BF16),
+            ],
             [((2, half, D), BF16)],
             [
                 scalars, mixed, x, grad_full[s], cot_slot, mod, out_weight, fc1_weight, fc2_weight, lines,
@@ -949,7 +992,7 @@
         kept_of.append(dict(
             rest=[
                 scalars, mixed, inverse, x, grad_full[s], cot_slot, mod, out_weight, fc1_weight, fc2_weight,
-                lines, attended, hidden, du,
+                lines, attended, hidden, du, biases,
             ],
             groups=[spread_far, qaug_far, kaug_far, vaug_far], sources=[whole, lowered, slot, qkv_weight],
             small=[scalars, kept, mod], keep=keep, send=send,
@@ -967,7 +1010,7 @@
         call(
             functools.partial(feed_rest_kernel, slots),
             [
-                ((8, D), F32), ((own, D), BF16), ((padded, D), BF16), ((rows, D), F32), ((rows, D), BF16),
+                ((16, D), F32), ((own, D), BF16), ((padded, D), BF16), ((rows, D), F32), ((rows, D), BF16),
                 ((HEADS, rows, 128), BF16), ((D, D), BF16),
             ],
             [((rows, D), BF16), ((rows, D), F32), ((HEADS, rows, 128), BF16), ((D, D), BF16)],
@@ -1018,24 +1061,22 @@
     out_full = jnp.stack([rest[1] for rest in rests])
     out_masked = jnp.stack([rest[2][:slots] for rest in rests])
     layer_half = assemble(*parts)
+    other = swap_cores(layer_half, dp)
+    first = widen_near(sides, layer_half)
     last_half = after(last_half, layer_half)
-    grad_fc1_bias, grad_fc2_bias, grad_fc1, grad_fc2 = call(
-        layer_kernel,
-        [((FF,), F32), ((D,), F32), ((D, FF), F32), ((FF, D), F32)],
-        [((D, FF), F32), ((FF, D), F32)],
-        [sides, layer_half, swap_cores(layer_half, dp)],
-        scalars=1, away=2, copies=8, micros=3,
-    )
-    grad_qv, grad_rel, grad_out_bias, grad_ada_bias, grad_qkv, grad_ada, grad_table, grad_out = call(
+    grad_fc1, grad_fc2 = widen_far(sides, other, first)
+    found = call(
         functools.partial(last_kernel, everyone),
         [
-            ((2, D), F32), ((HEADS, 2, 2 * GRID - 1), F32), ((D,), F32), ((6 * D,), F32),
+            ((2, D), F32), ((HEADS, 2, 2 * GRID - 1), F32), ((D,), F32), ((6 * D,), F32), ((FF,), F32), ((D,), F32),
             ((D, 3 * D), F32), ((D, 6 * D), F32), ((classes, D), F32), ((D, D), F32),
         ],
         [((D, 3 * D), F32), ((D, 6 * D), F32), ((classes, D), F32), ((D, D), F32), (ada_weight.shape, BF16)],
         [sides, last_half, swap_cores(last_half, dp), in_hbm(ada_weight)],
         scalars=1, far=1, away=4, copies=12, micros=4, limit=16,
     )
+    grad_qv, grad_rel, grad_out_bias, grad_ada_bias, grad_fc1_bias, grad_fc2_bias = found[:6]
+    grad_qkv, grad_ada, grad_table, grad_out = found[6:]
     grad_rel = grad_rel.transpose(1, 0, 2)
     grad_qkv, last_moved = lax.optimization_barrier((grad_qkv, last_moved))
     grad_input = []

time: 130 us -> 129 us (level)
  waiting for transfers between devices: 29.4 us -> 24.9 us
  starting transfers between devices: 30.4 us -> 33.9 us
    all_to_all x3, waiting for transfers between devices: 11.5 us -> 3.17 us  [exchange(): return lax.all_to_all(value, AXES, 0, 0, axis_index_groups=groups)]
    ppermute x2, waiting for transfers between devices: 7.12 us -> 0.05 us  [gather_chunks(): lax.ppermute(value, 'seq', [(n, n ^ 1) for n in range(seq)])]
    ppermute x2, waiting for transfers between devices: 3.79 us -> 10.3 us  [gather_chunks(): lax.ppermute(value, 'dp', [(n, n ^ 2) for n in range(dp)])]
    pallas_call x10 -> x9, Pallas kernels: 40 us -> 36.8 us  [call(): pl.pallas_call(kernel, out_shape=[jax.ShapeDtypeStruct(shape, dtype) for...]
    pallas_call x0 -> x2, Pallas kernels: none -> 2.95 us  [the longest x1 1.48 us: widen_far(): pl.pallas_call(far_half_kernel, out_shape=[pltpu.HBM((D, FF), F32), pltpu...]
    ppermute x2, waiting for transfers between devices: 2.73 us -> 5.55 us  [far_half(): lax.ppermute(near, 'dp', [(n, (n + dp // 2) % dp) for n in range(dp)])]
    ppermute x2, starting transfers between devices: 2.73 us -> 4.9 us  [far_half(): lax.ppermute(near, 'dp', [(n, (n + dp // 2) % dp) for n in range(dp)])]
    ppermute x1, waiting for transfers between devices: 0.22 us -> 2.13 us  [gather_chunks(): lax.ppermute(chunk, 'dp', [(n, n ^ 4) for n in range(dp)])]
  transfers between devices with their start and end apart: 17 -> 17, of which waited for: 11 -> 6; matrix products, arithmetic and copies ran while one was open for 0% -> 0% of each run, Pallas kernels for 31% -> 31%
where the time goes in v6:
time: 129 us; the launch traced here: 128 us
  Pallas kernels  64.3 us (50%)
  starting transfers between devices  33.9 us (26%)
  waiting for transfers between devices  24.9 us (19%)
  between operations  3.59 us (3%)
  other arithmetic  1.41 us (1%)
    pallas_call x9, Pallas kernels, call(): pl.pallas_call(kernel, out_shape=[jax.ShapeDtypeStruct(shape, dtype) for...  36.8 us
    pallas_call x1, Pallas kernels, back_call(): pl.pallas_call(functools.partial(back_kernel, own, everyone), grid=(group...  19.7 us
    all_to_all x3, starting transfers between devices, exchange(): return lax.all_to_all(value, AXES, 0, 0, axis_index_groups=groups)  13.7 us
    ppermute x2, waiting for transfers between devices, gather_chunks(): lax.ppermute(value, 'dp', [(n, n ^ 2) for n in range(dp)])  10.3 us
    ppermute x2, waiting for transfers between devices, far_half(): lax.ppermute(near, 'dp', [(n, (n + dp // 2) % dp) for n in range(dp)])  5.55 us
    ppermute x2, starting transfers between devices, far_half(): lax.ppermute(near, 'dp', [(n, (n + dp // 2) % dp) for n in range(dp)])  4.9 us
    pallas_call x1, Pallas kernels, own_call(): pl.pallas_call(own_kernel, out_shape=[jax.ShapeDtypeStruct(shape, dtype)...  4.89 us
    ppermute x2, starting transfers between devices, gather_chunks(): lax.ppermute(value, 'dp', [(n, n ^ 2) for n in range(dp)])  3.54 us
  transfers between devices with their start and end apart: 17, of which 6 were waited for; matrix products, arithmetic and copies ran while one was open for 0% of the time, Pallas kernels for 31%

profile of v6, /device:TPU:0, one launch (start us, length us, event | category | flops | bytes accessed | tf_op | source)
XLA Modules:
  0.0 128.2 jit_solution(11607723170739112169)
XLA Ops:
  0.6 3.0 %collective-permute-start = (bf16[512,384]{1,0:T(8,128)(2,1)}, bf16[512,384]{1,0:T(8,128)(2,1)S(1)}, u32[]{:S(2)}, u32[]{:S(2)}) collective-permute-start(bf16[512,384]{1,0:T(8,128)(2,1)} %bitcast.28), channel_id=1, source_target_pairs={{0,1},{1,0},{2,3},{3,2},{4,5},{5,4},{6,7},{7,6},{8,9},{9,8},{10,11... | collective-permute-start | bytes 1179656 | tf_op jit(solution)/shard_map/ppermute | solution.py:935
  6.3 0.0 copy-start.2
  6.3 0.0 copy-start.3
  6.3 4.9 %shard_map.307 = (s32[10]{0:T(128)S(1)}, s32[704,1]{1,0:T(8,128)S(1)}, f32[16,384]{1,0:T(8,128)S(1)}, f32[8,384]{1,0:T(8,128)S(1)}, bf16[512,384]{1,0:T(8,128)(2...) custom-call(s32[10]{0:T(128)S(1)} %compare_select_fusion.6.start_ref, ...), custom_call_target="tpu_custom_call" | custom-call | flops 3000000000 | bytes 1048576 | tf_op jit(solution)/shard_map/pallas_call | solution.py:636
  11.2 1.8 %collective-permute-done.refs_1_ = bf16[512,384]{1,0:T(8,128)(2,1)S(1)} collective-permute-done((bf16[512,384]{1,0:T(8,128)(2,1)}, bf16[512,384]{1,0:T(8,128)(2,1)S(1)}, u32[]{:S(2)}, u32[]{:S(2)}) %collective-permute-start) | collective-permute-done | bytes 393248 | tf_op jit(solution)/shard_map/ppermute | solution.py:935
  13.0 3.6 %shard_map.308 = (bf16[6,864,128]{2,1,0:T(8,128)(2,1)S(1)}, bf16[6,1024,128]{2,1,0:T(8,128)(2,1)S(1)}, bf16[6,1024,128]{2,1,0:T(8,128)(2,1)S(1)}, bf16[864,384]{...) custom-call(s32[10]{0:T(128)S(1)} %get-tuple-element.89.scalar_ref, ...), custom_call_target="tpu_custom_call" | custom-call | flops 3000000000 | bytes 1048576 | tf_op jit(solution)/shard_map/pallas_call | solution.py:623
  16.7 0.0 copy-start
  16.7 0.0 copy-start.1
  16.7 0.0 copy-start.4
  16.7 0.0 copy-start.5
  16.7 0.0 copy-start.6
  16.7 9.6 %shard_map.309 = (f32[3,864,128]{2,1,0:T(8,128)S(1)}, f32[3,864,128]{2,1,0:T(8,128)S(1)}, bf16[6,864,1024]{2,1,0:T(8,128)(2,1)}, bf16[6,864,128]{2,1,0:T(8,128)(...) custom-call(bf16[6,864,128]{2,1,0:T(8,128)(2,1)S(1)} %get-tuple-element.99.qaug_ref, ...), custom_call_target="tpu_custom_call" | custom-call | flops 10000000000 | bytes 1048576 | tf_op jit(solution)/shard_map/pallas_call | solution.py:623
  26.4 8.8 %shard_map.310 = (f32[864,384]{1,0:T(8,128)S(1)}, bf16[864,1536]{1,0:T(8,128)(2,1)S(1)}, bf16[864,1536]{1,0:T(8,128)(2,1)S(1)}, f32[8,384]{1,0:T(8,128)S(1)}, bf...) custom-call(s32[10]{0:T(128)S(1)} %get-tuple-element.89.scalar_ref, ...), custom_call_target="tpu_custom_call" | custom-call | flops 10000000000 | bytes 1048576 | tf_op jit(solution)/shard_map/pallas_call | solution.py:623
  35.2 0.1 collective-permute-start.1
  35.3 6.2 %shard_map.312 = (f32[16,384]{1,0:T(8,128)S(1)}, bf16[512,384]{1,0:T(8,128)(2,1)}, bf16[352,384]{1,0:T(8,128)(2,1)}, f32[864,384]{1,0:T(8,128)}, bf16[864,384]{1...) custom-call(s32[10]{0:T(128)S(1)} %get-tuple-element.89.scalar_ref, ...), custom_call_target="tpu_custom_call" | custom-call | flops 6000000000 | bytes 1048576 | tf_op jit(solution)/shard_map/pallas_call | solution.py:623
  41.6 1.1 shard_map.311
  42.7 5.0 %all-to-all-start = ((bf16[8,192,384]{2,1,0:T(8,128)(2,1)}), bf16[8,192,384]{2,1,0:T(8,128)(2,1)S(1)}, u32[]{:S(2)}, u32[]{:S(2)}) async-start(bf16[8,192,384]{2,1,0:T(8,128)(2,1)} %bitcast.37), calls=%async_computation | async-start | bytes 2359296 | tf_op jit(solution)/shard_map/all_to_all | solution.py:843
  47.7 19.7 %shard_map.313 = (bf16[832,384]{1,0:T(8,128)(2,1)S(1)}, bf16[832,384]{1,0:T(8,128)(2,1)S(1)}, bf16[1,512,384]{2,1,0:T(8,128)(2,1)}, f32[512,384]{1,0:T(8,128)}) custom-call(s32[10]{0:T(128)S(1)} %get-tuple-element.89.scalar_ref, s32[704,1]{1,0:T(8,128)S(1)} %get-tuple-element.96.refs_8_.kept_ref, f32[8,384]{1,0:T(8,128)S(1)} %get-tuple-element.97.refs_9_.mod_ref, ...), custom_call_target="tpu_custom_call" | custom-call | flops 17999998976 | bytes 1048576 | tf_op jit(solution)/shard_map/pallas_call | solution.py:701
  67.4 0.3 collective-permute-start.3
  67.6 1.9 %collective-permute-done.3.right_ref = bf16[832,384]{1,0:T(8,128)(2,1)S(1)} collective-permute-done((bf16[832,384]{1,0:T(8,128)(2,1)S(1)}, bf16[832,384]{1,0:T(8,128)(2,1)S(1)}, u32[]{:S(2)}, u32[]{:S(2)}) %collective-permute-start.3) | collective-permute-done | bytes 639008 | tf_op jit(solution)/shard_map/ppermute | solution.py:834
  69.5 0.9 shard_map.314
  70.4 0.0 copy-start.8
  70.4 5.2 %all-to-all-start.1 = ((bf16[8,104,384]{2,1,0:T(8,128)(2,1)}), bf16[8,104,384]{2,1,0:T(8,128)(2,1)S(1)}, u32[]{:S(2)}, u32[]{:S(2)}) async-start(bf16[8,104,384]{2,1,0:T(8,128)(2,1)} %bitcast.38), calls=%async_computation.1 | async-start | bytes 1277952 | tf_op jit(solution)/shard_map/all_to_all | solution.py:843
  75.7 0.2 reduce_sum.25
  75.8 2.7 %collective-permute-start.5 = (bf16[192,384]{1,0:T(8,128)(2,1)S(1)}, bf16[192,384]{1,0:T(8,128)(2,1)S(1)}, u32[]{:S(2)}, u32[]{:S(2)}) collective-permute-start(bf16[192,384]{1,0:T(8,128)(2,1)S(1)} %reduce_sum.25), channel_id=1, source_target_pairs={{0,16},{2,18},{4,20},{6,22},{8,24},{10,26},{12,28},{14,30},{16,0},... | collective-permute-start | bytes 442376 | tf_op jit(solution)/shard_map/ppermute | solution.py:851
  78.5 2.1 %collective-permute-start.2 = (bf16[256,384]{1,0:T(8,128)(2,1)S(1)}, bf16[256,384]{1,0:T(8,128)(2,1)S(1)}, u32[]{:S(2)}, u32[]{:S(2)}) collective-permute-start(bf16[256,384]{1,0:T(8,128)(2,1)S(1)} %get-tuple-element.164), channel_id=1, source_target_pairs={{0,1},{1,0},{2,3},{3,2},{4,5},{5,4},{6,7},{7,6},{8,9},{9,8},{10,11... | collective-permute-start | bytes 589832 | tf_op jit(solution)/shard_map/ppermute | solution.py:906
  80.6 5.5 %collective-permute-done.5 = bf16[192,384]{1,0:T(8,128)(2,1)S(1)} collective-permute-done((bf16[192,384]{1,0:T(8,128)(2,1)S(1)}, bf16[192,384]{1,0:T(8,128)(2,1)S(1)}, u32[]{:S(2)}, u32[]{:S(2)}) %collective-permute-start.5) | collective-permute-done | bytes 147488 | tf_op jit(solution)/shard_map/ppermute | solution.py:851
  86.2 3.2 %all-to-all-done.1 = bf16[8,104,384]{2,1,0:T(8,128)(2,1)S(1)} async-done(((bf16[8,104,384]{2,1,0:T(8,128)(2,1)}), bf16[8,104,384]{2,1,0:T(8,128)(2,1)S(1)}, u32[]{:S(2)}, u32[]{:S(2)}) %all-to-all-start.1) | async-done | bytes 639008 | tf_op jit(solution)/shard_map/all_to_all | solution.py:843
  89.4 0.1 reduce_sum.24.near_ref
  89.5 1.7 %collective-permute-start.6 = (bf16[192,384]{1,0:T(8,128)(2,1)S(1)}, bf16[192,384]{1,0:T(8,128)(2,1)S(1)}, u32[]{:S(2)}, u32[]{:S(2)}) collective-permute-start(bf16[192,384]{1,0:T(8,128)(2,1)S(1)} %add_convert_fusion), channel_id=1, source_target_pairs={{0,8},{2,10},{4,12},{6,14},{8,0},{10,2},{12,4},{14,6},{16,24},{18,... | collective-permute-start | bytes 442376 | tf_op jit(solution)/shard_map/ppermute | solution.py:887
  91.2 2.2 %collective-permute-start.4 = (bf16[104,384]{1,0:T(8,128)(2,1)S(1)}, bf16[104,384]{1,0:T(8,128)(2,1)S(1)}, u32[]{:S(2)}, u32[]{:S(2)}) collective-permute-start(bf16[104,384]{1,0:T(8,128)(2,1)S(1)} %reduce_sum.24.near_ref), channel_id=1, source_target_pairs={{0,16},{2,18},{4,20},{6,22},{8,24},{10,26},{12,28},{14,30},{16,0},... | collective-permute-start | bytes 239624 | tf_op jit(solution)/shard_map/ppermute | solution.py:851
  93.4 2.1 %collective-permute-done.6 = bf16[192,384]{1,0:T(8,128)(2,1)S(1)} collective-permute-done((bf16[192,384]{1,0:T(8,128)(2,1)S(1)}, bf16[192,384]{1,0:T(8,128)(2,1)S(1)}, u32[]{:S(2)}, u32[]{:S(2)}) %collective-permute-start.6) | collective-permute-done | bytes 147488 | tf_op jit(solution)/shard_map/ppermute | solution.py:887
  95.6 1.1 collective-permute-start.7
  96.7 1.5 %collective-permute-start.8 = (bf16[2,96,384]{2,1,0:T(8,128)(2,1)S(1)}, bf16[2,96,384]{2,1,0:T(8,128)(2,1)S(1)}, u32[]{:S(2)}, u32[]{:S(2)}) collective-permute-start(bf16[2,96,384]{2,1,0:T(8,128)(2,1)S(1)} %get-tuple-element.165), channel_id=1, source_target_pairs={{0,4},{2,6},{4,0},{6,2},{8,12},{10,14},{12,8},{14,10},{16,20},{18,... | collective-permute-start | bytes 442376 | tf_op jit(solution)/shard_map/ppermute | solution.py:883
  98.2 0.9 shard_map.315
  99.1 3.6 %all-to-all-start.2 = ((bf16[8,104,384]{2,1,0:T(8,128)(2,1)}), bf16[8,104,384]{2,1,0:T(8,128)(2,1)S(1)}, u32[]{:S(2)}, u32[]{:S(2)}) async-start(bf16[8,104,384]{2,1,0:T(8,128)(2,1)} %shard_map.315), calls=%async_computation.2 | async-start | bytes 1277952 | tf_op jit(solution)/shard_map/all_to_all | solution.py:843
  102.7 2.1 %collective-permute-start.9 = (bf16[2,2,96,384]{3,2,1,0:T(8,128)(2,1)S(1)}, bf16[2,2,96,384]{3,2,1,0:T(8,128)(2,1)S(1)}, u32[]{:S(2)}, u32[]{:S(2)}) collective-permute-start(bf16[2,2,96,384]{3,2,1,0:T(8,128)(2,1)S(1)} %pad_maximum_fusion.1), channel_id=1, source_target_pairs={{0,4},{2,6},{4,0},{6,2},{8,12},{10,14},{12,8},{14,10},{16,20},{18,... | collective-permute-start | bytes 884744 | tf_op jit(solution)/shard_map/ppermute | solution.py:883
  104.8 1.5 %collective-permute-start.10 = (bf16[2,2,96,384]{3,2,1,0:T(8,128)(2,1)S(1)}, bf16[2,2,96,384]{3,2,1,0:T(8,128)(2,1)S(1)}, u32[]{:S(2)}, u32[]{:S(2)}) collective-permute-start(bf16[2,2,96,384]{3,2,1,0:T(8,128)(2,1)S(1)} %pad_maximum_fusion.2), channel_id=1, source_target_pairs={{0,1},{1,0},{2,3},{3,2},{4,5},{5,4},{6,7},{7,6},{8,9},{9,8},{10,11... | collective-permute-start | bytes 884744 | tf_op jit(solution)/shard_map/ppermute | solution.py:884
  106.3 10.3 %collective-permute-done.9.a2_ref = bf16[2,2,96,384]{3,2,1,0:T(8,128)(2,1)S(1)} collective-permute-done((bf16[2,2,96,384]{3,2,1,0:T(8,128)(2,1)S(1)}, bf16[2,2,96,384]{3,2,1,0:T(8,128)(2,1)S(1)}, u32[]{:S(2)}, u32[]{:S(2)}) %collective-permute-start.9) | collective-permute-done | bytes 294944 | tf_op jit(solution)/shard_map/ppermute | solution.py:883
  116.6 0.0 collective-permute-done.10.b2_ref
  116.7 0.1 shard_map.316.half_ref
  116.8 0.1 collective-permute-start.13
  116.9 0.5 collective-permute-start.11
  117.3 1.4 %collective-permute-start.12 = (bf16[256,384]{1,0:T(8,128)(2,1)S(1)}, bf16[256,384]{1,0:T(8,128)(2,1)S(1)}, u32[]{:S(2)}, u32[]{:S(2)}) collective-permute-start(bf16[256,384]{1,0:T(8,128)(2,1)S(1)} %get-tuple-element.163), channel_id=1, source_target_pairs={{0,1},{1,0},{2,3},{3,2},{4,5},{5,4},{6,7},{7,6},{8,9},{9,8},{10,11... | collective-permute-start | bytes 589832 | tf_op jit(solution)/shard_map/ppermute | solution.py:906
  118.8 1.5 %shard_map.318 = (f32[384,1536]{1,0:T(8,128)}, f32[1536,384]{1,0:T(8,128)}) custom-call(s32[1]{0:T(128)} %bitcast.7.side_ref, bf16[1536,384]{1,0:T(8,128)(2,1)S(1)} %shard_map.316.half_ref), custom_call_target="tpu_custom_call" | custom-call | flops 1000000000 | bytes 1048576 | tf_op jit(solution)/shard_map/pallas_call | solution.py:754
  120.3 1.5 %shard_map.319 = (f32[384,1536]{1,0:T(8,128)}, f32[1536,384]{1,0:T(8,128)}) custom-call(s32[1]{0:T(128)} %bitcast.7.side_ref, bf16[1536,384]{1,0:T(8,128)(2,1)S(1)} %collective-permute-done.13.half_ref, f32[384,1536]{1,0:T(8,128)} %get-tuple-element.157.g1_in, f32[1536,384]{1,0:T(8,128)} %get-tuple-element.158.g2_in), custom_call_target="tpu_custom_call", output_to_operand_aliasing={{0}: (2, {}), {1}: (3, {})} | custom-call | flops 1000000000 | bytes 1048576 | tf_op jit(solution)/shard_map/pallas_call | solution.py:766
  121.8 5.4 %shard_map.317 = (f32[2,384]{1,0:T(2,128)}, f32[6,2,63]{2,1,0:T(2,128)}, f32[384]{0:T(512)}, f32[2304]{0:T(1024)}, f32[1536]{0:T(1024)}, /*index=5*/f32[384]{0:T...) custom-call(s32[1]{0:T(128)} %bitcast.7.side_ref, ...), custom_call_target="tpu_custom_call" | custom-call | flops 4000000000 | bytes 1048576 | tf_op jit(solution)/shard_map/pallas_call | solution.py:623
  127.2 1.0 add_bitcast_fusion
  (27 shorter events, 0.3 us)
Async XLA Ops:
  0.6 12.4 %collective-permute-start = (bf16[512,384]{1,0:T(8,128)(2,1)}, bf16[512,384]{1,0:T(8,128)(2,1)S(1)}, u32[]{:S(2)}, u32[]{:S(2)}) collective-permute-start(bf16[512,384]{1,0:T(8,128)(2,1)} %bitcast.28), channel_id=1, source_target_pairs={{0,1},{1,0},{2,3},{3,2},{4,5},{5,4},{6,7},{7,6},{8,9},{9,8},{10,11... | collective-permute-start | bytes 1179656 | tf_op jit(solution)/shard_map/ppermute | solution.py:935
  6.3 6.7 %copy-start.2 = (bf16[384,1152]{1,0:T(8,128)(2,1)S(1)}, bf16[384,1152]{1,0:T(8,128)(2,1)}, u32[]{:S(2)}) copy-start(bf16[384,1152]{1,0:T(8,128)(2,1)} %refs_9_.1) | copy-start | bytes 2654212
  6.3 6.7 %copy-start.3 = (bf16[1,512,384]{2,1,0:T(8,128)(2,1)S(1)}, bf16[1,512,384]{2,1,0:T(8,128)(2,1)}, u32[]{:S(2)}) copy-start(bf16[1,512,384]{2,1,0:T(8,128)(2,1)} %param.20) | copy-start | bytes 1179652
  16.7 9.7 %copy-start = (bf16[384,1536]{1,0:T(8,128)(2,1)S(1)}, bf16[384,1536]{1,0:T(8,128)(2,1)}, u32[]{:S(2)}) copy-start(bf16[384,1536]{1,0:T(8,128)(2,1)} %w1_ref.3) | copy-start | bytes 3538948
  16.7 9.7 %copy-start.1 = (bf16[1536,384]{1,0:T(8,128)(2,1)S(1)}, bf16[1536,384]{1,0:T(8,128)(2,1)}, u32[]{:S(2)}) copy-start(bf16[1536,384]{1,0:T(8,128)(2,1)} %w2_ref.3) | copy-start | bytes 3538948
  16.7 9.7 %copy-start.4 = (bf16[1,512,384]{2,1,0:T(8,128)(2,1)S(1)}, bf16[1,512,384]{2,1,0:T(8,128)(2,1)}, u32[]{:S(2)}) copy-start(bf16[1,512,384]{2,1,0:T(8,128)(2,1)} %param.38) | copy-start | bytes 1179652
  16.7 9.7 %copy-start.5 = (bf16[384,384]{1,0:T(8,128)(2,1)S(1)}, bf16[384,384]{1,0:T(8,128)(2,1)}, u32[]{:S(2)}) copy-start(bf16[384,384]{1,0:T(8,128)(2,1)} %wout_ref.3) | copy-start | bytes 884740
  16.7 9.7 %copy-start.6 = (bf16[1,352,384]{2,1,0:T(8,128)(2,1)S(1)}, bf16[1,352,384]{2,1,0:T(8,128)(2,1)}, u32[]{:S(2)}) copy-start(bf16[1,352,384]{2,1,0:T(8,128)(2,1)} %param.39) | copy-start | bytes 811012
  35.2 6.3 %collective-permute-start.1 = (bf16[1536,384]{1,0:T(8,128)(2,1)S(1)}, bf16[1536,384]{1,0:T(8,128)(2,1)S(1)}, u32[]{:S(2)}, u32[]{:S(2)}) collective-permute-start(bf16[1536,384]{1,0:T(8,128)(2,1)S(1)} %get-tuple-element.106), channel_id=1, source_target_pairs={{0,2},{2,0},{4,6},{6,4},{8,10},{10,8},{12,14},{14,12},{16,18},{18,... | collective-permute-start | bytes 3538952 | tf_op jit(solution)/shard_map/ppermute | solution.py:834
  42.7 24.7 %all-to-all-start = ((bf16[8,192,384]{2,1,0:T(8,128)(2,1)}), bf16[8,192,384]{2,1,0:T(8,128)(2,1)S(1)}, u32[]{:S(2)}, u32[]{:S(2)}) async-start(bf16[8,192,384]{2,1,0:T(8,128)(2,1)} %bitcast.37), calls=%async_computation | async-start | bytes 2359296 | tf_op jit(solution)/shard_map/all_to_all | solution.py:843
  67.4 2.1 %collective-permute-start.3 = (bf16[832,384]{1,0:T(8,128)(2,1)S(1)}, bf16[832,384]{1,0:T(8,128)(2,1)S(1)}, u32[]{:S(2)}, u32[]{:S(2)}) collective-permute-start(bf16[832,384]{1,0:T(8,128)(2,1)S(1)} %get-tuple-element.140), channel_id=1, source_target_pairs={{0,2},{2,0},{4,6},{6,4},{8,10},{10,8},{12,14},{14,12},{16,18},{18,... | collective-permute-start | bytes 1916936 | tf_op jit(solution)/shard_map/ppermute | solution.py:834
  70.4 8.1 %copy-start.8 = (bf16[1,512,384]{2,1,0:T(8,128)(2,1)S(1)}, bf16[1,512,384]{2,1,0:T(8,128)(2,1)}, u32[]{:S(2)}) copy-start(bf16[1,512,384]{2,1,0:T(8,128)(2,1)} %get-tuple-element.134) | copy-start | bytes 1179652
  70.4 18.9 %all-to-all-start.1 = ((bf16[8,104,384]{2,1,0:T(8,128)(2,1)}), bf16[8,104,384]{2,1,0:T(8,128)(2,1)S(1)}, u32[]{:S(2)}, u32[]{:S(2)}) async-start(bf16[8,104,384]{2,1,0:T(8,128)(2,1)} %bitcast.38), calls=%async_computation.1 | async-start | bytes 1277952 | tf_op jit(solution)/shard_map/all_to_all | solution.py:843
  75.8 10.3 %collective-permute-start.5 = (bf16[192,384]{1,0:T(8,128)(2,1)S(1)}, bf16[192,384]{1,0:T(8,128)(2,1)S(1)}, u32[]{:S(2)}, u32[]{:S(2)}) collective-permute-start(bf16[192,384]{1,0:T(8,128)(2,1)S(1)} %reduce_sum.25), channel_id=1, source_target_pairs={{0,16},{2,18},{4,20},{6,22},{8,24},{10,26},{12,28},{14,30},{16,0},... | collective-permute-start | bytes 442376 | tf_op jit(solution)/shard_map/ppermute | solution.py:851
  78.5 10.9 %collective-permute-start.2 = (bf16[256,384]{1,0:T(8,128)(2,1)S(1)}, bf16[256,384]{1,0:T(8,128)(2,1)S(1)}, u32[]{:S(2)}, u32[]{:S(2)}) collective-permute-start(bf16[256,384]{1,0:T(8,128)(2,1)S(1)} %get-tuple-element.164), channel_id=1, source_target_pairs={{0,1},{1,0},{2,3},{3,2},{4,5},{5,4},{6,7},{7,6},{8,9},{9,8},{10,11... | collective-permute-start | bytes 589832 | tf_op jit(solution)/shard_map/ppermute | solution.py:906
  89.5 6.1 %collective-permute-start.6 = (bf16[192,384]{1,0:T(8,128)(2,1)S(1)}, bf16[192,384]{1,0:T(8,128)(2,1)S(1)}, u32[]{:S(2)}, u32[]{:S(2)}) collective-permute-start(bf16[192,384]{1,0:T(8,128)(2,1)S(1)} %add_convert_fusion), channel_id=1, source_target_pairs={{0,8},{2,10},{4,12},{6,14},{8,0},{10,2},{12,4},{14,6},{16,24},{18,... | collective-permute-start | bytes 442376 | tf_op jit(solution)/shard_map/ppermute | solution.py:887
  91.2 7.0 %collective-permute-start.4 = (bf16[104,384]{1,0:T(8,128)(2,1)S(1)}, bf16[104,384]{1,0:T(8,128)(2,1)S(1)}, u32[]{:S(2)}, u32[]{:S(2)}) collective-permute-start(bf16[104,384]{1,0:T(8,128)(2,1)S(1)} %reduce_sum.24.near_ref), channel_id=1, source_target_pairs={{0,16},{2,18},{4,20},{6,22},{8,24},{10,26},{12,28},{14,30},{16,0},... | collective-permute-start | bytes 239624 | tf_op jit(solution)/shard_map/ppermute | solution.py:851
  95.6 7.0 %collective-permute-start.7 = (bf16[2,96,384]{2,1,0:T(8,128)(2,1)S(1)}, bf16[2,96,384]{2,1,0:T(8,128)(2,1)S(1)}, u32[]{:S(2)}, u32[]{:S(2)}) collective-permute-start(bf16[2,96,384]{2,1,0:T(8,128)(2,1)S(1)} %get-tuple-element.166), channel_id=1, source_target_pairs={{0,1},{1,0},{2,3},{3,2},{4,5},{5,4},{6,7},{7,6},{8,9},{9,8},{10,11... | collective-permute-start | bytes 442376 | tf_op jit(solution)/shard_map/ppermute | solution.py:884
  96.7 6.0 %collective-permute-start.8 = (bf16[2,96,384]{2,1,0:T(8,128)(2,1)S(1)}, bf16[2,96,384]{2,1,0:T(8,128)(2,1)S(1)}, u32[]{:S(2)}, u32[]{:S(2)}) collective-permute-start(bf16[2,96,384]{2,1,0:T(8,128)(2,1)S(1)} %get-tuple-element.165), channel_id=1, source_target_pairs={{0,4},{2,6},{4,0},{6,2},{8,12},{10,14},{12,8},{14,10},{16,20},{18,... | collective-permute-start | bytes 442376 | tf_op jit(solution)/shard_map/ppermute | solution.py:883
  99.1 17.8 %all-to-all-start.2 = ((bf16[8,104,384]{2,1,0:T(8,128)(2,1)}), bf16[8,104,384]{2,1,0:T(8,128)(2,1)S(1)}, u32[]{:S(2)}, u32[]{:S(2)}) async-start(bf16[8,104,384]{2,1,0:T(8,128)(2,1)} %shard_map.315), calls=%async_computation.2 | async-start | bytes 1277952 | tf_op jit(solution)/shard_map/all_to_all | solution.py:843
  102.7 13.9 %collective-permute-start.9 = (bf16[2,2,96,384]{3,2,1,0:T(8,128)(2,1)S(1)}, bf16[2,2,96,384]{3,2,1,0:T(8,128)(2,1)S(1)}, u32[]{:S(2)}, u32[]{:S(2)}) collective-permute-start(bf16[2,2,96,384]{3,2,1,0:T(8,128)(2,1)S(1)} %pad_maximum_fusion.1), channel_id=1, source_target_pairs={{0,4},{2,6},{4,0},{6,2},{8,12},{10,14},{12,8},{14,10},{16,20},{18,... | collective-permute-start | bytes 884744 | tf_op jit(solution)/shard_map/ppermute | solution.py:883
  104.8 11.8 %collective-permute-start.10 = (bf16[2,2,96,384]{3,2,1,0:T(8,128)(2,1)S(1)}, bf16[2,2,96,384]{3,2,1,0:T(8,128)(2,1)S(1)}, u32[]{:S(2)}, u32[]{:S(2)}) collective-permute-start(bf16[2,2,96,384]{3,2,1,0:T(8,128)(2,1)S(1)} %pad_maximum_fusion.2), channel_id=1, source_target_pairs={{0,1},{1,0},{2,3},{3,2},{4,5},{5,4},{6,7},{7,6},{8,9},{9,8},{10,11... | collective-permute-start | bytes 884744 | tf_op jit(solution)/shard_map/ppermute | solution.py:884
  116.8 3.5 %collective-permute-start.13 = (bf16[1536,384]{1,0:T(8,128)(2,1)S(1)}, bf16[1536,384]{1,0:T(8,128)(2,1)S(1)}, u32[]{:S(2)}, u32[]{:S(2)}) collective-permute-start(bf16[1536,384]{1,0:T(8,128)(2,1)S(1)} %shard_map.316.half_ref), channel_id=1, source_target_pairs={{0,2},{2,0},{4,6},{6,4},{8,10},{10,8},{12,14},{14,12},{16,18},{18,... | collective-permute-start | bytes 3538952 | tf_op jit(solution)/shard_map/ppermute | solution.py:834
  116.9 4.9 %collective-permute-start.11 = (bf16[832,384]{1,0:T(8,128)(2,1)S(1)}, bf16[832,384]{1,0:T(8,128)(2,1)S(1)}, u32[]{:S(2)}, u32[]{:S(2)}) collective-permute-start(bf16[832,384]{1,0:T(8,128)(2,1)S(1)} %bitcast.24), channel_id=1, source_target_pairs={{0,2},{2,0},{4,6},{6,4},{8,10},{10,8},{12,14},{14,12},{16,18},{18,... | collective-permute-start | bytes 1916936 | tf_op jit(solution)/shard_map/ppermute | solution.py:834
  117.3 9.8 %collective-permute-start.12 = (bf16[256,384]{1,0:T(8,128)(2,1)S(1)}, bf16[256,384]{1,0:T(8,128)(2,1)S(1)}, u32[]{:S(2)}, u32[]{:S(2)}) collective-permute-start(bf16[256,384]{1,0:T(8,128)(2,1)S(1)} %get-tuple-element.163), channel_id=1, source_target_pairs={{0,1},{1,0},{2,3},{3,2},{4,5},{5,4},{6,7},{7,6},{8,9},{9,8},{10,11... | collective-permute-start | bytes 589832 | tf_op jit(solution)/shard_map/ppermute | solution.py:906
  121.7 5.5 %copy-start.7 = (f32[512,384]{1,0:T(8,128)S(1)}, f32[512,384]{1,0:T(8,128)}, u32[]{:S(2)}) copy-start(f32[512,384]{1,0:T(8,128)} %get-tuple-element.133) | copy-start | bytes 2359300

commit v7 on v6

--- a/solution.py
+++ b/solution.py
@@ -294,8 +294,8 @@
     copies.start(qaug_ref, qaug_out)
     copies.start(kaug_ref, kaug_out)
     copies.start(vaug_ref, vaug_out)
-    spans = [(at, size, False) for at, size in blocks_of(0, own, 256)]
-    spans += [(at, size, True) for at, size in blocks_of(own, rows - own, 256)]
+    spans = [(at, size, False) for at, size in blocks_of(0, own, 512)]
+    spans += [(at, size, True) for at, size in blocks_of(own, rows - own, 512)]
     items = [(side, *span) for side in range(2) for span in spans]
 
     def e_copy(head, n):
@@ -484,11 +484,11 @@
 def back_kernel(own, everyone, scalar_ref, kept_ref, mod_ref, prior_ref, *refs):
     group_sources, refs = refs[:5], refs[5:]
     sources, refs = refs[:7], refs[7:]
-    keep_ref, send_ref, dx_ref, dx_own_ref, refs = *refs[:4], refs[4:]
+    keep_ref, send_ref, dx_out, dx_own_out, refs = *refs[:4], refs[4:]
     group_local, refs = refs[:5], refs[5:]
     local, refs = refs[:7], refs[7:]
     dq_ref, dk_ref, dv_ref, tab_ref, normed_ref, inverse_ref, dxs_ref, dkt_ref, dvt_ref, pay_ref = refs[:10]
-    place_ref, part_ref, group_sems, sems, pay_sems = refs[10:]
+    place_ref, part_ref, dx_ref, dx_own_ref, group_sems, sems, pay_sems = refs[10:]
     tok_ref, a_ref, x_ref, slot_ref, weight_ref, dm_ref, go_ref = local
     step = pl.program_id(0)
     last = pl.num_programs(0) - 1
@@ -576,6 +576,9 @@
         others = dx_ref.shape[0]
         for n in range(others):
             dx_ref[n] = dxs_ref[row_span(scalar_ref, STARTS + 1 + others + n, own), :].astype(BF16)
+        halves = Copies(pay_sems)
+        halves.start(dx_own_ref, dx_own_out)
+        halves.start(dx_ref, dx_out)
         rel = table_sums([tab_ref[n] for n in range(groups)])
         first = jnp.where(scalar_ref[SEQ_PLACE] == 0, 1, 0)
         label = scalar_ref[LABEL]
@@ -598,7 +601,6 @@
         after = row - 7 * everyone
         wanted = jnp.where(after < 0, wanted, jnp.where(after < 11, after + 6, -1))
         pay_ref[4 * D :, :] = mm((lane == wanted).astype(F32).astype(BF16), smalls).astype(BF16)
-        halves = Copies(pay_sems)
         split_halves(halves, scalar_ref[SIDE], pay_ref, keep_ref, send_ref)
         halves.wait()
 
@@ -695,7 +697,7 @@
         ((groups, rows, 128), BF16), ((groups, total, 128), BF16), ((groups, total, 128), BF16),
         ((groups, 2 * GRID, 128), F32), ((total, D), F32), ((total, 128), F32), ((total, D), F32),
         ((128, total), F32), ((128, total), F32), ((2 * tail_half, D), BF16),
-        ((2 * GRID, rows), BF16), ((rows, 128), BF16),
+        ((2 * GRID, rows), BF16), ((rows, 128), BF16), outs[2], outs[3],
     ]
     small = [kept, mod, prior]
     return pl.pallas_call(
@@ -704,9 +706,9 @@
         out_shape=[jax.ShapeDtypeStruct(shape, dtype) for shape, dtype in outs[:2]]
         + [pltpu.HBM(shape, dtype) for shape, dtype in outs[2:]],
         in_specs=[smem] + [whole(value.shape) for value in small] + [hbm] * (len(groups_of) + len(sources)),
-        out_specs=[vmem, vmem] + [whole(shape) for shape, unused in outs[2:]],
+        out_specs=[vmem, vmem, hbm, hbm],
         scratch_shapes=[pltpu.VMEM(shape, dtype) for shape, dtype in scratch]
-        + [pltpu.SemaphoreType.DMA((2, 5)), pltpu.SemaphoreType.DMA((7,)), pltpu.SemaphoreType.DMA((2,))],
+        + [pltpu.SemaphoreType.DMA((2, 5)), pltpu.SemaphoreType.DMA((7,)), pltpu.SemaphoreType.DMA((4,))],
         compiler_params=pltpu.CompilerParams(
             vmem_limit_bytes=48 * MIB, dimension_semantics=("arbitrary",)
         ),
@@ -876,7 +878,7 @@
     return lax.optimization_barrier((value, *others))[0]
 
 
-def gather_chunks(chunk, last_near, before, finish, dp, seq):
+def gather_chunks(chunk, last_near, before, between, finish, dp, seq):
     rows = chunk.shape[0]
     cut = round_up(rows // 2, 16)
     place = lax.axis_index("dp") % (dp // 2) // 2 * seq + lax.axis_index("seq")
@@ -885,6 +887,7 @@
     chunk = after(chunk, last_near, before)
     last_wide = finish(last_near)
     pair = jnp.stack([chunk, lax.ppermute(chunk, "dp", [(n, n ^ 4) for n in range(dp)])])
+    pair = after(pair, between)
     a, b = pair[:, :cut], pair[:, cut:]
     a1, b1 = along_y(a), along_x(b)
     a, b = jnp.stack([a, a1]), jnp.stack([b, b1])
@@ -1041,8 +1044,8 @@
     near = near_sum(pieces)
     far = far_half(near, dp)
     first_moved = [scatter_rows(t[2][:, : own // 2], seq) for t in tails]
-    last_moved = [scatter_rows(t[2][:, own // 2 :], seq) for t in tails]
     last_near = near_sum(exchange(mine, dp, seq))
+    last_moved = [scatter_rows(after(t[2][:, own // 2 :], last_near), seq) for t in tails]
 
     def finish(last_near):
         wide = spread_call(last_near, far_half(last_near, dp), peers)
@@ -1050,7 +1053,7 @@
 
     if dp == 16 and seq == 2:
         chunk = (near.astype(F32) + far.astype(F32)).astype(BF16)
-        parts, assemble, last_wide, held = gather_chunks(chunk, last_near, first_moved, finish, dp, seq)
+        parts, assemble, last_wide, held = gather_chunks(chunk, last_near, first_moved, last_moved, finish, dp, seq)
     else:
         parts = exchange(spread_call(near, far, peers), dp, seq).reshape(half, D)
         assemble = lambda whole: whole
@@ -1063,7 +1066,12 @@
     layer_half = assemble(*parts)
     other = swap_cores(layer_half, dp)
     first = widen_near(sides, layer_half)
-    last_half = after(last_half, layer_half)
+    grad_input = []
+    for tail, *moved in zip(tails, first_moved, last_moved):
+        came = [jnp.concatenate(both).astype(F32) for both in zip(*moved)]
+        grad_input.append(functools.reduce(jnp.add, came, tail[3]))
+    grad_input = jnp.stack(grad_input)
+    last_half = after(last_half, layer_half, grad_input)
     grad_fc1, grad_fc2 = widen_far(sides, other, first)
     found = call(
         functools.partial(last_kernel, everyone),
@@ -1078,12 +1086,6 @@
     grad_qv, grad_rel, grad_out_bias, grad_ada_bias, grad_fc1_bias, grad_fc2_bias = found[:6]
     grad_qkv, grad_ada, grad_table, grad_out = found[6:]
     grad_rel = grad_rel.transpose(1, 0, 2)
-    grad_qkv, last_moved = lax.optimization_barrier((grad_qkv, last_moved))
-    grad_input = []
-    for tail, *moved in zip(tails, first_moved, last_moved):
-        came = [jnp.concatenate(both).astype(F32) for both in zip(*moved)]
-        grad_input.append(functools.reduce(jnp.add, came, tail[3]))
-    grad_input = jnp.stack(grad_input)
     return (
         out_full, out_masked, grad_input, grad_table, grad_ada, grad_ada_bias, grad_qkv, grad_qv,
         grad_rel, grad_out, grad_out_bias, grad_fc1, grad_fc1_bias, grad_fc2, grad_fc2_bias,

time: 129 us -> 128 us (level)
  starting transfers between devices: 33.9 us -> 32.5 us
    ppermute x2, waiting for transfers between devices: 0.01 us -> 1.62 us  [scatter_rows(): lax.ppermute(partial[step - 1], 'seq', [(n, (n + step) % seq) for n in ra...]
  transfers between devices with their start and end apart: 17 -> 17, of which waited for: 6 -> 8; matrix products, arithmetic and copies ran while one was open for 0% -> 1% of each run, Pallas kernels for 31% -> 27%
where the time goes in v7:
time: 128 us; the launch traced here: 127 us
  Pallas kernels  63.5 us (50%)
  starting transfers between devices  32.5 us (25%)
  waiting for transfers between devices  25.1 us (20%)
  between operations  3.75 us (3%)
  other arithmetic  1.37 us (1%)
    pallas_call x9, Pallas kernels, call(): pl.pallas_call(kernel, out_shape=[jax.ShapeDtypeStruct(shape, dtype) for...  36.3 us
    pallas_call x1, Pallas kernels, back_call(): pl.pallas_call(functools.partial(back_kernel, own, everyone), grid=(group...  19.3 us
    all_to_all x3, starting transfers between devices, exchange(): return lax.all_to_all(value, AXES, 0, 0, axis_index_groups=groups)  13.8 us
    ppermute x2, waiting for transfers between devices, gather_chunks(): lax.ppermute(value, 'dp', [(n, n ^ 2) for n in range(dp)])  9.54 us
    ppermute x2, waiting for transfers between devices, far_half(): lax.ppermute(near, 'dp', [(n, (n + dp // 2) % dp) for n in range(dp)])  5.55 us
    pallas_call x1, Pallas kernels, own_call(): pl.pallas_call(own_kernel, out_shape=[jax.ShapeDtypeStruct(shape, dtype)...  4.89 us
    ppermute x2, starting transfers between devices, far_half(): lax.ppermute(near, 'dp', [(n, (n + dp // 2) % dp) for n in range(dp)])  4.09 us
    ppermute x2, starting transfers between devices, scatter_rows(): lax.ppermute(partial[step - 1], 'seq', [(n, (n + step) % seq) for n in ra...  3.51 us
  transfers between devices with their start and end apart: 17, of which 8 were waited for; matrix products, arithmetic and copies ran while one was open for 1% of the time, Pallas kernels for 27%

profile of v7, /device:TPU:0, one launch (start us, length us, event | category | flops | bytes accessed | tf_op | source)
XLA Modules:
  0.0 127.3 jit_solution(17843787427824473725)
XLA Ops:
  0.6 3.0 %collective-permute-start = (bf16[512,384]{1,0:T(8,128)(2,1)}, bf16[512,384]{1,0:T(8,128)(2,1)S(1)}, u32[]{:S(2)}, u32[]{:S(2)}) collective-permute-start(bf16[512,384]{1,0:T(8,128)(2,1)} %bitcast.29), channel_id=1, source_target_pairs={{0,1},{1,0},{2,3},{3,2},{4,5},{5,4},{6,7},{7,6},{8,9},{9,8},{10,11... | collective-permute-start | bytes 1179656 | tf_op jit(solution)/shard_map/ppermute | solution.py:938
  6.3 0.0 copy-start.2
  6.3 0.0 copy-start.3
  6.3 4.9 %shard_map.307 = (s32[10]{0:T(128)S(1)}, s32[704,1]{1,0:T(8,128)S(1)}, f32[16,384]{1,0:T(8,128)S(1)}, f32[8,384]{1,0:T(8,128)S(1)}, bf16[512,384]{1,0:T(8,128)(2...) custom-call(s32[10]{0:T(128)S(1)} %compare_select_fusion.6.start_ref, ...), custom_call_target="tpu_custom_call" | custom-call | flops 3000000000 | bytes 1048576 | tf_op jit(solution)/shard_map/pallas_call | solution.py:638
  11.2 1.8 %collective-permute-done.refs_1_ = bf16[512,384]{1,0:T(8,128)(2,1)S(1)} collective-permute-done((bf16[512,384]{1,0:T(8,128)(2,1)}, bf16[512,384]{1,0:T(8,128)(2,1)S(1)}, u32[]{:S(2)}, u32[]{:S(2)}) %collective-permute-start) | collective-permute-done | bytes 393248 | tf_op jit(solution)/shard_map/ppermute | solution.py:938
  13.0 3.6 %shard_map.308 = (bf16[6,864,128]{2,1,0:T(8,128)(2,1)S(1)}, bf16[6,1024,128]{2,1,0:T(8,128)(2,1)S(1)}, bf16[6,1024,128]{2,1,0:T(8,128)(2,1)S(1)}, bf16[864,384]{...) custom-call(s32[10]{0:T(128)S(1)} %get-tuple-element.89.scalar_ref, ...), custom_call_target="tpu_custom_call" | custom-call | flops 3000000000 | bytes 1048576 | tf_op jit(solution)/shard_map/pallas_call | solution.py:625
  16.7 0.0 copy-start
  16.7 0.0 copy-start.5
  16.7 0.0 copy-start.6
  16.7 9.4 %shard_map.309 = (f32[3,864,128]{2,1,0:T(8,128)S(1)}, f32[3,864,128]{2,1,0:T(8,128)S(1)}, bf16[6,864,1024]{2,1,0:T(8,128)(2,1)}, bf16[6,864,128]{2,1,0:T(8,128)(...) custom-call(bf16[6,864,128]{2,1,0:T(8,128)(2,1)S(1)} %get-tuple-element.99.qaug_ref, ...), custom_call_target="tpu_custom_call" | custom-call | flops 10000000000 | bytes 1048576 | tf_op jit(solution)/shard_map/pallas_call | solution.py:625
  26.2 8.8 %shard_map.310 = (f32[864,384]{1,0:T(8,128)S(1)}, bf16[864,1536]{1,0:T(8,128)(2,1)S(1)}, bf16[864,1536]{1,0:T(8,128)(2,1)S(1)}, f32[8,384]{1,0:T(8,128)S(1)}, bf...) custom-call(s32[10]{0:T(128)S(1)} %get-tuple-element.89.scalar_ref, ...), custom_call_target="tpu_custom_call" | custom-call | flops 10000000000 | bytes 1048576 | tf_op jit(solution)/shard_map/pallas_call | solution.py:625
  35.0 0.1 collective-permute-start.1
  35.1 6.2 %shard_map.312 = (f32[16,384]{1,0:T(8,128)S(1)}, bf16[512,384]{1,0:T(8,128)(2,1)}, bf16[352,384]{1,0:T(8,128)(2,1)}, f32[864,384]{1,0:T(8,128)}, bf16[864,384]{1...) custom-call(s32[10]{0:T(128)S(1)} %get-tuple-element.89.scalar_ref, ...), custom_call_target="tpu_custom_call" | custom-call | flops 6000000000 | bytes 1048576 | tf_op jit(solution)/shard_map/pallas_call | solution.py:625
  41.4 1.1 shard_map.311
  42.5 5.0 %all-to-all-start = ((bf16[8,192,384]{2,1,0:T(8,128)(2,1)}), bf16[8,192,384]{2,1,0:T(8,128)(2,1)S(1)}, u32[]{:S(2)}, u32[]{:S(2)}) async-start(bf16[8,192,384]{2,1,0:T(8,128)(2,1)} %bitcast.36), calls=%async_computation | async-start | bytes 2359296 | tf_op jit(solution)/shard_map/all_to_all | solution.py:845
  47.5 19.3 %shard_map.313 = (bf16[832,384]{1,0:T(8,128)(2,1)S(1)}, bf16[832,384]{1,0:T(8,128)(2,1)S(1)}, bf16[1,512,384]{2,1,0:T(8,128)(2,1)}, f32[512,384]{1,0:T(8,128)}) custom-call(s32[10]{0:T(128)S(1)} %get-tuple-element.89.scalar_ref, s32[704,1]{1,0:T(8,128)S(1)} %get-tuple-element.96.refs_8_.kept_ref, f32[8,384]{1,0:T(8,128)S(1)} %get-tuple-element.97.refs_9_.mod_ref, ...), custom_call_target="tpu_custom_call" | custom-call | flops 17999998976 | bytes 1048576 | tf_op jit(solution)/shard_map/pallas_call | solution.py:703
  66.8 0.3 collective-permute-start.3
  67.0 1.9 %collective-permute-done.3.right_ref = bf16[832,384]{1,0:T(8,128)(2,1)S(1)} collective-permute-done((bf16[832,384]{1,0:T(8,128)(2,1)S(1)}, bf16[832,384]{1,0:T(8,128)(2,1)S(1)}, u32[]{:S(2)}, u32[]{:S(2)}) %collective-permute-start.3) | collective-permute-done | bytes 639008 | tf_op jit(solution)/shard_map/ppermute | solution.py:836
  68.9 0.9 shard_map.314
  69.8 0.0 copy-start.8
  69.8 5.2 %all-to-all-start.1 = ((bf16[8,104,384]{2,1,0:T(8,128)(2,1)}), bf16[8,104,384]{2,1,0:T(8,128)(2,1)S(1)}, u32[]{:S(2)}, u32[]{:S(2)}) async-start(bf16[8,104,384]{2,1,0:T(8,128)(2,1)} %bitcast.37), calls=%async_computation.1 | async-start | bytes 1277952 | tf_op jit(solution)/shard_map/all_to_all | solution.py:845
  75.0 0.2 reduce_sum.25
  75.2 2.7 %collective-permute-start.6 = (bf16[192,384]{1,0:T(8,128)(2,1)S(1)}, bf16[192,384]{1,0:T(8,128)(2,1)S(1)}, u32[]{:S(2)}, u32[]{:S(2)}) collective-permute-start(bf16[192,384]{1,0:T(8,128)(2,1)S(1)} %reduce_sum.25), channel_id=1, source_target_pairs={{0,16},{2,18},{4,20},{6,22},{8,24},{10,26},{12,28},{14,30},{16,0},... | collective-permute-start | bytes 442376 | tf_op jit(solution)/shard_map/ppermute | solution.py:853
  77.9 2.1 %collective-permute-start.2 = (bf16[256,384]{1,0:T(8,128)(2,1)S(1)}, bf16[256,384]{1,0:T(8,128)(2,1)S(1)}, u32[]{:S(2)}, u32[]{:S(2)}) collective-permute-start(bf16[256,384]{1,0:T(8,128)(2,1)S(1)} %get-tuple-element.163), channel_id=1, source_target_pairs={{0,1},{1,0},{2,3},{3,2},{4,5},{5,4},{6,7},{7,6},{8,9},{9,8},{10,11... | collective-permute-start | bytes 589832 | tf_op jit(solution)/shard_map/ppermute | solution.py:909
  80.0 5.5 %collective-permute-done.6 = bf16[192,384]{1,0:T(8,128)(2,1)S(1)} collective-permute-done((bf16[192,384]{1,0:T(8,128)(2,1)S(1)}, bf16[192,384]{1,0:T(8,128)(2,1)S(1)}, u32[]{:S(2)}, u32[]{:S(2)}) %collective-permute-start.6) | collective-permute-done | bytes 147488 | tf_op jit(solution)/shard_map/ppermute | solution.py:853
  85.6 3.2 %all-to-all-done.1 = bf16[8,104,384]{2,1,0:T(8,128)(2,1)S(1)} async-done(((bf16[8,104,384]{2,1,0:T(8,128)(2,1)}), bf16[8,104,384]{2,1,0:T(8,128)(2,1)S(1)}, u32[]{:S(2)}, u32[]{:S(2)}) %all-to-all-start.1) | async-done | bytes 639008 | tf_op jit(solution)/shard_map/all_to_all | solution.py:845
  88.8 0.1 reduce_sum.24.near_ref
  88.9 1.7 %collective-permute-start.7 = (bf16[192,384]{1,0:T(8,128)(2,1)S(1)}, bf16[192,384]{1,0:T(8,128)(2,1)S(1)}, u32[]{:S(2)}, u32[]{:S(2)}) collective-permute-start(bf16[192,384]{1,0:T(8,128)(2,1)S(1)} %add_convert_fusion), channel_id=1, source_target_pairs={{0,8},{2,10},{4,12},{6,14},{8,0},{10,2},{12,4},{14,6},{16,24},{18,... | collective-permute-start | bytes 442376 | tf_op jit(solution)/shard_map/ppermute | solution.py:889
  90.6 1.4 %collective-permute-start.4 = (bf16[256,384]{1,0:T(8,128)(2,1)S(1)}, bf16[256,384]{1,0:T(8,128)(2,1)S(1)}, u32[]{:S(2)}, u32[]{:S(2)}) collective-permute-start(bf16[256,384]{1,0:T(8,128)(2,1)S(1)} %bitcast.39), channel_id=1, source_target_pairs={{0,1},{1,0},{2,3},{3,2},{4,5},{5,4},{6,7},{7,6},{8,9},{9,8},{10,11... | collective-permute-start | bytes 589832 | tf_op jit(solution)/shard_map/ppermute | solution.py:909
  92.0 1.4 %collective-permute-start.5 = (bf16[104,384]{1,0:T(8,128)(2,1)S(1)}, bf16[104,384]{1,0:T(8,128)(2,1)S(1)}, u32[]{:S(2)}, u32[]{:S(2)}) collective-permute-start(bf16[104,384]{1,0:T(8,128)(2,1)S(1)} %reduce_sum.24.near_ref), channel_id=1, source_target_pairs={{0,16},{2,18},{4,20},{6,22},{8,24},{10,26},{12,28},{14,30},{16,0},... | collective-permute-start | bytes 239624 | tf_op jit(solution)/shard_map/ppermute | solution.py:853
  93.4 1.5 %collective-permute-done.7 = bf16[192,384]{1,0:T(8,128)(2,1)S(1)} collective-permute-done((bf16[192,384]{1,0:T(8,128)(2,1)S(1)}, bf16[192,384]{1,0:T(8,128)(2,1)S(1)}, u32[]{:S(2)}, u32[]{:S(2)}) %collective-permute-start.7) | collective-permute-done | bytes 147488 | tf_op jit(solution)/shard_map/ppermute | solution.py:889
  95.0 1.6 %collective-permute-done.4 = bf16[256,384]{1,0:T(8,128)(2,1)S(1)} collective-permute-done((bf16[256,384]{1,0:T(8,128)(2,1)S(1)}, bf16[256,384]{1,0:T(8,128)(2,1)S(1)}, u32[]{:S(2)}, u32[]{:S(2)}) %collective-permute-start.4) | collective-permute-done | bytes 196640 | tf_op jit(solution)/shard_map/ppermute | solution.py:909
  96.6 0.1 slice_bitcast_fusion.1
  96.7 1.1 collective-permute-start.8
  97.8 1.5 %collective-permute-start.9 = (bf16[2,96,384]{2,1,0:T(8,128)(2,1)S(1)}, bf16[2,96,384]{2,1,0:T(8,128)(2,1)S(1)}, u32[]{:S(2)}, u32[]{:S(2)}) collective-permute-start(bf16[2,96,384]{2,1,0:T(8,128)(2,1)S(1)} %get-tuple-element.167), channel_id=1, source_target_pairs={{0,4},{2,6},{4,0},{6,2},{8,12},{10,14},{12,8},{14,10},{16,20},{18,... | collective-permute-start | bytes 442376 | tf_op jit(solution)/shard_map/ppermute | solution.py:885
  99.3 0.9 shard_map.315
  100.2 3.6 %all-to-all-start.2 = ((bf16[8,104,384]{2,1,0:T(8,128)(2,1)}), bf16[8,104,384]{2,1,0:T(8,128)(2,1)S(1)}, u32[]{:S(2)}, u32[]{:S(2)}) async-start(bf16[8,104,384]{2,1,0:T(8,128)(2,1)} %shard_map.315), calls=%async_computation.2 | async-start | bytes 1277952 | tf_op jit(solution)/shard_map/all_to_all | solution.py:845
  103.8 2.0 %collective-permute-start.10 = (bf16[2,2,96,384]{3,2,1,0:T(8,128)(2,1)S(1)}, bf16[2,2,96,384]{3,2,1,0:T(8,128)(2,1)S(1)}, u32[]{:S(2)}, u32[]{:S(2)}) collective-permute-start(bf16[2,2,96,384]{3,2,1,0:T(8,128)(2,1)S(1)} %pad_maximum_fusion.1), channel_id=1, source_target_pairs={{0,4},{2,6},{4,0},{6,2},{8,12},{10,14},{12,8},{14,10},{16,20},{18,... | collective-permute-start | bytes 884744 | tf_op jit(solution)/shard_map/ppermute | solution.py:885
  105.8 1.5 %collective-permute-start.11 = (bf16[2,2,96,384]{3,2,1,0:T(8,128)(2,1)S(1)}, bf16[2,2,96,384]{3,2,1,0:T(8,128)(2,1)S(1)}, u32[]{:S(2)}, u32[]{:S(2)}) collective-permute-start(bf16[2,2,96,384]{3,2,1,0:T(8,128)(2,1)S(1)} %pad_maximum_fusion.2), channel_id=1, source_target_pairs={{0,1},{1,0},{2,3},{3,2},{4,5},{5,4},{6,7},{7,6},{8,9},{9,8},{10,11... | collective-permute-start | bytes 884744 | tf_op jit(solution)/shard_map/ppermute | solution.py:886
  107.3 9.5 %collective-permute-done.10.a2_ref = bf16[2,2,96,384]{3,2,1,0:T(8,128)(2,1)S(1)} collective-permute-done((bf16[2,2,96,384]{3,2,1,0:T(8,128)(2,1)S(1)}, bf16[2,2,96,384]{3,2,1,0:T(8,128)(2,1)S(1)}, u32[]{:S(2)}, u32[]{:S(2)}) %collective-permute-start.10) | collective-permute-done | bytes 294944 | tf_op jit(solution)/shard_map/ppermute | solution.py:885
  116.8 0.1 collective-permute-done.11.b2_ref
  116.9 0.1 shard_map.316.half_ref
  117.0 0.1 collective-permute-start.13
  117.1 0.9 copy-done.7
  118.0 0.9 add_bitcast_fusion
  119.0 1.5 %shard_map.318 = (f32[384,1536]{1,0:T(8,128)}, f32[1536,384]{1,0:T(8,128)}) custom-call(s32[1]{0:T(128)} %bitcast.11.side_ref, bf16[1536,384]{1,0:T(8,128)(2,1)S(1)} %shard_map.316.half_ref), custom_call_target="tpu_custom_call" | custom-call | flops 1000000000 | bytes 1048576 | tf_op jit(solution)/shard_map/pallas_call | solution.py:756
  120.5 1.5 %shard_map.319 = (f32[384,1536]{1,0:T(8,128)}, f32[1536,384]{1,0:T(8,128)}) custom-call(s32[1]{0:T(128)} %bitcast.11.side_ref, bf16[1536,384]{1,0:T(8,128)(2,1)S(1)} %collective-permute-done.13.half_ref, f32[384,1536]{1,0:T(8,128)} %get-tuple-element.157.g1_in, f32[1536,384]{1,0:T(8,128)} %get-tuple-element.158.g2_in), custom_call_target="tpu_custom_call", output_to_operand_aliasing={{0}: (2, {}), {1}: (3, {})} | custom-call | flops 1000000000 | bytes 1048576 | tf_op jit(solution)/shard_map/pallas_call | solution.py:768
  122.0 5.2 %shard_map.317 = (f32[2,384]{1,0:T(2,128)}, f32[6,2,63]{2,1,0:T(2,128)}, f32[384]{0:T(512)}, f32[2304]{0:T(1024)}, f32[1536]{0:T(1024)}, /*index=5*/f32[384]{0:T...) custom-call(s32[1]{0:T(128)} %bitcast.11.side_ref, ...), custom_call_target="tpu_custom_call" | custom-call | flops 4000000000 | bytes 1048576 | tf_op jit(solution)/shard_map/pallas_call | solution.py:625
  (27 shorter events, 0.3 us)
Async XLA Ops:
  0.6 12.4 %collective-permute-start = (bf16[512,384]{1,0:T(8,128)(2,1)}, bf16[512,384]{1,0:T(8,128)(2,1)S(1)}, u32[]{:S(2)}, u32[]{:S(2)}) collective-permute-start(bf16[512,384]{1,0:T(8,128)(2,1)} %bitcast.29), channel_id=1, source_target_pairs={{0,1},{1,0},{2,3},{3,2},{4,5},{5,4},{6,7},{7,6},{8,9},{9,8},{10,11... | collective-permute-start | bytes 1179656 | tf_op jit(solution)/shard_map/ppermute | solution.py:938
  6.3 6.7 %copy-start.2 = (bf16[384,1152]{1,0:T(8,128)(2,1)S(1)}, bf16[384,1152]{1,0:T(8,128)(2,1)}, u32[]{:S(2)}) copy-start(bf16[384,1152]{1,0:T(8,128)(2,1)} %refs_9_.1) | copy-start | bytes 2654212
  6.3 6.7 %copy-start.3 = (bf16[1,512,384]{2,1,0:T(8,128)(2,1)S(1)}, bf16[1,512,384]{2,1,0:T(8,128)(2,1)}, u32[]{:S(2)}) copy-start(bf16[1,512,384]{2,1,0:T(8,128)(2,1)} %param.20) | copy-start | bytes 1179652
  16.7 9.5 %copy-start = (bf16[384,1536]{1,0:T(8,128)(2,1)S(1)}, bf16[384,1536]{1,0:T(8,128)(2,1)}, u32[]{:S(2)}) copy-start(bf16[384,1536]{1,0:T(8,128)(2,1)} %w1_ref.3) | copy-start | bytes 3538948
  16.7 9.5 %copy-start.1 = (bf16[1536,384]{1,0:T(8,128)(2,1)S(1)}, bf16[1536,384]{1,0:T(8,128)(2,1)}, u32[]{:S(2)}) copy-start(bf16[1536,384]{1,0:T(8,128)(2,1)} %w2_ref.3) | copy-start | bytes 3538948
  16.7 9.5 %copy-start.4 = (bf16[1,512,384]{2,1,0:T(8,128)(2,1)S(1)}, bf16[1,512,384]{2,1,0:T(8,128)(2,1)}, u32[]{:S(2)}) copy-start(bf16[1,512,384]{2,1,0:T(8,128)(2,1)} %param.38) | copy-start | bytes 1179652
  16.7 9.5 %copy-start.5 = (bf16[384,384]{1,0:T(8,128)(2,1)S(1)}, bf16[384,384]{1,0:T(8,128)(2,1)}, u32[]{:S(2)}) copy-start(bf16[384,384]{1,0:T(8,128)(2,1)} %wout_ref.3) | copy-start | bytes 884740
  16.7 9.5 %copy-start.6 = (bf16[1,352,384]{2,1,0:T(8,128)(2,1)S(1)}, bf16[1,352,384]{2,1,0:T(8,128)(2,1)}, u32[]{:S(2)}) copy-start(bf16[1,352,384]{2,1,0:T(8,128)(2,1)} %param.39) | copy-start | bytes 811012
  35.0 6.3 %collective-permute-start.1 = (bf16[1536,384]{1,0:T(8,128)(2,1)S(1)}, bf16[1536,384]{1,0:T(8,128)(2,1)S(1)}, u32[]{:S(2)}, u32[]{:S(2)}) collective-permute-start(bf16[1536,384]{1,0:T(8,128)(2,1)S(1)} %get-tuple-element.106), channel_id=1, source_target_pairs={{0,2},{2,0},{4,6},{6,4},{8,10},{10,8},{12,14},{14,12},{16,18},{18,... | collective-permute-start | bytes 3538952 | tf_op jit(solution)/shard_map/ppermute | solution.py:836
  42.5 24.3 %all-to-all-start = ((bf16[8,192,384]{2,1,0:T(8,128)(2,1)}), bf16[8,192,384]{2,1,0:T(8,128)(2,1)S(1)}, u32[]{:S(2)}, u32[]{:S(2)}) async-start(bf16[8,192,384]{2,1,0:T(8,128)(2,1)} %bitcast.36), calls=%async_computation | async-start | bytes 2359296 | tf_op jit(solution)/shard_map/all_to_all | solution.py:845
  66.8 2.1 %collective-permute-start.3 = (bf16[832,384]{1,0:T(8,128)(2,1)S(1)}, bf16[832,384]{1,0:T(8,128)(2,1)S(1)}, u32[]{:S(2)}, u32[]{:S(2)}) collective-permute-start(bf16[832,384]{1,0:T(8,128)(2,1)S(1)} %get-tuple-element.140), channel_id=1, source_target_pairs={{0,2},{2,0},{4,6},{6,4},{8,10},{10,8},{12,14},{14,12},{16,18},{18,... | collective-permute-start | bytes 1916936 | tf_op jit(solution)/shard_map/ppermute | solution.py:836
  69.8 8.1 %copy-start.8 = (bf16[1,512,384]{2,1,0:T(8,128)(2,1)S(1)}, bf16[1,512,384]{2,1,0:T(8,128)(2,1)}, u32[]{:S(2)}) copy-start(bf16[1,512,384]{2,1,0:T(8,128)(2,1)} %get-tuple-element.134) | copy-start | bytes 1179652
  69.8 19.0 %all-to-all-start.1 = ((bf16[8,104,384]{2,1,0:T(8,128)(2,1)}), bf16[8,104,384]{2,1,0:T(8,128)(2,1)S(1)}, u32[]{:S(2)}, u32[]{:S(2)}) async-start(bf16[8,104,384]{2,1,0:T(8,128)(2,1)} %bitcast.37), calls=%async_computation.1 | async-start | bytes 1277952 | tf_op jit(solution)/shard_map/all_to_all | solution.py:845
  75.2 10.3 %collective-permute-start.6 = (bf16[192,384]{1,0:T(8,128)(2,1)S(1)}, bf16[192,384]{1,0:T(8,128)(2,1)S(1)}, u32[]{:S(2)}, u32[]{:S(2)}) collective-permute-start(bf16[192,384]{1,0:T(8,128)(2,1)S(1)} %reduce_sum.25), channel_id=1, source_target_pairs={{0,16},{2,18},{4,20},{6,22},{8,24},{10,26},{12,28},{14,30},{16,0},... | collective-permute-start | bytes 442376 | tf_op jit(solution)/shard_map/ppermute | solution.py:853
  77.9 10.9 %collective-permute-start.2 = (bf16[256,384]{1,0:T(8,128)(2,1)S(1)}, bf16[256,384]{1,0:T(8,128)(2,1)S(1)}, u32[]{:S(2)}, u32[]{:S(2)}) collective-permute-start(bf16[256,384]{1,0:T(8,128)(2,1)S(1)} %get-tuple-element.163), channel_id=1, source_target_pairs={{0,1},{1,0},{2,3},{3,2},{4,5},{5,4},{6,7},{7,6},{8,9},{9,8},{10,11... | collective-permute-start | bytes 589832 | tf_op jit(solution)/shard_map/ppermute | solution.py:909
  88.9 6.1 %collective-permute-start.7 = (bf16[192,384]{1,0:T(8,128)(2,1)S(1)}, bf16[192,384]{1,0:T(8,128)(2,1)S(1)}, u32[]{:S(2)}, u32[]{:S(2)}) collective-permute-start(bf16[192,384]{1,0:T(8,128)(2,1)S(1)} %add_convert_fusion), channel_id=1, source_target_pairs={{0,8},{2,10},{4,12},{6,14},{8,0},{10,2},{12,4},{14,6},{16,24},{18,... | collective-permute-start | bytes 442376 | tf_op jit(solution)/shard_map/ppermute | solution.py:889
  90.6 6.0 %collective-permute-start.4 = (bf16[256,384]{1,0:T(8,128)(2,1)S(1)}, bf16[256,384]{1,0:T(8,128)(2,1)S(1)}, u32[]{:S(2)}, u32[]{:S(2)}) collective-permute-start(bf16[256,384]{1,0:T(8,128)(2,1)S(1)} %bitcast.39), channel_id=1, source_target_pairs={{0,1},{1,0},{2,3},{3,2},{4,5},{5,4},{6,7},{7,6},{8,9},{9,8},{10,11... | collective-permute-start | bytes 589832 | tf_op jit(solution)/shard_map/ppermute | solution.py:909
  92.0 7.3 %collective-permute-start.5 = (bf16[104,384]{1,0:T(8,128)(2,1)S(1)}, bf16[104,384]{1,0:T(8,128)(2,1)S(1)}, u32[]{:S(2)}, u32[]{:S(2)}) collective-permute-start(bf16[104,384]{1,0:T(8,128)(2,1)S(1)} %reduce_sum.24.near_ref), channel_id=1, source_target_pairs={{0,16},{2,18},{4,20},{6,22},{8,24},{10,26},{12,28},{14,30},{16,0},... | collective-permute-start | bytes 239624 | tf_op jit(solution)/shard_map/ppermute | solution.py:853
  96.7 7.1 %collective-permute-start.8 = (bf16[2,96,384]{2,1,0:T(8,128)(2,1)S(1)}, bf16[2,96,384]{2,1,0:T(8,128)(2,1)S(1)}, u32[]{:S(2)}, u32[]{:S(2)}) collective-permute-start(bf16[2,96,384]{2,1,0:T(8,128)(2,1)S(1)} %get-tuple-element.168), channel_id=1, source_target_pairs={{0,1},{1,0},{2,3},{3,2},{4,5},{5,4},{6,7},{7,6},{8,9},{9,8},{10,11... | collective-permute-start | bytes 442376 | tf_op jit(solution)/shard_map/ppermute | solution.py:886
  97.8 6.0 %collective-permute-start.9 = (bf16[2,96,384]{2,1,0:T(8,128)(2,1)S(1)}, bf16[2,96,384]{2,1,0:T(8,128)(2,1)S(1)}, u32[]{:S(2)}, u32[]{:S(2)}) collective-permute-start(bf16[2,96,384]{2,1,0:T(8,128)(2,1)S(1)} %get-tuple-element.167), channel_id=1, source_target_pairs={{0,4},{2,6},{4,0},{6,2},{8,12},{10,14},{12,8},{14,10},{16,20},{18,... | collective-permute-start | bytes 442376 | tf_op jit(solution)/shard_map/ppermute | solution.py:885
  100.2 18.8 %all-to-all-start.2 = ((bf16[8,104,384]{2,1,0:T(8,128)(2,1)}), bf16[8,104,384]{2,1,0:T(8,128)(2,1)S(1)}, u32[]{:S(2)}, u32[]{:S(2)}) async-start(bf16[8,104,384]{2,1,0:T(8,128)(2,1)} %shard_map.315), calls=%async_computation.2 | async-start | bytes 1277952 | tf_op jit(solution)/shard_map/all_to_all | solution.py:845
  103.8 13.0 %collective-permute-start.10 = (bf16[2,2,96,384]{3,2,1,0:T(8,128)(2,1)S(1)}, bf16[2,2,96,384]{3,2,1,0:T(8,128)(2,1)S(1)}, u32[]{:S(2)}, u32[]{:S(2)}) collective-permute-start(bf16[2,2,96,384]{3,2,1,0:T(8,128)(2,1)S(1)} %pad_maximum_fusion.1), channel_id=1, source_target_pairs={{0,4},{2,6},{4,0},{6,2},{8,12},{10,14},{12,8},{14,10},{16,20},{18,... | collective-permute-start | bytes 884744 | tf_op jit(solution)/shard_map/ppermute | solution.py:885
  105.8 11.1 %collective-permute-start.11 = (bf16[2,2,96,384]{3,2,1,0:T(8,128)(2,1)S(1)}, bf16[2,2,96,384]{3,2,1,0:T(8,128)(2,1)S(1)}, u32[]{:S(2)}, u32[]{:S(2)}) collective-permute-start(bf16[2,2,96,384]{3,2,1,0:T(8,128)(2,1)S(1)} %pad_maximum_fusion.2), channel_id=1, source_target_pairs={{0,1},{1,0},{2,3},{3,2},{4,5},{5,4},{6,7},{7,6},{8,9},{9,8},{10,11... | collective-permute-start | bytes 884744 | tf_op jit(solution)/shard_map/ppermute | solution.py:886
  116.9 1.1 copy-start.7
  117.0 3.5 %collective-permute-start.13 = (bf16[1536,384]{1,0:T(8,128)(2,1)S(1)}, bf16[1536,384]{1,0:T(8,128)(2,1)S(1)}, u32[]{:S(2)}, u32[]{:S(2)}) collective-permute-start(bf16[1536,384]{1,0:T(8,128)(2,1)S(1)} %shard_map.316.half_ref), channel_id=1, source_target_pairs={{0,2},{2,0},{4,6},{6,4},{8,10},{10,8},{12,14},{14,12},{16,18},{18,... | collective-permute-start | bytes 3538952 | tf_op jit(solution)/shard_map/ppermute | solution.py:836
  119.0 3.0 %collective-permute-start.12 = (bf16[832,384]{1,0:T(8,128)(2,1)S(1)}, bf16[832,384]{1,0:T(8,128)(2,1)S(1)}, u32[]{:S(2)}, u32[]{:S(2)}) collective-permute-start(bf16[832,384]{1,0:T(8,128)(2,1)S(1)} %bitcast.25), channel_id=1, source_target_pairs={{0,2},{2,0},{4,6},{6,4},{8,10},{10,8},{12,14},{14,12},{16,18},{18,... | collective-permute-start | bytes 1916936 | tf_op jit(solution)/shard_map/ppermute | solution.py:836

commit v8 on v7

--- a/solution.py
+++ b/solution.py
@@ -579,6 +579,20 @@
         halves = Copies(pay_sems)
         halves.start(dx_own_ref, dx_own_out)
         halves.start(dx_ref, dx_out)
+        half = keep_ref.shape[0]
+
+        def part(which):
+            return pay_ref.at[pl.ds(which * half, half)]
+
+        def hand_over(which):
+            for target, chosen in ((keep_ref, scalar_ref[SIDE] == which), (send_ref, scalar_ref[SIDE] != which)):
+
+                @pl.when(chosen)
+                def start():
+                    pltpu.make_async_copy(part(which), target, pay_sems.at[2 + which]).start()
+
+        if half <= 4 * D:
+            hand_over(0)
         rel = table_sums([tab_ref[n] for n in range(groups)])
         first = jnp.where(scalar_ref[SEQ_PLACE] == 0, 1, 0)
         label = scalar_ref[LABEL]
@@ -601,7 +615,11 @@
         after = row - 7 * everyone
         wanted = jnp.where(after < 0, wanted, jnp.where(after < 11, after + 6, -1))
         pay_ref[4 * D :, :] = mm((lane == wanted).astype(F32).astype(BF16), smalls).astype(BF16)
-        split_halves(halves, scalar_ref[SIDE], pay_ref, keep_ref, send_ref)
+        if half > 4 * D:
+            hand_over(0)
+        hand_over(1)
+        for which in range(2):
+            pltpu.make_async_copy(part(which), keep_ref, pay_sems.at[2 + which]).wait()
         halves.wait()
 
 

time: 128 us -> 128 us (level)
  no operation moved by 1% of the time
where the time goes in v8:
time: 128 us; the launch traced here: 127 us
  Pallas kernels  63.3 us (49%)
  starting transfers between devices  32.5 us (25%)
  waiting for transfers between devices  25.1 us (20%)
  between operations  3.75 us (3%)
  other arithmetic  1.37 us (1%)
    pallas_call x9, Pallas kernels, call(): pl.pallas_call(kernel, out_shape=[jax.ShapeDtypeStruct(shape, dtype) for...  36.4 us
    pallas_call x1, Pallas kernels, back_call(): pl.pallas_call(functools.partial(back_kernel, own, everyone), grid=(group...  19.1 us
    all_to_all x3, starting transfers between devices, exchange(): return lax.all_to_all(value, AXES, 0, 0, axis_index_groups=groups)  13.8 us
    ppermute x2, waiting for transfers between devices, gather_chunks(): lax.ppermute(value, 'dp', [(n, n ^ 2) for n in range(dp)])  9.54 us
    ppermute x2, waiting for transfers between devices, far_half(): lax.ppermute(near, 'dp', [(n, (n + dp // 2) % dp) for n in range(dp)])  5.55 us
    pallas_call x1, Pallas kernels, own_call(): pl.pallas_call(own_kernel, out_shape=[jax.ShapeDtypeStruct(shape, dtype)...  4.89 us
    ppermute x2, starting transfers between devices, far_half(): lax.ppermute(near, 'dp', [(n, (n + dp // 2) % dp) for n in range(dp)])  4.09 us
    ppermute x2, starting transfers between devices, scatter_rows(): lax.ppermute(partial[step - 1], 'seq', [(n, (n + step) % seq) for n in ra...  3.51 us
  transfers between devices with their start and end apart: 17, of which 8 were waited for; matrix products, arithmetic and copies ran while one was open for 1% of the time, Pallas kernels for 27%

profile of v8, /device:TPU:0, one launch (start us, length us, event | category | flops | bytes accessed | tf_op | source)
XLA Modules:
  0.0 127.2 jit_solution(3813814183025922153)
XLA Ops:
  0.6 3.0 %collective-permute-start = (bf16[512,384]{1,0:T(8,128)(2,1)}, bf16[512,384]{1,0:T(8,128)(2,1)S(1)}, u32[]{:S(2)}, u32[]{:S(2)}) collective-permute-start(bf16[512,384]{1,0:T(8,128)(2,1)} %bitcast.29), channel_id=1, source_target_pairs={{0,1},{1,0},{2,3},{3,2},{4,5},{5,4},{6,7},{7,6},{8,9},{9,8},{10,11... | collective-permute-start | bytes 1179656 | tf_op jit(solution)/shard_map/ppermute | solution.py:956
  6.3 0.0 copy-start.2
  6.3 0.0 copy-start.3
  6.3 4.9 %shard_map.307 = (s32[10]{0:T(128)S(1)}, s32[704,1]{1,0:T(8,128)S(1)}, f32[16,384]{1,0:T(8,128)S(1)}, f32[8,384]{1,0:T(8,128)S(1)}, bf16[512,384]{1,0:T(8,128)(2...) custom-call(s32[10]{0:T(128)S(1)} %compare_select_fusion.6.start_ref, ...), custom_call_target="tpu_custom_call" | custom-call | flops 3000000000 | bytes 1048576 | tf_op jit(solution)/shard_map/pallas_call | solution.py:656
  11.2 1.8 %collective-permute-done.refs_1_ = bf16[512,384]{1,0:T(8,128)(2,1)S(1)} collective-permute-done((bf16[512,384]{1,0:T(8,128)(2,1)}, bf16[512,384]{1,0:T(8,128)(2,1)S(1)}, u32[]{:S(2)}, u32[]{:S(2)}) %collective-permute-start) | collective-permute-done | bytes 393248 | tf_op jit(solution)/shard_map/ppermute | solution.py:956
  13.0 3.6 %shard_map.308 = (bf16[6,864,128]{2,1,0:T(8,128)(2,1)S(1)}, bf16[6,1024,128]{2,1,0:T(8,128)(2,1)S(1)}, bf16[6,1024,128]{2,1,0:T(8,128)(2,1)S(1)}, bf16[864,384]{...) custom-call(s32[10]{0:T(128)S(1)} %get-tuple-element.89.scalar_ref, ...), custom_call_target="tpu_custom_call" | custom-call | flops 3000000000 | bytes 1048576 | tf_op jit(solution)/shard_map/pallas_call | solution.py:643
  16.7 0.0 copy-start
  16.7 0.0 copy-start.1
  16.7 0.0 copy-start.6
  16.7 9.4 %shard_map.309 = (f32[3,864,128]{2,1,0:T(8,128)S(1)}, f32[3,864,128]{2,1,0:T(8,128)S(1)}, bf16[6,864,1024]{2,1,0:T(8,128)(2,1)}, bf16[6,864,128]{2,1,0:T(8,128)(...) custom-call(bf16[6,864,128]{2,1,0:T(8,128)(2,1)S(1)} %get-tuple-element.99.qaug_ref, ...), custom_call_target="tpu_custom_call" | custom-call | flops 10000000000 | bytes 1048576 | tf_op jit(solution)/shard_map/pallas_call | solution.py:643
  26.2 8.8 %shard_map.310 = (f32[864,384]{1,0:T(8,128)S(1)}, bf16[864,1536]{1,0:T(8,128)(2,1)S(1)}, bf16[864,1536]{1,0:T(8,128)(2,1)S(1)}, f32[8,384]{1,0:T(8,128)S(1)}, bf...) custom-call(s32[10]{0:T(128)S(1)} %get-tuple-element.89.scalar_ref, ...), custom_call_target="tpu_custom_call" | custom-call | flops 10000000000 | bytes 1048576 | tf_op jit(solution)/shard_map/pallas_call | solution.py:643
  35.0 0.1 collective-permute-start.1
  35.1 6.2 %shard_map.312 = (f32[16,384]{1,0:T(8,128)S(1)}, bf16[512,384]{1,0:T(8,128)(2,1)}, bf16[352,384]{1,0:T(8,128)(2,1)}, f32[864,384]{1,0:T(8,128)}, bf16[864,384]{1...) custom-call(s32[10]{0:T(128)S(1)} %get-tuple-element.89.scalar_ref, ...), custom_call_target="tpu_custom_call" | custom-call | flops 6000000000 | bytes 1048576 | tf_op jit(solution)/shard_map/pallas_call | solution.py:643
  41.4 1.1 shard_map.311
  42.5 5.0 %all-to-all-start = ((bf16[8,192,384]{2,1,0:T(8,128)(2,1)}), bf16[8,192,384]{2,1,0:T(8,128)(2,1)S(1)}, u32[]{:S(2)}, u32[]{:S(2)}) async-start(bf16[8,192,384]{2,1,0:T(8,128)(2,1)} %bitcast.36), calls=%async_computation | async-start | bytes 2359296 | tf_op jit(solution)/shard_map/all_to_all | solution.py:863
  47.5 19.1 %shard_map.313 = (bf16[832,384]{1,0:T(8,128)(2,1)S(1)}, bf16[832,384]{1,0:T(8,128)(2,1)S(1)}, bf16[1,512,384]{2,1,0:T(8,128)(2,1)}, f32[512,384]{1,0:T(8,128)}) custom-call(s32[10]{0:T(128)S(1)} %get-tuple-element.89.scalar_ref, s32[704,1]{1,0:T(8,128)S(1)} %get-tuple-element.96.refs_8_.kept_ref, f32[8,384]{1,0:T(8,128)S(1)} %get-tuple-element.97.refs_9_.mod_ref, ...), custom_call_target="tpu_custom_call" | custom-call | flops 17999998976 | bytes 1048576 | tf_op jit(solution)/shard_map/pallas_call | solution.py:721
  66.6 0.3 collective-permute-start.3
  66.8 1.9 %collective-permute-done.3.right_ref = bf16[832,384]{1,0:T(8,128)(2,1)S(1)} collective-permute-done((bf16[832,384]{1,0:T(8,128)(2,1)S(1)}, bf16[832,384]{1,0:T(8,128)(2,1)S(1)}, u32[]{:S(2)}, u32[]{:S(2)}) %collective-permute-start.3) | collective-permute-done | bytes 639008 | tf_op jit(solution)/shard_map/ppermute | solution.py:854
  68.7 0.9 shard_map.314
  69.6 0.0 copy-start.8
  69.6 5.2 %all-to-all-start.1 = ((bf16[8,104,384]{2,1,0:T(8,128)(2,1)}), bf16[8,104,384]{2,1,0:T(8,128)(2,1)S(1)}, u32[]{:S(2)}, u32[]{:S(2)}) async-start(bf16[8,104,384]{2,1,0:T(8,128)(2,1)} %bitcast.37), calls=%async_computation.1 | async-start | bytes 1277952 | tf_op jit(solution)/shard_map/all_to_all | solution.py:863
  74.9 0.2 reduce_sum.25
  75.0 2.7 %collective-permute-start.6 = (bf16[192,384]{1,0:T(8,128)(2,1)S(1)}, bf16[192,384]{1,0:T(8,128)(2,1)S(1)}, u32[]{:S(2)}, u32[]{:S(2)}) collective-permute-start(bf16[192,384]{1,0:T(8,128)(2,1)S(1)} %reduce_sum.25), channel_id=1, source_target_pairs={{0,16},{2,18},{4,20},{6,22},{8,24},{10,26},{12,28},{14,30},{16,0},... | collective-permute-start | bytes 442376 | tf_op jit(solution)/shard_map/ppermute | solution.py:871
  77.7 2.1 %collective-permute-start.2 = (bf16[256,384]{1,0:T(8,128)(2,1)S(1)}, bf16[256,384]{1,0:T(8,128)(2,1)S(1)}, u32[]{:S(2)}, u32[]{:S(2)}) collective-permute-start(bf16[256,384]{1,0:T(8,128)(2,1)S(1)} %get-tuple-element.163), channel_id=1, source_target_pairs={{0,1},{1,0},{2,3},{3,2},{4,5},{5,4},{6,7},{7,6},{8,9},{9,8},{10,11... | collective-permute-start | bytes 589832 | tf_op jit(solution)/shard_map/ppermute | solution.py:927
  79.8 5.5 %collective-permute-done.6 = bf16[192,384]{1,0:T(8,128)(2,1)S(1)} collective-permute-done((bf16[192,384]{1,0:T(8,128)(2,1)S(1)}, bf16[192,384]{1,0:T(8,128)(2,1)S(1)}, u32[]{:S(2)}, u32[]{:S(2)}) %collective-permute-start.6) | collective-permute-done | bytes 147488 | tf_op jit(solution)/shard_map/ppermute | solution.py:871
  85.4 3.2 %all-to-all-done.1 = bf16[8,104,384]{2,1,0:T(8,128)(2,1)S(1)} async-done(((bf16[8,104,384]{2,1,0:T(8,128)(2,1)}), bf16[8,104,384]{2,1,0:T(8,128)(2,1)S(1)}, u32[]{:S(2)}, u32[]{:S(2)}) %all-to-all-start.1) | async-done | bytes 639008 | tf_op jit(solution)/shard_map/all_to_all | solution.py:863
  88.6 0.1 reduce_sum.24.near_ref
  88.7 1.7 %collective-permute-start.7 = (bf16[192,384]{1,0:T(8,128)(2,1)S(1)}, bf16[192,384]{1,0:T(8,128)(2,1)S(1)}, u32[]{:S(2)}, u32[]{:S(2)}) collective-permute-start(bf16[192,384]{1,0:T(8,128)(2,1)S(1)} %add_convert_fusion), channel_id=1, source_target_pairs={{0,8},{2,10},{4,12},{6,14},{8,0},{10,2},{12,4},{14,6},{16,24},{18,... | collective-permute-start | bytes 442376 | tf_op jit(solution)/shard_map/ppermute | solution.py:907
  90.4 1.4 %collective-permute-start.4 = (bf16[256,384]{1,0:T(8,128)(2,1)S(1)}, bf16[256,384]{1,0:T(8,128)(2,1)S(1)}, u32[]{:S(2)}, u32[]{:S(2)}) collective-permute-start(bf16[256,384]{1,0:T(8,128)(2,1)S(1)} %bitcast.39), channel_id=1, source_target_pairs={{0,1},{1,0},{2,3},{3,2},{4,5},{5,4},{6,7},{7,6},{8,9},{9,8},{10,11... | collective-permute-start | bytes 589832 | tf_op jit(solution)/shard_map/ppermute | solution.py:927
  91.8 1.4 %collective-permute-start.5 = (bf16[104,384]{1,0:T(8,128)(2,1)S(1)}, bf16[104,384]{1,0:T(8,128)(2,1)S(1)}, u32[]{:S(2)}, u32[]{:S(2)}) collective-permute-start(bf16[104,384]{1,0:T(8,128)(2,1)S(1)} %reduce_sum.24.near_ref), channel_id=1, source_target_pairs={{0,16},{2,18},{4,20},{6,22},{8,24},{10,26},{12,28},{14,30},{16,0},... | collective-permute-start | bytes 239624 | tf_op jit(solution)/shard_map/ppermute | solution.py:871
  93.2 1.5 %collective-permute-done.7 = bf16[192,384]{1,0:T(8,128)(2,1)S(1)} collective-permute-done((bf16[192,384]{1,0:T(8,128)(2,1)S(1)}, bf16[192,384]{1,0:T(8,128)(2,1)S(1)}, u32[]{:S(2)}, u32[]{:S(2)}) %collective-permute-start.7) | collective-permute-done | bytes 147488 | tf_op jit(solution)/shard_map/ppermute | solution.py:907
  94.8 1.6 %collective-permute-done.4 = bf16[256,384]{1,0:T(8,128)(2,1)S(1)} collective-permute-done((bf16[256,384]{1,0:T(8,128)(2,1)S(1)}, bf16[256,384]{1,0:T(8,128)(2,1)S(1)}, u32[]{:S(2)}, u32[]{:S(2)}) %collective-permute-start.4) | collective-permute-done | bytes 196640 | tf_op jit(solution)/shard_map/ppermute | solution.py:927
  96.4 0.1 slice_bitcast_fusion.1
  96.5 1.1 collective-permute-start.8
  97.6 1.5 %collective-permute-start.9 = (bf16[2,96,384]{2,1,0:T(8,128)(2,1)S(1)}, bf16[2,96,384]{2,1,0:T(8,128)(2,1)S(1)}, u32[]{:S(2)}, u32[]{:S(2)}) collective-permute-start(bf16[2,96,384]{2,1,0:T(8,128)(2,1)S(1)} %get-tuple-element.167), channel_id=1, source_target_pairs={{0,4},{2,6},{4,0},{6,2},{8,12},{10,14},{12,8},{14,10},{16,20},{18,... | collective-permute-start | bytes 442376 | tf_op jit(solution)/shard_map/ppermute | solution.py:903
  99.1 0.9 shard_map.315
  100.0 3.6 %all-to-all-start.2 = ((bf16[8,104,384]{2,1,0:T(8,128)(2,1)}), bf16[8,104,384]{2,1,0:T(8,128)(2,1)S(1)}, u32[]{:S(2)}, u32[]{:S(2)}) async-start(bf16[8,104,384]{2,1,0:T(8,128)(2,1)} %shard_map.315), calls=%async_computation.2 | async-start | bytes 1277952 | tf_op jit(solution)/shard_map/all_to_all | solution.py:863
  103.7 2.0 %collective-permute-start.10 = (bf16[2,2,96,384]{3,2,1,0:T(8,128)(2,1)S(1)}, bf16[2,2,96,384]{3,2,1,0:T(8,128)(2,1)S(1)}, u32[]{:S(2)}, u32[]{:S(2)}) collective-permute-start(bf16[2,2,96,384]{3,2,1,0:T(8,128)(2,1)S(1)} %pad_maximum_fusion.1), channel_id=1, source_target_pairs={{0,4},{2,6},{4,0},{6,2},{8,12},{10,14},{12,8},{14,10},{16,20},{18,... | collective-permute-start | bytes 884744 | tf_op jit(solution)/shard_map/ppermute | solution.py:903
  105.6 1.5 %collective-permute-start.11 = (bf16[2,2,96,384]{3,2,1,0:T(8,128)(2,1)S(1)}, bf16[2,2,96,384]{3,2,1,0:T(8,128)(2,1)S(1)}, u32[]{:S(2)}, u32[]{:S(2)}) collective-permute-start(bf16[2,2,96,384]{3,2,1,0:T(8,128)(2,1)S(1)} %pad_maximum_fusion.2), channel_id=1, source_target_pairs={{0,1},{1,0},{2,3},{3,2},{4,5},{5,4},{6,7},{7,6},{8,9},{9,8},{10,11... | collective-permute-start | bytes 884744 | tf_op jit(solution)/shard_map/ppermute | solution.py:904
  107.1 9.5 %collective-permute-done.10.a2_ref = bf16[2,2,96,384]{3,2,1,0:T(8,128)(2,1)S(1)} collective-permute-done((bf16[2,2,96,384]{3,2,1,0:T(8,128)(2,1)S(1)}, bf16[2,2,96,384]{3,2,1,0:T(8,128)(2,1)S(1)}, u32[]{:S(2)}, u32[]{:S(2)}) %collective-permute-start.10) | collective-permute-done | bytes 294944 | tf_op jit(solution)/shard_map/ppermute | solution.py:903
  116.6 0.1 collective-permute-done.11.b2_ref
  116.7 0.1 shard_map.316.half_ref
  116.8 0.1 collective-permute-start.13
  116.9 0.9 copy-done.7
  117.8 0.9 add_bitcast_fusion
  118.8 1.5 %shard_map.318 = (f32[384,1536]{1,0:T(8,128)}, f32[1536,384]{1,0:T(8,128)}) custom-call(s32[1]{0:T(128)} %bitcast.11.side_ref, bf16[1536,384]{1,0:T(8,128)(2,1)S(1)} %shard_map.316.half_ref), custom_call_target="tpu_custom_call" | custom-call | flops 1000000000 | bytes 1048576 | tf_op jit(solution)/shard_map/pallas_call | solution.py:774
  120.3 1.5 %shard_map.319 = (f32[384,1536]{1,0:T(8,128)}, f32[1536,384]{1,0:T(8,128)}) custom-call(s32[1]{0:T(128)} %bitcast.11.side_ref, bf16[1536,384]{1,0:T(8,128)(2,1)S(1)} %collective-permute-done.13.half_ref, f32[384,1536]{1,0:T(8,128)} %get-tuple-element.157.g1_in, f32[1536,384]{1,0:T(8,128)} %get-tuple-element.158.g2_in), custom_call_target="tpu_custom_call", output_to_operand_aliasing={{0}: (2, {}), {1}: (3, {})} | custom-call | flops 1000000000 | bytes 1048576 | tf_op jit(solution)/shard_map/pallas_call | solution.py:786
  121.8 5.2 %shard_map.317 = (f32[2,384]{1,0:T(2,128)}, f32[6,2,63]{2,1,0:T(2,128)}, f32[384]{0:T(512)}, f32[2304]{0:T(1024)}, f32[1536]{0:T(1024)}, /*index=5*/f32[384]{0:T...) custom-call(s32[1]{0:T(128)} %bitcast.11.side_ref, ...), custom_call_target="tpu_custom_call" | custom-call | flops 4000000000 | bytes 1048576 | tf_op jit(solution)/shard_map/pallas_call | solution.py:643
  (27 shorter events, 0.3 us)
Async XLA Ops:
  0.6 12.4 %collective-permute-start = (bf16[512,384]{1,0:T(8,128)(2,1)}, bf16[512,384]{1,0:T(8,128)(2,1)S(1)}, u32[]{:S(2)}, u32[]{:S(2)}) collective-permute-start(bf16[512,384]{1,0:T(8,128)(2,1)} %bitcast.29), channel_id=1, source_target_pairs={{0,1},{1,0},{2,3},{3,2},{4,5},{5,4},{6,7},{7,6},{8,9},{9,8},{10,11... | collective-permute-start | bytes 1179656 | tf_op jit(solution)/shard_map/ppermute | solution.py:956
  6.3 6.7 %copy-start.2 = (bf16[384,1152]{1,0:T(8,128)(2,1)S(1)}, bf16[384,1152]{1,0:T(8,128)(2,1)}, u32[]{:S(2)}) copy-start(bf16[384,1152]{1,0:T(8,128)(2,1)} %refs_9_.1) | copy-start | bytes 2654212
  6.3 6.7 %copy-start.3 = (bf16[1,512,384]{2,1,0:T(8,128)(2,1)S(1)}, bf16[1,512,384]{2,1,0:T(8,128)(2,1)}, u32[]{:S(2)}) copy-start(bf16[1,512,384]{2,1,0:T(8,128)(2,1)} %param.20) | copy-start | bytes 1179652
  16.7 9.5 %copy-start = (bf16[384,1536]{1,0:T(8,128)(2,1)S(1)}, bf16[384,1536]{1,0:T(8,128)(2,1)}, u32[]{:S(2)}) copy-start(bf16[384,1536]{1,0:T(8,128)(2,1)} %w1_ref.3) | copy-start | bytes 3538948
  16.7 9.5 %copy-start.1 = (bf16[1536,384]{1,0:T(8,128)(2,1)S(1)}, bf16[1536,384]{1,0:T(8,128)(2,1)}, u32[]{:S(2)}) copy-start(bf16[1536,384]{1,0:T(8,128)(2,1)} %w2_ref.3) | copy-start | bytes 3538948
  16.7 9.5 %copy-start.4 = (bf16[1,512,384]{2,1,0:T(8,128)(2,1)S(1)}, bf16[1,512,384]{2,1,0:T(8,128)(2,1)}, u32[]{:S(2)}) copy-start(bf16[1,512,384]{2,1,0:T(8,128)(2,1)} %param.38) | copy-start | bytes 1179652
  16.7 9.5 %copy-start.5 = (bf16[384,384]{1,0:T(8,128)(2,1)S(1)}, bf16[384,384]{1,0:T(8,128)(2,1)}, u32[]{:S(2)}) copy-start(bf16[384,384]{1,0:T(8,128)(2,1)} %wout_ref.3) | copy-start | bytes 884740
  16.7 9.5 %copy-start.6 = (bf16[1,352,384]{2,1,0:T(8,128)(2,1)S(1)}, bf16[1,352,384]{2,1,0:T(8,128)(2,1)}, u32[]{:S(2)}) copy-start(bf16[1,352,384]{2,1,0:T(8,128)(2,1)} %param.39) | copy-start | bytes 811012
  35.0 6.3 %collective-permute-start.1 = (bf16[1536,384]{1,0:T(8,128)(2,1)S(1)}, bf16[1536,384]{1,0:T(8,128)(2,1)S(1)}, u32[]{:S(2)}, u32[]{:S(2)}) collective-permute-start(bf16[1536,384]{1,0:T(8,128)(2,1)S(1)} %get-tuple-element.106), channel_id=1, source_target_pairs={{0,2},{2,0},{4,6},{6,4},{8,10},{10,8},{12,14},{14,12},{16,18},{18,... | collective-permute-start | bytes 3538952 | tf_op jit(solution)/shard_map/ppermute | solution.py:854
  42.5 24.1 %all-to-all-start = ((bf16[8,192,384]{2,1,0:T(8,128)(2,1)}), bf16[8,192,384]{2,1,0:T(8,128)(2,1)S(1)}, u32[]{:S(2)}, u32[]{:S(2)}) async-start(bf16[8,192,384]{2,1,0:T(8,128)(2,1)} %bitcast.36), calls=%async_computation | async-start | bytes 2359296 | tf_op jit(solution)/shard_map/all_to_all | solution.py:863
  66.6 2.1 %collective-permute-start.3 = (bf16[832,384]{1,0:T(8,128)(2,1)S(1)}, bf16[832,384]{1,0:T(8,128)(2,1)S(1)}, u32[]{:S(2)}, u32[]{:S(2)}) collective-permute-start(bf16[832,384]{1,0:T(8,128)(2,1)S(1)} %get-tuple-element.140), channel_id=1, source_target_pairs={{0,2},{2,0},{4,6},{6,4},{8,10},{10,8},{12,14},{14,12},{16,18},{18,... | collective-permute-start | bytes 1916936 | tf_op jit(solution)/shard_map/ppermute | solution.py:854
  69.6 8.1 %copy-start.8 = (bf16[1,512,384]{2,1,0:T(8,128)(2,1)S(1)}, bf16[1,512,384]{2,1,0:T(8,128)(2,1)}, u32[]{:S(2)}) copy-start(bf16[1,512,384]{2,1,0:T(8,128)(2,1)} %get-tuple-element.134) | copy-start | bytes 1179652
  69.6 19.0 %all-to-all-start.1 = ((bf16[8,104,384]{2,1,0:T(8,128)(2,1)}), bf16[8,104,384]{2,1,0:T(8,128)(2,1)S(1)}, u32[]{:S(2)}, u32[]{:S(2)}) async-start(bf16[8,104,384]{2,1,0:T(8,128)(2,1)} %bitcast.37), calls=%async_computation.1 | async-start | bytes 1277952 | tf_op jit(solution)/shard_map/all_to_all | solution.py:863
  75.0 10.3 %collective-permute-start.6 = (bf16[192,384]{1,0:T(8,128)(2,1)S(1)}, bf16[192,384]{1,0:T(8,128)(2,1)S(1)}, u32[]{:S(2)}, u32[]{:S(2)}) collective-permute-start(bf16[192,384]{1,0:T(8,128)(2,1)S(1)} %reduce_sum.25), channel_id=1, source_target_pairs={{0,16},{2,18},{4,20},{6,22},{8,24},{10,26},{12,28},{14,30},{16,0},... | collective-permute-start | bytes 442376 | tf_op jit(solution)/shard_map/ppermute | solution.py:871
  77.7 10.9 %collective-permute-start.2 = (bf16[256,384]{1,0:T(8,128)(2,1)S(1)}, bf16[256,384]{1,0:T(8,128)(2,1)S(1)}, u32[]{:S(2)}, u32[]{:S(2)}) collective-permute-start(bf16[256,384]{1,0:T(8,128)(2,1)S(1)} %get-tuple-element.163), channel_id=1, source_target_pairs={{0,1},{1,0},{2,3},{3,2},{4,5},{5,4},{6,7},{7,6},{8,9},{9,8},{10,11... | collective-permute-start | bytes 589832 | tf_op jit(solution)/shard_map/ppermute | solution.py:927
  88.7 6.1 %collective-permute-start.7 = (bf16[192,384]{1,0:T(8,128)(2,1)S(1)}, bf16[192,384]{1,0:T(8,128)(2,1)S(1)}, u32[]{:S(2)}, u32[]{:S(2)}) collective-permute-start(bf16[192,384]{1,0:T(8,128)(2,1)S(1)} %add_convert_fusion), channel_id=1, source_target_pairs={{0,8},{2,10},{4,12},{6,14},{8,0},{10,2},{12,4},{14,6},{16,24},{18,... | collective-permute-start | bytes 442376 | tf_op jit(solution)/shard_map/ppermute | solution.py:907
  90.4 6.0 %collective-permute-start.4 = (bf16[256,384]{1,0:T(8,128)(2,1)S(1)}, bf16[256,384]{1,0:T(8,128)(2,1)S(1)}, u32[]{:S(2)}, u32[]{:S(2)}) collective-permute-start(bf16[256,384]{1,0:T(8,128)(2,1)S(1)} %bitcast.39), channel_id=1, source_target_pairs={{0,1},{1,0},{2,3},{3,2},{4,5},{5,4},{6,7},{7,6},{8,9},{9,8},{10,11... | collective-permute-start | bytes 589832 | tf_op jit(solution)/shard_map/ppermute | solution.py:927
  91.8 7.3 %collective-permute-start.5 = (bf16[104,384]{1,0:T(8,128)(2,1)S(1)}, bf16[104,384]{1,0:T(8,128)(2,1)S(1)}, u32[]{:S(2)}, u32[]{:S(2)}) collective-permute-start(bf16[104,384]{1,0:T(8,128)(2,1)S(1)} %reduce_sum.24.near_ref), channel_id=1, source_target_pairs={{0,16},{2,18},{4,20},{6,22},{8,24},{10,26},{12,28},{14,30},{16,0},... | collective-permute-start | bytes 239624 | tf_op jit(solution)/shard_map/ppermute | solution.py:871
  96.5 7.1 %collective-permute-start.8 = (bf16[2,96,384]{2,1,0:T(8,128)(2,1)S(1)}, bf16[2,96,384]{2,1,0:T(8,128)(2,1)S(1)}, u32[]{:S(2)}, u32[]{:S(2)}) collective-permute-start(bf16[2,96,384]{2,1,0:T(8,128)(2,1)S(1)} %get-tuple-element.168), channel_id=1, source_target_pairs={{0,1},{1,0},{2,3},{3,2},{4,5},{5,4},{6,7},{7,6},{8,9},{9,8},{10,11... | collective-permute-start | bytes 442376 | tf_op jit(solution)/shard_map/ppermute | solution.py:904
  97.6 6.0 %collective-permute-start.9 = (bf16[2,96,384]{2,1,0:T(8,128)(2,1)S(1)}, bf16[2,96,384]{2,1,0:T(8,128)(2,1)S(1)}, u32[]{:S(2)}, u32[]{:S(2)}) collective-permute-start(bf16[2,96,384]{2,1,0:T(8,128)(2,1)S(1)} %get-tuple-element.167), channel_id=1, source_target_pairs={{0,4},{2,6},{4,0},{6,2},{8,12},{10,14},{12,8},{14,10},{16,20},{18,... | collective-permute-start | bytes 442376 | tf_op jit(solution)/shard_map/ppermute | solution.py:903
  100.0 18.8 %all-to-all-start.2 = ((bf16[8,104,384]{2,1,0:T(8,128)(2,1)}), bf16[8,104,384]{2,1,0:T(8,128)(2,1)S(1)}, u32[]{:S(2)}, u32[]{:S(2)}) async-start(bf16[8,104,384]{2,1,0:T(8,128)(2,1)} %shard_map.315), calls=%async_computation.2 | async-start | bytes 1277952 | tf_op jit(solution)/shard_map/all_to_all | solution.py:863
  103.7 13.0 %collective-permute-start.10 = (bf16[2,2,96,384]{3,2,1,0:T(8,128)(2,1)S(1)}, bf16[2,2,96,384]{3,2,1,0:T(8,128)(2,1)S(1)}, u32[]{:S(2)}, u32[]{:S(2)}) collective-permute-start(bf16[2,2,96,384]{3,2,1,0:T(8,128)(2,1)S(1)} %pad_maximum_fusion.1), channel_id=1, source_target_pairs={{0,4},{2,6},{4,0},{6,2},{8,12},{10,14},{12,8},{14,10},{16,20},{18,... | collective-permute-start | bytes 884744 | tf_op jit(solution)/shard_map/ppermute | solution.py:903
  105.6 11.1 %collective-permute-start.11 = (bf16[2,2,96,384]{3,2,1,0:T(8,128)(2,1)S(1)}, bf16[2,2,96,384]{3,2,1,0:T(8,128)(2,1)S(1)}, u32[]{:S(2)}, u32[]{:S(2)}) collective-permute-start(bf16[2,2,96,384]{3,2,1,0:T(8,128)(2,1)S(1)} %pad_maximum_fusion.2), channel_id=1, source_target_pairs={{0,1},{1,0},{2,3},{3,2},{4,5},{5,4},{6,7},{7,6},{8,9},{9,8},{10,11... | collective-permute-start | bytes 884744 | tf_op jit(solution)/shard_map/ppermute | solution.py:904
  116.7 1.1 copy-start.7
  116.8 3.5 %collective-permute-start.13 = (bf16[1536,384]{1,0:T(8,128)(2,1)S(1)}, bf16[1536,384]{1,0:T(8,128)(2,1)S(1)}, u32[]{:S(2)}, u32[]{:S(2)}) collective-permute-start(bf16[1536,384]{1,0:T(8,128)(2,1)S(1)} %shard_map.316.half_ref), channel_id=1, source_target_pairs={{0,2},{2,0},{4,6},{6,4},{8,10},{10,8},{12,14},{14,12},{16,18},{18,... | collective-permute-start | bytes 3538952 | tf_op jit(solution)/shard_map/ppermute | solution.py:854
  118.8 3.0 %collective-permute-start.12 = (bf16[832,384]{1,0:T(8,128)(2,1)S(1)}, bf16[832,384]{1,0:T(8,128)(2,1)S(1)}, u32[]{:S(2)}, u32[]{:S(2)}) collective-permute-start(bf16[832,384]{1,0:T(8,128)(2,1)S(1)} %bitcast.25), channel_id=1, source_target_pairs={{0,2},{2,0},{4,6},{6,4},{8,10},{10,8},{12,14},{14,12},{16,18},{18,... | collective-permute-start | bytes 1916936 | tf_op jit(solution)/shard_map/ppermute | solution.py:854
